TPU v7x, 32 devices: a whole 2x2x4 slice. The times are simulated.
32 devices in a mesh: stream: 4 (over y, core), lat: 8 (over z, x).
Axes of the slice: x: 2, y: 2, z: 4, core: 2. Of those that a mesh axis runs over, the one named last changes fastest.
Arguments:
- inverse: bfloat16 [16, 4, 4, 512, 512], P('lat', 'stream'), may hold values from -2 to 2
- upwind: bfloat16 [16, 4, 4, 64, 512], P('lat', 'stream'), may hold values from -0.75 to 0.75
- lateral: bfloat16 [16, 4, 4, 64, 512], P('lat', 'stream'), may hold values from -0.375 to 0.375
- inlet_trace: float32 [16, 64, 256], P('lat'), may hold values from -6 to 6
- previous: bfloat16 [16, 4, 4, 512, 256], P('lat', 'stream'), may hold values from -6 to 6
- uptake_rate: float32 [256], replicated, may hold values from 0.3 to 3
- affinity: float32 [256], replicated, may hold values from 0.5 to 4
- flow_order: int32 [16, 4, 4], P('lat', 'stream'), may hold values from 0 to 3, each once within a row
Outputs:
- concentration: bfloat16 [16, 4, 4, 512, 256], P('lat', 'stream')
Inputs may be any that keep to these rules, and one draw needn't show every extreme that they name: `flow_order`: each row of 4 entries lists 0 to 3 once each.
All inputs are finite; a program needn't handle non-finite values.
Results may differ from a plain program's by a relative error of at most 0.002.
Values sent between devices are 32-bit elements; how exact they have to be, the bound alone decides.
No kernel may reach another device: no remote copies, remote signals or barrier semaphores. Data moves between devices by JAX's collectives and lax.ppermute only.
A program may use at most 64 MiB of HBM per device.

v0:
```python
import jax
import jax.numpy as jnp
from jax import lax
from jax.sharding import PartitionSpec as P

NODES_1D = 8
ITERS = 2


HIGHEST = lax.Precision.HIGHEST


def from_behind(value, axis, steps):
    count = lax.axis_size(axis)
    initial, last = (max(0, -steps), min(count, count - steps))
    return lax.ppermute(value, axis, [(source, source + steps) for source in range(initial, last)])


def carried_in(part, axis, combine, identity):
    place = lax.axis_index(axis)
    gathered = jax.tree.map(lambda a: lax.all_gather(a, axis), part)
    state = jax.tree.map(lambda a, e: jnp.zeros_like(a) + jnp.asarray(e, a.dtype), part, identity)

    def one(lap, state):
        return combine(
            state, jax.tree.map(lambda a: lax.dynamic_index_in_dim(a, lap, 0, False), gathered)
        )

    return lax.fori_loop(0, place, one, state)


def lateral_face(nodal_field, per_side):
    leading = nodal_field.shape[:-2]
    tracer_count = nodal_field.shape[-1]
    shaped = nodal_field.reshape(leading + (per_side, per_side, per_side, tracer_count))
    return shaped[..., :, per_side - 1, :, :].reshape(leading + (per_side * per_side, tracer_count))


def carry_through(mapping, trace_in):
    return jnp.einsum("cfk,ckg->cfg", mapping, trace_in, precision=HIGHEST)


def compose(earlier, latter):
    return (
        jnp.einsum("cfk,ckl->cfl", latter[0], earlier[0], precision=HIGHEST),
        carry_through(latter[0], earlier[1]) + latter[1],
    )


def per_device(inverse, upwind, lateral, inlet_trace, previous, uptake_rate, affinity, flow_order):
    col_count = inverse.shape[0]
    row_count = inverse.shape[2]
    node_count = inverse.shape[3]
    face_count = upwind.shape[3]
    per_side = NODES_1D
    columns = jnp.arange(col_count)
    order_local = flow_order[:, 0]
    storage_rank = jnp.argsort(order_local, axis=1)
    inverse_local = inverse[:, 0]
    upwind_local = upwind[:, 0]
    lateral_local = lateral[:, 0]
    unit_maps = jnp.broadcast_to(
        jnp.eye(face_count, dtype=jnp.float32), (col_count, face_count, face_count)
    )
    current = previous[:, 0].astype(jnp.float32)
    for sweep_index in range(ITERS):
        lagged = current
        traces = lateral_face(lagged, per_side)
        arrived = from_behind(traces[-1:], "lat", 1)
        lateral_in = jnp.concatenate([arrived, traces[:-1]], axis=0)

        def element_step(carried, position):
            inflow, mapping = carried
            chosen = lax.dynamic_index_in_dim(order_local, position, 1, False)
            matrix = inverse_local[columns, chosen].astype(jnp.float32)
            up_part = upwind_local[columns, chosen].astype(jnp.float32)
            side_part = lateral_local[columns, chosen].astype(jnp.float32)
            nodal_lag = lagged[columns, chosen]
            source = uptake_rate * nodal_lag / (1.0 + affinity * jnp.abs(nodal_lag))
            right_side = source + jnp.einsum(
                "cfn,cfg->cng", side_part, lateral_in[columns, chosen], precision=HIGHEST
            )
            right_side = right_side + jnp.einsum("cfn,cfg->cng", up_part, inflow, precision=HIGHEST)
            free_part = jnp.einsum("cmn,cng->cmg", matrix, right_side, precision=HIGHEST)
            lifted = jnp.einsum("cfn,cfk->cnk", up_part, mapping, precision=HIGHEST)
            response = jnp.einsum("cmn,cnk->cmk", matrix, lifted, precision=HIGHEST)
            return (
                (
                    free_part[:, node_count - face_count :, :],
                    response[:, node_count - face_count :, :],
                ),
                (free_part, response),
            )

        initial = (jnp.zeros_like(inlet_trace), unit_maps)
        (offset, transfer_map), (free_all, response_all) = lax.scan(
            element_step, initial, jnp.arange(row_count)
        )
        identity = (unit_maps, jnp.zeros_like(offset))
        before_map, before_offset = carried_in((transfer_map, offset), "stream", compose, identity)
        entering = carry_through(before_map, inlet_trace) + before_offset
        solved = free_all + jnp.einsum("rcmk,ckg->rcmg", response_all, entering, precision=HIGHEST)
        placed = jnp.moveaxis(solved, 0, 1)
        current = jnp.take_along_axis(placed, storage_rank[:, :, None, None], axis=1)
    return current[:, None].astype(jnp.bfloat16)


def solution(mesh):
    placed = (
        P("lat", "stream", None, None, None),
        P("lat", "stream", None, None, None),
        P("lat", "stream", None, None, None),
        P("lat", None, None),
        P("lat", "stream", None, None, None),
        P(),
        P(),
        P("lat", "stream", None),
    )
    return jax.shard_map(
        per_device,
        mesh=mesh,
        in_specs=placed,
        out_specs=P("lat", "stream", None, None, None),
        check_vma=False,
    )
```

profile of v0, /device:TPU:13, one launch (start us, length us, event | category | flops | bytes accessed | tf_op | source)
XLA Modules:
  0.0 273.8 jit_solution(4226159327153104029)
XLA Ops:
  0.0 4.1 %bitcast_convert_fusion = (f32[2,1,4,512,256]{4,3,2,0,1:T(8,128)S(1)}, f32[2,4,512,256]{3,2,1,0:T(8,128)}) fusion(bf16[2,1,4,512,256]{4,3,2,1,0:T(8,128)(2,1)} %param.22), kind=kLoop, calls=%fused_computation.56 | loop fusion | flops 1048576 | bytes 10485760 | tf_op jit(solution)/shard_map/convert_element_type | solution.py:65
  4.2 3.1 %collective-permute-start = (f32[1,4,64,256]{3,2,1,0:T(8,128)S(1)}, f32[1,4,64,256]{3,2,1,0:T(8,128)S(1)}, u32[]{:S(2)}, u32[]{:S(2)}) collective-permute-start(f32[1,4,64,256]{3,2,1,0:T(8,128)S(1)} %get-tuple-element.514), channel_id=1, source_target_pairs={{0,1},{1,2},{2,3},{3,4},{4,5},{5,6},{6,7},{8,9},{9,10},{10,11},{11... | collective-permute-start | bytes 786440 | tf_op jit(solution)/shard_map/ppermute | solution.py:16
  9.0 5.2 %collective-permute-done = f32[1,4,64,256]{3,2,1,0:T(8,128)S(1)} collective-permute-done((f32[1,4,64,256]{3,2,1,0:T(8,128)S(1)}, f32[1,4,64,256]{3,2,1,0:T(8,128)S(1)}, u32[]{:S(2)}, u32[]{:S(2)}) %collective-permute-start) | collective-permute-done | bytes 262176 | tf_op jit(solution)/shard_map/ppermute | solution.py:16
  19.3 85.4 %while.60 = (s32[]{:T(128)}, f32[2,64,256]{2,1,0:T(8,128)S(1)}, f32[2,64,64]{1,2,0:T(8,128)}, f32[4,2,512,256]{2,3,0,1:T(8,128)}, f32[4,2,512,64]{2,3,0,1:T(8,12...) while((s32[]{:T(128)}, f32[2,64,256]{2,1,0:T(8,128)S(1)}, ...), condition=%wide.region_1.2_spmd.clone, body=%wide.region_0.0_spmd.clone.sunk | while | flops 2468085760 | bytes 19631592 | solution.py:96
  22.0 2.8 %gather_fusion.3 = f32[2,512,256]{2,1,0:T(8,128)S(1)} fusion(f32[2,4,512,256]{3,2,1,0:T(8,128)} %get-tuple-element.815, s32[2]{0:T(128)S(1)} %fusion.125), kind=kCustom, calls=%fused_computation.1.clone.clone.1 | custom fusion | bytes 2097168 | tf_op jit(solution)/shard_map/while/body/eval_jaxpr/gather | solution.py:78
  31.8 2.8 %gather_fusion = bf16[2,512,512]{2,1,0:T(8,128)(2,1)S(1)} fusion(bf16[2,4,512,512]{3,2,1,0:T(8,128)(2,1)} %get-tuple-element.813, s32[2]{0:T(128)S(1)} %fusion.125), kind=kCustom, calls=%fused_computation.clone.clone.1 | custom fusion | bytes 2097168 | tf_op jit(solution)/shard_map/while/body/eval_jaxpr/gather | solution.py:75
  43.4 2.8 %gather_fusion.3 = f32[2,512,256]{2,1,0:T(8,128)S(1)} fusion(f32[2,4,512,256]{3,2,1,0:T(8,128)} %get-tuple-element.815, s32[2]{0:T(128)S(1)} %fusion.125), kind=kCustom, calls=%fused_computation.1.clone.clone.1 | custom fusion | bytes 2097168 | tf_op jit(solution)/shard_map/while/body/eval_jaxpr/gather | solution.py:78
  53.1 2.8 %gather_fusion = bf16[2,512,512]{2,1,0:T(8,128)(2,1)S(1)} fusion(bf16[2,4,512,512]{3,2,1,0:T(8,128)(2,1)} %get-tuple-element.813, s32[2]{0:T(128)S(1)} %fusion.125), kind=kCustom, calls=%fused_computation.clone.clone.1 | custom fusion | bytes 2097168 | tf_op jit(solution)/shard_map/while/body/eval_jaxpr/gather | solution.py:75
  64.7 2.8 %gather_fusion.3 = f32[2,512,256]{2,1,0:T(8,128)S(1)} fusion(f32[2,4,512,256]{3,2,1,0:T(8,128)} %get-tuple-element.815, s32[2]{0:T(128)S(1)} %fusion.125), kind=kCustom, calls=%fused_computation.1.clone.clone.1 | custom fusion | bytes 2097168 | tf_op jit(solution)/shard_map/while/body/eval_jaxpr/gather | solution.py:78
  74.4 2.8 %gather_fusion = bf16[2,512,512]{2,1,0:T(8,128)(2,1)S(1)} fusion(bf16[2,4,512,512]{3,2,1,0:T(8,128)(2,1)} %get-tuple-element.813, s32[2]{0:T(128)S(1)} %fusion.125), kind=kCustom, calls=%fused_computation.clone.clone.1 | custom fusion | bytes 2097168 | tf_op jit(solution)/shard_map/while/body/eval_jaxpr/gather | solution.py:75
  86.0 2.8 %gather_fusion.3 = f32[2,512,256]{2,1,0:T(8,128)S(1)} fusion(f32[2,4,512,256]{3,2,1,0:T(8,128)} %get-tuple-element.815, s32[2]{0:T(128)S(1)} %fusion.125), kind=kCustom, calls=%fused_computation.1.clone.clone.1 | custom fusion | bytes 2097168 | tf_op jit(solution)/shard_map/while/body/eval_jaxpr/gather | solution.py:78
  95.7 2.8 %gather_fusion = bf16[2,512,512]{2,1,0:T(8,128)(2,1)S(1)} fusion(bf16[2,4,512,512]{3,2,1,0:T(8,128)(2,1)} %get-tuple-element.813, s32[2]{0:T(128)S(1)} %fusion.125), kind=kCustom, calls=%fused_computation.clone.clone.1 | custom fusion | bytes 2097168 | tf_op jit(solution)/shard_map/while/body/eval_jaxpr/gather | solution.py:75
  104.7 8.0 %all-gather.1 = f32[8,64,256]{2,1,0:T(8,128)S(1)} all-gather(f32[2,64,256]{2,1,0:T(8,128)S(1)} %get-tuple-element.237), channel_id=3, replica_groups=mesh['stream'=4,'lat'=8] {'stream'}, dimensions={0}, use_global_device_ids=true | all-gather | bytes 655360 | tf_op jit(solution)/shard_map/all_gather | solution.py:21
  113.6 5.9 %all-gather = f32[8,64,64]{2,1,0:T(8,128)S(1)} all-gather(f32[2,64,64]{2,1,0:T(8,128)S(1)} %copy.51), channel_id=2, replica_groups=mesh['stream'=4,'lat'=8] {'stream'}, dimensions={0}, use_global_device_ids=true | all-gather | bytes 163840 | tf_op jit(solution)/shard_map/all_gather | solution.py:21
  122.2 3.5 %fusion.35 = f32[2,256,4,512]{3,1,2,0:T(8,128)S(1)} fusion(f32[2,64,256,1]{2,1,3,0:T(8,128)S(1)} %fusion.28, f32[4,2,512,64]{2,3,0,1:T(8,128)S(1)} %copy-done.4), kind=kOutput, calls=%fused_computation.78 | convolution fusion | flops 805306368 | bytes 5373952 | tf_op jit(solution)/shard_map/rcmk,ckg->rcmg/dot_general | solution.py:102
  125.7 3.0 %fusion.25 = f32[2,4,512,256]{2,3,1,0:T(8,128)} fusion(f32[4,2,512,256]{2,3,0,1:T(8,128)S(1)} %copy-done.2, f32[2,256,4,512]{3,1,2,0:T(8,128)S(1)} %fusion.35), kind=kLoop, calls=%fused_computation.53 | loop fusion | flops 1048576 | bytes 12582912 | tf_op jit(solution)/shard_map/transpose | solution.py:103
  128.7 5.0 %gather_fusion.10 = f32[8,512,256]{1,2,0:T(8,128)} fusion(f32[2,4,512,256]{2,3,1,0:T(8,128)} %fusion.25, s32[8]{0:T(128)S(1)} %reshape.181), kind=kCustom, calls=%fused_computation.5.clone | custom fusion | bytes 8388672 | tf_op jit(solution)/shard_map/jit(take_along_axis)/gather | solution.py:104
  133.7 5.3 %copy.55 = f32[2,4,512,256]{3,2,1,0:T(8,128)} copy(f32[2,4,512,256]{2,3,1,0:T(8,128)} %bitcast.212) | data formatting | bytes 8388608 | tf_op jit(solution)/shard_map/jit(take_along_axis)/gather | solution.py:104
  146.1 8.6 %collective-permute-done.1 = f32[1,4,64,256]{3,2,1,0:T(8,128)S(1)} collective-permute-done((f32[1,4,64,256]{3,2,1,0:T(8,128)S(1)}, f32[1,4,64,256]{3,2,1,0:T(8,128)S(1)}, u32[]{:S(2)}, u32[]{:S(2)}) %collective-permute-start.1) | collective-permute-done | bytes 262176 | tf_op jit(solution)/shard_map/ppermute | solution.py:16
  159.9 85.5 %while.61 = (s32[]{:T(128)}, f32[2,64,256]{2,1,0:T(8,128)S(1)}, f32[2,64,64]{1,2,0:T(8,128)}, f32[4,2,512,256]{2,3,0,1:T(8,128)}, f32[4,2,512,64]{2,3,0,1:T(8,12...) while((s32[]{:T(128)}, f32[2,64,256]{2,1,0:T(8,128)S(1)}, ...), condition=%wide.region_6.8_spmd.clone, body=%wide.region_5.7_spmd.clone.sunk | while | flops 2468085760 | bytes 19631592 | solution.py:96
  162.6 2.8 %gather_fusion.8 = f32[2,512,256]{2,1,0:T(8,128)S(1)} fusion(f32[2,4,512,256]{3,2,1,0:T(8,128)} %get-tuple-element.893, s32[2]{0:T(128)S(1)} %fusion.138), kind=kCustom, calls=%fused_computation.7.clone.clone.1 | custom fusion | bytes 2097168 | tf_op jit(solution)/shard_map/while/body/eval_jaxpr/gather | solution.py:78
  172.3 2.8 %gather_fusion.5 = bf16[2,512,512]{2,1,0:T(8,128)(2,1)S(1)} fusion(bf16[2,4,512,512]{3,2,1,0:T(8,128)(2,1)} %get-tuple-element.891, s32[2]{0:T(128)S(1)} %fusion.138), kind=kCustom, calls=%fused_computation.6.clone.clone.1 | custom fusion | bytes 2097168 | tf_op jit(solution)/shard_map/while/body/eval_jaxpr/gather | solution.py:75
  184.0 2.8 %gather_fusion.8 = f32[2,512,256]{2,1,0:T(8,128)S(1)} fusion(f32[2,4,512,256]{3,2,1,0:T(8,128)} %get-tuple-element.893, s32[2]{0:T(128)S(1)} %fusion.138), kind=kCustom, calls=%fused_computation.7.clone.clone.1 | custom fusion | bytes 2097168 | tf_op jit(solution)/shard_map/while/body/eval_jaxpr/gather | solution.py:78
  193.7 2.8 %gather_fusion.5 = bf16[2,512,512]{2,1,0:T(8,128)(2,1)S(1)} fusion(bf16[2,4,512,512]{3,2,1,0:T(8,128)(2,1)} %get-tuple-element.891, s32[2]{0:T(128)S(1)} %fusion.138), kind=kCustom, calls=%fused_computation.6.clone.clone.1 | custom fusion | bytes 2097168 | tf_op jit(solution)/shard_map/while/body/eval_jaxpr/gather | solution.py:75
  205.3 2.8 %gather_fusion.8 = f32[2,512,256]{2,1,0:T(8,128)S(1)} fusion(f32[2,4,512,256]{3,2,1,0:T(8,128)} %get-tuple-element.893, s32[2]{0:T(128)S(1)} %fusion.138), kind=kCustom, calls=%fused_computation.7.clone.clone.1 | custom fusion | bytes 2097168 | tf_op jit(solution)/shard_map/while/body/eval_jaxpr/gather | solution.py:78
  215.0 2.8 %gather_fusion.5 = bf16[2,512,512]{2,1,0:T(8,128)(2,1)S(1)} fusion(bf16[2,4,512,512]{3,2,1,0:T(8,128)(2,1)} %get-tuple-element.891, s32[2]{0:T(128)S(1)} %fusion.138), kind=kCustom, calls=%fused_computation.6.clone.clone.1 | custom fusion | bytes 2097168 | tf_op jit(solution)/shard_map/while/body/eval_jaxpr/gather | solution.py:75
  226.7 2.8 %gather_fusion.8 = f32[2,512,256]{2,1,0:T(8,128)S(1)} fusion(f32[2,4,512,256]{3,2,1,0:T(8,128)} %get-tuple-element.893, s32[2]{0:T(128)S(1)} %fusion.138), kind=kCustom, calls=%fused_computation.7.clone.clone.1 | custom fusion | bytes 2097168 | tf_op jit(solution)/shard_map/while/body/eval_jaxpr/gather | solution.py:78
  236.4 2.8 %gather_fusion.5 = bf16[2,512,512]{2,1,0:T(8,128)(2,1)S(1)} fusion(bf16[2,4,512,512]{3,2,1,0:T(8,128)(2,1)} %get-tuple-element.891, s32[2]{0:T(128)S(1)} %fusion.138), kind=kCustom, calls=%fused_computation.6.clone.clone.1 | custom fusion | bytes 2097168 | tf_op jit(solution)/shard_map/while/body/eval_jaxpr/gather | solution.py:75
  245.3 7.4 %all-gather.3 = f32[8,64,256]{2,1,0:T(8,128)S(1)} all-gather(f32[2,64,256]{2,1,0:T(8,128)S(1)} %get-tuple-element.244), channel_id=5, replica_groups=mesh['stream'=4,'lat'=8] {'stream'}, dimensions={0}, use_global_device_ids=true | all-gather | bytes 655360 | tf_op jit(solution)/shard_map/all_gather | solution.py:21
  253.7 5.9 %all-gather.2 = f32[8,64,64]{2,1,0:T(8,128)S(1)} all-gather(f32[2,64,64]{2,1,0:T(8,128)S(1)} %copy.59), channel_id=4, replica_groups=mesh['stream'=4,'lat'=8] {'stream'}, dimensions={0}, use_global_device_ids=true | all-gather | bytes 163840 | tf_op jit(solution)/shard_map/all_gather | solution.py:21
  262.2 3.5 %fusion.36 = f32[2,256,4,512]{3,1,2,0:T(8,128)S(1)} fusion(f32[2,64,256,1]{2,1,3,0:T(8,128)S(1)} %fusion.27, f32[4,2,512,64]{2,3,0,1:T(8,128)S(1)} %copy-done.5), kind=kOutput, calls=%fused_computation.79 | convolution fusion | flops 805306368 | bytes 5373952 | tf_op jit(solution)/shard_map/rcmk,ckg->rcmg/dot_general | solution.py:102
  268.9 2.8 %copy.63 = bf16[2,4,512,256]{3,2,1,0:T(8,128)(2,1)S(1)} copy(bf16[2,4,512,256]{2,3,1,0:T(8,128)(2,1)} %bitcast.213) | data formatting | bytes 4194304 | tf_op jit(solution)/shard_map/jit(take_along_axis)/gather | solution.py:104
  (224 shorter events, 143.1 us)
Async XLA Ops:
  0.0 121.9 %copy-start = (f32[2,64,256]{2,1,0:T(8,128)S(1)}, f32[2,64,256]{2,1,0:T(8,128)}, u32[]{:S(2)}) copy-start(f32[2,64,256]{2,1,0:T(8,128)} %param.21) | copy-start | bytes 393220
  0.0 7.3 %copy-start.8 = (s32[2,1,4]{2,1,0:T(1,128)S(1)}, s32[2,1,4]{2,1,0:T(1,128)}, u32[]{:S(2)}) copy-start(s32[2,1,4]{2,1,0:T(1,128)} %param.25) | copy-start | bytes 100
  4.2 10.0 %collective-permute-start = (f32[1,4,64,256]{3,2,1,0:T(8,128)S(1)}, f32[1,4,64,256]{3,2,1,0:T(8,128)S(1)}, u32[]{:S(2)}, u32[]{:S(2)}) collective-permute-start(f32[1,4,64,256]{3,2,1,0:T(8,128)S(1)} %get-tuple-element.514), channel_id=1, source_target_pairs={{0,1},{1,2},{2,3},{3,4},{4,5},{5,6},{6,7},{8,9},{9,10},{10,11},{11... | collective-permute-start | bytes 786440 | tf_op jit(solution)/shard_map/ppermute | solution.py:16
  8.2 11.2 %copy-start.6 = (f32[64,64]{0,1:T(8,128)}, f32[64,64]{0,1:T(8,128)S(1)}, u32[]{:S(2)}) copy-start(f32[64,64]{0,1:T(8,128)S(1)} %fusion.30) | copy-start | bytes 49156
  19.3 2.7 copy-start.11
  35.6 5.0 %copy-start.12 = (s32[4]{0:T(128)S(1)}, s32[4]{0:T(128)}, u32[]{:S(2)}) copy-start(s32[4]{0:T(128)} %copy-done.11) | copy-start | bytes 52 | tf_op jit(solution)/shard_map/while
  40.7 2.7 copy-start.11
  57.0 5.0 %copy-start.12 = (s32[4]{0:T(128)S(1)}, s32[4]{0:T(128)}, u32[]{:S(2)}) copy-start(s32[4]{0:T(128)} %copy-done.11) | copy-start | bytes 52 | tf_op jit(solution)/shard_map/while
  62.0 2.7 copy-start.11
  78.3 5.0 %copy-start.12 = (s32[4]{0:T(128)S(1)}, s32[4]{0:T(128)}, u32[]{:S(2)}) copy-start(s32[4]{0:T(128)} %copy-done.11) | copy-start | bytes 52 | tf_op jit(solution)/shard_map/while
  83.3 2.7 copy-start.11
  99.6 5.1 %copy-start.12 = (s32[4]{0:T(128)S(1)}, s32[4]{0:T(128)}, u32[]{:S(2)}) copy-start(s32[4]{0:T(128)} %copy-done.11) | copy-start | bytes 52 | tf_op jit(solution)/shard_map/while
  104.7 17.5 %copy-start.4 = (f32[4,2,512,64]{2,3,0,1:T(8,128)S(1)}, f32[4,2,512,64]{2,3,0,1:T(8,128)}, u32[]{:S(2)}) copy-start(f32[4,2,512,64]{2,3,0,1:T(8,128)} %get-tuple-element.240) | copy-start | bytes 3145732
  121.9 3.8 %copy-start.2 = (f32[4,2,512,256]{2,3,0,1:T(8,128)S(1)}, f32[4,2,512,256]{2,3,0,1:T(8,128)}, u32[]{:S(2)}) copy-start(f32[4,2,512,256]{2,3,0,1:T(8,128)} %get-tuple-element.235) | copy-start | bytes 12582916
  139.0 16.6 %copy-start.7 = (f32[64,64]{0,1:T(8,128)S(1)}, f32[64,64]{0,1:T(8,128)}, u32[]{:S(2)}) copy-start(f32[64,64]{0,1:T(8,128)} %copy-done.6) | copy-start | bytes 49156
  141.7 2.0 copy-start.1
  143.7 11.0 %collective-permute-start.1 = (f32[1,4,64,256]{3,2,1,0:T(8,128)S(1)}, f32[1,4,64,256]{3,2,1,0:T(8,128)S(1)}, u32[]{:S(2)}, u32[]{:S(2)}) collective-permute-start(f32[1,4,64,256]{3,2,1,0:T(8,128)S(1)} %get-tuple-element.512), channel_id=1, source_target_pairs={{0,1},{1,2},{2,3},{3,4},{4,5},{5,6},{6,7},{8,9},{9,10},{10,11},{11... | collective-permute-start | bytes 786440 | tf_op jit(solution)/shard_map/ppermute | solution.py:16
  159.9 2.7 copy-start.9
  176.2 5.0 %copy-start.10 = (s32[4]{0:T(128)S(1)}, s32[4]{0:T(128)}, u32[]{:S(2)}) copy-start(s32[4]{0:T(128)} %copy-done.9) | copy-start | bytes 52 | tf_op jit(solution)/shard_map/while
  181.2 2.7 copy-start.9
  197.6 5.0 %copy-start.10 = (s32[4]{0:T(128)S(1)}, s32[4]{0:T(128)}, u32[]{:S(2)}) copy-start(s32[4]{0:T(128)} %copy-done.9) | copy-start | bytes 52 | tf_op jit(solution)/shard_map/while
  202.6 2.7 copy-start.9
  218.9 5.0 %copy-start.10 = (s32[4]{0:T(128)S(1)}, s32[4]{0:T(128)}, u32[]{:S(2)}) copy-start(s32[4]{0:T(128)} %copy-done.9) | copy-start | bytes 52 | tf_op jit(solution)/shard_map/while
  223.9 2.7 copy-start.9
  240.3 5.1 %copy-start.10 = (s32[4]{0:T(128)S(1)}, s32[4]{0:T(128)}, u32[]{:S(2)}) copy-start(s32[4]{0:T(128)} %copy-done.9) | copy-start | bytes 52 | tf_op jit(solution)/shard_map/while
  245.3 16.9 %copy-start.5 = (f32[4,2,512,64]{2,3,0,1:T(8,128)S(1)}, f32[4,2,512,64]{2,3,0,1:T(8,128)}, u32[]{:S(2)}) copy-start(f32[4,2,512,64]{2,3,0,1:T(8,128)} %get-tuple-element.247) | copy-start | bytes 3145732
  261.9 3.8 %copy-start.3 = (f32[4,2,512,256]{2,3,0,1:T(8,128)S(1)}, f32[4,2,512,256]{2,3,0,1:T(8,128)}, u32[]{:S(2)}) copy-start(f32[4,2,512,256]{2,3,0,1:T(8,128)} %get-tuple-element.242) | copy-start | bytes 12582916
where the time goes:
time: 277 us; the launch traced here: 274 us
  local copies, waits for them, and re-layouts  136 us (49%)
  matrix products  58.4 us (21%)
  blocking collectives  27.2 us (10%)
  loops' own time  17.4 us (6%)
  other arithmetic  15.6 us (6%)
  waiting for transfers between devices  13.8 us (5%)
  starting transfers between devices  5.52 us (2%)
    all_gather x4, blocking collectives, carried_in(): gathered = jax.tree.map(lambda a: lax.all_gather(a, axis), part)  27.2 us
    gather x8, local copies, waits for them, and re-layouts, element_step(): matrix = inverse_local[columns, chosen].astype(jnp.float32)  22.4 us
    gather x8, local copies, waits for them, and re-layouts, element_step(): nodal_lag = lagged[columns, chosen]  22.4 us
    another operation x2, loops' own time, per_device(): lax.scan(element_step, initial, jnp.arange(row_count))  17.1 us
    gather x5, local copies, waits for them, and re-layouts, per_device(): jnp.take_along_axis(placed, storage_rank[:, :, None, None], axis=1)  15.1 us
    dot_general x8, matrix products, element_step(): response = jnp.einsum('cmn,cnk->cmk', matrix, lifted, precision=HIGHEST)  14.2 us
    ppermute x2, waiting for transfers between devices, from_behind(): lax.ppermute(value, axis, [(source, source + steps) for source in range(i...  13.8 us
    gather x8, local copies, waits for them, and re-layouts, element_step(): side_part = lateral_local[columns, chosen].astype(jnp.float32)  12.8 us
  transfers between devices with their start and end apart: 2, of which 2 were waited for; matrix products, arithmetic and copies ran while one was open for 1% of the time, Pallas kernels for 0%

commit v1 on v0

v1 whole, which is shorter than its diff:
```python
import functools

import jax
import jax.numpy as jnp
from jax import lax
from jax.experimental import pallas as pl
from jax.experimental.pallas import tpu as pltpu
from jax.sharding import PartitionSpec as P

NODES_1D = 8
F32 = jnp.float32
BF16 = jnp.bfloat16
MIB = 1 << 20


def from_behind(value, axis, steps):
    count = lax.axis_size(axis)
    initial, last = (max(0, -steps), min(count, count - steps))
    return lax.ppermute(value, axis, [(source, source + steps) for source in range(initial, last)])


def split(x):
    high = x.astype(BF16)
    return high, (x - high.astype(F32)).astype(BF16)


def dot(x, y):
    return jnp.dot(x, y, preferred_element_type=F32)


def dot_split(x, y):
    return dot(x[0], y[0]) + (dot(x[0], y[1]) + dot(x[1], y[0]))


def langmuir(lagged, rate, affinity):
    below = 1.0 + affinity * jnp.abs(lagged)
    guess = pl.reciprocal(below, approx=True)
    guess = guess * (2.0 - below * guess)
    guess = guess * (2.0 - below * guess)
    return rate * lagged * guess


def lateral_rows(field, per_side):
    plane = per_side * per_side
    return jnp.concatenate(
        [field[a * plane + plane - per_side : (a + 1) * plane] for a in range(per_side)], axis=0
    )


def traces_kernel(per_side, prev, out):
    plane = per_side * per_side
    for c in range(out.shape[0]):
        for j in range(out.shape[1]):
            for a in range(per_side):
                rows = prev[c, j, a].astype(F32)
                out[c, j, a * per_side : (a + 1) * per_side] = rows[rows.shape[0] - per_side :]


def first_kernel(
    per_side, order, inv_hbm, up_hbm, lat_hbm, prev_hbm, rate, affinity,
    inv, maps, free, side_maps, tails, rows_high, rows_low, block_map,
    faces, lagged, tail_scratch, row_scratch, sems,
):
    cols, count = order.shape[0], order.shape[2]
    face = up_hbm.shape[3]
    nodes = inv.shape[1]

    def copies(i):
        c, p = i // count, i % count
        j = order[c, 0, p]
        return (
            pltpu.make_async_copy(inv_hbm.at[c, 0, j], inv.at[i], sems.at[0, i]),
            pltpu.make_async_copy(up_hbm.at[c, 0, j], faces.at[i, pl.ds(0, face)], sems.at[1, i]),
            pltpu.make_async_copy(lat_hbm.at[c, 0, j], faces.at[i, pl.ds(face, face)], sems.at[2, i]),
            pltpu.make_async_copy(prev_hbm.at[c, 0, j], lagged.at[i], sems.at[3, i]),
        )

    for i in range(cols * count):
        for copy in copies(i):
            copy.start()

    def element(i, _):
        for copy in copies(i):
            copy.wait()
        matrix = inv[i]
        both = lax.dot_general(matrix, faces[i], (((1,), (1,)), ((), ())), preferred_element_type=F32)
        high, low = split(both)
        maps[i] = jnp.concatenate([high, high, low], axis=1)
        tail = both[nodes - face :]
        tail_scratch[i] = tail
        side = lateral_rows(both, per_side)
        s_high, s_low = split(side)
        side_maps[i] = jnp.concatenate([s_high, s_high, s_low], axis=1)
        source = langmuir(lagged[i].astype(F32), rate[...], affinity[...])
        s_high, s_low = split(source)
        free[i] = dot(matrix, s_high) + dot(matrix, s_low)
        return 0

    lax.fori_loop(0, cols * count, element, 0)

    wide = count * face
    row_id = lax.broadcasted_iota(jnp.int32, (face, wide), 0)
    lane_id = lax.broadcasted_iota(jnp.int32, (face, wide), 1)
    for p in range(count):
        for c in range(cols):
            i = c * count + p
            unit = jnp.where(lane_id == row_id + p * face, 1.0, 0.0)
            if p == 0:
                row = unit
            else:
                row = row_scratch[c] + unit
            r = split(row)
            rows_high[c, pl.ds(p * face, face)] = r[0]
            rows_low[c, pl.ds(p * face, face)] = r[1]
            step = split(tail_scratch[i][:, :face])
            row_scratch[c] = dot_split(step, r)
            tails[i] = tail_scratch[i]
    for c in range(cols):
        r = split(row_scratch[c])
        rows_high[c, pl.ds(count * face, face)] = r[0]
        rows_low[c, pl.ds(count * face, face)] = r[1]
        block_map[c] = row_scratch[c][:, :face]


def side_kernel(
    with_map, order, arrived, local, free, tails, rows_high, rows_low, block_map,
    sides, ends, message, high, low,
):
    cols, count = order.shape[0], order.shape[2]
    nodes, tracers = free.shape[1:]
    face = tails.shape[1]
    for c in range(cols):
        for p in range(count):
            i = c * count + p
            j = order[c, 0, p]
            side = arrived[j] if c == 0 else local[c - 1, j]
            s = split(side)
            sides[i, 0] = s[0]
            sides[i, 1] = s[1]
            tail = split(tails[i][:, face:])
            ends[i] = free[i, pl.ds(nodes - face, face)] + dot_split(tail, s)
    for c in range(cols):
        for p in range(count - 1):
            e = split(ends[c * count + p])
            high[c, pl.ds(p * face, face)] = e[0]
            low[c, pl.ds(p * face, face)] = e[1]
        last = pl.ds(count * face, face)
        row = (rows_high[c, last][:, face:], rows_low[c, last][:, face:])
        offset = ends[c * count + count - 1] + dot_split(row, (high[c], low[c]))
        message[c, :, pl.ds(0, tracers)] = offset
        if with_map:
            message[c, :, pl.ds(tracers, face)] = block_map[c]


def enter(place, inlet, gathered, mapped, rows_high, rows_low, sides, ends, stack, high, low):
    cols, face, tracers = inlet.shape
    count = ends.shape[0] // cols
    for c in range(cols):
        def block(k, entering):
            m = split(mapped[k, c, :, pl.ds(tracers, face)])
            return dot_split(m, split(entering)) + gathered[k, c, :, pl.ds(0, tracers)]

        entering = lax.fori_loop(0, place[0], block, inlet[c])
        e = split(entering)
        high[c, pl.ds(0, face)] = e[0]
        low[c, pl.ds(0, face)] = e[1]
        for p in range(count - 1):
            e = split(ends[c * count + p])
            high[c, pl.ds((p + 1) * face, face)] = e[0]
            low[c, pl.ds((p + 1) * face, face)] = e[1]
        span = pl.ds(0, count * face)
        inflow = dot_split((rows_high[c, span], rows_low[c, span]), (high[c], low[c]))
        for p in range(count):
            i = c * count + p
            f = split(inflow[p * face : (p + 1) * face])
            stack[i, pl.ds(0, face)] = f[0]
            stack[i, pl.ds(face, face)] = sides[i, 0]
            stack[i, pl.ds(2 * face, face)] = f[1]
            stack[i, pl.ds(3 * face, face)] = sides[i, 1]
            stack[i, pl.ds(4 * face, face)] = f[0]
            stack[i, pl.ds(5 * face, face)] = sides[i, 0]


def trace_kernel(
    per_side, order, place, inlet, gathered, rows_high, rows_low, sides, ends, free, side_maps,
    stack, trace, high, low,
):
    enter(place, inlet, gathered, gathered, rows_high, rows_low, sides, ends, stack, high, low)
    cols, count = order.shape[0], order.shape[2]
    for p in range(count):
        i = (cols - 1) * count + p
        trace[order[cols - 1, 0, p]] = lateral_rows(free.at[i], per_side) + dot(side_maps[i], stack[i])


def second_kernel(per_side, order, inv, maps, free, stack, rate, affinity, free_out, local):
    cols, count = order.shape[0], order.shape[2]

    def element(i, _):
        swept = free[i] + dot(maps[i], stack[i])
        local[i // count, order[i // count, 0, i % count]] = lateral_rows(swept, per_side)
        s_high, s_low = split(langmuir(swept, rate[...], affinity[...]))
        matrix = inv[i]
        free_out[i] = dot(matrix, s_high) + dot(matrix, s_low)
        return 0

    lax.fori_loop(0, cols * count, element, 0)


def last_kernel(
    order, place, inlet, gathered, mapped, rows_high, rows_low, sides, ends, free, maps,
    out_hbm, stack, high, low, staged, sems,
):
    enter(place, inlet, gathered, mapped, rows_high, rows_low, sides, ends, stack, high, low)
    cols, count = order.shape[0], order.shape[2]

    def copy(i):
        c, p = i // count, i % count
        return pltpu.make_async_copy(staged.at[i], out_hbm.at[c, 0, order[c, 0, p]], sems.at[i])

    def element(i, _):
        staged[i] = (free[i] + dot(maps[i], stack[i])).astype(BF16)
        copy(i).start()
        return 0

    lax.fori_loop(0, cols * count, element, 0)

    def finish(i, _):
        copy(i).wait()
        return 0

    lax.fori_loop(0, cols * count, finish, 0)


def per_device(inverse, upwind, lateral, inlet_trace, previous, uptake_rate, affinity, flow_order):
    cols, _, count, nodes, _ = inverse.shape
    face = upwind.shape[3]
    tracers = previous.shape[-1]
    per_side = NODES_1D
    items = cols * count
    wide = count * face

    def vmem(shape, kind=F32):
        return pltpu.VMEM(shape, kind)

    whole = pl.BlockSpec(memory_space=pltpu.VMEM)
    small = pl.BlockSpec(memory_space=pltpu.SMEM)
    hbm = pl.BlockSpec(memory_space=pl.ANY)

    def call(kernel, name, ins, outs, scratch, flops, limit=24):
        return pl.pallas_call(
            kernel,
            name=name,
            in_specs=ins,
            out_specs=[hbm if isinstance(o, jax.ShapeDtypeStruct) else whole for o in outs],
            out_shape=outs,
            scratch_shapes=scratch,
            cost_estimate=pl.CostEstimate(flops=flops, bytes_accessed=MIB, transcendentals=0),
            compiler_params=pltpu.CompilerParams(vmem_limit_bytes=limit * MIB),
        )

    rate, aff = uptake_rate.reshape(1, tracers), affinity.reshape(1, tracers)
    place = lax.axis_index("stream").astype(jnp.int32).reshape(1)
    dense = 2 * items * nodes * nodes * tracers

    block = 2 * per_side
    shaped = previous.reshape(cols, count, per_side, per_side * per_side, tracers)
    old_traces = pl.pallas_call(
        functools.partial(traces_kernel, per_side),
        name="old_traces",
        grid=(1,),
        in_specs=[
            pl.BlockSpec(
                (cols, count, per_side, block, tracers),
                lambda _: (0, 0, 0, per_side * per_side // block - 1, 0),
            )
        ],
        out_specs=pl.BlockSpec((cols, count, face, tracers), lambda _: (0, 0, 0, 0)),
        out_shape=jax.ShapeDtypeStruct((cols, count, face, tracers), F32),
    )(shaped)
    arrived = from_behind(old_traces[cols - 1], "lat", 1)

    inv, maps, free, side_maps, tails, rows_high, rows_low, block_map = call(
        functools.partial(first_kernel, per_side),
        "first_sweep",
        [small, hbm, hbm, hbm, hbm, whole, whole],
        [
            vmem((items, nodes, nodes), BF16),
            vmem((items, nodes, 6 * face), BF16),
            vmem((items, nodes, tracers)),
            vmem((items, face, 6 * face), BF16),
            vmem((items, face, 2 * face)),
            vmem((cols, wide + face, wide), BF16),
            vmem((cols, wide + face, wide), BF16),
            vmem((cols, face, face)),
        ],
        [
            vmem((items, 2 * face, nodes), BF16),
            vmem((items, nodes, tracers), BF16),
            vmem((items, face, 2 * face)),
            vmem((cols, face, wide)),
            pltpu.SemaphoreType.DMA((4, items)),
        ],
        3 * dense,
    )(flow_order, inverse, upwind, lateral, previous, rate, aff)

    def add_sides(arrived, local, free, with_map):
        return call(
            functools.partial(side_kernel, with_map),
            "add_sides",
            [small] + [whole] * 7,
            [
                vmem((items, 2, face, tracers), BF16),
                vmem((items, face, tracers)),
                vmem((cols, face, tracers + (face if with_map else 0))),
            ],
            [vmem((cols, wide - face, tracers), BF16)] * 2,
            dense // 100,
        )(flow_order, arrived, local, free, tails, rows_high, rows_low, block_map)

    sides, ends, message = add_sides(arrived, old_traces, free, True)
    mapped = lax.all_gather(message, "stream")

    stack, trace = call(
        functools.partial(trace_kernel, per_side),
        "entering",
        [small, small] + [whole] * 8,
        [vmem((items, 6 * face, tracers), BF16), vmem((count, face, tracers))],
        [vmem((cols, wide, tracers), BF16)] * 2,
        dense // 100,
    )(flow_order, place, inlet_trace, mapped, rows_high, rows_low, sides, ends, free, side_maps)
    arrived = from_behind(trace, "lat", 1)

    free, local = call(
        functools.partial(second_kernel, per_side),
        "second_sweep",
        [small] + [whole] * 6,
        [vmem((items, nodes, tracers)), vmem((cols, count, face, tracers))],
        [],
        3 * dense,
    )(flow_order, inv, maps, free, stack, rate, aff)

    sides, ends, message = add_sides(arrived, local, free, False)
    gathered = lax.all_gather(message, "stream")

    (out,) = call(
        last_kernel,
        "result",
        [small, small] + [whole] * 9,
        [jax.ShapeDtypeStruct(previous.shape, BF16)],
        [
            vmem((items, 6 * face, tracers), BF16),
            vmem((cols, wide, tracers), BF16),
            vmem((cols, wide, tracers), BF16),
            vmem((items, nodes, tracers), BF16),
            pltpu.SemaphoreType.DMA((items,)),
        ],
        dense,
    )(flow_order, place, inlet_trace, gathered, mapped, rows_high, rows_low, sides, ends, free, maps)
    return out


def solution(mesh):
    placed = (
        P("lat", "stream", None, None, None),
        P("lat", "stream", None, None, None),
        P("lat", "stream", None, None, None),
        P("lat", None, None),
        P("lat", "stream", None, None, None),
        P(),
        P(),
        P("lat", "stream", None),
    )
    return jax.shard_map(
        per_device,
        mesh=mesh,
        in_specs=placed,
        out_specs=P("lat", "stream", None, None, None),
        check_vma=False,
    )
```

time: 277 us -> 62.5 us (0.23)
  the two profiles are of different devices: /device:TPU:13 before, /device:TPU:0 now
where the time goes in v1:
time: 62.5 us; the launch traced here: 61.8 us
  Pallas kernels  28.5 us (46%)
  blocking collectives  16 us (26%)
  local copies, waits for them, and re-layouts  8.89 us (14%)
  starting transfers between devices  8.32 us (13%)
    pallas_call x1, Pallas kernels, per_device(): call(functools.partial(second_kernel, per_side), 'second_sweep', [small]...  9.54 us
    pallas_call x1, Pallas kernels, per_device(): call(functools.partial(first_kernel, per_side), 'first_sweep', [small, hb...  9 us
    all_gather x1, blocking collectives, per_device(): mapped = lax.all_gather(message, 'stream')  8.63 us
    ppermute x2, starting transfers between devices, from_behind(): lax.ppermute(value, axis, [(source, source + steps) for source in range(i...  8.32 us
    unnamed x24, local copies, waits for them, and re-layouts  7.92 us
    all_gather x1, blocking collectives, per_device(): gathered = lax.all_gather(message, 'stream')  7.33 us
    pallas_call x1, Pallas kernels, per_device(): call(last_kernel, 'result', [small, small] + [whole] * 9, [jax.ShapeDtype...  4.25 us
    pallas_call x2, Pallas kernels, add_sides(): call(functools.partial(side_kernel, with_map), 'add_sides', [small] + [wh...  2.32 us
  transfers between devices with their start and end apart: 2, of which 0 were waited for; matrix products, arithmetic and copies ran while one was open for 0% of the time, Pallas kernels for 30%

profile of v1, /device:TPU:0, one launch (start us, length us, event | category | flops | bytes accessed | tf_op | source)
XLA Modules:
  0.0 61.8 jit_solution(4141885615070275202)
XLA Ops:
  0.0 1.9 %old_traces.1.local = f32[2,4,64,256]{3,2,1,0:T(8,128)} custom-call(bf16[2,4,8,64,256]{4,3,2,1,0:T(8,128)(2,1)} %bitcast.11), custom_call_target="tpu_custom_call" | custom-call | tf_op jit(solution)/shard_map/old_traces/pallas_call | solution.py:267
  1.9 1.0 %slice_bitcast_fusion = f32[4,64,256]{2,1,0:T(8,128)S(1)} fusion(f32[2,4,64,256]{3,2,1,0:T(8,128)} %old_traces.1.local), kind=kLoop, calls=%fused_computation | loop fusion | bytes 524288 | tf_op jit(solution)/shard_map/squeeze | solution.py:280
  2.8 4.9 %collective-permute-start = (f32[4,64,256]{2,1,0:T(8,128)S(1)}, f32[4,64,256]{2,1,0:T(8,128)S(1)}, u32[]{:S(2)}, u32[]{:S(2)}) collective-permute-start(f32[4,64,256]{2,1,0:T(8,128)S(1)} %slice_bitcast_fusion), channel_id=1, source_target_pairs={{0,1},{1,2},{2,3},{3,4},{4,5},{5,6},{6,7},{8,9},{9,10},{10,11},{11... | collective-permute-start | bytes 786440 | tf_op jit(solution)/shard_map/ppermute | solution.py:19
  7.7 0.0 copy-start.1
  7.7 1.6 %copy-done.1 = bf16[2,1,4,512,256]{4,3,2,1,0:T(8,128)(2,1)S(1)} copy-done((bf16[2,1,4,512,256]{4,3,2,1,0:T(8,128)(2,1)S(1)}, bf16[2,1,4,512,256]{4,3,2,1,0:T(8,128)(2,1)}, u32[]{:S(2)}) %copy-start.1) | copy-done | bytes 2097176
  9.3 0.0 copy-start.3
  9.3 0.7 %copy-done.3 = s32[2,1,4]{2,1,0:T(1,128)S(1)} copy-done((s32[2,1,4]{2,1,0:T(1,128)S(1)}, s32[2,1,4]{2,1,0:T(1,128)}, u32[]{:S(2)}) %copy-start.3) | copy-done | bytes 56
  10.0 0.7 %copy-done.5 = f32[256]{0:T(256)S(1)} copy-done((f32[256]{0:T(256)S(1)}, f32[256]{0:T(256)}, u32[]{:S(2)}) %copy-start.5) | copy-done | bytes 1048
  10.7 0.7 %copy-done.7 = f32[256]{0:T(256)S(1)} copy-done((f32[256]{0:T(256)S(1)}, f32[256]{0:T(256)}, u32[]{:S(2)}) %copy-start.7) | copy-done | bytes 1048
  11.4 2.2 %copy-done.9 = bf16[2,1,4,512,512]{4,3,2,1,0:T(8,128)(2,1)S(1)} copy-done((bf16[2,1,4,512,512]{4,3,2,1,0:T(8,128)(2,1)S(1)}, bf16[2,1,4,512,512]{4,3,2,1,0:T(8,128)(2,1)}, u32[]{:S(2)}) %copy-start.9) | copy-done | bytes 4194328
  13.5 1.0 %copy-done.10 = bf16[2,1,4,64,512]{4,3,2,1,0:T(8,128)(2,1)S(1)} copy-done((bf16[2,1,4,64,512]{4,3,2,1,0:T(8,128)(2,1)S(1)}, bf16[2,1,4,64,512]{4,3,2,1,0:T(8,128)(2,1)}, u32[]{:S(2)}) %copy-start.10) | copy-done | bytes 524312
  14.6 1.0 %copy-done.11 = bf16[2,1,4,64,512]{4,3,2,1,0:T(8,128)(2,1)S(1)} copy-done((bf16[2,1,4,64,512]{4,3,2,1,0:T(8,128)(2,1)S(1)}, bf16[2,1,4,64,512]{4,3,2,1,0:T(8,128)(2,1)}, u32[]{:S(2)}) %copy-start.11) | copy-done | bytes 524312
  15.6 9.0 %first_sweep.1 = (bf16[8,512,512]{2,1,0:T(8,128)(2,1)S(1)}, bf16[8,512,384]{2,1,0:T(8,128)(2,1)S(1)}, f32[8,512,256]{2,1,0:T(8,128)S(1)}, bf16[8,64,384]{2,1,0:T...) custom-call(s32[2,1,4]{2,1,0:T(1,128)S(1)} %copy-done.3, ...), custom_call_target="tpu_custom_call" | custom-call | flops 3221225472 | bytes 1048576 | tf_op jit(solution)/shard_map/first_sweep/pallas_call | solution.py:282
  24.6 0.0 copy-start.2
  24.7 0.0 collective-permute-done.arrived
  24.7 0.0 copy-done
  24.7 1.2 %add_sides.2 = (bf16[8,2,64,256]{3,2,1,0:T(8,128)(2,1)S(1)}, f32[8,64,256]{2,1,0:T(8,128)S(1)}, f32[2,64,320]{2,1,0:T(8,128)S(1)}) custom-call(s32[2,1,4]{2,1,0:T(1,128)S(1)} %copy-done.3, f32[4,64,256]{2,1,0:T(8,128)S(1)} %collective-permute-done.arrived, f32[2,4,64,256]{3,2,1,0:T(8,128)S(1)} %copy-done, f32[8,512,256]{2,1,0:T(8,128)S(1)} %get-tuple-element.23.free, ...), custom_call_target="tpu_custom_call" | custom-call | flops 10737418 | bytes 1048576 | tf_op jit(solution)/shard_map/add_sides/pallas_call | solution.py:307
  25.8 0.0 copy-start.4
  25.9 0.0 copy-start.6
  25.9 0.0 copy-start.8
  25.9 8.6 %all-gather = f32[8,64,320]{2,1,0:T(8,128)S(1)} all-gather(f32[2,64,320]{2,1,0:T(8,128)S(1)} %get-tuple-element.28), channel_id=2, replica_groups=mesh['stream'=4,'lat'=8] {'stream'}, dimensions={0}, use_global_device_ids=true | all-gather | bytes 819200 | tf_op jit(solution)/shard_map/all_gather | solution.py:321
  34.5 0.0 copy-done.2
  34.5 1.5 %entering.1 = (bf16[8,384,256]{2,1,0:T(8,128)(2,1)S(1)}, f32[4,64,256]{2,1,0:T(8,128)S(1)}) custom-call(s32[2,1,4]{2,1,0:T(1,128)S(1)} %copy-done.3, s32[1]{0:T(128)} %bitcast.place, f32[2,64,256]{2,1,0:T(8,128)S(1)} %copy-done.2, f32[4,2,64,320]{3,2,1,0:T(8,128)S(1)} %bitcast.8, bf16[2,320,256]{2,1,0:T(8,128)(2,1)S(1)} %get-tuple-element.25.rows_high, ...), custom_call_target="tpu_custom_call" | custom-call | flops 10737418 | bytes 1048576 | tf_op jit(solution)/shard_map/entering/pallas_call | solution.py:323
  36.0 3.5 %collective-permute-start.1 = (f32[4,64,256]{2,1,0:T(8,128)S(1)}, f32[4,64,256]{2,1,0:T(8,128)S(1)}, u32[]{:S(2)}, u32[]{:S(2)}) collective-permute-start(f32[4,64,256]{2,1,0:T(8,128)S(1)} %get-tuple-element.32), channel_id=1, source_target_pairs={{0,1},{1,2},{2,3},{3,4},{4,5},{5,6},{6,7},{8,9},{9,10},{10,11},{11... | collective-permute-start | bytes 786440 | tf_op jit(solution)/shard_map/ppermute | solution.py:19
  39.5 0.0 copy-done.4
  39.5 0.0 copy-done.6
  39.5 0.0 copy-done.8
  39.5 9.5 %second_sweep.1 = (f32[8,512,256]{2,1,0:T(8,128)S(1)}, f32[2,4,64,256]{3,2,1,0:T(8,128)S(1)}) custom-call(s32[2,1,4]{2,1,0:T(1,128)S(1)} %copy-done.4, bf16[8,512,512]{2,1,0:T(8,128)(2,1)S(1)} %get-tuple-element.33.inv, bf16[8,512,384]{2,1,0:T(8,128)(2,1)S(1)} %get-tuple-element.34.maps, f32[8,512,256]{2,1,0:T(8,128)S(1)} %get-tuple-element.23.free, ...), custom_call_target="tpu_custom_call" | custom-call | flops 3221225472 | bytes 1048576 | tf_op jit(solution)/shard_map/second_sweep/pallas_call | solution.py:333
  49.0 0.0 collective-permute-done.1.arrived
  49.0 1.2 %add_sides.3 = (bf16[8,2,64,256]{3,2,1,0:T(8,128)(2,1)S(1)}, f32[8,64,256]{2,1,0:T(8,128)S(1)}, f32[2,64,256]{2,1,0:T(8,128)S(1)}) custom-call(s32[2,1,4]{2,1,0:T(1,128)S(1)} %copy-done.4, f32[4,64,256]{2,1,0:T(8,128)S(1)} %collective-permute-done.1.arrived, f32[2,4,64,256]{3,2,1,0:T(8,128)S(1)} %get-tuple-element.36.local, ...), custom_call_target="tpu_custom_call" | custom-call | flops 10737418 | bytes 1048576 | tf_op jit(solution)/shard_map/add_sides/pallas_call | solution.py:307
  50.2 7.3 %all-gather.1 = f32[8,64,256]{2,1,0:T(8,128)S(1)} all-gather(f32[2,64,256]{2,1,0:T(8,128)S(1)} %get-tuple-element.38), channel_id=3, replica_groups=mesh['stream'=4,'lat'=8] {'stream'}, dimensions={0}, use_global_device_ids=true | all-gather | bytes 655360 | tf_op jit(solution)/shard_map/all_gather | solution.py:343
  57.5 4.3 %result.1 = bf16[2,1,4,512,256]{4,3,2,1,0:T(8,128)(2,1)} custom-call(s32[2,1,4]{2,1,0:T(1,128)S(1)} %copy-done.4, s32[1]{0:T(128)} %bitcast.place, f32[2,64,256]{2,1,0:T(8,128)S(1)} %copy-done.2, f32[4,2,64,256]{3,2,1,0:T(8,128)S(1)} %bitcast.10, f32[4,2,64,320]{3,2,1,0:T(8,128)S(1)} %bitcast.9, bf16[2,320,256]{2,1,0:T(8,128)(2,1)S(1)} %get-tuple-element.25.rows_high, ...), custom_call_target="tpu_custom_call" | custom-call | flops 1073741824 | bytes 1048576 | tf_op jit(solution)/shard_map/result/pallas_call | solution.py:345
  (6 shorter events, 0.0 us)
Async XLA Ops:
  2.8 21.8 %collective-permute-start = (f32[4,64,256]{2,1,0:T(8,128)S(1)}, f32[4,64,256]{2,1,0:T(8,128)S(1)}, u32[]{:S(2)}, u32[]{:S(2)}) collective-permute-start(f32[4,64,256]{2,1,0:T(8,128)S(1)} %slice_bitcast_fusion), channel_id=1, source_target_pairs={{0,1},{1,2},{2,3},{3,4},{4,5},{5,6},{6,7},{8,9},{9,10},{10,11},{11... | collective-permute-start | bytes 786440 | tf_op jit(solution)/shard_map/ppermute | solution.py:19
  7.7 1.6 %copy-start.1 = (bf16[2,1,4,512,256]{4,3,2,1,0:T(8,128)(2,1)S(1)}, bf16[2,1,4,512,256]{4,3,2,1,0:T(8,128)(2,1)}, u32[]{:S(2)}) copy-start(bf16[2,1,4,512,256]{4,3,2,1,0:T(8,128)(2,1)} %prev_hbm.1) | copy-start | bytes 6291460
  9.3 0.7 %copy-start.3 = (s32[2,1,4]{2,1,0:T(1,128)S(1)}, s32[2,1,4]{2,1,0:T(1,128)}, u32[]{:S(2)}) copy-start(s32[2,1,4]{2,1,0:T(1,128)} %order.11) | copy-start | bytes 100
  10.0 0.7 %copy-start.5 = (f32[256]{0:T(256)S(1)}, f32[256]{0:T(256)}, u32[]{:S(2)}) copy-start(f32[256]{0:T(256)} %param.13) | copy-start | bytes 3076
  10.7 0.7 %copy-start.7 = (f32[256]{0:T(256)S(1)}, f32[256]{0:T(256)}, u32[]{:S(2)}) copy-start(f32[256]{0:T(256)} %param.14) | copy-start | bytes 3076
  11.4 2.2 %copy-start.9 = (bf16[2,1,4,512,512]{4,3,2,1,0:T(8,128)(2,1)S(1)}, bf16[2,1,4,512,512]{4,3,2,1,0:T(8,128)(2,1)}, u32[]{:S(2)}) copy-start(bf16[2,1,4,512,512]{4,3,2,1,0:T(8,128)(2,1)} %inv_hbm.1) | copy-start | bytes 12582916
  13.5 1.0 %copy-start.10 = (bf16[2,1,4,64,512]{4,3,2,1,0:T(8,128)(2,1)S(1)}, bf16[2,1,4,64,512]{4,3,2,1,0:T(8,128)(2,1)}, u32[]{:S(2)}) copy-start(bf16[2,1,4,64,512]{4,3,2,1,0:T(8,128)(2,1)} %up_hbm.1) | copy-start | bytes 1572868
  14.6 1.0 %copy-start.11 = (bf16[2,1,4,64,512]{4,3,2,1,0:T(8,128)(2,1)S(1)}, bf16[2,1,4,64,512]{4,3,2,1,0:T(8,128)(2,1)}, u32[]{:S(2)}) copy-start(bf16[2,1,4,64,512]{4,3,2,1,0:T(8,128)(2,1)} %lat_hbm.1) | copy-start | bytes 1572868
  15.6 9.0 %copy-start = (f32[2,4,64,256]{3,2,1,0:T(8,128)S(1)}, f32[2,4,64,256]{3,2,1,0:T(8,128)}, u32[]{:S(2)}) copy-start(f32[2,4,64,256]{3,2,1,0:T(8,128)} %old_traces.1.local) | copy-start | bytes 1572868
  24.6 9.9 %copy-start.2 = (f32[2,64,256]{2,1,0:T(8,128)S(1)}, f32[2,64,256]{2,1,0:T(8,128)}, u32[]{:S(2)}) copy-start(f32[2,64,256]{2,1,0:T(8,128)} %inlet.3) | copy-start | bytes 393220
  25.8 13.6 %copy-start.4 = (s32[2,1,4]{2,1,0:T(1,128)S(1)}, s32[2,1,4]{2,1,0:T(1,128)}, u32[]{:S(2)}) copy-start(s32[2,1,4]{2,1,0:T(1,128)} %order.11) | copy-start | bytes 100
  25.9 13.6 %copy-start.6 = (f32[256]{0:T(256)S(1)}, f32[256]{0:T(256)}, u32[]{:S(2)}) copy-start(f32[256]{0:T(256)} %param.13) | copy-start | bytes 3076
  25.9 13.6 %copy-start.8 = (f32[256]{0:T(256)S(1)}, f32[256]{0:T(256)}, u32[]{:S(2)}) copy-start(f32[256]{0:T(256)} %param.14) | copy-start | bytes 3076
  36.0 13.0 %collective-permute-start.1 = (f32[4,64,256]{2,1,0:T(8,128)S(1)}, f32[4,64,256]{2,1,0:T(8,128)S(1)}, u32[]{:S(2)}, u32[]{:S(2)}) collective-permute-start(f32[4,64,256]{2,1,0:T(8,128)S(1)} %get-tuple-element.32), channel_id=1, source_target_pairs={{0,1},{1,2},{2,3},{3,4},{4,5},{5,6},{6,7},{8,9},{9,10},{10,11},{11... | collective-permute-start | bytes 786440 | tf_op jit(solution)/shard_map/ppermute | solution.py:19

commit v2 on v0

v2 whole, which is shorter than its diff:
```python
import jax
import jax.numpy as jnp
from jax import lax
from jax.experimental import pallas as pl
from jax.experimental.pallas import tpu as pltpu
from jax.sharding import PartitionSpec as P

NODES_1D = 8
F32 = jnp.float32
BF16 = jnp.bfloat16
MIB = 1 << 20

WHOLE = pl.BlockSpec(memory_space=pltpu.VMEM)
SMALL = pl.BlockSpec(memory_space=pltpu.SMEM)
HBM = pl.BlockSpec(memory_space=pltpu.HBM)


def run(body, name, ins, outs, scratch, flops):
    names = [*ins, *outs, *scratch]

    def kernel(*refs):
        body(**dict(zip(names, refs)))

    values = pl.pallas_call(
        kernel,
        name=name,
        in_specs=[spec for _, spec in ins.values()],
        out_specs=[HBM if isinstance(o, jax.ShapeDtypeStruct) else WHOLE for o in outs.values()],
        out_shape=list(outs.values()),
        scratch_shapes=list(scratch.values()),
        cost_estimate=pl.CostEstimate(flops=flops, bytes_accessed=MIB, transcendentals=0),
        compiler_params=pltpu.CompilerParams(vmem_limit_bytes=24 * MIB),
    )(*[array for array, _ in ins.values()])
    return dict(zip(outs, values))


def split(x):
    high = x.astype(BF16)
    return high, (x - high.astype(F32)).astype(BF16)


def dot(x, y):
    return jnp.dot(x, y, preferred_element_type=F32)


def dot_split(x, y):
    return dot(x[0], y[0]) + (dot(x[0], y[1]) + dot(x[1], y[0]))


def langmuir(lagged, rate, affinity):
    below = 1.0 + affinity * jnp.abs(lagged)
    guess = pltpu.reciprocal(below, approx=True)
    guess = guess * (2.0 - below * guess)
    guess = guess * (2.0 - below * guess)
    return rate * lagged * guess


def lateral_rows(field, per_side):
    plane = per_side * per_side
    return jnp.concatenate(
        [field[a * plane + plane - per_side : (a + 1) * plane] for a in range(per_side)], axis=0
    )


def pack_map(mapping, lanes):
    face = mapping.shape[0]
    rows = face * face // lanes
    return jnp.concatenate([mapping[q * rows : (q + 1) * rows] for q in range(lanes // face)], axis=1)


def unpack_map(packed, face):
    return jnp.concatenate(
        [packed[:, q * face : (q + 1) * face] for q in range(packed.shape[1] // face)], axis=0
    )


def per_device(inverse, upwind, lateral, inlet_trace, previous, uptake_rate, affinity, flow_order):
    cols, _, count, nodes, _ = inverse.shape
    face = upwind.shape[3]
    tracers = previous.shape[-1]
    per_side = NODES_1D
    plane = per_side * per_side
    wide = count * face
    packed = face * face // tracers
    streams, lats = lax.axis_size("stream"), lax.axis_size("lat")
    stages = streams.bit_length() - 1
    assert streams == 1 << stages
    groups = [list(range(1, cols)), [0]] if cols > 1 else [[0]]

    rate = (uptake_rate.reshape(1, tracers), WHOLE)
    aff = (affinity.reshape(1, tracers), WHOLE)
    order = (flow_order, SMALL)
    place = (jnp.stack([lax.axis_index("stream"), lax.axis_index("lat")]).astype(jnp.int32), SMALL)
    dense = 2 * count * nodes * nodes * tracers
    vmem = pltpu.VMEM
    whole = lambda *arrays: [(a, WHOLE) for a in arrays]

    def to_next(value):
        return lax.ppermute(value, "lat", [(i, (i + 1) % lats) for i in range(lats)])

    def swap(value, stage):
        return lax.ppermute(value, "stream", [(i, i ^ (1 << stage)) for i in range(streams)])

    def bit(place, stage):
        return ((place[0] >> stage) & 1) == 1

    shaped = previous.reshape(cols, count, per_side, plane, tracers)
    tail_rows = pl.ds(plane - 2 * per_side, 2 * per_side)

    def old_trace(old, trace, staged, sem):
        copy = pltpu.make_async_copy(old.at[cols - 1, :, :, tail_rows], staged, sem)
        copy.start()
        copy.wait()
        for j in range(count):
            for a in range(per_side):
                trace[j, pl.ds(a * per_side, per_side)] = staged[j, a].astype(F32)[per_side:]

    trace = run(
        old_trace,
        "old_trace",
        {"old": (shaped, HBM)},
        {"trace": vmem((count, face, tracers), F32)},
        {"staged": vmem((count, per_side, 2 * per_side, tracers), BF16), "sem": pltpu.SemaphoreType.DMA},
        dense // 100,
    )["trace"]
    arrived = to_next(trace)

    def add_side(i, side, free, tails, sides, ends):
        s = split(side)
        sides[i, 0] = s[0]
        sides[i, 1] = s[1]
        tail = split(tails[i][:, face:])
        ends[i] = free[i, pl.ds(nodes - face, face)] + dot_split(tail, s)

    def offset(n, rows_high, rows_low, ends, high, low):
        for p in range(count - 1):
            e = split(ends[n * count + p])
            high[n, pl.ds(p * face, face)] = e[0]
            low[n, pl.ds(p * face, face)] = e[1]
        last = pl.ds(wide, face)
        row = (rows_high[n, last][:, face:], rows_low[n, last][:, face:])
        return ends[n * count + count - 1] + dot_split(row, (high[n], low[n]))

    side_outs = lambda size: {
        "sides": vmem((size * count, 2, face, tracers), BF16),
        "ends": vmem((size * count, face, tracers), F32),
    }
    offset_scratch = lambda size: {
        "high": vmem((size, wide - face, tracers), BF16),
        "low": vmem((size, wide - face, tracers), BF16),
    }

    def first(group):
        size = len(group)
        items = size * count
        local = group[0] > 0

        def body(
            order, inverse, upwind, lateral, previous, old, rate, affinity, inv, maps, free, side_maps, tails,
            rows_high, rows_low, faces, lagged, source_high, source_low, row, sems,
            sides=None, ends=None, message=None, block_map=None, high=None, low=None, staged=None, old_sems=None,
        ):
            def copies(i):
                c, p = group[i // count], i % count
                j = order[c, 0, p]
                return (
                    pltpu.make_async_copy(previous.at[c, 0, j], lagged.at[i], sems.at[0, i]),
                    pltpu.make_async_copy(upwind.at[c, 0, j], faces.at[i, pl.ds(0, face)], sems.at[1, i]),
                    pltpu.make_async_copy(lateral.at[c, 0, j], faces.at[i, pl.ds(face, face)], sems.at[2, i]),
                    pltpu.make_async_copy(inverse.at[c, 0, j], inv.at[i], sems.at[3, i]),
                )

            def old_copy(n):
                return pltpu.make_async_copy(
                    old.at[group[n] - 1, :, :, tail_rows], staged.at[n], old_sems.at[n]
                )

            for i in range(items):
                for copy in copies(i):
                    copy.start()
            if local:
                for n in range(size):
                    old_copy(n).start()

            row_id = lax.broadcasted_iota(jnp.int32, (face, wide), 0)
            lane_id = lax.broadcasted_iota(jnp.int32, (face, wide), 1)
            for i in range(items + 1):
                if i < items:
                    n, p = i // count, i % count
                    for copy in copies(i):
                        copy.wait()
                    both = lax.dot_general(
                        inv[i], faces[i], (((1,), (1,)), ((), ())), preferred_element_type=F32
                    )
                    b_high, b_low = split(both)
                    maps[i] = jnp.concatenate([b_high, b_high, b_low], axis=1)
                    tails[i] = both[nodes - face :]
                    s = split(lateral_rows(both, per_side))
                    side_maps[i] = jnp.concatenate([s[0], s[0], s[1]], axis=1)
                    s = split(langmuir(lagged[i].astype(F32), rate[...], affinity[...]))
                    source_high[i % 2], source_low[i % 2] = s
                    unit = jnp.where(lane_id == row_id + p * face, 1.0, 0.0)
                    r = split(unit if p == 0 else row[n] + unit)
                    rows_high[n, pl.ds(p * face, face)] = r[0]
                    rows_low[n, pl.ds(p * face, face)] = r[1]
                    row[n] = dot_split(split(tails[i][:, :face]), r)
                    if p == count - 1:
                        r = split(row[n])
                        rows_high[n, pl.ds(wide, face)] = r[0]
                        rows_low[n, pl.ds(wide, face)] = r[1]
                        if not local:
                            block_map[n] = pack_map(row[n][:, :face], tracers)
                if i > 0:
                    k = (i - 1) % 2
                    free[i - 1] = dot(inv[i - 1], source_high[k]) + dot(inv[i - 1], source_low[k])
            if local:
                for n in range(size):
                    old_copy(n).wait()
                    for p in range(count):
                        j = order[group[n], 0, p]
                        side = jnp.concatenate(
                            [staged[n, j, a].astype(F32)[per_side:] for a in range(per_side)], axis=0
                        )
                        add_side(n * count + p, side, free, tails, sides, ends)
                    message[n, pl.ds(0, face)] = offset(n, rows_high, rows_low, ends, high, low)
                    message[n, pl.ds(face, packed)] = pack_map(row[n][:, :face], tracers)

        outs = {
            "inv": vmem((items, nodes, nodes), BF16),
            "maps": vmem((items, nodes, 6 * face), BF16),
            "free": vmem((items, nodes, tracers), F32),
            "side_maps": vmem((items, face, 6 * face), BF16),
            "tails": vmem((items, face, 2 * face), F32),
            "rows_high": vmem((size, wide + face, wide), BF16),
            "rows_low": vmem((size, wide + face, wide), BF16),
        }
        scratch = {
            "faces": vmem((items, 2 * face, nodes), BF16),
            "lagged": vmem((items, nodes, tracers), BF16),
            "source_high": vmem((2, nodes, tracers), BF16),
            "source_low": vmem((2, nodes, tracers), BF16),
            "row": vmem((size, face, wide), F32),
            "sems": pltpu.SemaphoreType.DMA((4, items)),
        }
        if local:
            outs |= side_outs(size) | {"message": vmem((size, face + packed, tracers), F32)}
            scratch |= offset_scratch(size) | {
                "staged": vmem((size, count, per_side, 2 * per_side, tracers), BF16),
                "old_sems": pltpu.SemaphoreType.DMA((size,)),
            }
        else:
            outs |= {"block_map": vmem((size, packed, tracers), F32)}
        ins = {
            "order": order,
            "inverse": (inverse, HBM),
            "upwind": (upwind, HBM),
            "lateral": (lateral, HBM),
            "previous": (previous, HBM),
            "old": (shaped, HBM),
            "rate": rate,
            "affinity": aff,
        }
        return run(body, "first_sweep", ins, outs, scratch, 3 * size * dense)

    def arrived_side(place, arrived, j):
        return jnp.where(place[1] > 0, arrived[j], 0.0)

    def first_sides(state, arrived):
        def body(
            order, place, arrived, free, tails, rows_high, rows_low, block_map, sides, ends, message, high, low
        ):
            for p in range(count):
                add_side(p, arrived_side(place, arrived, order[0, 0, p]), free, tails, sides, ends)
            message[0, pl.ds(0, face)] = offset(0, rows_high, rows_low, ends, high, low)
            message[0, pl.ds(face, packed)] = block_map[0]

        keys = ("free", "tails", "rows_high", "rows_low", "block_map")
        ins = {"order": order, "place": place, "arrived": (arrived, WHOLE)}
        outs = side_outs(1) | {"message": vmem((1, face + packed, tracers), F32)}
        return run(
            body, "first_sides", ins | {k: (state[k], WHOLE) for k in keys}, outs, offset_scratch(1), dense // 50
        )

    def combine_first(stage, own, other):
        size = own.shape[0]

        def body(place, own, other, message):
            upper = bit(place, stage)
            for n in range(size):
                up = jnp.where(upper, own[n], other[n])
                low = jnp.where(upper, other[n], own[n])
                m = split(unpack_map(up[face:], face))
                message[n, pl.ds(0, face)] = dot_split(m, split(low[:face])) + up[:face]
                mapped = dot_split(m, split(unpack_map(low[face:], face)))
                message[n, pl.ds(face, packed)] = pack_map(mapped, tracers)

        ins = {"place": place, "own": (own, WHOLE), "other": (other, WHOLE)}
        return run(body, "combine", ins, {"message": vmem(own.shape, F32)}, {}, dense // 100)["message"]

    def combine_second(stage, own, other, old):
        def body(place, own, other, message, **old):
            upper = bit(place, stage)
            for g, group in enumerate(groups):
                for n, c in enumerate(group):
                    mine, theirs = old["own%d" % g], old["other%d" % g]
                    m = jnp.where(upper, mine[n, pl.ds(face, packed)], theirs[n, pl.ds(face, packed)])
                    up = jnp.where(upper, own[c], other[c])
                    low = jnp.where(upper, other[c], own[c])
                    message[c] = dot_split(split(unpack_map(m, face)), split(low)) + up

        ins = {"place": place, "own": (own, WHOLE), "other": (other, WHOLE)}
        old = {"%s%d" % (k, g): (a[g], WHOLE) for g in range(len(groups)) for k, a in old.items()}
        names = {k: old[k] for k in sorted(old)}
        ordered = ins | names

        def by_name(**refs):
            body(**refs)

        return run(by_name, "combine", ordered, {"message": vmem(own.shape, F32)}, {}, dense // 100)["message"]

    def enter(place, group, inlet, offsets, mapped, rows_high, rows_low, sides, ends, stack, high, low):
        for n, c in enumerate(group):
            entering = inlet[c]
            for stage in reversed(range(stages)):
                m = split(unpack_map(mapped[stage](n, c), face))
                beyond = dot_split(m, split(entering)) + offsets[stage](n, c)
                entering = jnp.where(bit(place, stage), beyond, entering)
            e = split(entering)
            high[n, pl.ds(0, face)] = e[0]
            low[n, pl.ds(0, face)] = e[1]
            for p in range(count - 1):
                e = split(ends[n * count + p])
                high[n, pl.ds((p + 1) * face, face)] = e[0]
                low[n, pl.ds((p + 1) * face, face)] = e[1]
            span = pl.ds(0, wide)
            inflow = dot_split((rows_high[n, span], rows_low[n, span]), (high[n], low[n]))
            for p in range(count):
                i = n * count + p
                f = split(inflow[p * face : (p + 1) * face])
                stack[i, pl.ds(0, face)] = f[0]
                stack[i, pl.ds(face, face)] = sides[i, 0]
                stack[i, pl.ds(2 * face, face)] = f[1]
                stack[i, pl.ds(3 * face, face)] = sides[i, 1]
                stack[i, pl.ds(4 * face, face)] = f[0]
                stack[i, pl.ds(5 * face, face)] = sides[i, 0]

    def enter_first(group, state, received):
        size = len(group)
        last = group[-1] == cols - 1

        def body(
            order, place, inlet, rows_high, rows_low, sides, ends, free, side_maps, stack, high, low,
            trace=None, **received,
        ):
            got = [received["got%d" % s] for s in range(stages)]
            enter(
                place, group, inlet,
                [lambda n, c, r=r: r[n, pl.ds(0, face)] for r in got],
                [lambda n, c, r=r: r[n, pl.ds(face, packed)] for r in got],
                rows_high, rows_low, sides, ends, stack, high, low,
            )
            if last:
                for p in range(count):
                    i = (size - 1) * count + p
                    trace[order[cols - 1, 0, p]] = lateral_rows(free.at[i], per_side) + dot(
                        side_maps[i], stack[i]
                    )

        keys = ("rows_high", "rows_low", "sides", "ends", "free", "side_maps")
        ins = {"order": order, "place": place, "inlet": (inlet_trace, WHOLE)}
        ins |= {k: (state[k], WHOLE) for k in keys} | {"got%d" % s: (r, WHOLE) for s, r in enumerate(received)}
        outs = {"stack": vmem((size * count, 6 * face, tracers), BF16)}
        if last:
            outs["trace"] = vmem((count, face, tracers), F32)
        scratch = {"high": vmem((size, wide, tracers), BF16), "low": vmem((size, wide, tracers), BF16)}
        return run(body, "entering", ins, outs, scratch, dense // 50)

    def second(group, state):
        size = len(group)
        items = size * count

        def body(order, inv, maps, free, stack, rate, affinity, fresh, traces, source_high, source_low):
            for i in range(items + 1):
                if i < items:
                    swept = free[i] + dot(maps[i], stack[i])
                    traces[i // count, order[group[i // count], 0, i % count]] = lateral_rows(swept, per_side)
                    s = split(langmuir(swept, rate[...], affinity[...]))
                    source_high[i % 2], source_low[i % 2] = s
                if i > 0:
                    k = (i - 1) % 2
                    fresh[i - 1] = dot(inv[i - 1], source_high[k]) + dot(inv[i - 1], source_low[k])

        ins = {"order": order} | {k: (state[k], WHOLE) for k in ("inv", "maps", "free", "stack")}
        ins |= {"rate": rate, "affinity": aff}
        outs = {
            "fresh": vmem((items, nodes, tracers), F32),
            "traces": vmem((size, count, face, tracers), F32),
        }
        scratch = {
            "source_high": vmem((2, nodes, tracers), BF16),
            "source_low": vmem((2, nodes, tracers), BF16),
        }
        return run(body, "second_sweep", ins, outs, scratch, 3 * size * dense)

    def spread(states, keys):
        return {"%s%d" % (k, g): (state[k], WHOLE) for g, state in enumerate(states) for k in keys}

    def second_sides(states, arrived):
        def body(order, place, arrived, message, **refs):
            get = lambda key, g: refs["%s%d" % (key, g)]
            for g, group in enumerate(groups):
                for n, c in enumerate(group):
                    for p in range(count):
                        j = order[c, 0, p]
                        if c == 0:
                            side = arrived_side(place, arrived, j)
                        else:
                            h = next(h for h, other in enumerate(groups) if c - 1 in other)
                            side = get("traces", h)[groups[h].index(c - 1), j]
                        add_side(n * count + p, side, get("fresh", g), get("tails", g), get("sides", g), get("ends", g))
                    message[c] = offset(
                        n, get("rows_high", g), get("rows_low", g), get("ends", g), get("high", g), get("low", g)
                    )

        ins = {"order": order, "place": place, "arrived": (arrived, WHOLE)}
        ins |= spread(states, ("fresh", "traces", "tails", "rows_high", "rows_low"))
        outs = {"message": vmem((cols, face, tracers), F32)}
        scratch = {}
        for g, group in enumerate(groups):
            outs |= {"%s%d" % (k, g): v for k, v in side_outs(len(group)).items()}
            scratch |= {"%s%d" % (k, g): v for k, v in offset_scratch(len(group)).items()}
        return run(body, "second_sides", ins, outs, scratch, dense // 50)

    def result(states, offsets):
        def body(order, place, inlet, out, staged, sems, **refs):
            get = lambda key, g: refs["%s%d" % (key, g)]
            started = []
            for g, group in enumerate(groups):
                enter(
                    place, group, inlet,
                    [lambda n, c, s=s: refs["offset%d" % s][c] for s in range(stages)],
                    [lambda n, c, s=s: refs["mapped%d_%d" % (s, g)][n, pl.ds(face, packed)] for s in range(stages)],
                    get("rows_high", g), get("rows_low", g), get("sides", g), get("ends", g),
                    get("stack", g), get("high", g), get("low", g),
                )
            for g, group in enumerate(groups):
                for n, c in enumerate(group):
                    for p in range(count):
                        i, k = n * count + p, len(started)
                        staged[k] = (get("fresh", g)[i] + dot(get("maps", g)[i], get("stack", g)[i])).astype(BF16)
                        copy = pltpu.make_async_copy(staged.at[k], out.at[c, 0, order[c, 0, p]], sems.at[k])
                        copy.start()
                        started.append(copy)
            for copy in started:
                copy.wait()

        ins = {"order": order, "place": place, "inlet": (inlet_trace, WHOLE)}
        ins |= {"offset%d" % s: (o, WHOLE) for s, o in enumerate(offsets)}
        for g, state in enumerate(states):
            ins |= {"mapped%d_%d" % (s, g): (r, WHOLE) for s, r in enumerate(state["received"])}
        ins |= spread(states, ("rows_high", "rows_low", "sides", "ends", "fresh", "maps"))
        scratch = {
            "staged": vmem((cols * count, nodes, tracers), BF16),
            "sems": pltpu.SemaphoreType.DMA((cols * count,)),
        }
        for g, group in enumerate(groups):
            scratch["stack%d" % g] = vmem((len(group) * count, 6 * face, tracers), BF16)
            scratch["high%d" % g] = vmem((len(group), wide, tracers), BF16)
            scratch["low%d" % g] = vmem((len(group), wide, tracers), BF16)
        outs = {"out": jax.ShapeDtypeStruct(previous.shape, BF16)}
        return run(body, "result", ins, outs, scratch, cols * dense)["out"]

    def exchange_first(message):
        sent, received = [message], [swap(message, 0)] if stages else []
        for stage in range(1, stages):
            sent.append(combine_first(stage - 1, sent[-1], received[-1]))
            received.append(swap(sent[-1], stage))
        return sent, received

    states = []
    for group in groups:
        state = first(group)
        if 0 in group:
            state |= first_sides(state, arrived)
        state["sent"], state["received"] = exchange_first(state["message"])
        states.append(state)
    for group, state in zip(groups, states):
        state |= enter_first(group, state, state["received"])
        if "trace" in state:
            arrived = to_next(state["trace"])
    for group, state in zip(groups, states):
        state |= second(group, state)
    sided = second_sides(states, arrived)
    for g, state in enumerate(states):
        state["sides"], state["ends"] = sided["sides%d" % g], sided["ends%d" % g]
    message, offsets = sided["message"], []
    for stage in range(stages):
        offsets.append(swap(message, stage))
        if stage + 1 < stages:
            old = {"own": [s["sent"][stage] for s in states], "other": [s["received"][stage] for s in states]}
            message = combine_second(stage, message, offsets[-1], old)
    return result(states, offsets)


def solution(mesh):
    placed = (
        P("lat", "stream", None, None, None),
        P("lat", "stream", None, None, None),
        P("lat", "stream", None, None, None),
        P("lat", None, None),
        P("lat", "stream", None, None, None),
        P(),
        P(),
        P("lat", "stream", None),
    )
    return jax.shard_map(
        per_device,
        mesh=mesh,
        in_specs=placed,
        out_specs=P("lat", "stream", None, None, None),
        check_vma=False,
    )
```

time: 277 us -> 66.2 us (0.24)
  the two profiles are of different devices: /device:TPU:13 before, /device:TPU:0 now
where the time goes in v2:
time: 66.2 us; the launch traced here: 65.7 us
  Pallas kernels  32.8 us (50%)
  local copies, waits for them, and re-layouts  16.8 us (25%)
  starting transfers between devices  8.01 us (12%)
  waiting for transfers between devices  7.56 us (11%)
    pallas_call x13, Pallas kernels, run(): pl.pallas_call(kernel, name=name, in_specs=[spec for _, spec in ins.value...  32.8 us
    unnamed x60, local copies, waits for them, and re-layouts  16.8 us
    ppermute x6, waiting for transfers between devices, swap(): lax.ppermute(value, 'stream', [(i, i ^ 1 << stage) for i in range(streams)])  7.38 us
    ppermute x2, starting transfers between devices, to_next(): lax.ppermute(value, 'lat', [(i, (i + 1) % lats) for i in range(lats)])  4.72 us
    ppermute x6, starting transfers between devices, swap(): lax.ppermute(value, 'stream', [(i, i ^ 1 << stage) for i in range(streams)])  3.29 us
  transfers between devices with their start and end apart: 8, of which 4 were waited for; matrix products, arithmetic and copies ran while one was open for 0% of the time, Pallas kernels for 30%

profile of v2, /device:TPU:0, one launch (start us, length us, event | category | flops | bytes accessed | tf_op | source)
XLA Modules:
  0.0 65.7 jit_solution(10262813898028588733)
XLA Ops:
  0.0 1.6 %copy-done = bf16[2,1,4,512,256]{4,3,2,1,0:T(8,128)(2,1)S(1)} copy-done((bf16[2,1,4,512,256]{4,3,2,1,0:T(8,128)(2,1)S(1)}, bf16[2,1,4,512,256]{4,3,2,1,0:T(8,128)(2,1)}, u32[]{:S(2)}) %copy-start) | copy-done | bytes 2097176
  1.6 2.2 %copy-done.2 = bf16[2,1,4,512,512]{4,3,2,1,0:T(8,128)(2,1)S(1)} copy-done((bf16[2,1,4,512,512]{4,3,2,1,0:T(8,128)(2,1)S(1)}, bf16[2,1,4,512,512]{4,3,2,1,0:T(8,128)(2,1)}, u32[]{:S(2)}) %copy-start.2) | copy-done | bytes 4194328
  3.8 1.0 %copy-done.8 = bf16[2,1,4,64,512]{4,3,2,1,0:T(8,128)(2,1)S(1)} copy-done((bf16[2,1,4,64,512]{4,3,2,1,0:T(8,128)(2,1)S(1)}, bf16[2,1,4,64,512]{4,3,2,1,0:T(8,128)(2,1)}, u32[]{:S(2)}) %copy-start.8) | copy-done | bytes 524312
  4.8 1.0 %copy-done.10 = bf16[2,1,4,64,512]{4,3,2,1,0:T(8,128)(2,1)S(1)} copy-done((bf16[2,1,4,64,512]{4,3,2,1,0:T(8,128)(2,1)S(1)}, bf16[2,1,4,64,512]{4,3,2,1,0:T(8,128)(2,1)}, u32[]{:S(2)}) %copy-start.10) | copy-done | bytes 524312
  5.9 0.7 %copy-done.23 = s32[2,1,4]{2,1,0:T(1,128)S(1)} copy-done((s32[2,1,4]{2,1,0:T(1,128)S(1)}, s32[2,1,4]{2,1,0:T(1,128)}, u32[]{:S(2)}) %copy-start.23) | copy-done | bytes 56
  6.5 0.7 %copy-done.26 = f32[256]{0:T(256)S(1)} copy-done((f32[256]{0:T(256)S(1)}, f32[256]{0:T(256)}, u32[]{:S(2)}) %copy-start.26) | copy-done | bytes 1048
  7.2 0.7 %copy-done.28 = f32[256]{0:T(256)S(1)} copy-done((f32[256]{0:T(256)S(1)}, f32[256]{0:T(256)}, u32[]{:S(2)}) %copy-start.28) | copy-done | bytes 1048
  7.9 7.4 %first_sweep.2 = (bf16[4,512,512]{2,1,0:T(8,128)(2,1)S(1)}, bf16[4,512,384]{2,1,0:T(8,128)(2,1)S(1)}, f32[4,512,256]{2,1,0:T(8,128)S(1)}, bf16[4,64,384]{2,1,0:T...) custom-call(s32[2,1,4]{2,1,0:T(1,128)S(1)} %copy-done.23, ...), custom_call_target="tpu_custom_call" | custom-call | flops 1610612736 | bytes 1048576 | tf_op jit(solution)/shard_map/first_sweep/pallas_call | solution.py:24
  15.3 1.1 %copy-done.6 = bf16[4,512,384]{2,1,0:T(8,128)(2,1)} copy-done((bf16[4,512,384]{2,1,0:T(8,128)(2,1)}, bf16[4,512,384]{2,1,0:T(8,128)(2,1)S(1)}, u32[]{:S(2)}) %copy-start.6) | copy-done | bytes 1572888
  16.5 1.4 %copy-done.12 = bf16[4,512,512]{2,1,0:T(8,128)(2,1)} copy-done((bf16[4,512,512]{2,1,0:T(8,128)(2,1)}, bf16[4,512,512]{2,1,0:T(8,128)(2,1)S(1)}, u32[]{:S(2)}) %copy-start.12) | copy-done | bytes 2097176
  17.8 0.7 %copy-done.17 = f32[4,64,256]{2,1,0:T(8,128)} copy-done((f32[4,64,256]{2,1,0:T(8,128)}, f32[4,64,256]{2,1,0:T(8,128)S(1)}, u32[]{:S(2)}) %copy-start.17) | copy-done | bytes 262168
  18.5 0.7 %copy-done.19 = bf16[4,64,384]{2,1,0:T(8,128)(2,1)} copy-done((bf16[4,64,384]{2,1,0:T(8,128)(2,1)}, bf16[4,64,384]{2,1,0:T(8,128)(2,1)S(1)}, u32[]{:S(2)}) %copy-start.19) | copy-done | bytes 196632
  20.4 0.8 %old_trace.1 = f32[4,64,256]{2,1,0:T(8,128)} custom-call(bf16[2,4,8,64,256]{4,3,2,1,0:T(8,128)(2,1)S(1)} %bitcast.6), custom_call_target="tpu_custom_call" | custom-call | flops 5368709 | bytes 1048576 | tf_op jit(solution)/shard_map/old_trace/pallas_call | solution.py:24
  21.3 2.9 %collective-permute-start.3 = (f32[4,64,256]{2,1,0:T(8,128)}, f32[4,64,256]{2,1,0:T(8,128)}, u32[]{:S(2)}, u32[]{:S(2)}) collective-permute-start(f32[4,64,256]{2,1,0:T(8,128)} %old_trace.1), channel_id=1, source_target_pairs={{0,1},{1,2},{2,3},{3,4},{4,5},{5,6},{6,7},{7,0},{8,9},{9,10},{10,1... | collective-permute-start | bytes 786440 | tf_op jit(solution)/shard_map/ppermute | solution.py:99
  24.3 1.2 %combine.3 = f32[1,80,256]{2,1,0:T(8,128)S(1)} custom-call(s32[2]{0:T(128)S(1)} %pad_add_fusion.refs_0_.refs_1_, f32[1,80,256]{2,1,0:T(8,128)} %get-tuple-element.43.refs_1_.refs_5_, f32[1,80,256]{2,1,0:T(8,128)S(1)} %collective-permute-done.refs_2_.refs_9_.refs_3_.refs_5_), custom_call_target="tpu_custom_call" | custom-call | flops 5368709 | bytes 1048576 | tf_op jit(solution)/shard_map/combine/pallas_call | solution.py:24
  25.5 1.5 %collective-permute-start.1 = (f32[1,80,256]{2,1,0:T(8,128)S(1)}, f32[1,80,256]{2,1,0:T(8,128)S(1)}, u32[]{:S(2)}, u32[]{:S(2)}) collective-permute-start(f32[1,80,256]{2,1,0:T(8,128)S(1)} %combine.3), channel_id=1, source_target_pairs={{0,16},{8,24},{16,0},{24,8},{1,17},{9,25},{17,1},{25,9},{2,18},{10... | collective-permute-start | bytes 245768 | tf_op jit(solution)/shard_map/ppermute | solution.py:102
  27.1 2.2 %copy-done.3 = bf16[2,1,4,512,512]{4,3,2,1,0:T(8,128)(2,1)S(1)} copy-done((bf16[2,1,4,512,512]{4,3,2,1,0:T(8,128)(2,1)S(1)}, bf16[2,1,4,512,512]{4,3,2,1,0:T(8,128)(2,1)}, u32[]{:S(2)}) %copy-start.3) | copy-done | bytes 4194328
  29.2 0.7 %copy-done.24 = s32[2,1,4]{2,1,0:T(1,128)S(1)} copy-done((s32[2,1,4]{2,1,0:T(1,128)S(1)}, s32[2,1,4]{2,1,0:T(1,128)}, u32[]{:S(2)}) %copy-start.24) | copy-done | bytes 56
  31.3 6.2 %first_sweep.3 = (bf16[4,512,512]{2,1,0:T(8,128)(2,1)S(1)}, bf16[4,512,384]{2,1,0:T(8,128)(2,1)S(1)}, f32[4,512,256]{2,1,0:T(8,128)S(1)}, bf16[4,64,384]{2,1,0:T...) custom-call(s32[2,1,4]{2,1,0:T(1,128)S(1)} %copy-done.24, ...), custom_call_target="tpu_custom_call" | custom-call | flops 1610612736 | bytes 1048576 | tf_op jit(solution)/shard_map/first_sweep/pallas_call | solution.py:24
  37.6 1.6 %first_sides.1 = (bf16[4,2,64,256]{3,2,1,0:T(8,128)(2,1)S(1)}, f32[4,64,256]{2,1,0:T(8,128)S(1)}, f32[1,80,256]{2,1,0:T(8,128)S(1)}) custom-call(s32[2,1,4]{2,1,0:T(1,128)S(1)} %copy-done.24, s32[2]{0:T(128)S(1)} %pad_add_fusion.refs_0_.refs_1_, f32[4,64,256]{2,1,0:T(8,128)} %collective-permute-done.3.refs_2_, ...), custom_call_target="tpu_custom_call" | custom-call | flops 10737418 | bytes 1048576 | tf_op jit(solution)/shard_map/first_sides/pallas_call | solution.py:24
  39.3 1.6 %entering.2 = (bf16[4,384,256]{2,1,0:T(8,128)(2,1)S(1)}, f32[4,64,256]{2,1,0:T(8,128)S(1)}) custom-call(s32[2,1,4]{2,1,0:T(1,128)S(1)} %copy-done.24, s32[2]{0:T(128)S(1)} %pad_add_fusion.refs_0_.refs_1_, f32[2,64,256]{2,1,0:T(8,128)S(1)} %copy-done.14, bf16[1,320,256]{2,1,0:T(8,128)(2,1)S(1)} %get-tuple-element.37.refs_3_.refs_6_.refs_9_, ...), custom_call_target="tpu_custom_call" | custom-call | flops 10737418 | bytes 1048576 | tf_op jit(solution)/shard_map/entering/pallas_call | solution.py:24
  40.9 1.8 %collective-permute-start.2 = (f32[4,64,256]{2,1,0:T(8,128)S(1)}, f32[4,64,256]{2,1,0:T(8,128)S(1)}, u32[]{:S(2)}, u32[]{:S(2)}) collective-permute-start(f32[4,64,256]{2,1,0:T(8,128)S(1)} %get-tuple-element.44), channel_id=1, source_target_pairs={{0,1},{1,2},{2,3},{3,4},{4,5},{5,6},{6,7},{7,0},{8,9},{9,10},{10,1... | collective-permute-start | bytes 786440 | tf_op jit(solution)/shard_map/ppermute | solution.py:99
  42.7 0.8 %combine.4 = f32[1,80,256]{2,1,0:T(8,128)S(1)} custom-call(s32[2]{0:T(128)S(1)} %pad_add_fusion.refs_0_.refs_1_, f32[1,80,256]{2,1,0:T(8,128)S(1)} %get-tuple-element.61.refs_1_.refs_6_, f32[1,80,256]{2,1,0:T(8,128)S(1)} %collective-permute-done.4.refs_2_.refs_9_.refs_4_.refs_7_), custom_call_target="tpu_custom_call" | custom-call | flops 5368709 | bytes 1048576 | tf_op jit(solution)/shard_map/combine/pallas_call | solution.py:24
  44.1 3.0 %second_sweep.2 = (f32[4,512,256]{2,1,0:T(8,128)S(1)}, f32[1,4,64,256]{3,2,1,0:T(8,128)S(1)}) custom-call(s32[2,1,4]{2,1,0:T(1,128)S(1)} %copy-done.25, bf16[4,512,512]{2,1,0:T(8,128)(2,1)S(1)} %copy-done.13, bf16[4,512,384]{2,1,0:T(8,128)(2,1)S(1)} %copy-done.7, f32[4,512,256]{2,1,0:T(8,128)S(1)} %copy-done.5, ...), custom_call_target="tpu_custom_call" | custom-call | flops 1610612736 | bytes 1048576 | tf_op jit(solution)/shard_map/second_sweep/pallas_call | solution.py:24
  47.1 1.0 %collective-permute-done.5.refs_10_.refs_8_ = f32[1,80,256]{2,1,0:T(8,128)S(1)} collective-permute-done((f32[1,80,256]{2,1,0:T(8,128)S(1)}, f32[1,80,256]{2,1,0:T(8,128)S(1)}, u32[]{:S(2)}, u32[]{:S(2)}) %collective-permute-start.5) | collective-permute-done | bytes 81952 | tf_op jit(solution)/shard_map/ppermute | solution.py:102
  48.1 1.2 %entering.3.refs_4_ = bf16[4,384,256]{2,1,0:T(8,128)(2,1)S(1)} custom-call(s32[2,1,4]{2,1,0:T(1,128)S(1)} %copy-done.25, s32[2]{0:T(128)S(1)} %pad_add_fusion.refs_0_.refs_1_, f32[2,64,256]{2,1,0:T(8,128)S(1)} %copy-done.14, bf16[1,320,256]{2,1,0:T(8,128)(2,1)S(1)} %get-tuple-element.54.refs_5_.refs_3_.refs_11_.refs_15_, ...), custom_call_target="tpu_custom_call" | custom-call | flops 10737418 | bytes 1048576 | tf_op jit(solution)/shard_map/entering/pallas_call | solution.py:24
  49.3 3.0 %second_sweep.3 = (f32[4,512,256]{2,1,0:T(8,128)S(1)}, f32[1,4,64,256]{3,2,1,0:T(8,128)S(1)}) custom-call(s32[2,1,4]{2,1,0:T(1,128)S(1)} %copy-done.25, bf16[4,512,512]{2,1,0:T(8,128)(2,1)S(1)} %get-tuple-element.51.refs_1_, bf16[4,512,384]{2,1,0:T(8,128)(2,1)S(1)} %get-tuple-element.52.refs_2_.refs_20_, ...), custom_call_target="tpu_custom_call" | custom-call | flops 1610612736 | bytes 1048576 | tf_op jit(solution)/shard_map/second_sweep/pallas_call | solution.py:24
  52.5 1.3 %second_sides.1 = (f32[2,64,256]{2,1,0:T(8,128)S(1)}, bf16[4,2,64,256]{3,2,1,0:T(8,128)(2,1)S(1)}, f32[4,64,256]{2,1,0:T(8,128)S(1)}, bf16[4,2,64,256]{3,2,1,0:T(8,128)(2,1)S(1)}, f32[4,64,256]{2,1,0:T(8,128)S(1)}) custom-call(s32[2,1,4]{2,1,0:T(1,128)S(1)} %copy-done.25, s32[2]{0:T(128)S(1)} %pad_add_fusion.refs_0_.refs_1_, ...), custom_call_target="tpu_custom_call" | custom-call | flops 10737418 | bytes 1048576 | tf_op jit(solution)/shard_map/second_sides/pallas_call | solution.py:24
  53.9 1.3 %collective-permute-done.6.refs_2_.refs_3_ = f32[2,64,256]{2,1,0:T(8,128)S(1)} collective-permute-done((f32[2,64,256]{2,1,0:T(8,128)S(1)}, f32[2,64,256]{2,1,0:T(8,128)S(1)}, u32[]{:S(2)}, u32[]{:S(2)}) %collective-permute-start.6) | collective-permute-done | bytes 131104 | tf_op jit(solution)/shard_map/ppermute | solution.py:102
  55.3 1.1 %combine.5 = f32[2,64,256]{2,1,0:T(8,128)S(1)} custom-call(s32[2]{0:T(128)S(1)} %pad_add_fusion.refs_0_.refs_1_, f32[2,64,256]{2,1,0:T(8,128)S(1)} %get-tuple-element.64.refs_1_, f32[2,64,256]{2,1,0:T(8,128)S(1)} %collective-permute-done.6.refs_2_.refs_3_, f32[1,80,256]{2,1,0:T(8,128)S(1)} %collective-permute-done.refs_2_.refs_9_.refs_3_.refs_5_, ...), custom_call_target="tpu_custom_call" | custom-call | flops 5368709 | bytes 1048576 | tf_op jit(solution)/shard_map/combine/pallas_call | solution.py:24
  57.0 5.0 %collective-permute-done.7.refs_4_ = f32[2,64,256]{2,1,0:T(8,128)S(1)} collective-permute-done((f32[2,64,256]{2,1,0:T(8,128)S(1)}, f32[2,64,256]{2,1,0:T(8,128)S(1)}, u32[]{:S(2)}, u32[]{:S(2)}) %collective-permute-start.7) | collective-permute-done | bytes 131104 | tf_op jit(solution)/shard_map/ppermute | solution.py:102
  62.0 3.5 %result.1 = bf16[2,1,4,512,256]{4,3,2,1,0:T(8,128)(2,1)} custom-call(s32[2,1,4]{2,1,0:T(1,128)S(1)} %copy-done.25, s32[2]{0:T(128)S(1)} %pad_add_fusion.refs_0_.refs_1_, f32[2,64,256]{2,1,0:T(8,128)S(1)} %copy-done.14, f32[2,64,256]{2,1,0:T(8,128)S(1)} %collective-permute-done.6.refs_2_.refs_3_, f32[2,64,256]{2,1,0:T(8,128)S(1)} %collective-permute-done.7.refs_4_, ...), custom_call_target="tpu_custom_call" | custom-call | flops 1073741824 | bytes 1048576 | tf_op jit(solution)/shard_map/result/pallas_call | solution.py:24
  (58 shorter events, 4.2 us)
Async XLA Ops:
  0.0 1.6 %copy-start = (bf16[2,1,4,512,256]{4,3,2,1,0:T(8,128)(2,1)S(1)}, bf16[2,1,4,512,256]{4,3,2,1,0:T(8,128)(2,1)}, u32[]{:S(2)}) copy-start(bf16[2,1,4,512,256]{4,3,2,1,0:T(8,128)(2,1)} %refs_4_.3) | copy-start | bytes 6291460
  1.6 2.2 %copy-start.2 = (bf16[2,1,4,512,512]{4,3,2,1,0:T(8,128)(2,1)S(1)}, bf16[2,1,4,512,512]{4,3,2,1,0:T(8,128)(2,1)}, u32[]{:S(2)}) copy-start(bf16[2,1,4,512,512]{4,3,2,1,0:T(8,128)(2,1)} %refs_1_.3) | copy-start | bytes 12582916
  3.8 1.0 %copy-start.8 = (bf16[2,1,4,64,512]{4,3,2,1,0:T(8,128)(2,1)S(1)}, bf16[2,1,4,64,512]{4,3,2,1,0:T(8,128)(2,1)}, u32[]{:S(2)}) copy-start(bf16[2,1,4,64,512]{4,3,2,1,0:T(8,128)(2,1)} %refs_2_.7) | copy-start | bytes 1572868
  4.8 1.0 %copy-start.10 = (bf16[2,1,4,64,512]{4,3,2,1,0:T(8,128)(2,1)S(1)}, bf16[2,1,4,64,512]{4,3,2,1,0:T(8,128)(2,1)}, u32[]{:S(2)}) copy-start(bf16[2,1,4,64,512]{4,3,2,1,0:T(8,128)(2,1)} %refs_3_.3) | copy-start | bytes 1572868
  5.9 0.7 %copy-start.23 = (s32[2,1,4]{2,1,0:T(1,128)S(1)}, s32[2,1,4]{2,1,0:T(1,128)}, u32[]{:S(2)}) copy-start(s32[2,1,4]{2,1,0:T(1,128)} %refs_0_.17) | copy-start | bytes 100
  7.9 19.1 %copy-start.11 = (bf16[2,1,4,64,512]{4,3,2,1,0:T(8,128)(2,1)S(1)}, bf16[2,1,4,64,512]{4,3,2,1,0:T(8,128)(2,1)}, u32[]{:S(2)}) copy-start(bf16[2,1,4,64,512]{4,3,2,1,0:T(8,128)(2,1)} %refs_3_.3) | copy-start | bytes 1572868
  15.3 1.2 %copy-start.6 = (bf16[4,512,384]{2,1,0:T(8,128)(2,1)}, bf16[4,512,384]{2,1,0:T(8,128)(2,1)S(1)}, u32[]{:S(2)}) copy-start(bf16[4,512,384]{2,1,0:T(8,128)(2,1)S(1)} %get-tuple-element.46.refs_2_.refs_14_) | copy-start | bytes 4718596
  16.5 1.4 %copy-start.12 = (bf16[4,512,512]{2,1,0:T(8,128)(2,1)}, bf16[4,512,512]{2,1,0:T(8,128)(2,1)S(1)}, u32[]{:S(2)}) copy-start(bf16[4,512,512]{2,1,0:T(8,128)(2,1)S(1)} %get-tuple-element.45.refs_1_) | copy-start | bytes 6291460
  17.8 0.7 %copy-start.17 = (f32[4,64,256]{2,1,0:T(8,128)}, f32[4,64,256]{2,1,0:T(8,128)S(1)}, u32[]{:S(2)}) copy-start(f32[4,64,256]{2,1,0:T(8,128)S(1)} %get-tuple-element.40.refs_6_) | copy-start | bytes 786436
  18.5 0.7 %copy-start.19 = (bf16[4,64,384]{2,1,0:T(8,128)(2,1)}, bf16[4,64,384]{2,1,0:T(8,128)(2,1)S(1)}, u32[]{:S(2)}) copy-start(bf16[4,64,384]{2,1,0:T(8,128)(2,1)S(1)} %get-tuple-element.42.refs_8_) | copy-start | bytes 589828
  19.9 1.4 %copy-start.4 = (f32[4,512,256]{2,1,0:T(8,128)}, f32[4,512,256]{2,1,0:T(8,128)S(1)}, u32[]{:S(2)}) copy-start(f32[4,512,256]{2,1,0:T(8,128)S(1)} %get-tuple-element.41.refs_7_.refs_3_) | copy-start | bytes 6291460
  19.9 4.3 %copy-start.15 = (bf16[4,2,64,256]{3,2,1,0:T(8,128)(2,1)}, bf16[4,2,64,256]{3,2,1,0:T(8,128)(2,1)S(1)}, u32[]{:S(2)}) copy-start(bf16[4,2,64,256]{3,2,1,0:T(8,128)(2,1)S(1)} %get-tuple-element.39.refs_5_) | copy-start | bytes 786436
  19.9 7.2 %copy-start.1 = (bf16[2,1,4,512,256]{4,3,2,1,0:T(8,128)(2,1)S(1)}, bf16[2,1,4,512,256]{4,3,2,1,0:T(8,128)(2,1)}, u32[]{:S(2)}) copy-start(bf16[2,1,4,512,256]{4,3,2,1,0:T(8,128)(2,1)} %refs_4_.3) | copy-start | bytes 6291460
  19.9 7.2 %copy-start.9 = (bf16[2,1,4,64,512]{4,3,2,1,0:T(8,128)(2,1)S(1)}, bf16[2,1,4,64,512]{4,3,2,1,0:T(8,128)(2,1)}, u32[]{:S(2)}) copy-start(bf16[2,1,4,64,512]{4,3,2,1,0:T(8,128)(2,1)} %refs_2_.7) | copy-start | bytes 1572868
  19.9 4.4 %collective-permute-start = (f32[1,80,256]{2,1,0:T(8,128)}, f32[1,80,256]{2,1,0:T(8,128)S(1)}, u32[]{:S(2)}, u32[]{:S(2)}) collective-permute-start(f32[1,80,256]{2,1,0:T(8,128)} %get-tuple-element.43.refs_1_.refs_5_), channel_id=1, source_target_pairs={{0,8},{8,0},{16,24},{24,16},{1,9},{9,1},{17,25},{25,17},{2,10},{10... | collective-permute-start | bytes 245768 | tf_op jit(solution)/shard_map/ppermute | solution.py:102
  21.3 16.3 %collective-permute-start.3 = (f32[4,64,256]{2,1,0:T(8,128)}, f32[4,64,256]{2,1,0:T(8,128)}, u32[]{:S(2)}, u32[]{:S(2)}) collective-permute-start(f32[4,64,256]{2,1,0:T(8,128)} %old_trace.1), channel_id=1, source_target_pairs={{0,1},{1,2},{2,3},{3,4},{4,5},{5,6},{6,7},{7,0},{8,9},{9,10},{10,1... | collective-permute-start | bytes 786440 | tf_op jit(solution)/shard_map/ppermute | solution.py:99
  25.5 13.7 %collective-permute-start.1 = (f32[1,80,256]{2,1,0:T(8,128)S(1)}, f32[1,80,256]{2,1,0:T(8,128)S(1)}, u32[]{:S(2)}, u32[]{:S(2)}) collective-permute-start(f32[1,80,256]{2,1,0:T(8,128)S(1)} %combine.3), channel_id=1, source_target_pairs={{0,16},{8,24},{16,0},{24,8},{1,17},{9,25},{17,1},{25,9},{2,18},{10... | collective-permute-start | bytes 245768 | tf_op jit(solution)/shard_map/ppermute | solution.py:102
  27.1 2.2 %copy-start.3 = (bf16[2,1,4,512,512]{4,3,2,1,0:T(8,128)(2,1)S(1)}, bf16[2,1,4,512,512]{4,3,2,1,0:T(8,128)(2,1)}, u32[]{:S(2)}) copy-start(bf16[2,1,4,512,512]{4,3,2,1,0:T(8,128)(2,1)} %refs_1_.3) | copy-start | bytes 12582916
  31.3 8.0 %copy-start.20 = (bf16[4,64,384]{2,1,0:T(8,128)(2,1)S(1)}, bf16[4,64,384]{2,1,0:T(8,128)(2,1)}, u32[]{:S(2)}) copy-start(bf16[4,64,384]{2,1,0:T(8,128)(2,1)} %copy-done.19) | copy-start | bytes 589828
  37.5 1.8 %copy-start.5 = (f32[4,512,256]{2,1,0:T(8,128)S(1)}, f32[4,512,256]{2,1,0:T(8,128)}, u32[]{:S(2)}) copy-start(f32[4,512,256]{2,1,0:T(8,128)} %copy-done.4) | copy-start | bytes 6291460
  37.5 1.8 %copy-start.14 = (f32[2,64,256]{2,1,0:T(8,128)S(1)}, f32[2,64,256]{2,1,0:T(8,128)}, u32[]{:S(2)}) copy-start(f32[2,64,256]{2,1,0:T(8,128)} %refs_2_.9) | copy-start | bytes 393220
  37.5 1.8 %copy-start.16 = (bf16[4,2,64,256]{3,2,1,0:T(8,128)(2,1)S(1)}, bf16[4,2,64,256]{3,2,1,0:T(8,128)(2,1)}, u32[]{:S(2)}) copy-start(bf16[4,2,64,256]{3,2,1,0:T(8,128)(2,1)} %copy-done.15) | copy-start | bytes 786436
  37.5 1.8 %copy-start.18 = (f32[4,64,256]{2,1,0:T(8,128)S(1)}, f32[4,64,256]{2,1,0:T(8,128)}, u32[]{:S(2)}) copy-start(f32[4,64,256]{2,1,0:T(8,128)} %copy-done.17) | copy-start | bytes 786436
  39.1 4.9 %copy-start.7 = (bf16[4,512,384]{2,1,0:T(8,128)(2,1)S(1)}, bf16[4,512,384]{2,1,0:T(8,128)(2,1)}, u32[]{:S(2)}) copy-start(bf16[4,512,384]{2,1,0:T(8,128)(2,1)} %copy-done.6) | copy-start | bytes 4718596
  39.2 4.9 %copy-start.13 = (bf16[4,512,512]{2,1,0:T(8,128)(2,1)S(1)}, bf16[4,512,512]{2,1,0:T(8,128)(2,1)}, u32[]{:S(2)}) copy-start(bf16[4,512,512]{2,1,0:T(8,128)(2,1)} %copy-done.12) | copy-start | bytes 6291460
  39.2 4.9 %copy-start.25 = (s32[2,1,4]{2,1,0:T(1,128)S(1)}, s32[2,1,4]{2,1,0:T(1,128)}, u32[]{:S(2)}) copy-start(s32[2,1,4]{2,1,0:T(1,128)} %refs_0_.17) | copy-start | bytes 100
  39.2 3.5 %collective-permute-start.4 = (f32[1,80,256]{2,1,0:T(8,128)S(1)}, f32[1,80,256]{2,1,0:T(8,128)S(1)}, u32[]{:S(2)}, u32[]{:S(2)}) collective-permute-start(f32[1,80,256]{2,1,0:T(8,128)S(1)} %get-tuple-element.61.refs_1_.refs_6_), channel_id=1, source_target_pairs={{0,8},{8,0},{16,24},{24,16},{1,9},{9,1},{17,25},{25,17},{2,10},{10... | collective-permute-start | bytes 245768 | tf_op jit(solution)/shard_map/ppermute | solution.py:102
  40.9 11.6 %collective-permute-start.2 = (f32[4,64,256]{2,1,0:T(8,128)S(1)}, f32[4,64,256]{2,1,0:T(8,128)S(1)}, u32[]{:S(2)}, u32[]{:S(2)}) collective-permute-start(f32[4,64,256]{2,1,0:T(8,128)S(1)} %get-tuple-element.44), channel_id=1, source_target_pairs={{0,1},{1,2},{2,3},{3,4},{4,5},{5,6},{6,7},{7,0},{8,9},{9,10},{10,1... | collective-permute-start | bytes 786440 | tf_op jit(solution)/shard_map/ppermute | solution.py:99
  43.5 4.6 %collective-permute-start.5 = (f32[1,80,256]{2,1,0:T(8,128)S(1)}, f32[1,80,256]{2,1,0:T(8,128)S(1)}, u32[]{:S(2)}, u32[]{:S(2)}) collective-permute-start(f32[1,80,256]{2,1,0:T(8,128)S(1)} %combine.4), channel_id=1, source_target_pairs={{0,16},{8,24},{16,0},{24,8},{1,17},{9,25},{17,1},{25,9},{2,18},{10... | collective-permute-start | bytes 245768 | tf_op jit(solution)/shard_map/ppermute | solution.py:102
  49.3 3.2 %copy-start.22 = (f32[4,64,128]{2,1,0:T(8,128)S(1)}, f32[4,64,128]{2,1,0:T(8,128)}, u32[]{:S(2)}) copy-start(f32[4,64,128]{2,1,0:T(8,128)} %copy-done.21) | copy-start | bytes 393220
  53.8 1.4 %collective-permute-start.6 = (f32[2,64,256]{2,1,0:T(8,128)S(1)}, f32[2,64,256]{2,1,0:T(8,128)S(1)}, u32[]{:S(2)}, u32[]{:S(2)}) collective-permute-start(f32[2,64,256]{2,1,0:T(8,128)S(1)} %get-tuple-element.64.refs_1_), channel_id=1, source_target_pairs={{0,8},{8,0},{16,24},{24,16},{1,9},{9,1},{17,25},{25,17},{2,10},{10... | collective-permute-start | bytes 393224 | tf_op jit(solution)/shard_map/ppermute | solution.py:102
  56.4 5.6 %collective-permute-start.7 = (f32[2,64,256]{2,1,0:T(8,128)S(1)}, f32[2,64,256]{2,1,0:T(8,128)S(1)}, u32[]{:S(2)}, u32[]{:S(2)}) collective-permute-start(f32[2,64,256]{2,1,0:T(8,128)S(1)} %combine.5), channel_id=1, source_target_pairs={{0,16},{8,24},{16,0},{24,8},{1,17},{9,25},{17,1},{25,9},{2,18},{10... | collective-permute-start | bytes 393224 | tf_op jit(solution)/shard_map/ppermute | solution.py:102
  (6 other events, 4.0 us)

commit v3 on v0

v3 whole, which is shorter than its diff:
```python
from types import SimpleNamespace

import jax
import jax.numpy as jnp
from jax import lax
from jax.experimental import pallas as pl
from jax.experimental.pallas import tpu as pltpu
from jax.sharding import PartitionSpec as P

NODES_1D = 8
F32 = jnp.float32
BF16 = jnp.bfloat16
MIB = 1 << 20
VMEM = pltpu.VMEM
HBM = pltpu.HBM
SMEM = pltpu.SMEM


def run(body, name, ins, outs, scratch, flops):
    pairs = [a if isinstance(a, tuple) else (a, VMEM) for a in ins]
    return pl.pallas_call(
        body,
        name=name,
        in_specs=[pl.BlockSpec(memory_space=space) for _, space in pairs],
        out_specs=[pl.BlockSpec(memory_space=o.memory_space) for o in outs],
        out_shape=outs,
        scratch_shapes=scratch,
        cost_estimate=pl.CostEstimate(flops=flops, bytes_accessed=MIB, transcendentals=0),
        compiler_params=pltpu.CompilerParams(vmem_limit_bytes=24 * MIB),
    )(*[a if space is VMEM else pltpu.with_memory_space_constraint(a, space) for a, space in pairs])


def split(x):
    high = x.astype(BF16)
    return high, (x - high.astype(F32)).astype(BF16)


def dot(x, y):
    return jnp.dot(x, y, preferred_element_type=F32)


def dot_split(x, y):
    return dot(x[0], y[0]) + (dot(x[0], y[1]) + dot(x[1], y[0]))


def langmuir(lagged, rate, affinity):
    return rate * lagged * pltpu.reciprocal(1.0 + affinity * jnp.abs(lagged), approx=True)


def lateral_rows(field, per_side):
    plane = per_side * per_side
    return jnp.concatenate(
        [field[a * plane + plane - per_side : (a + 1) * plane] for a in range(per_side)], axis=0
    )


def pack_map(mapping, lanes):
    face = mapping.shape[0]
    rows = face * face // lanes
    return jnp.concatenate([mapping[q * rows : (q + 1) * rows] for q in range(lanes // face)], axis=1)


def unpack_map(packed, face):
    return jnp.concatenate(
        [packed[:, q * face : (q + 1) * face] for q in range(packed.shape[1] // face)], axis=0
    )


def bit(stage):
    return ((lax.axis_index("stream") >> stage) & 1) == 1


def per_device(inverse, upwind, lateral, inlet_trace, previous, uptake_rate, affinity, flow_order):
    cols, _, count, nodes, _ = inverse.shape
    face = upwind.shape[3]
    tracers = previous.shape[-1]
    per_side = NODES_1D
    plane = per_side * per_side
    wide = count * face
    packed = face * face // tracers
    streams, lats = lax.axis_size("stream"), lax.axis_size("lat")
    stages = streams.bit_length() - 1
    assert streams == 1 << stages
    groups = [list(range(1, cols)), [0]] if cols > 1 else [[0]]
    home = {c: (g, n) for g, group in enumerate(groups) for n, c in enumerate(group)}
    dense = 2 * count * nodes * nodes * tracers

    def to_next(value):
        return lax.ppermute(value, "lat", [(i, (i + 1) % lats) for i in range(lats)])

    def swap(value, stage):
        return lax.ppermute(value, "stream", [(i, i ^ (1 << stage)) for i in range(streams)])

    shaped = previous.reshape(cols, count, per_side, plane, tracers)

    def load_small(old, order, rate, aff, inlet, o_trace, o_old, o_order, o_rate, o_aff, o_inlet, staged, sems):
        rows = pl.ds(plane - 2 * per_side, 2 * per_side)
        copies = [pltpu.make_async_copy(old.at[c, :, :, rows], staged.at[c], sems.at[c]) for c in range(cols)]
        small = ((order, o_order), (rate, o_rate), (aff, o_aff), (inlet, o_inlet))
        copies += [pltpu.make_async_copy(a, b, sems.at[cols + k]) for k, (a, b) in enumerate(small)]
        for copy in reversed(copies[:cols]):
            copy.start()
        for copy in copies[cols:]:
            copy.start()
        for c in reversed(range(cols)):
            copies[c].wait()
            for j in range(count):
                for a in range(per_side):
                    part = staged[c, j, a].astype(F32)[per_side:]
                    if c == cols - 1:
                        o_trace[j, pl.ds(a * per_side, per_side)] = part
                    else:
                        o_old[c, j, pl.ds(a * per_side, per_side)] = part
        for copy in copies[cols:]:
            copy.wait()

    trace, old, order, rate, aff, inlet = run(
        load_small,
        "load_small",
        [
            (shaped, HBM),
            (flow_order.reshape(cols, count), HBM),
            (uptake_rate.reshape(1, tracers), HBM),
            (affinity.reshape(1, tracers), HBM),
            (inlet_trace, HBM),
        ],
        [
            VMEM((count, face, tracers), F32),
            VMEM((max(cols - 1, 1), count, face, tracers), F32),
            SMEM((cols, count), jnp.int32),
            VMEM((1, tracers), F32),
            VMEM((1, tracers), F32),
            VMEM((cols, face, tracers), F32),
        ],
        [VMEM((cols, count, per_side, 2 * per_side, tracers), BF16), pltpu.SemaphoreType.DMA((cols + 4,))],
        dense // 100,
    )
    order = (order, SMEM)
    arrived = to_next(trace)

    def end_of(free, tails, i, s):
        return free[i, pl.ds(nodes - face, face)] + dot_split(split(tails[i][:, face:]), s)

    def offset(n, rows_high, rows_low, ends, high, low):
        for p in range(count - 1):
            e = split(ends[n * count + p])
            high[n, pl.ds(p * face, face)] = e[0]
            low[n, pl.ds(p * face, face)] = e[1]
        last = pl.ds(wide, face)
        row = (rows_high[n, last][:, face:], rows_low[n, last][:, face:])
        return ends[n * count + count - 1] + dot_split(row, (high[n], low[n]))

    def side_outs(size):
        return [VMEM((size * count, 2, face, tracers), BF16), VMEM((size * count, face, tracers), F32)]

    def offset_scratch(size):
        return [VMEM((size, wide - face, tracers), BF16)] * 2

    def sweep_scratch():
        return [VMEM((2, nodes, tracers), BF16)] * 2

    def loaded(size):
        return [
            VMEM((size * count, nodes, nodes), BF16),
            VMEM((size * count, 2 * face, nodes), BF16),
            VMEM((size * count, nodes, tracers), BF16),
        ]

    def first(g, fetched):
        group = groups[g]
        size = len(group)
        items = size * count
        local = group[0] > 0
        loads = fetched is None

        def body(*refs):
            refs = list(refs)
            take = lambda k: [refs.pop(0) for _ in range(k)]
            (order_r,) = take(1)
            if loads:
                hbm = take(4)
            else:
                fields = take(3)
            rate_r, aff_r, old_r = take(3)
            if loads:
                fields_of = [take(1) if h == g else take(3) for h in range(len(groups))]
            maps, free, side_maps, tails, rows_high, rows_low, message = take(7)
            if local:
                sides, ends = take(2)
            source_high, source_low, row = take(3)
            if loads:
                (sems,) = take(1)
                fields_of[g] += take(2)
                fields = fields_of[g]

                def copies(h, i):
                    c, j = groups[h][i // count], i % count
                    to_inv, to_faces, to_lagged = fields_of[h]
                    k = c * count + j
                    return (
                        pltpu.make_async_copy(hbm[3].at[c, 0, j], to_lagged.at[i], sems.at[0, k]),
                        pltpu.make_async_copy(hbm[1].at[c, 0, j], to_faces.at[i, pl.ds(0, face)], sems.at[1, k]),
                        pltpu.make_async_copy(hbm[2].at[c, 0, j], to_faces.at[i, pl.ds(face, face)], sems.at[2, k]),
                        pltpu.make_async_copy(hbm[0].at[c, 0, j], to_inv.at[i], sems.at[3, k]),
                    )

                for h in range(len(groups)):
                    for i in range(len(groups[h]) * count):
                        for copy in copies(h, i):
                            copy.start()

            inv, faces, lagged = fields
            for i in range(items + 1):
                if i < items:
                    if loads:
                        for copy in copies(g, i):
                            copy.wait()
                    both = lax.dot_general(
                        inv[i], faces[i], (((1,), (1,)), ((), ())), preferred_element_type=F32
                    )
                    b_high, b_low = split(both)
                    maps[i] = jnp.concatenate([b_high, b_high, b_low], axis=1)
                    tails[i] = both[nodes - face :]
                    s = split(lateral_rows(both, per_side))
                    side_maps[i] = jnp.concatenate([s[0], s[0], s[1]], axis=1)
                    s = split(langmuir(lagged[i].astype(F32), rate_r[...], aff_r[...]))
                    source_high[i % 2], source_low[i % 2] = s
                if i > 0:
                    k = (i - 1) % 2
                    free[i - 1] = dot(inv[i - 1], source_high[k]) + dot(inv[i - 1], source_low[k])

            row_id = lax.broadcasted_iota(jnp.int32, (face, wide), 0)
            lane_id = lax.broadcasted_iota(jnp.int32, (face, wide), 1)
            outflow = [None] * size
            for p in range(count):
                for n, c in enumerate(group):
                    j = order_r[c, p]
                    i = n * count + j
                    step = split(tails[i][:, :face])
                    unit = jnp.where(lane_id == row_id + p * face, 1.0, 0.0)
                    r = split(unit if p == 0 else row[n] + unit)
                    rows_high[n, pl.ds(p * face, face)] = r[0]
                    rows_low[n, pl.ds(p * face, face)] = r[1]
                    row[n] = dot_split(step, r)
                    if local:
                        s = split(old_r[c - 1, j])
                        sides[n * count + p, 0] = s[0]
                        sides[n * count + p, 1] = s[1]
                        end = end_of(free, tails, i, s)
                        ends[n * count + p] = end
                        outflow[n] = end if p == 0 else end + dot_split(step, split(outflow[n]))
            for n in range(size):
                r = split(row[n])
                rows_high[n, pl.ds(wide, face)] = r[0]
                rows_low[n, pl.ds(wide, face)] = r[1]
                message[n, pl.ds(face, packed)] = pack_map(row[n][:, :face], tracers)
                if local:
                    message[n, pl.ds(0, face)] = outflow[n]
            if loads:
                for h in range(len(groups)):
                    if h != g:
                        for i in range(len(groups[h]) * count):
                            for copy in copies(h, i):
                                copy.wait()

        outs = [
            VMEM((items, nodes, 6 * face), BF16),
            VMEM((items, nodes, tracers), F32),
            VMEM((items, face, 6 * face), BF16),
            VMEM((items, face, 2 * face), F32),
            VMEM((size, wide + face, wide), BF16),
            VMEM((size, wide + face, wide), BF16),
            VMEM((size, face + packed, tracers), F32),
        ]
        if local:
            outs += side_outs(size)
        scratch = sweep_scratch() + [VMEM((size, face, wide), F32)]
        if loads:
            others = [loaded(len(groups[h])) for h in range(len(groups))]
            scratch += [pltpu.SemaphoreType.DMA((4, cols * count))] + others[g][1:]
            others[g] = others[g][:1]
            outs = sum(others, []) + outs
            fields = [(a, HBM) for a in (inverse, upwind, lateral, previous)]
        else:
            fields = fetched[g]
        values = run(body, "first", [order, *fields, rate, aff, old], outs, scratch, 3 * size * dense)
        if loads:
            fetched = []
            for other in others:
                fetched.append(values[: len(other)])
                values = values[len(other) :]
        state = SimpleNamespace(inv=fetched[g][0])
        state.maps, state.free, state.side_maps, state.tails, state.high, state.low, state.message = values[:7]
        if local:
            state.sides, state.ends = values[7:]
        return state, fetched

    def arrived_side(arrived, j):
        return split(jnp.where(lax.axis_index("lat") > 0, arrived[j], 0.0))

    def first_sides(state, arrived):
        def body(order, arrived, free, tails, rows_high, rows_low, mapped, sides, ends, message, high, low):
            for p in range(count):
                j = order[0, p]
                s = arrived_side(arrived, j)
                sides[p, 0] = s[0]
                sides[p, 1] = s[1]
                ends[p] = end_of(free, tails, j, s)
            message[0, pl.ds(0, face)] = offset(0, rows_high, rows_low, ends, high, low)
            message[0, pl.ds(face, packed)] = mapped[0, pl.ds(face, packed)]

        state.sides, state.ends, state.message = run(
            body,
            "first_sides",
            [order, arrived, state.free, state.tails, state.high, state.low, state.message],
            side_outs(1) + [VMEM((1, face + packed, tracers), F32)],
            offset_scratch(1),
            dense // 50,
        )

    def combine_first(stage, own, other):
        def body(own, other, message):
            upper = bit(stage)
            for n in range(own.shape[0]):
                up = jnp.where(upper, own[n], other[n])
                low = jnp.where(upper, other[n], own[n])
                m = split(unpack_map(up[face:], face))
                message[n, pl.ds(0, face)] = dot_split(m, split(low[:face])) + up[:face]
                mapped = dot_split(m, split(unpack_map(low[face:], face)))
                message[n, pl.ds(face, packed)] = pack_map(mapped, tracers)

        return run(body, "combine", [own, other], [VMEM(own.shape, F32)], [], dense // 100)[0]

    def combine_second(stage, own, other, old_own, old_other):
        def body(own, other, *refs):
            message = refs[-1]
            upper = bit(stage)
            for c in range(cols):
                g, n = home[c]
                mine, theirs = refs[2 * g], refs[2 * g + 1]
                m = jnp.where(upper, mine[n, pl.ds(face, packed)], theirs[n, pl.ds(face, packed)])
                up = jnp.where(upper, own[c], other[c])
                low = jnp.where(upper, other[c], own[c])
                message[c] = dot_split(split(unpack_map(m, face)), split(low)) + up

        ins = [own, other]
        for pair in zip(old_own, old_other):
            ins += pair
        return run(body, "combine", ins, [VMEM(own.shape, F32)], [], dense // 100)[0]

    def enter(group, order, inlet, offsets, mapped, rows_high, rows_low, sides, ends, stack, high, low):
        for n, c in enumerate(group):
            entering = inlet[c]
            for stage in reversed(range(stages)):
                m = split(unpack_map(mapped[stage](n, c), face))
                beyond = dot_split(m, split(entering)) + offsets[stage](n, c)
                entering = jnp.where(bit(stage), beyond, entering)
            e = split(entering)
            high[n, pl.ds(0, face)] = e[0]
            low[n, pl.ds(0, face)] = e[1]
            for p in range(count - 1):
                e = split(ends[n * count + p])
                high[n, pl.ds((p + 1) * face, face)] = e[0]
                low[n, pl.ds((p + 1) * face, face)] = e[1]
            span = pl.ds(0, wide)
            inflow = dot_split((rows_high[n, span], rows_low[n, span]), (high[n], low[n]))
            for p in range(count):
                i = n * count + order[c, p]
                f = split(inflow[p * face : (p + 1) * face])
                side = (sides[n * count + p, 0], sides[n * count + p, 1])
                for q, part in enumerate((f[0], side[0], f[1], side[1], f[0], side[0])):
                    stack[i, pl.ds(q * face, face)] = part

    def enter_scratch(size):
        return [VMEM((size, wide, tracers), BF16)] * 2

    def enter_first(group, state):
        size = len(group)
        last = group[-1] == cols - 1

        def body(order, inlet, rows_high, rows_low, sides, ends, free, side_maps, *refs):
            got, refs = refs[:stages], refs[stages:]
            stack, (high, low) = refs[0], refs[-2:]
            enter(
                group, order, inlet,
                [lambda n, c, r=r: r[n, pl.ds(0, face)] for r in got],
                [lambda n, c, r=r: r[n, pl.ds(face, packed)] for r in got],
                rows_high, rows_low, sides, ends, stack, high, low,
            )
            if last:
                for j in range(count):
                    i = (size - 1) * count + j
                    refs[1][j] = lateral_rows(free.at[i], per_side) + dot(side_maps[i], stack[i])

        outs = [VMEM((size * count, 6 * face, tracers), BF16)]
        if last:
            outs.append(VMEM((count, face, tracers), F32))
        ins = [order, inlet, state.high, state.low, state.sides, state.ends, state.free, state.side_maps]
        values = run(body, "enter", ins + state.received, outs, enter_scratch(size), dense // 50)
        state.stack = values[0]
        return values[1] if last else None

    def second(group, state):
        size = len(group)
        items = size * count

        def body(inv, maps, free, stack, rate, aff, fresh, traces, source_high, source_low):
            for i in range(items + 1):
                if i < items:
                    swept = free[i] + dot(maps[i], stack[i])
                    traces[i // count, i % count] = lateral_rows(swept, per_side)
                    source_high[i % 2], source_low[i % 2] = split(langmuir(swept, rate[...], aff[...]))
                if i > 0:
                    k = (i - 1) % 2
                    fresh[i - 1] = dot(inv[i - 1], source_high[k]) + dot(inv[i - 1], source_low[k])

        state.fresh, state.traces = run(
            body,
            "second",
            [state.inv, state.maps, state.free, state.stack, rate, aff],
            [VMEM((items, nodes, tracers), F32), VMEM((size, count, face, tracers), F32)],
            sweep_scratch(),
            3 * size * dense,
        )

    def second_sides(arrived):
        per = 5

        def body(order, arrived, *refs):
            got = [refs[per * g : per * g + per] for g in range(len(groups))]
            refs = refs[per * len(groups) :]
            message, refs = refs[0], refs[1:]
            for g, group in enumerate(groups):
                fresh, _, tails, rows_high, rows_low = got[g]
                sides, ends = refs[2 * g : 2 * g + 2]
                high, low = refs[2 * (len(groups) + g) : 2 * (len(groups) + g) + 2]
                for n, c in enumerate(group):
                    for p in range(count):
                        j = order[c, p]
                        if c == 0:
                            s = arrived_side(arrived, j)
                        else:
                            h, m = home[c - 1]
                            s = split(got[h][1][m, j])
                        sides[n * count + p, 0] = s[0]
                        sides[n * count + p, 1] = s[1]
                        ends[n * count + p] = end_of(fresh, tails, n * count + j, s)
                    message[c] = offset(n, rows_high, rows_low, ends, high, low)

        ins = [order, arrived]
        outs, scratch = [VMEM((cols, face, tracers), F32)], []
        for group, state in zip(groups, states):
            ins += [state.fresh, state.traces, state.tails, state.high, state.low]
            outs += side_outs(len(group))
            scratch += offset_scratch(len(group))
        message, *values = run(body, "second_sides", ins, outs, scratch, dense // 50)
        for g, state in enumerate(states):
            state.sides, state.ends = values[2 * g : 2 * g + 2]
        return message

    def result(offsets):
        per = 6 + stages

        def body(order, inlet, *refs):
            offs, refs = refs[:stages], refs[stages:]
            got = [refs[per * g : per * g + per] for g in range(len(groups))]
            out, staged, sems, *refs = refs[per * len(groups) :]
            for g, group in enumerate(groups):
                rows_high, rows_low, sides, ends, _, _, *mapped = got[g]
                enter(
                    group, order, inlet,
                    [lambda n, c, r=r: r[c] for r in offs],
                    [lambda n, c, r=r: r[n, pl.ds(face, packed)] for r in mapped],
                    rows_high, rows_low, sides, ends, *refs[3 * g : 3 * g + 3],
                )
            started = []
            for g, group in enumerate(groups):
                fresh, maps = got[g][4:6]
                for n, c in enumerate(group):
                    for j in range(count):
                        i, k = n * count + j, len(started)
                        staged[k] = (fresh[i] + dot(maps[i], refs[3 * g][i])).astype(BF16)
                        copy = pltpu.make_async_copy(staged.at[k], out.at[c, 0, j], sems.at[k])
                        copy.start()
                        started.append(copy)
            for copy in started:
                copy.wait()

        ins = [order, inlet, *offsets]
        scratch = [VMEM((cols * count, nodes, tracers), BF16), pltpu.SemaphoreType.DMA((cols * count,))]
        for group, state in zip(groups, states):
            ins += [state.high, state.low, state.sides, state.ends, state.fresh, state.maps, *state.received]
            scratch += [VMEM((len(group) * count, 6 * face, tracers), BF16)] + enter_scratch(len(group))
        return run(body, "result", ins, [HBM(previous.shape, BF16)], scratch, cols * dense)[0]

    states, fetched = [], None
    for g, group in enumerate(groups):
        state, fetched = first(g, fetched)
        if 0 in group:
            first_sides(state, arrived)
        state.sent, state.received = [state.message], []
        for stage in range(stages):
            if stage:
                state.sent.append(combine_first(stage - 1, state.sent[-1], state.received[-1]))
            state.received.append(swap(state.sent[-1], stage))
        states.append(state)
    for group, state in zip(groups, states):
        trace = enter_first(group, state)
        if trace is not None:
            arrived = to_next(trace)
    for group, state in zip(groups, states):
        second(group, state)
    message, offsets = second_sides(arrived), []
    for stage in range(stages):
        offsets.append(swap(message, stage))
        if stage + 1 < stages:
            message = combine_second(
                stage, message, offsets[-1], [s.sent[stage] for s in states], [s.received[stage] for s in states]
            )
    return result(offsets)


def solution(mesh):
    placed = (
        P("lat", "stream", None, None, None),
        P("lat", "stream", None, None, None),
        P("lat", "stream", None, None, None),
        P("lat", None, None),
        P("lat", "stream", None, None, None),
        P(),
        P(),
        P("lat", "stream", None),
    )
    return jax.shard_map(
        per_device,
        mesh=mesh,
        in_specs=placed,
        out_specs=P("lat", "stream", None, None, None),
        check_vma=False,
    )
```

time: 277 us -> 39.9 us (0.14)
  the two profiles are of different devices: /device:TPU:13 before, /device:TPU:0 now
where the time goes in v3:
time: 39.9 us; the launch traced here: 39.8 us
  Pallas kernels  20 us (50%)
  waiting for transfers between devices  11 us (28%)
  starting transfers between devices  8.56 us (21%)
    pallas_call x13, Pallas kernels, run(): pl.pallas_call(body, name=name, in_specs=[pl.BlockSpec(memory_space=space...  20 us
    ppermute x6, waiting for transfers between devices, swap(): lax.ppermute(value, 'stream', [(i, i ^ 1 << stage) for i in range(streams)])  8.71 us
    ppermute x2, starting transfers between devices, to_next(): lax.ppermute(value, 'lat', [(i, (i + 1) % lats) for i in range(lats)])  4.77 us
    ppermute x6, starting transfers between devices, swap(): lax.ppermute(value, 'stream', [(i, i ^ 1 << stage) for i in range(streams)])  3.79 us
    ppermute x2, waiting for transfers between devices, to_next(): lax.ppermute(value, 'lat', [(i, (i + 1) % lats) for i in range(lats)])  2.26 us
  transfers between devices with their start and end apart: 8, of which 5 were waited for; matrix products, arithmetic and copies ran while one was open for 0% of the time, Pallas kernels for 37%

profile of v3, /device:TPU:0, one launch (start us, length us, event | category | flops | bytes accessed | tf_op | source)
XLA Modules:
  0.0 39.8 jit_solution(11462483194494352668)
XLA Ops:
  0.0 1.1 %load_small.1 = (f32[4,64,256]{2,1,0:T(8,128)S(1)}, f32[1,4,64,256]{3,2,1,0:T(8,128)S(1)}, s32[2,4]{1,0:T(2,128)S(4)}, f32[1,256]{1,0:T(1,128)S(1)}, f32[1,256]{1,0:T(1,128)S(1)}, /*index=5*/f32[2,64,256]{2,1,0:T(8,128)S(1)}) custom-call(bf16[2,4,8,64,256]{4,3,2,1,0:T(8,128)(2,1)} %bitcast.4, s32[2,4]{1,0:T(2,128)} %bitcast.5, f32[1,256]{1,0:T(1,128)} %bitcast.6, ...), custom_call_target="tpu_custom_call" | custom-call | flops 5368709 | bytes 1048576 | tf_op jit(solution)/shard_map/load_small/pallas_call | solution.py:21
  1.2 3.0 %collective-permute-start.3 = (f32[4,64,256]{2,1,0:T(8,128)S(1)}, f32[4,64,256]{2,1,0:T(8,128)S(1)}, u32[]{:S(2)}, u32[]{:S(2)}) collective-permute-start(f32[4,64,256]{2,1,0:T(8,128)S(1)} %get-tuple-element.71), channel_id=1, source_target_pairs={{0,1},{1,2},{2,3},{3,4},{4,5},{5,6},{6,7},{7,0},{8,9},{9,10},{10,1... | collective-permute-start | bytes 786440 | tf_op jit(solution)/shard_map/ppermute | solution.py:89
  4.1 5.4 %first.2 = (bf16[4,512,512]{2,1,0:T(8,128)(2,1)S(1)}, bf16[4,512,512]{2,1,0:T(8,128)(2,1)S(1)}, bf16[4,128,512]{2,1,0:T(8,128)(2,1)S(1)}, bf16[4,512,256]{2,1,0:...) custom-call(s32[2,4]{1,0:T(2,128)S(4)} %get-tuple-element.45.refs_0_, ...), custom_call_target="tpu_custom_call" | custom-call | flops 1610612736 | bytes 1048576 | tf_op jit(solution)/shard_map/first/pallas_call | solution.py:21
  9.6 0.1 collective-permute-start
  9.6 1.3 %collective-permute-done.other.refs_0_.refs_1_.refs_8_ = f32[1,80,256]{2,1,0:T(8,128)S(1)} collective-permute-done((f32[1,80,256]{2,1,0:T(8,128)S(1)}, f32[1,80,256]{2,1,0:T(8,128)S(1)}, u32[]{:S(2)}, u32[]{:S(2)}) %collective-permute-start) | collective-permute-done | bytes 81952 | tf_op jit(solution)/shard_map/ppermute | solution.py:92
  10.9 0.3 combine.3
  11.2 1.5 %collective-permute-start.1 = (f32[1,80,256]{2,1,0:T(8,128)S(1)}, f32[1,80,256]{2,1,0:T(8,128)S(1)}, u32[]{:S(2)}, u32[]{:S(2)}) collective-permute-start(f32[1,80,256]{2,1,0:T(8,128)S(1)} %combine.3), channel_id=1, source_target_pairs={{0,16},{8,24},{16,0},{24,8},{1,17},{9,25},{17,1},{25,9},{2,18},{10... | collective-permute-start | bytes 245768 | tf_op jit(solution)/shard_map/ppermute | solution.py:92
  12.7 2.5 %first.3 = (bf16[4,512,384]{2,1,0:T(8,128)(2,1)S(1)}, f32[4,512,256]{2,1,0:T(8,128)S(1)}, bf16[4,64,384]{2,1,0:T(8,128)(2,1)S(1)}, f32[4,64,128]{2,1,0:T(8,128)S...) custom-call(s32[2,4]{1,0:T(2,128)S(4)} %get-tuple-element.45.refs_0_.order, ...), custom_call_target="tpu_custom_call" | custom-call | flops 1610612736 | bytes 1048576 | tf_op jit(solution)/shard_map/first/pallas_call | solution.py:21
  15.2 0.0 collective-permute-done.3.arrived
  15.2 0.5 %first_sides.1 = (bf16[4,2,64,256]{3,2,1,0:T(8,128)(2,1)S(1)}, f32[4,64,256]{2,1,0:T(8,128)S(1)}, f32[1,80,256]{2,1,0:T(8,128)S(1)}) custom-call(s32[2,4]{1,0:T(2,128)S(4)} %get-tuple-element.45.refs_0_.order, f32[4,64,256]{2,1,0:T(8,128)S(1)} %collective-permute-done.3.arrived, f32[4,512,256]{2,1,0:T(8,128)S(1)} %get-tuple-element.68.free, ...), custom_call_target="tpu_custom_call" | custom-call | flops 10737418 | bytes 1048576 | tf_op jit(solution)/shard_map/first_sides/pallas_call | solution.py:21
  15.7 0.1 collective-permute-start.4
  15.8 0.0 collective-permute-done.1.refs_1_.refs_9_
  15.8 1.1 %enter.2 = (bf16[4,384,256]{2,1,0:T(8,128)(2,1)S(1)}, f32[4,64,256]{2,1,0:T(8,128)S(1)}) custom-call(s32[2,4]{1,0:T(2,128)S(4)} %get-tuple-element.45.refs_0_.order, f32[2,64,256]{2,1,0:T(8,128)S(1)} %get-tuple-element.46.inlet, bf16[1,320,256]{2,1,0:T(8,128)(2,1)S(1)} %get-tuple-element.50.rows_high.refs_3_.refs_2_, ...), custom_call_target="tpu_custom_call" | custom-call | flops 10737418 | bytes 1048576 | tf_op jit(solution)/shard_map/enter/pallas_call | solution.py:21
  16.9 1.8 %collective-permute-start.2 = (f32[4,64,256]{2,1,0:T(8,128)S(1)}, f32[4,64,256]{2,1,0:T(8,128)S(1)}, u32[]{:S(2)}, u32[]{:S(2)}) collective-permute-start(f32[4,64,256]{2,1,0:T(8,128)S(1)} %get-tuple-element.57), channel_id=1, source_target_pairs={{0,1},{1,2},{2,3},{3,4},{4,5},{5,6},{6,7},{7,0},{8,9},{9,10},{10,1... | collective-permute-start | bytes 786440 | tf_op jit(solution)/shard_map/ppermute | solution.py:89
  18.7 0.0 collective-permute-done.4.other.refs_0_.refs_3_.refs_16_
  18.7 0.3 combine.4
  19.0 1.5 %collective-permute-start.5 = (f32[1,80,256]{2,1,0:T(8,128)S(1)}, f32[1,80,256]{2,1,0:T(8,128)S(1)}, u32[]{:S(2)}, u32[]{:S(2)}) collective-permute-start(f32[1,80,256]{2,1,0:T(8,128)S(1)} %combine.4), channel_id=1, source_target_pairs={{0,16},{8,24},{16,0},{24,8},{1,17},{9,25},{17,1},{25,9},{2,18},{10... | collective-permute-start | bytes 245768 | tf_op jit(solution)/shard_map/ppermute | solution.py:92
  20.4 2.0 %second.2 = (f32[4,512,256]{2,1,0:T(8,128)S(1)}, f32[1,4,64,256]{3,2,1,0:T(8,128)S(1)}) custom-call(bf16[4,512,512]{2,1,0:T(8,128)(2,1)S(1)} %get-tuple-element.58.inv, bf16[4,512,384]{2,1,0:T(8,128)(2,1)S(1)} %get-tuple-element.59.maps.refs_7_, f32[4,512,256]{2,1,0:T(8,128)S(1)} %get-tuple-element.54.free, ...), custom_call_target="tpu_custom_call" | custom-call | flops 1610612736 | bytes 1048576 | tf_op jit(solution)/shard_map/second/pallas_call | solution.py:21
  22.5 1.1 %collective-permute-done.5.refs_1_.refs_17_ = f32[1,80,256]{2,1,0:T(8,128)S(1)} collective-permute-done((f32[1,80,256]{2,1,0:T(8,128)S(1)}, f32[1,80,256]{2,1,0:T(8,128)S(1)}, u32[]{:S(2)}, u32[]{:S(2)}) %collective-permute-start.5) | collective-permute-done | bytes 81952 | tf_op jit(solution)/shard_map/ppermute | solution.py:92
  23.5 0.7 %enter.3.stack = bf16[4,384,256]{2,1,0:T(8,128)(2,1)S(1)} custom-call(s32[2,4]{1,0:T(2,128)S(4)} %get-tuple-element.45.refs_0_.order, f32[2,64,256]{2,1,0:T(8,128)S(1)} %get-tuple-element.46.inlet, bf16[1,320,256]{2,1,0:T(8,128)(2,1)S(1)} %get-tuple-element.69.rows_high.refs_8_.refs_10_, ...), custom_call_target="tpu_custom_call" | custom-call | flops 10737418 | bytes 1048576 | tf_op jit(solution)/shard_map/enter/pallas_call | solution.py:21
  24.2 2.0 %second.3 = (f32[4,512,256]{2,1,0:T(8,128)S(1)}, f32[1,4,64,256]{3,2,1,0:T(8,128)S(1)}) custom-call(bf16[4,512,512]{2,1,0:T(8,128)(2,1)S(1)} %get-tuple-element.64.refs_1_.inv, bf16[4,512,384]{2,1,0:T(8,128)(2,1)S(1)} %get-tuple-element.67.maps.refs_15_, f32[4,512,256]{2,1,0:T(8,128)S(1)} %get-tuple-element.68.free, bf16[4,384,256]{2,1,0:T(8,128)(2,1)S(1)} %enter.3.stack, ...), custom_call_target="tpu_custom_call" | custom-call | flops 1610612736 | bytes 1048576 | tf_op jit(solution)/shard_map/second/pallas_call | solution.py:21
  26.3 2.3 %collective-permute-done.2.arrived = f32[4,64,256]{2,1,0:T(8,128)S(1)} collective-permute-done((f32[4,64,256]{2,1,0:T(8,128)S(1)}, f32[4,64,256]{2,1,0:T(8,128)S(1)}, u32[]{:S(2)}, u32[]{:S(2)}) %collective-permute-start.2) | collective-permute-done | bytes 262176 | tf_op jit(solution)/shard_map/ppermute | solution.py:89
  28.5 0.8 %second_sides.1 = (f32[2,64,256]{2,1,0:T(8,128)S(1)}, bf16[4,2,64,256]{3,2,1,0:T(8,128)(2,1)S(1)}, f32[4,64,256]{2,1,0:T(8,128)S(1)}, bf16[4,2,64,256]{3,2,1,0:T(8,128)(2,1)S(1)}, f32[4,64,256]{2,1,0:T(8,128)S(1)}) custom-call(s32[2,4]{1,0:T(2,128)S(4)} %get-tuple-element.45.refs_0_.order, f32[4,64,256]{2,1,0:T(8,128)S(1)} %collective-permute-done.2.arrived, ...), custom_call_target="tpu_custom_call" | custom-call | flops 10737418 | bytes 1048576 | tf_op jit(solution)/shard_map/second_sides/pallas_call | solution.py:21
  29.3 0.1 collective-permute-start.6
  29.4 1.3 %collective-permute-done.6.other.refs_0_ = f32[2,64,256]{2,1,0:T(8,128)S(1)} collective-permute-done((f32[2,64,256]{2,1,0:T(8,128)S(1)}, f32[2,64,256]{2,1,0:T(8,128)S(1)}, u32[]{:S(2)}, u32[]{:S(2)}) %collective-permute-start.6) | collective-permute-done | bytes 131104 | tf_op jit(solution)/shard_map/ppermute | solution.py:92
  30.7 0.3 combine.5
  31.0 0.6 %collective-permute-start.7 = (f32[2,64,256]{2,1,0:T(8,128)S(1)}, f32[2,64,256]{2,1,0:T(8,128)S(1)}, u32[]{:S(2)}, u32[]{:S(2)}) collective-permute-start(f32[2,64,256]{2,1,0:T(8,128)S(1)} %combine.5), channel_id=1, source_target_pairs={{0,16},{8,24},{16,0},{24,8},{1,17},{9,25},{17,1},{25,9},{2,18},{10... | collective-permute-start | bytes 393224 | tf_op jit(solution)/shard_map/ppermute | solution.py:92
  31.5 5.0 %collective-permute-done.7.refs_1_ = f32[2,64,256]{2,1,0:T(8,128)S(1)} collective-permute-done((f32[2,64,256]{2,1,0:T(8,128)S(1)}, f32[2,64,256]{2,1,0:T(8,128)S(1)}, u32[]{:S(2)}, u32[]{:S(2)}) %collective-permute-start.7) | collective-permute-done | bytes 131104 | tf_op jit(solution)/shard_map/ppermute | solution.py:92
  36.6 3.0 %result.1 = bf16[2,1,4,512,256]{4,3,2,1,0:T(8,128)(2,1)} custom-call(s32[2,4]{1,0:T(2,128)S(4)} %get-tuple-element.45.refs_0_.order, f32[2,64,256]{2,1,0:T(8,128)S(1)} %get-tuple-element.46.inlet, f32[2,64,256]{2,1,0:T(8,128)S(1)} %collective-permute-done.6.other.refs_0_, f32[2,64,256]{2,1,0:T(8,128)S(1)} %collective-permute-done.7.refs_1_, ...), custom_call_target="tpu_custom_call" | custom-call | flops 1073741824 | bytes 1048576 | tf_op jit(solution)/shard_map/result/pallas_call | solution.py:21
Async XLA Ops:
  1.2 14.1 %collective-permute-start.3 = (f32[4,64,256]{2,1,0:T(8,128)S(1)}, f32[4,64,256]{2,1,0:T(8,128)S(1)}, u32[]{:S(2)}, u32[]{:S(2)}) collective-permute-start(f32[4,64,256]{2,1,0:T(8,128)S(1)} %get-tuple-element.71), channel_id=1, source_target_pairs={{0,1},{1,2},{2,3},{3,4},{4,5},{5,6},{6,7},{7,0},{8,9},{9,10},{10,1... | collective-permute-start | bytes 786440 | tf_op jit(solution)/shard_map/ppermute | solution.py:89
  9.6 1.3 %collective-permute-start = (f32[1,80,256]{2,1,0:T(8,128)S(1)}, f32[1,80,256]{2,1,0:T(8,128)S(1)}, u32[]{:S(2)}, u32[]{:S(2)}) collective-permute-start(f32[1,80,256]{2,1,0:T(8,128)S(1)} %get-tuple-element.56.own.refs_0_), channel_id=1, source_target_pairs={{0,8},{8,0},{16,24},{24,16},{1,9},{9,1},{17,25},{25,17},{2,10},{10... | collective-permute-start | bytes 245768 | tf_op jit(solution)/shard_map/ppermute | solution.py:92
  11.2 4.6 %collective-permute-start.1 = (f32[1,80,256]{2,1,0:T(8,128)S(1)}, f32[1,80,256]{2,1,0:T(8,128)S(1)}, u32[]{:S(2)}, u32[]{:S(2)}) collective-permute-start(f32[1,80,256]{2,1,0:T(8,128)S(1)} %combine.3), channel_id=1, source_target_pairs={{0,16},{8,24},{16,0},{24,8},{1,17},{9,25},{17,1},{25,9},{2,18},{10... | collective-permute-start | bytes 245768 | tf_op jit(solution)/shard_map/ppermute | solution.py:92
  15.7 3.0 %collective-permute-start.4 = (f32[1,80,256]{2,1,0:T(8,128)S(1)}, f32[1,80,256]{2,1,0:T(8,128)S(1)}, u32[]{:S(2)}, u32[]{:S(2)}) collective-permute-start(f32[1,80,256]{2,1,0:T(8,128)S(1)} %get-tuple-element.77.own.refs_2_), channel_id=1, source_target_pairs={{0,8},{8,0},{16,24},{24,16},{1,9},{9,1},{17,25},{25,17},{2,10},{10... | collective-permute-start | bytes 245768 | tf_op jit(solution)/shard_map/ppermute | solution.py:92
  16.9 11.6 %collective-permute-start.2 = (f32[4,64,256]{2,1,0:T(8,128)S(1)}, f32[4,64,256]{2,1,0:T(8,128)S(1)}, u32[]{:S(2)}, u32[]{:S(2)}) collective-permute-start(f32[4,64,256]{2,1,0:T(8,128)S(1)} %get-tuple-element.57), channel_id=1, source_target_pairs={{0,1},{1,2},{2,3},{3,4},{4,5},{5,6},{6,7},{7,0},{8,9},{9,10},{10,1... | collective-permute-start | bytes 786440 | tf_op jit(solution)/shard_map/ppermute | solution.py:89
  19.0 4.6 %collective-permute-start.5 = (f32[1,80,256]{2,1,0:T(8,128)S(1)}, f32[1,80,256]{2,1,0:T(8,128)S(1)}, u32[]{:S(2)}, u32[]{:S(2)}) collective-permute-start(f32[1,80,256]{2,1,0:T(8,128)S(1)} %combine.4), channel_id=1, source_target_pairs={{0,16},{8,24},{16,0},{24,8},{1,17},{9,25},{17,1},{25,9},{2,18},{10... | collective-permute-start | bytes 245768 | tf_op jit(solution)/shard_map/ppermute | solution.py:92
  29.3 1.4 %collective-permute-start.6 = (f32[2,64,256]{2,1,0:T(8,128)S(1)}, f32[2,64,256]{2,1,0:T(8,128)S(1)}, u32[]{:S(2)}, u32[]{:S(2)}) collective-permute-start(f32[2,64,256]{2,1,0:T(8,128)S(1)} %get-tuple-element.80.own), channel_id=1, source_target_pairs={{0,8},{8,0},{16,24},{24,16},{1,9},{9,1},{17,25},{25,17},{2,10},{10... | collective-permute-start | bytes 393224 | tf_op jit(solution)/shard_map/ppermute | solution.py:92
  31.0 5.6 %collective-permute-start.7 = (f32[2,64,256]{2,1,0:T(8,128)S(1)}, f32[2,64,256]{2,1,0:T(8,128)S(1)}, u32[]{:S(2)}, u32[]{:S(2)}) collective-permute-start(f32[2,64,256]{2,1,0:T(8,128)S(1)} %combine.5), channel_id=1, source_target_pairs={{0,16},{8,24},{16,0},{24,8},{1,17},{9,25},{17,1},{25,9},{2,18},{10... | collective-permute-start | bytes 393224 | tf_op jit(solution)/shard_map/ppermute | solution.py:92

commit v4 on v3

v4 whole, which is shorter than its diff:
```python
from types import SimpleNamespace

import jax
import jax.numpy as jnp
from jax import lax
from jax.experimental import pallas as pl
from jax.experimental.pallas import tpu as pltpu
from jax.sharding import PartitionSpec as P

NODES_1D = 8
F32 = jnp.float32
BF16 = jnp.bfloat16
MIB = 1 << 20
VMEM = pltpu.VMEM
HBM = pltpu.HBM
SMEM = pltpu.SMEM


def run(body, name, ins, outs, scratch, flops):
    pairs = [a if isinstance(a, tuple) else (a, VMEM) for a in ins]
    return pl.pallas_call(
        body,
        name=name,
        in_specs=[pl.BlockSpec(memory_space=space) for _, space in pairs],
        out_specs=[pl.BlockSpec(memory_space=o.memory_space) for o in outs],
        out_shape=outs,
        scratch_shapes=scratch,
        cost_estimate=pl.CostEstimate(flops=flops, bytes_accessed=MIB, transcendentals=0),
        compiler_params=pltpu.CompilerParams(vmem_limit_bytes=24 * MIB),
    )(*[a if space is VMEM else pltpu.with_memory_space_constraint(a, space) for a, space in pairs])


def split(x):
    high = x.astype(BF16)
    return high, (x - high.astype(F32)).astype(BF16)


def dot(x, y):
    return jnp.dot(x, y, preferred_element_type=F32)


def dot_split(x, y):
    return dot(x[0], y[0]) + (dot(x[0], y[1]) + dot(x[1], y[0]))


def langmuir(lagged, rate, affinity):
    return rate * lagged * pltpu.reciprocal(1.0 + affinity * jnp.abs(lagged), approx=True)


def lateral_rows(field, per_side):
    plane = per_side * per_side
    return jnp.concatenate(
        [field[a * plane + plane - per_side : (a + 1) * plane] for a in range(per_side)], axis=0
    )


def pack_map(mapping, lanes):
    face = mapping.shape[0]
    rows = face * face // lanes
    return jnp.concatenate([mapping[q * rows : (q + 1) * rows] for q in range(lanes // face)], axis=1)


def unpack_map(packed, face):
    return jnp.concatenate(
        [packed[:, q * face : (q + 1) * face] for q in range(packed.shape[1] // face)], axis=0
    )


def stack_maps(both):
    face = both.shape[1] // 2
    turned = pltpu.roll(both, face, 1)
    first = lax.broadcasted_iota(jnp.int32, both.shape, 1) < face
    low = split(both)[1]
    return jnp.concatenate(
        [jnp.where(first, both, turned).astype(BF16), low, jnp.where(first, turned, both).astype(BF16)], axis=1
    )


def stack_inflow(f):
    return (f[0], f[1], f[0])


def stack_side(s):
    return (s[0], s[0], s[1])


def bit(stage):
    return ((lax.axis_index("stream") >> stage) & 1) == 1


def per_device(inverse, upwind, lateral, inlet_trace, previous, uptake_rate, affinity, flow_order):
    cols, _, count, nodes, _ = inverse.shape
    face = upwind.shape[3]
    tracers = previous.shape[-1]
    per_side = NODES_1D
    plane = per_side * per_side
    wide = count * face
    packed = face * face // tracers
    streams, lats = lax.axis_size("stream"), lax.axis_size("lat")
    stages = streams.bit_length() - 1
    assert streams == 1 << stages
    assert cols > 1
    early, late = list(range(1, cols)), [0]
    groups = [early, late]
    home = {c: (g, n) for g, group in enumerate(groups) for n, c in enumerate(group)}
    ending = pl.ds(nodes - face, face)
    dense = 2 * count * nodes * nodes * tracers

    def to_next(value):
        return lax.ppermute(value, "lat", [(i, (i + 1) % lats) for i in range(lats)])

    def swap(value, stage):
        return lax.ppermute(value, "stream", [(i, i ^ (1 << stage)) for i in range(streams)])

    shaped = previous.reshape(cols, count, per_side, plane, tracers)

    def face_outs(size):
        return [
            VMEM((size * count, nodes, 6 * face), BF16),
            VMEM((size * count, nodes, tracers), F32),
            VMEM((size * count, face, 6 * face), BF16),
        ]

    def chain_outs(size):
        return [
            VMEM((size * count, face, 2 * face), F32),
            VMEM((size, wide + face, wide), BF16),
            VMEM((size, wide + face, wide), BF16),
        ]

    def side_outs(size):
        return [VMEM((size * count, 2, face, tracers), BF16), VMEM((size * count, face, tracers), F32)]

    def offset_scratch(size):
        return [VMEM((size, wide - face, tracers), BF16)] * 2

    def source_outs(size):
        return [VMEM((size * count, nodes, tracers), BF16)] * 2

    def field_outs(size):
        return [VMEM((size * count, nodes, nodes), BF16), VMEM((size * count, 2 * face, nodes), BF16)]

    def times(inv, i, high, low, k, rows=None):
        matrix = inv[i] if rows is None else inv[i, rows]
        return dot(matrix, high[k]) + dot(matrix, low[k])

    def face_maps(inv, faces, i, rows=None):
        matrix = inv[i] if rows is None else inv[i, rows]
        return lax.dot_general(matrix, faces[i], (((1,), (1,)), ((), ())), preferred_element_type=F32)

    def side_of(tails, i, s):
        return dot_split(split(tails[i][:, face:]), s)

    def link(n, p, step, rows_high, rows_low, row):
        row_id = lax.broadcasted_iota(jnp.int32, (face, wide), 0)
        lane_id = lax.broadcasted_iota(jnp.int32, (face, wide), 1)
        unit = jnp.where(lane_id == row_id + p * face, 1.0, 0.0)
        r = split(unit if p == 0 else row + unit)
        rows_high[n, pl.ds(p * face, face)] = r[0]
        rows_low[n, pl.ds(p * face, face)] = r[1]
        row = dot_split(step, r)
        if p == count - 1:
            r = split(row)
            rows_high[n, pl.ds(wide, face)] = r[0]
            rows_low[n, pl.ds(wide, face)] = r[1]
        return row

    def offset(n, rows_high, rows_low, ends, high, low):
        for p in range(count - 1):
            e = split(ends[n * count + p])
            high[n, pl.ds(p * face, face)] = e[0]
            low[n, pl.ds(p * face, face)] = e[1]
        last = pl.ds(wide, face)
        row = (rows_high[n, last][:, face:], rows_low[n, last][:, face:])
        return ends[n * count + count - 1] + dot_split(row, (high[n], low[n]))

    def begin():
        size = len(early)
        items = size * count

        def body(
            order, rate, aff, inlet, old, inverse, upwind, lateral, previous,
            trace, o_order, o_rate, o_aff, o_inlet, inv, faces, source_high, source_low,
            tails, rows_high, rows_low, sides, ends, message, lagged, staged, sems,
        ):
            counter = iter(range(sems.shape[0]))
            copy = lambda a, b: pltpu.make_async_copy(a, b, sems.at[next(counter)])
            lead = [copy(rate, o_rate), copy(aff, o_aff), copy(order, o_order)]
            parts = []
            for i in range(items):
                c, j = early[i // count], i % count
                parts.append([
                    copy(previous.at[c, 0, j], lagged.at[i]),
                    copy(inverse.at[c, 0, j, ending], inv.at[i, ending]),
                    copy(upwind.at[c, 0, j], faces.at[i, pl.ds(0, face)]),
                    copy(lateral.at[c, 0, j], faces.at[i, pl.ds(face, face)]),
                ])
            side = copy(old.at[0, :, :, pl.ds(plane - 2 * per_side, 2 * per_side)], staged)
            rest = [copy(inlet, o_inlet)]
            body_rows = pl.ds(0, nodes - face)
            for i in range(items):
                c, j = early[i // count], i % count
                rest.append(copy(inverse.at[c, 0, j, body_rows], inv.at[i, body_rows]))
            for one in lead + sum(parts, []) + [side]:
                one.start()
            for i in range(items):
                for one in (lead if i == 0 else []) + parts[i]:
                    one.wait()
                if i == min(1, items - 1):
                    for one in rest:
                        one.start()
                lag = lagged[i].astype(F32)
                if early[i // count] == cols - 1:
                    trace[i % count] = lateral_rows(lag, per_side)
                source_high[i], source_low[i] = split(langmuir(lag, o_rate[...], o_aff[...]))
                tails[i] = face_maps(inv, faces, i, ending)
                ends[i] = times(inv, i, source_high, source_low, i, ending)
            side.wait()
            rows, outflow, own = [None] * size, [None] * size, {}
            for n in range(size):
                for p in range(count):
                    own[n, p] = ends[n * count + o_order[early[n], p]]
            for p in range(count):
                for n, c in enumerate(early):
                    j = o_order[c, p]
                    i = n * count + j
                    step = split(tails[i][:, :face])
                    rows[n] = link(n, p, step, rows_high, rows_low, rows[n])
                    if c == 1:
                        s = [staged[j, a].astype(F32)[per_side:] for a in range(per_side)]
                        s = split(jnp.concatenate(s, axis=0))
                    else:
                        s = split(lateral_rows(lagged[i - count].astype(F32), per_side))
                    sides[n * count + p, 0] = s[0]
                    sides[n * count + p, 1] = s[1]
                    end = own[n, p] + side_of(tails, i, s)
                    ends[n * count + p] = end
                    outflow[n] = end if p == 0 else end + dot_split(step, split(outflow[n]))
            for n in range(size):
                message[n, pl.ds(0, face)] = outflow[n]
                message[n, pl.ds(face, packed)] = pack_map(rows[n][:, :face], tracers)
            for one in rest:
                one.wait()

        values = run(
            body,
            "begin",
            [
                (flow_order.reshape(cols, count), HBM),
                (uptake_rate.reshape(1, tracers), HBM),
                (affinity.reshape(1, tracers), HBM),
                (inlet_trace, HBM),
                (shaped, HBM),
                (inverse, HBM),
                (upwind, HBM),
                (lateral, HBM),
                (previous, HBM),
            ],
            [
                VMEM((count, face, tracers), F32),
                SMEM((cols, count), jnp.int32),
                VMEM((1, tracers), F32),
                VMEM((1, tracers), F32),
                VMEM((cols, face, tracers), F32),
                *field_outs(size),
                *source_outs(size),
                *chain_outs(size),
                *side_outs(size),
                VMEM((size, face + packed, tracers), F32),
            ],
            [
                VMEM((items, nodes, tracers), BF16),
                VMEM((count, per_side, 2 * per_side, tracers), BF16),
                pltpu.SemaphoreType.DMA((5 + 5 * items,)),
            ],
            size * dense,
        )
        state = SimpleNamespace()
        state.inv, state.faces, state.source_high, state.source_low = values[5:9]
        state.tails, state.high, state.low, state.sides, state.ends, state.message = values[9:]
        return values[:5], state

    def finish_early(state, after):
        size = len(early)
        items = size * count

        def body(
            inv, faces, source_high, source_low, _, inverse, upwind, lateral, previous,
            maps, free, side_maps, o_inv, o_faces, o_lagged, sems,
        ):
            copies = []
            for i in range(len(late) * count):
                c, j = late[i // count], i % count
                for k, (a, b) in enumerate((
                    (previous.at[c, 0, j], o_lagged.at[i]),
                    (upwind.at[c, 0, j], o_faces.at[i, pl.ds(0, face)]),
                    (lateral.at[c, 0, j], o_faces.at[i, pl.ds(face, face)]),
                    (inverse.at[c, 0, j], o_inv.at[i]),
                )):
                    copies.append(pltpu.make_async_copy(a, b, sems.at[k, i]))
                    copies[-1].start()
            for i in range(items):
                both = face_maps(inv, faces, i)
                maps[i] = stack_maps(both)
                side_maps[i] = stack_maps(lateral_rows(both, per_side))
                free[i] = times(inv, i, source_high, source_low, i)
            for one in copies:
                one.wait()

        state.maps, state.free, state.side_maps, *fetched = run(
            body,
            "finish_early",
            [state.inv, state.faces, state.source_high, state.source_low, after]
            + [(a, HBM) for a in (inverse, upwind, lateral, previous)],
            face_outs(size) + field_outs(len(late)) + [VMEM((len(late) * count, nodes, tracers), BF16)],
            [pltpu.SemaphoreType.DMA((4, len(late) * count))],
            3 * size * dense,
        )
        return fetched

    def begin_late(fetched, after):
        size = len(late)
        items = size * count

        def body(
            order, inv, faces, lagged, rate, aff, _,
            maps, free, side_maps, tails, rows_high, rows_low, mapped, source_high, source_low,
        ):
            for i in range(items):
                tails[i] = face_maps(inv, faces, i, ending)
            rows = [None] * size
            for i in range(items + 1):
                if i < items:
                    both = face_maps(inv, faces, i)
                    maps[i] = stack_maps(both)
                    side_maps[i] = stack_maps(lateral_rows(both, per_side))
                    s = split(langmuir(lagged[i].astype(F32), rate[...], aff[...]))
                    source_high[i % 2], source_low[i % 2] = s
                    n, p = i // count, i % count
                    step = split(tails[n * count + order[late[n], p]][:, :face])
                    rows[n] = link(n, p, step, rows_high, rows_low, rows[n])
                if i > 0:
                    free[i - 1] = times(inv, i - 1, source_high, source_low, (i - 1) % 2)
            for n in range(size):
                mapped[n] = pack_map(rows[n][:, :face], tracers)

        state = SimpleNamespace(inv=fetched[0])
        values = run(
            body,
            "begin_late",
            [order, *fetched, rate, aff, after],
            face_outs(size) + chain_outs(size) + [VMEM((size, packed, tracers), F32)],
            [VMEM((2, nodes, tracers), BF16)] * 2,
            3 * size * dense,
        )
        state.maps, state.free, state.side_maps, state.tails, state.high, state.low, state.mapped = values
        return state

    def arrived_side(arrived, j):
        return split(jnp.where(lax.axis_index("lat") > 0, arrived[j], 0.0))

    def first_sides(state, arrived):
        def body(order, arrived, free, tails, rows_high, rows_low, mapped, sides, ends, message, high, low):
            for p in range(count):
                j = order[0, p]
                s = arrived_side(arrived, j)
                sides[p, 0] = s[0]
                sides[p, 1] = s[1]
                ends[p] = free[j, ending] + side_of(tails, j, s)
            message[0, pl.ds(0, face)] = offset(0, rows_high, rows_low, ends, high, low)
            message[0, pl.ds(face, packed)] = mapped[0]

        state.sides, state.ends, state.message = run(
            body,
            "first_sides",
            [order, arrived, state.free, state.tails, state.high, state.low, state.mapped],
            side_outs(1) + [VMEM((1, face + packed, tracers), F32)],
            offset_scratch(1),
            dense // 50,
        )

    def combine_first(stage, own, other):
        def body(own, other, message):
            upper = bit(stage)
            for n in range(own.shape[0]):
                up = jnp.where(upper, own[n], other[n])
                low = jnp.where(upper, other[n], own[n])
                m = split(unpack_map(up[face:], face))
                message[n, pl.ds(0, face)] = dot_split(m, split(low[:face])) + up[:face]
                mapped = dot_split(m, split(unpack_map(low[face:], face)))
                message[n, pl.ds(face, packed)] = pack_map(mapped, tracers)

        return run(body, "combine", [own, other], [VMEM(own.shape, F32)], [], dense // 100)[0]

    def combine_second(stage, own, other, old_own, old_other):
        def body(own, other, *refs):
            message = refs[-1]
            upper = bit(stage)
            for c in range(cols):
                g, n = home[c]
                mine, theirs = refs[2 * g], refs[2 * g + 1]
                m = jnp.where(upper, mine[n, pl.ds(face, packed)], theirs[n, pl.ds(face, packed)])
                up = jnp.where(upper, own[c], other[c])
                low = jnp.where(upper, other[c], own[c])
                message[c] = dot_split(split(unpack_map(m, face)), split(low)) + up

        ins = [own, other]
        for pair in zip(old_own, old_other):
            ins += pair
        return run(body, "combine", ins, [VMEM(own.shape, F32)], [], dense // 100)[0]

    def entering(start, offsets, maps):
        for stage in reversed(range(stages)):
            m = split(unpack_map(maps[stage], face))
            beyond = dot_split(m, split(start)) + offsets[stage]
            start = jnp.where(bit(stage), beyond, start)
        return start

    def enter_first(group, state):
        size = len(group)
        last = group[-1] == cols - 1

        def body(order, inlet, rows_high, rows_low, sides, ends, free, side_maps, *refs):
            got, refs = refs[:stages], refs[stages:]
            stack, (high, low) = refs[0], refs[-2:]
            for n, c in enumerate(group):
                for p in range(count - 1):
                    e = split(ends[n * count + p])
                    high[n, pl.ds((p + 1) * face, face)] = e[0]
                    low[n, pl.ds((p + 1) * face, face)] = e[1]
                maps = [r[n, pl.ds(face, packed)] for r in got]
                e = split(entering(inlet[c], [r[n, pl.ds(0, face)] for r in got], maps))
                high[n, pl.ds(0, face)] = e[0]
                low[n, pl.ds(0, face)] = e[1]
                span = pl.ds(0, wide)
                inflow = dot_split((rows_high[n, span], rows_low[n, span]), (high[n], low[n]))
                for p in range(count):
                    i = n * count + order[c, p]
                    f = split(inflow[p * face : (p + 1) * face])
                    s = (sides[n * count + p, 0], sides[n * count + p, 1])
                    for q, part in enumerate(stack_inflow(f) + stack_side(s)):
                        stack[i, pl.ds(q * face, face)] = part
            if last:
                for j in range(count):
                    i = (size - 1) * count + j
                    refs[1][j] = lateral_rows(free.at[i], per_side) + dot(side_maps[i], stack[i])

        outs = [VMEM((size * count, 6 * face, tracers), BF16)]
        if last:
            outs.append(VMEM((count, face, tracers), F32))
        ins = [order, inlet, state.high, state.low, state.sides, state.ends, state.free, state.side_maps]
        scratch = [VMEM((size, wide, tracers), BF16)] * 2
        values = run(body, "enter", ins + state.received, outs, scratch, dense // 50)
        state.stack = values[0]
        return values[1] if last else None

    def second_early(state, after):
        size = len(early)
        items = size * count

        def body(inv, maps, free, stack, rate, aff, _, fresh, traces, own, source_high, source_low):
            for i in range(items + 1):
                if i < items:
                    swept = free[i] + dot(maps[i], stack[i])
                    traces[i] = lateral_rows(swept, per_side)
                    source_high[i % 2], source_low[i % 2] = split(langmuir(swept, rate[...], aff[...]))
                if i > 0:
                    value = times(inv, i - 1, source_high, source_low, (i - 1) % 2)
                    fresh[i - 1] = value
                    own[i - 1] = value[nodes - face :]

        state.fresh, state.traces, state.own = run(
            body,
            "second_early",
            [state.inv, state.maps, state.free, state.stack, rate, aff, after],
            [VMEM((items, nodes, tracers), F32)] + [VMEM((items, face, tracers), F32)] * 2,
            [VMEM((2, nodes, tracers), BF16)] * 2,
            3 * size * dense,
        )

    def second_late(state):
        items = len(late) * count

        def body(inv, maps, free, stack, rate, aff, source_high, source_low, traces, own):
            for i in range(items + 1):
                if i < items:
                    swept = free[i] + dot(maps[i], stack[i])
                    traces[i] = lateral_rows(swept, per_side)
                    source_high[i], source_low[i] = split(langmuir(swept, rate[...], aff[...]))
                if i > 0:
                    own[i - 1] = times(inv, i - 1, source_high, source_low, i - 1, ending)

        state.source_high, state.source_low, state.traces, state.own = run(
            body,
            "second_late",
            [state.inv, state.maps, state.free, state.stack, rate, aff],
            source_outs(len(late)) + [VMEM((items, face, tracers), F32)] * 2,
            [],
            2 * len(late) * dense,
        )

    def second_sides(arrived):
        def body(order, arrived, *refs):
            got = [refs[5 * g : 5 * g + 5] for g in range(len(groups))]
            message, *refs = refs[5 * len(groups) :]
            for g, group in enumerate(groups):
                own, _, tails, rows_high, rows_low = got[g]
                stack, ends = refs[2 * g : 2 * g + 2]
                high, low = refs[2 * (len(groups) + g) : 2 * (len(groups) + g) + 2]
                for n, c in enumerate(group):
                    for p in range(count):
                        j = order[c, p]
                        i = n * count + j
                        if c == 0:
                            s = arrived_side(arrived, j)
                        else:
                            h, m = home[c - 1]
                            s = split(got[h][1][m * count + j])
                        stack[i, pl.ds(0, face)] = jnp.zeros((face, tracers), BF16)
                        for q, part in enumerate(stack_side(s)):
                            stack[i, pl.ds((q + 1) * face, face)] = part
                        ends[n * count + p] = own[i] + side_of(tails, i, s)
                    message[c] = offset(n, rows_high, rows_low, ends, high, low)

        ins = [order, arrived]
        outs, scratch = [VMEM((cols, face, tracers), F32)], []
        for group, state in zip(groups, states):
            ins += [state.own, state.traces, state.tails, state.high, state.low]
            outs.append(VMEM((len(group) * count, 4 * face, tracers), BF16))
            outs.append(VMEM((len(group) * count, face, tracers), F32))
            scratch += offset_scratch(len(group))
        message, *values = run(body, "second_sides", ins, outs, scratch, dense // 50)
        for g, state in enumerate(states):
            state.side_stack, state.ends = values[2 * g : 2 * g + 2]
        return message

    def settle(after):
        def body(_, inv, source_high, source_low, fresh, *refs):
            got = [refs[5 * g : 5 * g + 5] for g in range(len(groups))]
            outs = refs[5 * len(groups) :]
            for g, group in enumerate(groups):
                maps, stack, ends, rows_high, rows_low = got[g]
                base, within, high, low = outs[2 * g], outs[2 * g + 1], outs[-2], outs[-1]
                for i in range(len(group) * count):
                    own = fresh[i] if g == 0 else times(inv, i, source_high, source_low, i)
                    base[i] = own + dot(maps[i][:, 2 * face :], stack[i])
                for n in range(len(group)):
                    for p in range(count - 1):
                        e = split(ends[n * count + p])
                        high[pl.ds(p * face, face)] = e[0]
                        low[pl.ds(p * face, face)] = e[1]
                    span = pl.ds(0, wide)
                    rows = (rows_high[n, span][:, face:], rows_low[n, span][:, face:])
                    within[n] = dot_split(rows, (high[...], low[...]))

        ins = [after, states[1].inv, states[1].source_high, states[1].source_low, states[0].fresh]
        outs = []
        for group, state in zip(groups, states):
            ins += [state.maps, state.side_stack, state.ends, state.high, state.low]
            outs.append(VMEM((len(group) * count, nodes, tracers), F32))
            outs.append(VMEM((len(group), wide, tracers), F32))
        scratch = [VMEM((wide - face, tracers), BF16)] * 2
        values = run(body, "settle", ins, outs, scratch, 3 * cols * dense)
        for g, state in enumerate(states):
            state.base, state.within = values[2 * g : 2 * g + 2]

    def result(offsets):
        per = 5 + stages

        def body(order, inlet, *refs):
            offs, refs = refs[:stages], refs[stages:]
            got = [refs[per * g : per * g + per] for g in range(len(groups))]
            out, staged, sems, *stacks = refs[per * len(groups) :]
            for g, group in enumerate(groups):
                rows_high, rows_low, within, _, _, *mapped = got[g]
                for n, c in enumerate(group):
                    maps = [r[n, pl.ds(face, packed)] for r in mapped]
                    e = split(entering(inlet[c], [r[c] for r in offs], maps))
                    span = pl.ds(0, wide)
                    rows = (rows_high[n, span][:, :face], rows_low[n, span][:, :face])
                    inflow = within[n] + dot_split(rows, e)
                    for p in range(count):
                        i = n * count + order[c, p]
                        for q, part in enumerate(stack_inflow(split(inflow[p * face : (p + 1) * face]))):
                            stacks[g][i, pl.ds(q * face, face)] = part
            started = []
            for g, group in enumerate(groups):
                base, maps = got[g][3:5]
                for n, c in enumerate(group):
                    for j in range(count):
                        i, k = n * count + j, len(started)
                        staged[k] = (base[i] + dot(maps[i][:, : 3 * face], stacks[g][i])).astype(BF16)
                        copy = pltpu.make_async_copy(staged.at[k], out.at[c, 0, j], sems.at[k])
                        copy.start()
                        started.append(copy)
            for copy in started:
                copy.wait()

        ins = [order, inlet, *offsets]
        scratch = [VMEM((cols * count, nodes, tracers), BF16), pltpu.SemaphoreType.DMA((cols * count,))]
        for group, state in zip(groups, states):
            ins += [state.high, state.low, state.within, state.base, state.maps, *state.received]
            scratch.append(VMEM((len(group) * count, 3 * face, tracers), BF16))
        return run(body, "result", ins, [HBM(previous.shape, BF16)], scratch, cols * dense)[0]

    def exchange_first(state):
        state.sent, state.received = [state.message], []
        for stage in range(stages):
            if stage:
                state.sent.append(combine_first(stage - 1, state.sent[-1], state.received[-1]))
            state.received.append(swap(state.sent[-1], stage))

    (trace, order, rate, aff, inlet), one = begin()
    order = (order, SMEM)
    exchange_first(one)
    arrived = to_next(trace)
    fetched = finish_early(one, one.sent[-1])
    trace = enter_first(early, one)
    arrived_next = to_next(trace)
    two = begin_late(fetched, trace)
    states = [one, two]
    first_sides(two, arrived)
    exchange_first(two)
    second_early(one, two.sent[-1])
    enter_first(late, two)
    second_late(two)
    message, offsets = second_sides(arrived_next), []
    for stage in range(stages):
        offsets.append(swap(message, stage))
        if stage + 1 < stages:
            message = combine_second(
                stage, message, offsets[-1], [s.sent[stage] for s in states], [s.received[stage] for s in states]
            )
    settle(message)
    return result(offsets)


def solution(mesh):
    placed = (
        P("lat", "stream", None, None, None),
        P("lat", "stream", None, None, None),
        P("lat", "stream", None, None, None),
        P("lat", None, None),
        P("lat", "stream", None, None, None),
        P(),
        P(),
        P("lat", "stream", None),
    )
    return jax.shard_map(
        per_device,
        mesh=mesh,
        in_specs=placed,
        out_specs=P("lat", "stream", None, None, None),
        check_vma=False,
    )
```

time: 39.9 us -> 39.4 us (0.987)
  waiting for transfers between devices: 11 us -> 8.8 us
  Pallas kernels: 20 us -> 21.6 us
    ppermute x6, waiting for transfers between devices: 8.71 us -> 4.8 us  [swap(): lax.ppermute(value, 'stream', [(i, i ^ 1 << stage) for i in range(streams)])]
    ppermute x2, waiting for transfers between devices: 2.26 us -> 3.99 us  [to_next(): lax.ppermute(value, 'lat', [(i, (i + 1) % lats) for i in range(lats)])]
    pallas_call x13 -> x14, Pallas kernels: 20 us -> 21.6 us  [run(): pl.pallas_call(body, name=name, in_specs=[pl.BlockSpec(memory_space=space...]
    ppermute x6, starting transfers between devices: 3.79 us -> 5.3 us  [swap(): lax.ppermute(value, 'stream', [(i, i ^ 1 << stage) for i in range(streams)])]
    ppermute x2, starting transfers between devices: 4.77 us -> 3.33 us  [to_next(): lax.ppermute(value, 'lat', [(i, (i + 1) % lats) for i in range(lats)])]
  transfers between devices with their start and end apart: 8 -> 8, of which waited for: 5 -> 6; matrix products, arithmetic and copies ran while one was open for 0% -> 0% of each run, Pallas kernels for 37% -> 36%
where the time goes in v4:
time: 39.4 us; the launch traced here: 39.3 us
  Pallas kernels  21.6 us (55%)
  waiting for transfers between devices  8.8 us (22%)
  starting transfers between devices  8.63 us (22%)
    pallas_call x14, Pallas kernels, run(): pl.pallas_call(body, name=name, in_specs=[pl.BlockSpec(memory_space=space...  21.6 us
    ppermute x6, starting transfers between devices, swap(): lax.ppermute(value, 'stream', [(i, i ^ 1 << stage) for i in range(streams)])  5.3 us
    ppermute x6, waiting for transfers between devices, swap(): lax.ppermute(value, 'stream', [(i, i ^ 1 << stage) for i in range(streams)])  4.8 us
    ppermute x2, waiting for transfers between devices, to_next(): lax.ppermute(value, 'lat', [(i, (i + 1) % lats) for i in range(lats)])  3.99 us
    ppermute x2, starting transfers between devices, to_next(): lax.ppermute(value, 'lat', [(i, (i + 1) % lats) for i in range(lats)])  3.33 us
  transfers between devices with their start and end apart: 8, of which 6 were waited for; matrix products, arithmetic and copies ran while one was open for 0% of the time, Pallas kernels for 36%

profile of v4, /device:TPU:0, one launch (start us, length us, event | category | flops | bytes accessed | tf_op | source)
XLA Modules:
  0.0 39.3 jit_solution(8593457622428882412)
XLA Ops:
  0.0 3.7 %begin.1 = (f32[4,64,256]{2,1,0:T(8,128)S(1)}, s32[2,4]{1,0:T(2,128)S(4)}, f32[1,256]{1,0:T(1,128)S(1)}, f32[1,256]{1,0:T(1,128)S(1)}, f32[2,64,256]{2,1,0:T(8,1...) custom-call(s32[2,4]{1,0:T(2,128)} %bitcast.5, ...), custom_call_target="tpu_custom_call" | custom-call | flops 536870912 | bytes 1048576 | tf_op jit(solution)/shard_map/begin/pallas_call | solution.py:21
  3.7 0.5 %collective-permute-start = (f32[1,80,256]{2,1,0:T(8,128)S(1)}, f32[1,80,256]{2,1,0:T(8,128)S(1)}, u32[]{:S(2)}, u32[]{:S(2)}) collective-permute-start(f32[1,80,256]{2,1,0:T(8,128)S(1)} %get-tuple-element.64.own.refs_0_), channel_id=1, source_target_pairs={{0,8},{8,0},{16,24},{24,16},{1,9},{9,1},{17,25},{25,17},{2,10},{10... | collective-permute-start | bytes 245768 | tf_op jit(solution)/shard_map/ppermute | solution.py:113
  4.2 2.6 %collective-permute-start.3 = (f32[4,64,256]{2,1,0:T(8,128)S(1)}, f32[4,64,256]{2,1,0:T(8,128)S(1)}, u32[]{:S(2)}, u32[]{:S(2)}) collective-permute-start(f32[4,64,256]{2,1,0:T(8,128)S(1)} %get-tuple-element.72), channel_id=1, source_target_pairs={{0,1},{1,2},{2,3},{3,4},{4,5},{5,6},{6,7},{7,0},{8,9},{9,10},{10,1... | collective-permute-start | bytes 786440 | tf_op jit(solution)/shard_map/ppermute | solution.py:110
  6.8 0.0 collective-permute-done.other.refs_0_.refs_1_.refs_7_
  6.8 0.3 combine.3._
  7.1 1.5 %collective-permute-start.1 = (f32[1,80,256]{2,1,0:T(8,128)S(1)}, f32[1,80,256]{2,1,0:T(8,128)S(1)}, u32[]{:S(2)}, u32[]{:S(2)}) collective-permute-start(f32[1,80,256]{2,1,0:T(8,128)S(1)} %combine.3._), channel_id=1, source_target_pairs={{0,16},{8,24},{16,0},{24,8},{1,17},{9,25},{17,1},{25,9},{2,18},{10... | collective-permute-start | bytes 245768 | tf_op jit(solution)/shard_map/ppermute | solution.py:113
  8.6 3.6 %finish_early.1 = (bf16[4,512,384]{2,1,0:T(8,128)(2,1)S(1)}, f32[4,512,256]{2,1,0:T(8,128)S(1)}, bf16[4,64,384]{2,1,0:T(8,128)(2,1)S(1)}, bf16[4,512,512]{2,1,0:...) custom-call(bf16[4,512,512]{2,1,0:T(8,128)(2,1)S(1)} %get-tuple-element.60.inv, ...), custom_call_target="tpu_custom_call" | custom-call | flops 1610612736 | bytes 1048576 | tf_op jit(solution)/shard_map/finish_early/pallas_call | solution.py:21
  12.2 0.0 collective-permute-done.1.refs_1_.refs_8_
  12.2 1.1 %enter.2 = (bf16[4,384,256]{2,1,0:T(8,128)(2,1)S(1)}, f32[4,64,256]{2,1,0:T(8,128)S(1)}) custom-call(s32[2,4]{1,0:T(2,128)S(4)} %get-tuple-element.54.order, f32[2,64,256]{2,1,0:T(8,128)S(1)} %get-tuple-element.55.inlet, bf16[1,320,256]{2,1,0:T(8,128)(2,1)S(1)} %get-tuple-element.56.rows_high.refs_3_.refs_2_, ...), custom_call_target="tpu_custom_call" | custom-call | flops 10737418 | bytes 1048576 | tf_op jit(solution)/shard_map/enter/pallas_call | solution.py:21
  13.3 2.4 %begin_late.1 = (bf16[4,512,384]{2,1,0:T(8,128)(2,1)S(1)}, f32[4,512,256]{2,1,0:T(8,128)S(1)}, bf16[4,64,384]{2,1,0:T(8,128)(2,1)S(1)}, f32[4,64,128]{2,1,0:T(8,...) custom-call(s32[2,4]{1,0:T(2,128)S(4)} %get-tuple-element.54.order, ...), custom_call_target="tpu_custom_call" | custom-call | flops 1610612736 | bytes 1048576 | tf_op jit(solution)/shard_map/begin_late/pallas_call | solution.py:21
  15.7 1.0 %collective-permute-done.3.arrived = f32[4,64,256]{2,1,0:T(8,128)S(1)} collective-permute-done((f32[4,64,256]{2,1,0:T(8,128)S(1)}, f32[4,64,256]{2,1,0:T(8,128)S(1)}, u32[]{:S(2)}, u32[]{:S(2)}) %collective-permute-start.3) | collective-permute-done | bytes 262176 | tf_op jit(solution)/shard_map/ppermute | solution.py:110
  16.7 0.5 %first_sides.1 = (bf16[4,2,64,256]{3,2,1,0:T(8,128)(2,1)S(1)}, f32[4,64,256]{2,1,0:T(8,128)S(1)}, f32[1,80,256]{2,1,0:T(8,128)S(1)}) custom-call(s32[2,4]{1,0:T(2,128)S(4)} %get-tuple-element.54.order, f32[4,64,256]{2,1,0:T(8,128)S(1)} %collective-permute-done.3.arrived, f32[4,512,256]{2,1,0:T(8,128)S(1)} %get-tuple-element.76.free, ...), custom_call_target="tpu_custom_call" | custom-call | flops 10737418 | bytes 1048576 | tf_op jit(solution)/shard_map/first_sides/pallas_call | solution.py:21
  17.2 0.1 collective-permute-start.4
  17.2 0.8 %collective-permute-start.2 = (f32[4,64,256]{2,1,0:T(8,128)S(1)}, f32[4,64,256]{2,1,0:T(8,128)S(1)}, u32[]{:S(2)}, u32[]{:S(2)}) collective-permute-start(f32[4,64,256]{2,1,0:T(8,128)S(1)} %get-tuple-element.67._), channel_id=1, source_target_pairs={{0,1},{1,2},{2,3},{3,4},{4,5},{5,6},{6,7},{7,0},{8,9},{9,10},{10,1... | collective-permute-start | bytes 786440 | tf_op jit(solution)/shard_map/ppermute | solution.py:110
  18.0 0.5 %collective-permute-done.4.other.refs_0_.refs_3_.refs_14_ = f32[1,80,256]{2,1,0:T(8,128)S(1)} collective-permute-done((f32[1,80,256]{2,1,0:T(8,128)S(1)}, f32[1,80,256]{2,1,0:T(8,128)S(1)}, u32[]{:S(2)}, u32[]{:S(2)}) %collective-permute-start.4) | collective-permute-done | bytes 81952 | tf_op jit(solution)/shard_map/ppermute | solution.py:113
  18.5 0.3 combine.4._
  18.8 1.5 %collective-permute-start.5 = (f32[1,80,256]{2,1,0:T(8,128)S(1)}, f32[1,80,256]{2,1,0:T(8,128)S(1)}, u32[]{:S(2)}, u32[]{:S(2)}) collective-permute-start(f32[1,80,256]{2,1,0:T(8,128)S(1)} %combine.4._), channel_id=1, source_target_pairs={{0,16},{8,24},{16,0},{24,8},{1,17},{9,25},{17,1},{25,9},{2,18},{10... | collective-permute-start | bytes 245768 | tf_op jit(solution)/shard_map/ppermute | solution.py:113
  20.4 2.0 %second_early.1 = (f32[4,512,256]{2,1,0:T(8,128)S(1)}, f32[4,64,256]{2,1,0:T(8,128)S(1)}, f32[4,64,256]{2,1,0:T(8,128)S(1)}) custom-call(bf16[4,512,512]{2,1,0:T(8,128)(2,1)S(1)} %get-tuple-element.60.inv, bf16[4,512,384]{2,1,0:T(8,128)(2,1)S(1)} %get-tuple-element.68.maps.refs_0_.refs_6_, f32[4,512,256]{2,1,0:T(8,128)S(1)} %get-tuple-element.65.free, ...), custom_call_target="tpu_custom_call" | custom-call | flops 1610612736 | bytes 1048576 | tf_op jit(solution)/shard_map/second_early/pallas_call | solution.py:21
  22.3 1.0 %collective-permute-done.5.refs_1_.refs_15_ = f32[1,80,256]{2,1,0:T(8,128)S(1)} collective-permute-done((f32[1,80,256]{2,1,0:T(8,128)S(1)}, f32[1,80,256]{2,1,0:T(8,128)S(1)}, u32[]{:S(2)}, u32[]{:S(2)}) %collective-permute-start.5) | collective-permute-done | bytes 81952 | tf_op jit(solution)/shard_map/ppermute | solution.py:113
  23.3 0.7 %enter.3.stack = bf16[4,384,256]{2,1,0:T(8,128)(2,1)S(1)} custom-call(s32[2,4]{1,0:T(2,128)S(4)} %get-tuple-element.54.order, f32[2,64,256]{2,1,0:T(8,128)S(1)} %get-tuple-element.55.inlet, bf16[1,320,256]{2,1,0:T(8,128)(2,1)S(1)} %get-tuple-element.78.rows_high.refs_8_.refs_9_, bf16[1,320,256]{2,1,0:T(8,128)(2,1)S(1)} %get-tuple-element.79.rows_low.refs_9_.refs_10_, ...), custom_call_target="tpu_custom_call" | custom-call | flops 10737418 | bytes 1048576 | tf_op jit(solution)/shard_map/enter/pallas_call | solution.py:21
  24.0 1.7 %second_late.1 = (bf16[4,512,256]{2,1,0:T(8,128)(2,1)S(1)}, bf16[4,512,256]{2,1,0:T(8,128)(2,1)S(1)}, f32[4,64,256]{2,1,0:T(8,128)S(1)}, f32[4,64,256]{2,1,0:T(8,128)S(1)}) custom-call(bf16[4,512,512]{2,1,0:T(8,128)(2,1)S(1)} %get-tuple-element.73.inv, bf16[4,512,384]{2,1,0:T(8,128)(2,1)S(1)} %get-tuple-element.85.maps.refs_5_.refs_13_, ...), custom_call_target="tpu_custom_call" | custom-call | flops 1073741824 | bytes 1048576 | tf_op jit(solution)/shard_map/second_late/pallas_call | solution.py:21
  25.7 3.0 %collective-permute-done.2.arrived = f32[4,64,256]{2,1,0:T(8,128)S(1)} collective-permute-done((f32[4,64,256]{2,1,0:T(8,128)S(1)}, f32[4,64,256]{2,1,0:T(8,128)S(1)}, u32[]{:S(2)}, u32[]{:S(2)}) %collective-permute-start.2) | collective-permute-done | bytes 262176 | tf_op jit(solution)/shard_map/ppermute | solution.py:110
  28.7 0.8 %second_sides.1 = (f32[2,64,256]{2,1,0:T(8,128)S(1)}, bf16[4,256,256]{2,1,0:T(8,128)(2,1)S(1)}, f32[4,64,256]{2,1,0:T(8,128)S(1)}, bf16[4,256,256]{2,1,0:T(8,128)(2,1)S(1)}, f32[4,64,256]{2,1,0:T(8,128)S(1)}) custom-call(s32[2,4]{1,0:T(2,128)S(4)} %get-tuple-element.54.order, f32[4,64,256]{2,1,0:T(8,128)S(1)} %collective-permute-done.2.arrived, ...), custom_call_target="tpu_custom_call" | custom-call | flops 10737418 | bytes 1048576 | tf_op jit(solution)/shard_map/second_sides/pallas_call | solution.py:21
  29.4 0.1 collective-permute-start.6
  29.5 1.3 %collective-permute-done.6.other.refs_0_ = f32[2,64,256]{2,1,0:T(8,128)S(1)} collective-permute-done((f32[2,64,256]{2,1,0:T(8,128)S(1)}, f32[2,64,256]{2,1,0:T(8,128)S(1)}, u32[]{:S(2)}, u32[]{:S(2)}) %collective-permute-start.6) | collective-permute-done | bytes 131104 | tf_op jit(solution)/shard_map/ppermute | solution.py:113
  30.8 0.3 combine.5._
  31.1 1.6 %collective-permute-start.7 = (f32[2,64,256]{2,1,0:T(8,128)S(1)}, f32[2,64,256]{2,1,0:T(8,128)S(1)}, u32[]{:S(2)}, u32[]{:S(2)}) collective-permute-start(f32[2,64,256]{2,1,0:T(8,128)S(1)} %combine.5._), channel_id=1, source_target_pairs={{0,16},{8,24},{16,0},{24,8},{1,17},{9,25},{17,1},{25,9},{2,18},{10... | collective-permute-start | bytes 393224 | tf_op jit(solution)/shard_map/ppermute | solution.py:113
  32.7 2.0 %settle.1 = (f32[4,512,256]{2,1,0:T(8,128)S(1)}, f32[1,256,256]{2,1,0:T(8,128)S(1)}, f32[4,512,256]{2,1,0:T(8,128)S(1)}, f32[1,256,256]{2,1,0:T(8,128)S(1)}) custom-call(f32[2,64,256]{2,1,0:T(8,128)S(1)} %combine.5._, bf16[4,512,512]{2,1,0:T(8,128)(2,1)S(1)} %get-tuple-element.73.inv, bf16[4,512,256]{2,1,0:T(8,128)(2,1)S(1)} %get-tuple-element.92.source_high, ...), custom_call_target="tpu_custom_call" | custom-call | flops 3221225472 | bytes 1048576 | tf_op jit(solution)/shard_map/settle/pallas_call | solution.py:21
  34.7 2.0 %collective-permute-done.7.refs_1_ = f32[2,64,256]{2,1,0:T(8,128)S(1)} collective-permute-done((f32[2,64,256]{2,1,0:T(8,128)S(1)}, f32[2,64,256]{2,1,0:T(8,128)S(1)}, u32[]{:S(2)}, u32[]{:S(2)}) %collective-permute-start.7) | collective-permute-done | bytes 131104 | tf_op jit(solution)/shard_map/ppermute | solution.py:113
  36.7 2.4 %result.1 = bf16[2,1,4,512,256]{4,3,2,1,0:T(8,128)(2,1)} custom-call(s32[2,4]{1,0:T(2,128)S(4)} %get-tuple-element.54.order, f32[2,64,256]{2,1,0:T(8,128)S(1)} %get-tuple-element.55.inlet, f32[2,64,256]{2,1,0:T(8,128)S(1)} %collective-permute-done.6.other.refs_0_, f32[2,64,256]{2,1,0:T(8,128)S(1)} %collective-permute-done.7.refs_1_, ...), custom_call_target="tpu_custom_call" | custom-call | flops 1073741824 | bytes 1048576 | tf_op jit(solution)/shard_map/result/pallas_call | solution.py:21
Async XLA Ops:
  3.7 3.1 %collective-permute-start = (f32[1,80,256]{2,1,0:T(8,128)S(1)}, f32[1,80,256]{2,1,0:T(8,128)S(1)}, u32[]{:S(2)}, u32[]{:S(2)}) collective-permute-start(f32[1,80,256]{2,1,0:T(8,128)S(1)} %get-tuple-element.64.own.refs_0_), channel_id=1, source_target_pairs={{0,8},{8,0},{16,24},{24,16},{1,9},{9,1},{17,25},{25,17},{2,10},{10... | collective-permute-start | bytes 245768 | tf_op jit(solution)/shard_map/ppermute | solution.py:113
  4.2 12.5 %collective-permute-start.3 = (f32[4,64,256]{2,1,0:T(8,128)S(1)}, f32[4,64,256]{2,1,0:T(8,128)S(1)}, u32[]{:S(2)}, u32[]{:S(2)}) collective-permute-start(f32[4,64,256]{2,1,0:T(8,128)S(1)} %get-tuple-element.72), channel_id=1, source_target_pairs={{0,1},{1,2},{2,3},{3,4},{4,5},{5,6},{6,7},{7,0},{8,9},{9,10},{10,1... | collective-permute-start | bytes 786440 | tf_op jit(solution)/shard_map/ppermute | solution.py:110
  7.1 5.1 %collective-permute-start.1 = (f32[1,80,256]{2,1,0:T(8,128)S(1)}, f32[1,80,256]{2,1,0:T(8,128)S(1)}, u32[]{:S(2)}, u32[]{:S(2)}) collective-permute-start(f32[1,80,256]{2,1,0:T(8,128)S(1)} %combine.3._), channel_id=1, source_target_pairs={{0,16},{8,24},{16,0},{24,8},{1,17},{9,25},{17,1},{25,9},{2,18},{10... | collective-permute-start | bytes 245768 | tf_op jit(solution)/shard_map/ppermute | solution.py:113
  17.2 1.3 %collective-permute-start.4 = (f32[1,80,256]{2,1,0:T(8,128)S(1)}, f32[1,80,256]{2,1,0:T(8,128)S(1)}, u32[]{:S(2)}, u32[]{:S(2)}) collective-permute-start(f32[1,80,256]{2,1,0:T(8,128)S(1)} %get-tuple-element.81.own.refs_2_), channel_id=1, source_target_pairs={{0,8},{8,0},{16,24},{24,16},{1,9},{9,1},{17,25},{25,17},{2,10},{10... | collective-permute-start | bytes 245768 | tf_op jit(solution)/shard_map/ppermute | solution.py:113
  17.2 11.4 %collective-permute-start.2 = (f32[4,64,256]{2,1,0:T(8,128)S(1)}, f32[4,64,256]{2,1,0:T(8,128)S(1)}, u32[]{:S(2)}, u32[]{:S(2)}) collective-permute-start(f32[4,64,256]{2,1,0:T(8,128)S(1)} %get-tuple-element.67._), channel_id=1, source_target_pairs={{0,1},{1,2},{2,3},{3,4},{4,5},{5,6},{6,7},{7,0},{8,9},{9,10},{10,1... | collective-permute-start | bytes 786440 | tf_op jit(solution)/shard_map/ppermute | solution.py:110
  18.8 4.5 %collective-permute-start.5 = (f32[1,80,256]{2,1,0:T(8,128)S(1)}, f32[1,80,256]{2,1,0:T(8,128)S(1)}, u32[]{:S(2)}, u32[]{:S(2)}) collective-permute-start(f32[1,80,256]{2,1,0:T(8,128)S(1)} %combine.4._), channel_id=1, source_target_pairs={{0,16},{8,24},{16,0},{24,8},{1,17},{9,25},{17,1},{25,9},{2,18},{10... | collective-permute-start | bytes 245768 | tf_op jit(solution)/shard_map/ppermute | solution.py:113
  29.4 1.4 %collective-permute-start.6 = (f32[2,64,256]{2,1,0:T(8,128)S(1)}, f32[2,64,256]{2,1,0:T(8,128)S(1)}, u32[]{:S(2)}, u32[]{:S(2)}) collective-permute-start(f32[2,64,256]{2,1,0:T(8,128)S(1)} %get-tuple-element.91.own), channel_id=1, source_target_pairs={{0,8},{8,0},{16,24},{24,16},{1,9},{9,1},{17,25},{25,17},{2,10},{10... | collective-permute-start | bytes 393224 | tf_op jit(solution)/shard_map/ppermute | solution.py:113
  31.1 5.6 %collective-permute-start.7 = (f32[2,64,256]{2,1,0:T(8,128)S(1)}, f32[2,64,256]{2,1,0:T(8,128)S(1)}, u32[]{:S(2)}, u32[]{:S(2)}) collective-permute-start(f32[2,64,256]{2,1,0:T(8,128)S(1)} %combine.5._), channel_id=1, source_target_pairs={{0,16},{8,24},{16,0},{24,8},{1,17},{9,25},{17,1},{25,9},{2,18},{10... | collective-permute-start | bytes 393224 | tf_op jit(solution)/shard_map/ppermute | solution.py:113

commit v5 on v4

--- a/solution.py
+++ b/solution.py
@@ -475,7 +475,7 @@
             [state.inv, state.maps, state.free, state.stack, rate, aff, after],
             [VMEM((items, nodes, tracers), F32)] + [VMEM((items, face, tracers), F32)] * 2,
             [VMEM((2, nodes, tracers), BF16)] * 2,
-            3 * size * dense,
+            0,
         )
 
     def second_late(state):
@@ -496,7 +496,7 @@
             [state.inv, state.maps, state.free, state.stack, rate, aff],
             source_outs(len(late)) + [VMEM((items, face, tracers), F32)] * 2,
             [],
-            2 * len(late) * dense,
+            0,
         )
 
     def second_sides(arrived):

time: 39.4 us -> 37.3 us (0.947)
  waiting for transfers between devices: 8.8 us -> 6.78 us
    ppermute x2, waiting for transfers between devices: 3.99 us -> 0.01 us  [to_next(): lax.ppermute(value, 'lat', [(i, (i + 1) % lats) for i in range(lats)])]
    ppermute x6, waiting for transfers between devices: 4.8 us -> 6.78 us  [swap(): lax.ppermute(value, 'stream', [(i, i ^ 1 << stage) for i in range(streams)])]
    ppermute x6, starting transfers between devices: 5.3 us -> 4.1 us  [swap(): lax.ppermute(value, 'stream', [(i, i ^ 1 << stage) for i in range(streams)])]
    ppermute x2, starting transfers between devices: 3.33 us -> 4.34 us  [to_next(): lax.ppermute(value, 'lat', [(i, (i + 1) % lats) for i in range(lats)])]
  transfers between devices with their start and end apart: 8 -> 8, of which waited for: 6 -> 4; matrix products, arithmetic and copies ran while one was open for 0% -> 0% of each run, Pallas kernels for 36% -> 39%
where the time goes in v5:
time: 37.3 us; the launch traced here: 37.1 us
  Pallas kernels  21.6 us (58%)
  starting transfers between devices  8.44 us (23%)
  waiting for transfers between devices  6.78 us (18%)
    pallas_call x14, Pallas kernels, run(): pl.pallas_call(body, name=name, in_specs=[pl.BlockSpec(memory_space=space...  21.6 us
    ppermute x6, waiting for transfers between devices, swap(): lax.ppermute(value, 'stream', [(i, i ^ 1 << stage) for i in range(streams)])  6.78 us
    ppermute x2, starting transfers between devices, to_next(): lax.ppermute(value, 'lat', [(i, (i + 1) % lats) for i in range(lats)])  4.34 us
    ppermute x6, starting transfers between devices, swap(): lax.ppermute(value, 'stream', [(i, i ^ 1 << stage) for i in range(streams)])  4.1 us
  transfers between devices with their start and end apart: 8, of which 4 were waited for; matrix products, arithmetic and copies ran while one was open for 0% of the time, Pallas kernels for 39%

profile of v5, /device:TPU:0, one launch (start us, length us, event | category | flops | bytes accessed | tf_op | source)
XLA Modules:
  0.0 37.1 jit_solution(7695758506583910954)
XLA Ops:
  0.0 3.7 %begin.1 = (f32[4,64,256]{2,1,0:T(8,128)S(1)}, s32[2,4]{1,0:T(2,128)S(4)}, f32[1,256]{1,0:T(1,128)S(1)}, f32[1,256]{1,0:T(1,128)S(1)}, f32[2,64,256]{2,1,0:T(8,1...) custom-call(s32[2,4]{1,0:T(2,128)} %bitcast.5, ...), custom_call_target="tpu_custom_call" | custom-call | flops 536870912 | bytes 1048576 | tf_op jit(solution)/shard_map/begin/pallas_call | solution.py:21
  3.7 0.5 %collective-permute-start = (f32[1,80,256]{2,1,0:T(8,128)S(1)}, f32[1,80,256]{2,1,0:T(8,128)S(1)}, u32[]{:S(2)}, u32[]{:S(2)}) collective-permute-start(f32[1,80,256]{2,1,0:T(8,128)S(1)} %get-tuple-element.64.own.refs_0_), channel_id=1, source_target_pairs={{0,8},{8,0},{16,24},{24,16},{1,9},{9,1},{17,25},{25,17},{2,10},{10... | collective-permute-start | bytes 245768 | tf_op jit(solution)/shard_map/ppermute | solution.py:113
  4.2 2.6 %collective-permute-start.3 = (f32[4,64,256]{2,1,0:T(8,128)S(1)}, f32[4,64,256]{2,1,0:T(8,128)S(1)}, u32[]{:S(2)}, u32[]{:S(2)}) collective-permute-start(f32[4,64,256]{2,1,0:T(8,128)S(1)} %get-tuple-element.72), channel_id=1, source_target_pairs={{0,1},{1,2},{2,3},{3,4},{4,5},{5,6},{6,7},{7,0},{8,9},{9,10},{10,1... | collective-permute-start | bytes 786440 | tf_op jit(solution)/shard_map/ppermute | solution.py:110
  6.8 0.0 collective-permute-done.other.refs_0_.refs_1_.refs_7_
  6.8 0.3 combine.3._
  7.1 1.5 %collective-permute-start.1 = (f32[1,80,256]{2,1,0:T(8,128)S(1)}, f32[1,80,256]{2,1,0:T(8,128)S(1)}, u32[]{:S(2)}, u32[]{:S(2)}) collective-permute-start(f32[1,80,256]{2,1,0:T(8,128)S(1)} %combine.3._), channel_id=1, source_target_pairs={{0,16},{8,24},{16,0},{24,8},{1,17},{9,25},{17,1},{25,9},{2,18},{10... | collective-permute-start | bytes 245768 | tf_op jit(solution)/shard_map/ppermute | solution.py:113
  8.6 3.6 %finish_early.1 = (bf16[4,512,384]{2,1,0:T(8,128)(2,1)S(1)}, f32[4,512,256]{2,1,0:T(8,128)S(1)}, bf16[4,64,384]{2,1,0:T(8,128)(2,1)S(1)}, bf16[4,512,512]{2,1,0:...) custom-call(bf16[4,512,512]{2,1,0:T(8,128)(2,1)S(1)} %get-tuple-element.60.inv, ...), custom_call_target="tpu_custom_call" | custom-call | flops 1610612736 | bytes 1048576 | tf_op jit(solution)/shard_map/finish_early/pallas_call | solution.py:21
  12.2 0.0 collective-permute-done.1.refs_1_.refs_8_
  12.2 1.1 %enter.2 = (bf16[4,384,256]{2,1,0:T(8,128)(2,1)S(1)}, f32[4,64,256]{2,1,0:T(8,128)S(1)}) custom-call(s32[2,4]{1,0:T(2,128)S(4)} %get-tuple-element.54.order, f32[2,64,256]{2,1,0:T(8,128)S(1)} %get-tuple-element.55.inlet, bf16[1,320,256]{2,1,0:T(8,128)(2,1)S(1)} %get-tuple-element.56.rows_high.refs_3_.refs_2_, ...), custom_call_target="tpu_custom_call" | custom-call | flops 10737418 | bytes 1048576 | tf_op jit(solution)/shard_map/enter/pallas_call | solution.py:21
  13.3 1.8 %collective-permute-start.2 = (f32[4,64,256]{2,1,0:T(8,128)S(1)}, f32[4,64,256]{2,1,0:T(8,128)S(1)}, u32[]{:S(2)}, u32[]{:S(2)}) collective-permute-start(f32[4,64,256]{2,1,0:T(8,128)S(1)} %get-tuple-element.67._), channel_id=1, source_target_pairs={{0,1},{1,2},{2,3},{3,4},{4,5},{5,6},{6,7},{7,0},{8,9},{9,10},{10,1... | collective-permute-start | bytes 786440 | tf_op jit(solution)/shard_map/ppermute | solution.py:110
  15.1 2.4 %begin_late.1 = (bf16[4,512,384]{2,1,0:T(8,128)(2,1)S(1)}, f32[4,512,256]{2,1,0:T(8,128)S(1)}, bf16[4,64,384]{2,1,0:T(8,128)(2,1)S(1)}, f32[4,64,128]{2,1,0:T(8,...) custom-call(s32[2,4]{1,0:T(2,128)S(4)} %get-tuple-element.54.order, ...), custom_call_target="tpu_custom_call" | custom-call | flops 1610612736 | bytes 1048576 | tf_op jit(solution)/shard_map/begin_late/pallas_call | solution.py:21
  17.5 0.0 collective-permute-done.3.arrived
  17.5 0.5 %first_sides.1 = (bf16[4,2,64,256]{3,2,1,0:T(8,128)(2,1)S(1)}, f32[4,64,256]{2,1,0:T(8,128)S(1)}, f32[1,80,256]{2,1,0:T(8,128)S(1)}) custom-call(s32[2,4]{1,0:T(2,128)S(4)} %get-tuple-element.54.order, f32[4,64,256]{2,1,0:T(8,128)S(1)} %collective-permute-done.3.arrived, f32[4,512,256]{2,1,0:T(8,128)S(1)} %get-tuple-element.76.free, ...), custom_call_target="tpu_custom_call" | custom-call | flops 10737418 | bytes 1048576 | tf_op jit(solution)/shard_map/first_sides/pallas_call | solution.py:21
  17.9 0.1 collective-permute-start.4
  18.0 1.3 %collective-permute-done.4.other.refs_0_.refs_3_.refs_14_ = f32[1,80,256]{2,1,0:T(8,128)S(1)} collective-permute-done((f32[1,80,256]{2,1,0:T(8,128)S(1)}, f32[1,80,256]{2,1,0:T(8,128)S(1)}, u32[]{:S(2)}, u32[]{:S(2)}) %collective-permute-start.4) | collective-permute-done | bytes 81952 | tf_op jit(solution)/shard_map/ppermute | solution.py:113
  19.3 0.3 combine.4._
  19.6 0.9 %collective-permute-start.5 = (f32[1,80,256]{2,1,0:T(8,128)S(1)}, f32[1,80,256]{2,1,0:T(8,128)S(1)}, u32[]{:S(2)}, u32[]{:S(2)}) collective-permute-start(f32[1,80,256]{2,1,0:T(8,128)S(1)} %combine.4._), channel_id=1, source_target_pairs={{0,16},{8,24},{16,0},{24,8},{1,17},{9,25},{17,1},{25,9},{2,18},{10... | collective-permute-start | bytes 245768 | tf_op jit(solution)/shard_map/ppermute | solution.py:113
  20.5 2.0 %second_early.1 = (f32[4,512,256]{2,1,0:T(8,128)S(1)}, f32[4,64,256]{2,1,0:T(8,128)S(1)}, f32[4,64,256]{2,1,0:T(8,128)S(1)}) custom-call(bf16[4,512,512]{2,1,0:T(8,128)(2,1)S(1)} %get-tuple-element.60.inv, bf16[4,512,384]{2,1,0:T(8,128)(2,1)S(1)} %get-tuple-element.68.maps.refs_0_.refs_6_, f32[4,512,256]{2,1,0:T(8,128)S(1)} %get-tuple-element.65.free, ...), custom_call_target="tpu_custom_call" | custom-call | bytes 1048576 | tf_op jit(solution)/shard_map/second_early/pallas_call | solution.py:21
  22.5 1.6 %collective-permute-done.5.refs_1_.refs_15_ = f32[1,80,256]{2,1,0:T(8,128)S(1)} collective-permute-done((f32[1,80,256]{2,1,0:T(8,128)S(1)}, f32[1,80,256]{2,1,0:T(8,128)S(1)}, u32[]{:S(2)}, u32[]{:S(2)}) %collective-permute-start.5) | collective-permute-done | bytes 81952 | tf_op jit(solution)/shard_map/ppermute | solution.py:113
  24.1 0.7 %enter.3.stack = bf16[4,384,256]{2,1,0:T(8,128)(2,1)S(1)} custom-call(s32[2,4]{1,0:T(2,128)S(4)} %get-tuple-element.54.order, f32[2,64,256]{2,1,0:T(8,128)S(1)} %get-tuple-element.55.inlet, bf16[1,320,256]{2,1,0:T(8,128)(2,1)S(1)} %get-tuple-element.78.rows_high.refs_8_.refs_9_, bf16[1,320,256]{2,1,0:T(8,128)(2,1)S(1)} %get-tuple-element.79.rows_low.refs_9_.refs_10_, ...), custom_call_target="tpu_custom_call" | custom-call | flops 10737418 | bytes 1048576 | tf_op jit(solution)/shard_map/enter/pallas_call | solution.py:21
  24.8 1.7 %second_late.1 = (bf16[4,512,256]{2,1,0:T(8,128)(2,1)S(1)}, bf16[4,512,256]{2,1,0:T(8,128)(2,1)S(1)}, f32[4,64,256]{2,1,0:T(8,128)S(1)}, f32[4,64,256]{2,1,0:T(8,128)S(1)}) custom-call(bf16[4,512,512]{2,1,0:T(8,128)(2,1)S(1)} %get-tuple-element.73.inv, bf16[4,512,384]{2,1,0:T(8,128)(2,1)S(1)} %get-tuple-element.85.maps.refs_5_.refs_13_, ...), custom_call_target="tpu_custom_call" | custom-call | bytes 1048576 | tf_op jit(solution)/shard_map/second_late/pallas_call | solution.py:21
  26.5 0.0 collective-permute-done.2.arrived
  26.5 0.8 %second_sides.1 = (f32[2,64,256]{2,1,0:T(8,128)S(1)}, bf16[4,256,256]{2,1,0:T(8,128)(2,1)S(1)}, f32[4,64,256]{2,1,0:T(8,128)S(1)}, bf16[4,256,256]{2,1,0:T(8,128)(2,1)S(1)}, f32[4,64,256]{2,1,0:T(8,128)S(1)}) custom-call(s32[2,4]{1,0:T(2,128)S(4)} %get-tuple-element.54.order, f32[4,64,256]{2,1,0:T(8,128)S(1)} %collective-permute-done.2.arrived, ...), custom_call_target="tpu_custom_call" | custom-call | flops 10737418 | bytes 1048576 | tf_op jit(solution)/shard_map/second_sides/pallas_call | solution.py:21
  27.3 0.1 collective-permute-start.6
  27.3 1.3 %collective-permute-done.6.other.refs_0_ = f32[2,64,256]{2,1,0:T(8,128)S(1)} collective-permute-done((f32[2,64,256]{2,1,0:T(8,128)S(1)}, f32[2,64,256]{2,1,0:T(8,128)S(1)}, u32[]{:S(2)}, u32[]{:S(2)}) %collective-permute-start.6) | collective-permute-done | bytes 131104 | tf_op jit(solution)/shard_map/ppermute | solution.py:113
  28.7 0.3 combine.5._
  28.9 1.0 %collective-permute-start.7 = (f32[2,64,256]{2,1,0:T(8,128)S(1)}, f32[2,64,256]{2,1,0:T(8,128)S(1)}, u32[]{:S(2)}, u32[]{:S(2)}) collective-permute-start(f32[2,64,256]{2,1,0:T(8,128)S(1)} %combine.5._), channel_id=1, source_target_pairs={{0,16},{8,24},{16,0},{24,8},{1,17},{9,25},{17,1},{25,9},{2,18},{10... | collective-permute-start | bytes 393224 | tf_op jit(solution)/shard_map/ppermute | solution.py:113
  29.9 2.0 %settle.1 = (f32[4,512,256]{2,1,0:T(8,128)S(1)}, f32[1,256,256]{2,1,0:T(8,128)S(1)}, f32[4,512,256]{2,1,0:T(8,128)S(1)}, f32[1,256,256]{2,1,0:T(8,128)S(1)}) custom-call(f32[2,64,256]{2,1,0:T(8,128)S(1)} %combine.5._, bf16[4,512,512]{2,1,0:T(8,128)(2,1)S(1)} %get-tuple-element.73.inv, bf16[4,512,256]{2,1,0:T(8,128)(2,1)S(1)} %get-tuple-element.92.source_high, ...), custom_call_target="tpu_custom_call" | custom-call | flops 3221225472 | bytes 1048576 | tf_op jit(solution)/shard_map/settle/pallas_call | solution.py:21
  32.0 2.6 %collective-permute-done.7.refs_1_ = f32[2,64,256]{2,1,0:T(8,128)S(1)} collective-permute-done((f32[2,64,256]{2,1,0:T(8,128)S(1)}, f32[2,64,256]{2,1,0:T(8,128)S(1)}, u32[]{:S(2)}, u32[]{:S(2)}) %collective-permute-start.7) | collective-permute-done | bytes 131104 | tf_op jit(solution)/shard_map/ppermute | solution.py:113
  34.5 2.4 %result.1 = bf16[2,1,4,512,256]{4,3,2,1,0:T(8,128)(2,1)} custom-call(s32[2,4]{1,0:T(2,128)S(4)} %get-tuple-element.54.order, f32[2,64,256]{2,1,0:T(8,128)S(1)} %get-tuple-element.55.inlet, f32[2,64,256]{2,1,0:T(8,128)S(1)} %collective-permute-done.6.other.refs_0_, f32[2,64,256]{2,1,0:T(8,128)S(1)} %collective-permute-done.7.refs_1_, ...), custom_call_target="tpu_custom_call" | custom-call | flops 1073741824 | bytes 1048576 | tf_op jit(solution)/shard_map/result/pallas_call | solution.py:21
Async XLA Ops:
  3.7 3.1 %collective-permute-start = (f32[1,80,256]{2,1,0:T(8,128)S(1)}, f32[1,80,256]{2,1,0:T(8,128)S(1)}, u32[]{:S(2)}, u32[]{:S(2)}) collective-permute-start(f32[1,80,256]{2,1,0:T(8,128)S(1)} %get-tuple-element.64.own.refs_0_), channel_id=1, source_target_pairs={{0,8},{8,0},{16,24},{24,16},{1,9},{9,1},{17,25},{25,17},{2,10},{10... | collective-permute-start | bytes 245768 | tf_op jit(solution)/shard_map/ppermute | solution.py:113
  4.2 13.3 %collective-permute-start.3 = (f32[4,64,256]{2,1,0:T(8,128)S(1)}, f32[4,64,256]{2,1,0:T(8,128)S(1)}, u32[]{:S(2)}, u32[]{:S(2)}) collective-permute-start(f32[4,64,256]{2,1,0:T(8,128)S(1)} %get-tuple-element.72), channel_id=1, source_target_pairs={{0,1},{1,2},{2,3},{3,4},{4,5},{5,6},{6,7},{7,0},{8,9},{9,10},{10,1... | collective-permute-start | bytes 786440 | tf_op jit(solution)/shard_map/ppermute | solution.py:110
  7.1 5.1 %collective-permute-start.1 = (f32[1,80,256]{2,1,0:T(8,128)S(1)}, f32[1,80,256]{2,1,0:T(8,128)S(1)}, u32[]{:S(2)}, u32[]{:S(2)}) collective-permute-start(f32[1,80,256]{2,1,0:T(8,128)S(1)} %combine.3._), channel_id=1, source_target_pairs={{0,16},{8,24},{16,0},{24,8},{1,17},{9,25},{17,1},{25,9},{2,18},{10... | collective-permute-start | bytes 245768 | tf_op jit(solution)/shard_map/ppermute | solution.py:113
  13.3 13.2 %collective-permute-start.2 = (f32[4,64,256]{2,1,0:T(8,128)S(1)}, f32[4,64,256]{2,1,0:T(8,128)S(1)}, u32[]{:S(2)}, u32[]{:S(2)}) collective-permute-start(f32[4,64,256]{2,1,0:T(8,128)S(1)} %get-tuple-element.67._), channel_id=1, source_target_pairs={{0,1},{1,2},{2,3},{3,4},{4,5},{5,6},{6,7},{7,0},{8,9},{9,10},{10,1... | collective-permute-start | bytes 786440 | tf_op jit(solution)/shard_map/ppermute | solution.py:110
  17.9 1.3 %collective-permute-start.4 = (f32[1,80,256]{2,1,0:T(8,128)S(1)}, f32[1,80,256]{2,1,0:T(8,128)S(1)}, u32[]{:S(2)}, u32[]{:S(2)}) collective-permute-start(f32[1,80,256]{2,1,0:T(8,128)S(1)} %get-tuple-element.81.own.refs_2_), channel_id=1, source_target_pairs={{0,8},{8,0},{16,24},{24,16},{1,9},{9,1},{17,25},{25,17},{2,10},{10... | collective-permute-start | bytes 245768 | tf_op jit(solution)/shard_map/ppermute | solution.py:113
  19.6 4.5 %collective-permute-start.5 = (f32[1,80,256]{2,1,0:T(8,128)S(1)}, f32[1,80,256]{2,1,0:T(8,128)S(1)}, u32[]{:S(2)}, u32[]{:S(2)}) collective-permute-start(f32[1,80,256]{2,1,0:T(8,128)S(1)} %combine.4._), channel_id=1, source_target_pairs={{0,16},{8,24},{16,0},{24,8},{1,17},{9,25},{17,1},{25,9},{2,18},{10... | collective-permute-start | bytes 245768 | tf_op jit(solution)/shard_map/ppermute | solution.py:113
  27.3 1.4 %collective-permute-start.6 = (f32[2,64,256]{2,1,0:T(8,128)S(1)}, f32[2,64,256]{2,1,0:T(8,128)S(1)}, u32[]{:S(2)}, u32[]{:S(2)}) collective-permute-start(f32[2,64,256]{2,1,0:T(8,128)S(1)} %get-tuple-element.91.own), channel_id=1, source_target_pairs={{0,8},{8,0},{16,24},{24,16},{1,9},{9,1},{17,25},{25,17},{2,10},{10... | collective-permute-start | bytes 393224 | tf_op jit(solution)/shard_map/ppermute | solution.py:113
  28.9 5.6 %collective-permute-start.7 = (f32[2,64,256]{2,1,0:T(8,128)S(1)}, f32[2,64,256]{2,1,0:T(8,128)S(1)}, u32[]{:S(2)}, u32[]{:S(2)}) collective-permute-start(f32[2,64,256]{2,1,0:T(8,128)S(1)} %combine.5._), channel_id=1, source_target_pairs={{0,16},{8,24},{16,0},{24,8},{1,17},{9,25},{17,1},{25,9},{2,18},{10... | collective-permute-start | bytes 393224 | tf_op jit(solution)/shard_map/ppermute | solution.py:113

commit v6 on v5

--- a/solution.py
+++ b/solution.py
@@ -82,6 +82,14 @@
 
 def stack_side(s):
     return (s[0], s[0], s[1])
+
+
+def in_pairs(items, per, step):
+    def turn(t, _):
+        step([t * per + k for k in range(per)])
+        return 0
+
+    lax.fori_loop(0, items // per, turn, 0)
 
 
 def bit(stage):
@@ -104,6 +112,7 @@
     groups = [early, late]
     home = {c: (g, n) for g, group in enumerate(groups) for n, c in enumerate(group)}
     ending = pl.ds(nodes - face, face)
+    per = 2 if count % 2 == 0 else 1
     dense = 2 * count * nodes * nodes * tracers
 
     def to_next(value):
@@ -155,15 +164,14 @@
         row_id = lax.broadcasted_iota(jnp.int32, (face, wide), 0)
         lane_id = lax.broadcasted_iota(jnp.int32, (face, wide), 1)
         unit = jnp.where(lane_id == row_id + p * face, 1.0, 0.0)
-        r = split(unit if p == 0 else row + unit)
-        rows_high[n, pl.ds(p * face, face)] = r[0]
-        rows_low[n, pl.ds(p * face, face)] = r[1]
-        row = dot_split(step, r)
-        if p == count - 1:
-            r = split(row)
-            rows_high[n, pl.ds(wide, face)] = r[0]
-            rows_low[n, pl.ds(wide, face)] = r[1]
-        return row
+        r = split(jnp.where(p == 0, 0.0, row[n]) + unit)
+        here = pl.ds(pl.multiple_of(p * face, face), face)
+        rows_high[n, here] = r[0]
+        rows_low[n, here] = r[1]
+        r = split(dot_split(step, r))
+        rows_high[n, pl.ds(wide, face)] = r[0]
+        rows_low[n, pl.ds(wide, face)] = r[1]
+        row[n] = r[0].astype(F32) + r[1].astype(F32)
 
     def offset(n, rows_high, rows_low, ends, high, low):
         for p in range(count - 1):
@@ -181,66 +189,87 @@
         def body(
             order, rate, aff, inlet, old, inverse, upwind, lateral, previous,
             trace, o_order, o_rate, o_aff, o_inlet, inv, faces, source_high, source_low,
-            tails, rows_high, rows_low, sides, ends, message, lagged, staged, sems,
+            tails, sides, ends, message, lagged, staged, own, lead_sems, sems,
         ):
-            counter = iter(range(sems.shape[0]))
-            copy = lambda a, b: pltpu.make_async_copy(a, b, sems.at[next(counter)])
-            lead = [copy(rate, o_rate), copy(aff, o_aff), copy(order, o_order)]
-            parts = []
-            for i in range(items):
-                c, j = early[i // count], i % count
-                parts.append([
-                    copy(previous.at[c, 0, j], lagged.at[i]),
-                    copy(inverse.at[c, 0, j, ending], inv.at[i, ending]),
-                    copy(upwind.at[c, 0, j], faces.at[i, pl.ds(0, face)]),
-                    copy(lateral.at[c, 0, j], faces.at[i, pl.ds(face, face)]),
-                ])
-            side = copy(old.at[0, :, :, pl.ds(plane - 2 * per_side, 2 * per_side)], staged)
-            rest = [copy(inlet, o_inlet)]
-            body_rows = pl.ds(0, nodes - face)
-            for i in range(items):
-                c, j = early[i // count], i % count
-                rest.append(copy(inverse.at[c, 0, j, body_rows], inv.at[i, body_rows]))
-            for one in lead + sum(parts, []) + [side]:
+            lead = [
+                pltpu.make_async_copy(a, b, lead_sems.at[k])
+                for k, (a, b) in enumerate(((rate, o_rate), (aff, o_aff), (order, o_order), (inlet, o_inlet)))
+            ]
+            rows = pl.ds(plane - 2 * per_side, 2 * per_side)
+            lead.append(pltpu.make_async_copy(old.at[0, :, :, rows], staged, lead_sems.at[len(lead)]))
+
+            def parts(i):
+                c, j = early[0] + i // count, i % count
+                here, there = pl.ds(j, per), pl.ds(i, per)
+                pairs = (
+                    (previous.at[c, 0, here], lagged.at[there]),
+                    (inverse.at[c, 0, here, ending], inv.at[there, ending]),
+                    (upwind.at[c, 0, here], faces.at[there, pl.ds(0, face)]),
+                    (lateral.at[c, 0, here], faces.at[there, pl.ds(face, face)]),
+                )
+                return [pltpu.make_async_copy(a, b, sems.at[k, i]) for k, (a, b) in enumerate(pairs)]
+
+            def rest(i):
+                c, j = early[0] + i // count, i % count
+                others = pl.ds(0, nodes - face)
+                return pltpu.make_async_copy(
+                    inverse.at[c, 0, pl.ds(j, per), others], inv.at[pl.ds(i, per), others], sems.at[4, i]
+                )
+
+            def old_rows(field):
+                return jnp.concatenate([field(a).astype(F32)[per_side:] for a in range(per_side)], axis=0)
+
+            def lagged_rows(i):
+                starts = [a * plane + plane - 2 * per_side for a in range(per_side)]
+                return old_rows(lambda a: lagged[i, pl.ds(starts[a], 2 * per_side)])
+
+            for one in lead[:3]:
                 one.start()
-            for i in range(items):
-                for one in (lead if i == 0 else []) + parts[i]:
+            for i in range(0, items, per):
+                for one in parts(i):
+                    one.start()
+            for one in lead[3:]:
+                one.start()
+            for one in lead[:3]:
+                one.wait()
+
+            def step(members):
+                for one in parts(members[0]):
                     one.wait()
-                if i == min(1, items - 1):
-                    for one in rest:
-                        one.start()
-                lag = lagged[i].astype(F32)
-                if early[i // count] == cols - 1:
-                    trace[i % count] = lateral_rows(lag, per_side)
-                source_high[i], source_low[i] = split(langmuir(lag, o_rate[...], o_aff[...]))
-                tails[i] = face_maps(inv, faces, i, ending)
-                ends[i] = times(inv, i, source_high, source_low, i, ending)
-            side.wait()
-            rows, outflow, own = [None] * size, [None] * size, {}
-            for n in range(size):
+                rest(members[0]).start()
+                for i in members:
+                    lag = lagged[i].astype(F32)
+                    source_high[i], source_low[i] = split(langmuir(lag, o_rate[...], o_aff[...]))
+                for i in members:
+                    tails[i] = face_maps(inv, faces, i, ending)
+                    own[i] = times(inv, i, source_high, source_low, i, ending)
+
+            in_pairs(items, per, step)
+            for one in lead[3:]:
+                one.wait()
+            for j in range(count):
+                trace[j] = lagged_rows(items - count + j)
+            for n, c in enumerate(early):
+                links = []
                 for p in range(count):
-                    own[n, p] = ends[n * count + o_order[early[n], p]]
-            for p in range(count):
-                for n, c in enumerate(early):
                     j = o_order[c, p]
                     i = n * count + j
-                    step = split(tails[i][:, :face])
-                    rows[n] = link(n, p, step, rows_high, rows_low, rows[n])
-                    if c == 1:
-                        s = [staged[j, a].astype(F32)[per_side:] for a in range(per_side)]
-                        s = split(jnp.concatenate(s, axis=0))
-                    else:
-                        s = split(lateral_rows(lagged[i - count].astype(F32), per_side))
+                    s = split(old_rows(lambda a: staged[j, a]) if c == 1 else lagged_rows(i - count))
                     sides[n * count + p, 0] = s[0]
                     sides[n * count + p, 1] = s[1]
-                    end = own[n, p] + side_of(tails, i, s)
+                    end = own[i] + side_of(tails, i, s)
                     ends[n * count + p] = end
-                    outflow[n] = end if p == 0 else end + dot_split(step, split(outflow[n]))
-            for n in range(size):
-                message[n, pl.ds(0, face)] = outflow[n]
-                message[n, pl.ds(face, packed)] = pack_map(rows[n][:, :face], tracers)
-            for one in rest:
-                one.wait()
+                    links.append((tails[i][:, :face], end))
+                while len(links) > 1:
+                    paired = []
+                    for (low, start), (up, end) in zip(links[::2], links[1::2]):
+                        u = split(up)
+                        paired.append((dot_split(u, split(low)), end + dot_split(u, split(start))))
+                    links = paired + links[2 * len(paired) :]
+                message[n, pl.ds(0, face)] = links[0][1]
+                message[n, pl.ds(face, packed)] = pack_map(links[0][0], tracers)
+            for i in range(0, items, per):
+                rest(i).wait()
 
         values = run(
             body,
@@ -264,20 +293,22 @@
                 VMEM((cols, face, tracers), F32),
                 *field_outs(size),
                 *source_outs(size),
-                *chain_outs(size),
+                VMEM((items, face, 2 * face), F32),
                 *side_outs(size),
                 VMEM((size, face + packed, tracers), F32),
             ],
             [
                 VMEM((items, nodes, tracers), BF16),
                 VMEM((count, per_side, 2 * per_side, tracers), BF16),
-                pltpu.SemaphoreType.DMA((5 + 5 * items,)),
+                VMEM((items, face, tracers), F32),
+                pltpu.SemaphoreType.DMA((5,)),
+                pltpu.SemaphoreType.DMA((5, items)),
             ],
             size * dense,
         )
         state = SimpleNamespace()
         state.inv, state.faces, state.source_high, state.source_low = values[5:9]
-        state.tails, state.high, state.low, state.sides, state.ends, state.message = values[9:]
+        state.tails, state.sides, state.ends, state.message = values[9:]
         return values[:5], state
 
     def finish_early(state, after):
@@ -285,95 +316,136 @@
         items = size * count
 
         def body(
-            inv, faces, source_high, source_low, _, inverse, upwind, lateral, previous,
-            maps, free, side_maps, o_inv, o_faces, o_lagged, sems,
+            order, inv, faces, source_high, source_low, tails, _, inverse, upwind, lateral, previous,
+            maps, free, side_maps, rows_high, rows_low, o_inv, o_faces, o_lagged, row, sems,
         ):
             copies = []
-            for i in range(len(late) * count):
-                c, j = late[i // count], i % count
+            for n, c in enumerate(late):
+                there = pl.ds(n * count, count)
                 for k, (a, b) in enumerate((
-                    (previous.at[c, 0, j], o_lagged.at[i]),
-                    (upwind.at[c, 0, j], o_faces.at[i, pl.ds(0, face)]),
-                    (lateral.at[c, 0, j], o_faces.at[i, pl.ds(face, face)]),
-                    (inverse.at[c, 0, j], o_inv.at[i]),
+                    (previous.at[c, 0], o_lagged.at[there]),
+                    (upwind.at[c, 0], o_faces.at[there, pl.ds(0, face)]),
+                    (lateral.at[c, 0], o_faces.at[there, pl.ds(face, face)]),
+                    (inverse.at[c, 0], o_inv.at[there]),
                 )):
-                    copies.append(pltpu.make_async_copy(a, b, sems.at[k, i]))
+                    copies.append(pltpu.make_async_copy(a, b, sems.at[k, n]))
                     copies[-1].start()
-            for i in range(items):
-                both = face_maps(inv, faces, i)
-                maps[i] = stack_maps(both)
-                side_maps[i] = stack_maps(lateral_rows(both, per_side))
-                free[i] = times(inv, i, source_high, source_low, i)
+
+            def step(members):
+                for i in members:
+                    both = face_maps(inv, faces, i)
+                    maps[i] = stack_maps(both)
+                    side_maps[i] = stack_maps(lateral_rows(both, per_side))
+                    free[i] = times(inv, i, source_high, source_low, i)
+                    n, p = i // count, i % count
+                    head = tails[n * count + order[early[0] + n, p]][:, :face]
+                    link(n, p, split(head), rows_high, rows_low, row)
+
+            in_pairs(items, per, step)
             for one in copies:
                 one.wait()
 
-        state.maps, state.free, state.side_maps, *fetched = run(
+        state.maps, state.free, state.side_maps, state.high, state.low, *fetched = run(
             body,
             "finish_early",
-            [state.inv, state.faces, state.source_high, state.source_low, after]
+            [order, state.inv, state.faces, state.source_high, state.source_low, state.tails, after]
             + [(a, HBM) for a in (inverse, upwind, lateral, previous)],
-            face_outs(size) + field_outs(len(late)) + [VMEM((len(late) * count, nodes, tracers), BF16)],
-            [pltpu.SemaphoreType.DMA((4, len(late) * count))],
+            face_outs(size)
+            + chain_outs(size)[1:]
+            + field_outs(len(late))
+            + [VMEM((len(late) * count, nodes, tracers), BF16)],
+            [VMEM((size, face, wide), F32), pltpu.SemaphoreType.DMA((4, len(late)))],
             3 * size * dense,
         )
         return fetched
 
-    def begin_late(fetched, after):
+    def begin_late(fetched):
         size = len(late)
         items = size * count
 
         def body(
-            order, inv, faces, lagged, rate, aff, _,
-            maps, free, side_maps, tails, rows_high, rows_low, mapped, source_high, source_low,
+            order, inv, faces, lagged, rate, aff,
+            source_high, source_low, own, tails, rows_high, rows_low, mapped, row,
         ):
             for i in range(items):
                 tails[i] = face_maps(inv, faces, i, ending)
-            rows = [None] * size
             for i in range(items + 1):
                 if i < items:
-                    both = face_maps(inv, faces, i)
-                    maps[i] = stack_maps(both)
-                    side_maps[i] = stack_maps(lateral_rows(both, per_side))
-                    s = split(langmuir(lagged[i].astype(F32), rate[...], aff[...]))
-                    source_high[i % 2], source_low[i % 2] = s
+                    lag = lagged[i].astype(F32)
+                    source_high[i], source_low[i] = split(langmuir(lag, rate[...], aff[...]))
                     n, p = i // count, i % count
                     step = split(tails[n * count + order[late[n], p]][:, :face])
-                    rows[n] = link(n, p, step, rows_high, rows_low, rows[n])
+                    link(n, p, step, rows_high, rows_low, row)
                 if i > 0:
-                    free[i - 1] = times(inv, i - 1, source_high, source_low, (i - 1) % 2)
+                    own[i - 1] = times(inv, i - 1, source_high, source_low, i - 1, ending)
             for n in range(size):
-                mapped[n] = pack_map(rows[n][:, :face], tracers)
-
-        state = SimpleNamespace(inv=fetched[0])
+                mapped[n] = pack_map(row[n][:, :face], tracers)
+
+        state = SimpleNamespace(inv=fetched[0], faces=fetched[1])
         values = run(
             body,
             "begin_late",
-            [order, *fetched, rate, aff, after],
-            face_outs(size) + chain_outs(size) + [VMEM((size, packed, tracers), F32)],
-            [VMEM((2, nodes, tracers), BF16)] * 2,
-            3 * size * dense,
+            [order, *fetched, rate, aff],
+            source_outs(size)
+            + [VMEM((items, face, tracers), F32)]
+            + chain_outs(size)
+            + [VMEM((size, packed, tracers), F32)],
+            [VMEM((size, face, wide), F32)],
+            2 * size * dense,
         )
-        state.maps, state.free, state.side_maps, state.tails, state.high, state.low, state.mapped = values
+        state.source_high, state.source_low, state.own, state.tails, state.high, state.low, state.mapped = values
         return state
+
+    def late_maps(state, after):
+        items = len(late) * count
+
+        def body(inv, faces, _, maps):
+            for i in range(items):
+                maps[i] = stack_maps(face_maps(inv, faces, i))
+
+        (state.maps,) = run(
+            body,
+            "late_maps",
+            [state.inv, state.faces, after],
+            face_outs(len(late))[:1],
+            [],
+            len(late) * dense,
+        )
+
+    def late_free(state, after):
+        items = len(late) * count
+
+        def body(inv, source_high, source_low, _, free):
+            for i in range(items):
+                free[i] = times(inv, i, source_high, source_low, i)
+
+        (state.free,) = run(
+            body,
+            "late_free",
+            [state.inv, state.source_high, state.source_low, after],
+            [VMEM((items, nodes, tracers), F32)],
+            [],
+            2 * len(late) * dense,
+        )
 
     def arrived_side(arrived, j):
         return split(jnp.where(lax.axis_index("lat") > 0, arrived[j], 0.0))
 
     def first_sides(state, arrived):
-        def body(order, arrived, free, tails, rows_high, rows_low, mapped, sides, ends, message, high, low):
+        def body(order, arrived, own, tails, rows_high, rows_low, mapped, sides, ends, message, high, low):
             for p in range(count):
                 j = order[0, p]
                 s = arrived_side(arrived, j)
                 sides[p, 0] = s[0]
                 sides[p, 1] = s[1]
-                ends[p] = free[j, ending] + side_of(tails, j, s)
+                ends[p] = own[j] + side_of(tails, j, s)
             message[0, pl.ds(0, face)] = offset(0, rows_high, rows_low, ends, high, low)
             message[0, pl.ds(face, packed)] = mapped[0]
 
         state.sides, state.ends, state.message = run(
             body,
             "first_sides",
-            [order, arrived, state.free, state.tails, state.high, state.low, state.mapped],
+            [order, arrived, state.own, state.tails, state.high, state.low, state.mapped],
             side_outs(1) + [VMEM((1, face + packed, tracers), F32)],
             offset_scratch(1),
             dense // 50,
@@ -416,12 +488,14 @@
             start = jnp.where(bit(stage), beyond, start)
         return start
 
-    def enter_first(group, state):
+    def enter_first(group, state, after):
         size = len(group)
         last = group[-1] == cols - 1
 
-        def body(order, inlet, rows_high, rows_low, sides, ends, free, side_maps, *refs):
+        def body(order, inlet, rows_high, rows_low, sides, ends, *refs):
             got, refs = refs[:stages], refs[stages:]
+            if last:
+                (free, side_maps), refs = refs[:2], refs[3:]
             stack, (high, low) = refs[0], refs[-2:]
             for n, c in enumerate(group):
                 for p in range(count - 1):
@@ -448,40 +522,18 @@
         outs = [VMEM((size * count, 6 * face, tracers), BF16)]
         if last:
             outs.append(VMEM((count, face, tracers), F32))
-        ins = [order, inlet, state.high, state.low, state.sides, state.ends, state.free, state.side_maps]
+        ins = [order, inlet, state.high, state.low, state.sides, state.ends, *state.received]
+        if last:
+            ins += [state.free, state.side_maps, after]
         scratch = [VMEM((size, wide, tracers), BF16)] * 2
-        values = run(body, "enter", ins + state.received, outs, scratch, dense // 50)
+        values = run(body, "enter", ins, outs, scratch, dense // 50)
         state.stack = values[0]
         return values[1] if last else None
 
-    def second_early(state, after):
-        size = len(early)
-        items = size * count
-
-        def body(inv, maps, free, stack, rate, aff, _, fresh, traces, own, source_high, source_low):
-            for i in range(items + 1):
-                if i < items:
-                    swept = free[i] + dot(maps[i], stack[i])
-                    traces[i] = lateral_rows(swept, per_side)
-                    source_high[i % 2], source_low[i % 2] = split(langmuir(swept, rate[...], aff[...]))
-                if i > 0:
-                    value = times(inv, i - 1, source_high, source_low, (i - 1) % 2)
-                    fresh[i - 1] = value
-                    own[i - 1] = value[nodes - face :]
-
-        state.fresh, state.traces, state.own = run(
-            body,
-            "second_early",
-            [state.inv, state.maps, state.free, state.stack, rate, aff, after],
-            [VMEM((items, nodes, tracers), F32)] + [VMEM((items, face, tracers), F32)] * 2,
-            [VMEM((2, nodes, tracers), BF16)] * 2,
-            0,
-        )
-
-    def second_late(state):
-        items = len(late) * count
-
-        def body(inv, maps, free, stack, rate, aff, source_high, source_low, traces, own):
+    def second(group, state, after):
+        items = len(group) * count
+
+        def body(inv, maps, free, stack, rate, aff, _, source_high, source_low, traces, own):
             for i in range(items + 1):
                 if i < items:
                     swept = free[i] + dot(maps[i], stack[i])
@@ -492,9 +544,9 @@
 
         state.source_high, state.source_low, state.traces, state.own = run(
             body,
-            "second_late",
-            [state.inv, state.maps, state.free, state.stack, rate, aff],
-            source_outs(len(late)) + [VMEM((items, face, tracers), F32)] * 2,
+            "second",
+            [state.inv, state.maps, state.free, state.stack, rate, aff, after],
+            source_outs(len(group)) + [VMEM((items, face, tracers), F32)] * 2,
             [],
             0,
         )
@@ -535,14 +587,14 @@
         return message
 
     def settle(after):
-        def body(_, inv, source_high, source_low, fresh, *refs):
-            got = [refs[5 * g : 5 * g + 5] for g in range(len(groups))]
-            outs = refs[5 * len(groups) :]
+        def body(_, *refs):
+            got = [refs[8 * g : 8 * g + 8] for g in range(len(groups))]
+            outs = refs[8 * len(groups) :]
             for g, group in enumerate(groups):
-                maps, stack, ends, rows_high, rows_low = got[g]
+                inv, source_high, source_low, maps, stack, ends, rows_high, rows_low = got[g]
                 base, within, high, low = outs[2 * g], outs[2 * g + 1], outs[-2], outs[-1]
                 for i in range(len(group) * count):
-                    own = fresh[i] if g == 0 else times(inv, i, source_high, source_low, i)
+                    own = times(inv, i, source_high, source_low, i)
                     base[i] = own + dot(maps[i][:, 2 * face :], stack[i])
                 for n in range(len(group)):
                     for p in range(count - 1):
@@ -553,9 +605,10 @@
                     rows = (rows_high[n, span][:, face:], rows_low[n, span][:, face:])
                     within[n] = dot_split(rows, (high[...], low[...]))
 
-        ins = [after, states[1].inv, states[1].source_high, states[1].source_low, states[0].fresh]
+        ins = [after]
         outs = []
         for group, state in zip(groups, states):
+            ins += [state.inv, state.source_high, state.source_low]
             ins += [state.maps, state.side_stack, state.ends, state.high, state.low]
             outs.append(VMEM((len(group) * count, nodes, tracers), F32))
             outs.append(VMEM((len(group), wide, tracers), F32))
@@ -565,12 +618,12 @@
             state.base, state.within = values[2 * g : 2 * g + 2]
 
     def result(offsets):
-        per = 5 + stages
+        parts = 5 + stages
 
         def body(order, inlet, *refs):
             offs, refs = refs[:stages], refs[stages:]
-            got = [refs[per * g : per * g + per] for g in range(len(groups))]
-            out, staged, sems, *stacks = refs[per * len(groups) :]
+            got = [refs[parts * g : parts * g + parts] for g in range(len(groups))]
+            out, staged, sems, *stacks = refs[parts * len(groups) :]
             for g, group in enumerate(groups):
                 rows_high, rows_low, within, _, _, *mapped = got[g]
                 for n, c in enumerate(group):
@@ -615,15 +668,17 @@
     exchange_first(one)
     arrived = to_next(trace)
     fetched = finish_early(one, one.sent[-1])
-    trace = enter_first(early, one)
+    two = begin_late(fetched)
+    states = [one, two]
+    trace = enter_first(early, one, two.mapped)
     arrived_next = to_next(trace)
-    two = begin_late(fetched, trace)
-    states = [one, two]
     first_sides(two, arrived)
     exchange_first(two)
-    second_early(one, two.sent[-1])
-    enter_first(late, two)
-    second_late(two)
+    late_maps(two, two.sent[0])
+    second(early, one, two.sent[-1])
+    late_free(two, two.sent[-1])
+    enter_first(late, two, None)
+    second(late, two, two.sent[-1])
     message, offsets = second_sides(arrived_next), []
     for stage in range(stages):
         offsets.append(swap(message, stage))

time: 37.3 us -> 36.1 us (0.968)
  waiting for transfers between devices: 6.78 us -> 4.28 us
  starting transfers between devices: 8.44 us -> 9.63 us
    ppermute x6, waiting for transfers between devices: 6.78 us -> 2.85 us  [swap(): lax.ppermute(value, 'stream', [(i, i ^ 1 << stage) for i in range(streams)])]
    ppermute x2, waiting for transfers between devices: 0.01 us -> 1.43 us  [to_next(): lax.ppermute(value, 'lat', [(i, (i + 1) % lats) for i in range(lats)])]
    ppermute x6, starting transfers between devices: 4.1 us -> 5.3 us  [swap(): lax.ppermute(value, 'stream', [(i, i ^ 1 << stage) for i in range(streams)])]
    pallas_call x14 -> x16, Pallas kernels: 21.6 us -> 21.7 us  [run(): pl.pallas_call(body, name=name, in_specs=[pl.BlockSpec(memory_space=space...]
  transfers between devices with their start and end apart: 8 -> 8, of which waited for: 4 -> 5; matrix products, arithmetic and copies ran while one was open for 0% -> 0% of each run, Pallas kernels for 39% -> 42%
where the time goes in v6:
time: 36.1 us; the launch traced here: 35.9 us
  Pallas kernels  21.7 us (60%)
  starting transfers between devices  9.63 us (27%)
  waiting for transfers between devices  4.28 us (12%)
    pallas_call x16, Pallas kernels, run(): pl.pallas_call(body, name=name, in_specs=[pl.BlockSpec(memory_space=space...  21.7 us
    ppermute x6, starting transfers between devices, swap(): lax.ppermute(value, 'stream', [(i, i ^ 1 << stage) for i in range(streams)])  5.3 us
    ppermute x2, starting transfers between devices, to_next(): lax.ppermute(value, 'lat', [(i, (i + 1) % lats) for i in range(lats)])  4.33 us
    ppermute x6, waiting for transfers between devices, swap(): lax.ppermute(value, 'stream', [(i, i ^ 1 << stage) for i in range(streams)])  2.85 us
    ppermute x2, waiting for transfers between devices, to_next(): lax.ppermute(value, 'lat', [(i, (i + 1) % lats) for i in range(lats)])  1.43 us
  transfers between devices with their start and end apart: 8, of which 5 were waited for; matrix products, arithmetic and copies ran while one was open for 0% of the time, Pallas kernels for 42%

profile of v6, /device:TPU:0, one launch (start us, length us, event | category | flops | bytes accessed | tf_op | source)
XLA Modules:
  0.0 35.9 jit_solution(2251376354594442563)
XLA Ops:
  0.0 3.3 %begin.1 = (f32[4,64,256]{2,1,0:T(8,128)S(1)}, s32[2,4]{1,0:T(2,128)S(4)}, f32[1,256]{1,0:T(1,128)S(1)}, f32[1,256]{1,0:T(1,128)S(1)}, f32[2,64,256]{2,1,0:T(8,1...) custom-call(s32[2,4]{1,0:T(2,128)} %bitcast.5, ...), custom_call_target="tpu_custom_call" | custom-call | flops 536870912 | bytes 1048576 | tf_op jit(solution)/shard_map/begin/pallas_call | solution.py:21
  3.3 0.5 %collective-permute-start = (f32[1,80,256]{2,1,0:T(8,128)S(1)}, f32[1,80,256]{2,1,0:T(8,128)S(1)}, u32[]{:S(2)}, u32[]{:S(2)}) collective-permute-start(f32[1,80,256]{2,1,0:T(8,128)S(1)} %get-tuple-element.62.own.refs_0_), channel_id=1, source_target_pairs={{0,8},{8,0},{16,24},{24,16},{1,9},{9,1},{17,25},{25,17},{2,10},{10... | collective-permute-start | bytes 245768 | tf_op jit(solution)/shard_map/ppermute | solution.py:122
  3.8 2.6 %collective-permute-start.3 = (f32[4,64,256]{2,1,0:T(8,128)S(1)}, f32[4,64,256]{2,1,0:T(8,128)S(1)}, u32[]{:S(2)}, u32[]{:S(2)}) collective-permute-start(f32[4,64,256]{2,1,0:T(8,128)S(1)} %get-tuple-element.78), channel_id=1, source_target_pairs={{0,1},{1,2},{2,3},{3,4},{4,5},{5,6},{6,7},{7,0},{8,9},{9,10},{10,1... | collective-permute-start | bytes 786440 | tf_op jit(solution)/shard_map/ppermute | solution.py:119
  6.4 0.0 collective-permute-done.other.refs_0_.refs_1_.refs_7_
  6.4 0.3 combine.3._
  6.7 1.5 %collective-permute-start.1 = (f32[1,80,256]{2,1,0:T(8,128)S(1)}, f32[1,80,256]{2,1,0:T(8,128)S(1)}, u32[]{:S(2)}, u32[]{:S(2)}) collective-permute-start(f32[1,80,256]{2,1,0:T(8,128)S(1)} %combine.3._), channel_id=1, source_target_pairs={{0,16},{8,24},{16,0},{24,8},{1,17},{9,25},{17,1},{25,9},{2,18},{10... | collective-permute-start | bytes 245768 | tf_op jit(solution)/shard_map/ppermute | solution.py:122
  8.2 2.2 %finish_early.1 = (bf16[4,512,384]{2,1,0:T(8,128)(2,1)S(1)}, f32[4,512,256]{2,1,0:T(8,128)S(1)}, bf16[4,64,384]{2,1,0:T(8,128)(2,1)S(1)}, bf16[1,320,256]{2,1,0:...) custom-call(s32[2,4]{1,0:T(2,128)S(4)} %get-tuple-element.55.order, ...), custom_call_target="tpu_custom_call" | custom-call | flops 1610612736 | bytes 1048576 | tf_op jit(solution)/shard_map/finish_early/pallas_call | solution.py:21
  10.4 1.6 %begin_late.1 = (bf16[4,512,256]{2,1,0:T(8,128)(2,1)S(1)}, bf16[4,512,256]{2,1,0:T(8,128)(2,1)S(1)}, f32[4,64,256]{2,1,0:T(8,128)S(1)}, f32[4,64,128]{2,1,0:T(8,...) custom-call(s32[2,4]{1,0:T(2,128)S(4)} %get-tuple-element.55.order, ...), custom_call_target="tpu_custom_call" | custom-call | flops 1073741824 | bytes 1048576 | tf_op jit(solution)/shard_map/begin_late/pallas_call | solution.py:21
  12.0 0.0 collective-permute-done.1.refs_1_.refs_8_
  12.0 1.1 %enter.2 = (bf16[4,384,256]{2,1,0:T(8,128)(2,1)S(1)}, f32[4,64,256]{2,1,0:T(8,128)S(1)}) custom-call(s32[2,4]{1,0:T(2,128)S(4)} %get-tuple-element.55.order, f32[2,64,256]{2,1,0:T(8,128)S(1)} %get-tuple-element.56.inlet, bf16[1,320,256]{2,1,0:T(8,128)(2,1)S(1)} %get-tuple-element.63.rows_high.refs_3_.refs_6_.refs_2_, ...), custom_call_target="tpu_custom_call" | custom-call | flops 10737418 | bytes 1048576 | tf_op jit(solution)/shard_map/enter/pallas_call | solution.py:21
  13.1 1.8 %collective-permute-start.2 = (f32[4,64,256]{2,1,0:T(8,128)S(1)}, f32[4,64,256]{2,1,0:T(8,128)S(1)}, u32[]{:S(2)}, u32[]{:S(2)}) collective-permute-start(f32[4,64,256]{2,1,0:T(8,128)S(1)} %get-tuple-element.75), channel_id=1, source_target_pairs={{0,1},{1,2},{2,3},{3,4},{4,5},{5,6},{6,7},{7,0},{8,9},{9,10},{10,1... | collective-permute-start | bytes 786440 | tf_op jit(solution)/shard_map/ppermute | solution.py:119
  14.9 1.4 %collective-permute-done.3.arrived = f32[4,64,256]{2,1,0:T(8,128)S(1)} collective-permute-done((f32[4,64,256]{2,1,0:T(8,128)S(1)}, f32[4,64,256]{2,1,0:T(8,128)S(1)}, u32[]{:S(2)}, u32[]{:S(2)}) %collective-permute-start.3) | collective-permute-done | bytes 262176 | tf_op jit(solution)/shard_map/ppermute | solution.py:119
  16.3 0.5 %first_sides.1 = (bf16[4,2,64,256]{3,2,1,0:T(8,128)(2,1)S(1)}, f32[4,64,256]{2,1,0:T(8,128)S(1)}, f32[1,80,256]{2,1,0:T(8,128)S(1)}) custom-call(s32[2,4]{1,0:T(2,128)S(4)} %get-tuple-element.55.order, f32[4,64,256]{2,1,0:T(8,128)S(1)} %collective-permute-done.3.arrived, f32[4,64,256]{2,1,0:T(8,128)S(1)} %get-tuple-element.79.own, ...), custom_call_target="tpu_custom_call" | custom-call | flops 10737418 | bytes 1048576 | tf_op jit(solution)/shard_map/first_sides/pallas_call | solution.py:21
  16.8 0.1 collective-permute-start.4
  16.9 0.8 %late_maps.1.maps.refs_11_.refs_13_ = bf16[4,512,384]{2,1,0:T(8,128)(2,1)S(1)} custom-call(bf16[4,512,512]{2,1,0:T(8,128)(2,1)S(1)} %get-tuple-element.69.inv.refs_8_, bf16[4,128,512]{2,1,0:T(8,128)(2,1)S(1)} %get-tuple-element.70.faces, f32[1,80,256]{2,1,0:T(8,128)S(1)} %get-tuple-element.83.own._.refs_2_), custom_call_target="tpu_custom_call" | custom-call | flops 536870912 | bytes 1048576 | tf_op jit(solution)/shard_map/late_maps/pallas_call | solution.py:21
  17.7 0.5 %collective-permute-done.4.other.refs_0_.refs_3_.refs_14_ = f32[1,80,256]{2,1,0:T(8,128)S(1)} collective-permute-done((f32[1,80,256]{2,1,0:T(8,128)S(1)}, f32[1,80,256]{2,1,0:T(8,128)S(1)}, u32[]{:S(2)}, u32[]{:S(2)}) %collective-permute-start.4) | collective-permute-done | bytes 81952 | tf_op jit(solution)/shard_map/ppermute | solution.py:122
  18.1 0.3 combine.4._
  18.4 1.5 %collective-permute-start.5 = (f32[1,80,256]{2,1,0:T(8,128)S(1)}, f32[1,80,256]{2,1,0:T(8,128)S(1)}, u32[]{:S(2)}, u32[]{:S(2)}) collective-permute-start(f32[1,80,256]{2,1,0:T(8,128)S(1)} %combine.4._), channel_id=1, source_target_pairs={{0,16},{8,24},{16,0},{24,8},{1,17},{9,25},{17,1},{25,9},{2,18},{10... | collective-permute-start | bytes 245768 | tf_op jit(solution)/shard_map/ppermute | solution.py:122
  20.0 1.6 %second.2 = (bf16[4,512,256]{2,1,0:T(8,128)(2,1)S(1)}, bf16[4,512,256]{2,1,0:T(8,128)(2,1)S(1)}, f32[4,64,256]{2,1,0:T(8,128)S(1)}, f32[4,64,256]{2,1,0:T(8,128)S(1)}) custom-call(bf16[4,512,512]{2,1,0:T(8,128)(2,1)S(1)} %get-tuple-element.57.inv.refs_0_, bf16[4,512,384]{2,1,0:T(8,128)(2,1)S(1)} %get-tuple-element.76.maps.refs_3_.refs_6_, ...), custom_call_target="tpu_custom_call" | custom-call | bytes 1048576 | tf_op jit(solution)/shard_map/second/pallas_call | solution.py:21
  21.6 1.2 %late_free.1.free = f32[4,512,256]{2,1,0:T(8,128)S(1)} custom-call(bf16[4,512,512]{2,1,0:T(8,128)(2,1)S(1)} %get-tuple-element.69.inv.refs_8_, bf16[4,512,256]{2,1,0:T(8,128)(2,1)S(1)} %get-tuple-element.86.source_high, bf16[4,512,256]{2,1,0:T(8,128)(2,1)S(1)} %get-tuple-element.87.source_low, f32[1,80,256]{2,1,0:T(8,128)S(1)} %combine.4._), custom_call_target="tpu_custom_call" | custom-call | flops 1073741824 | bytes 1048576 | tf_op jit(solution)/shard_map/late_free/pallas_call | solution.py:21
  22.9 0.1 collective-permute-done.5.refs_1_.refs_15_
  23.0 0.7 %enter.3.stack = bf16[4,384,256]{2,1,0:T(8,128)(2,1)S(1)} custom-call(s32[2,4]{1,0:T(2,128)S(4)} %get-tuple-element.55.order, f32[2,64,256]{2,1,0:T(8,128)S(1)} %get-tuple-element.56.inlet, bf16[1,320,256]{2,1,0:T(8,128)(2,1)S(1)} %get-tuple-element.81.rows_high.refs_8_.refs_14_.refs_9_, ...), custom_call_target="tpu_custom_call" | custom-call | flops 10737418 | bytes 1048576 | tf_op jit(solution)/shard_map/enter/pallas_call | solution.py:21
  23.6 1.7 %second.3 = (bf16[4,512,256]{2,1,0:T(8,128)(2,1)S(1)}, bf16[4,512,256]{2,1,0:T(8,128)(2,1)S(1)}, f32[4,64,256]{2,1,0:T(8,128)S(1)}, f32[4,64,256]{2,1,0:T(8,128)S(1)}) custom-call(bf16[4,512,512]{2,1,0:T(8,128)(2,1)S(1)} %get-tuple-element.69.inv.refs_8_, bf16[4,512,384]{2,1,0:T(8,128)(2,1)S(1)} %late_maps.1.maps.refs_11_.refs_13_, ...), custom_call_target="tpu_custom_call" | custom-call | bytes 1048576 | tf_op jit(solution)/shard_map/second/pallas_call | solution.py:21
  25.3 0.0 collective-permute-done.2.arrived
  25.3 0.8 %second_sides.1 = (f32[2,64,256]{2,1,0:T(8,128)S(1)}, bf16[4,256,256]{2,1,0:T(8,128)(2,1)S(1)}, f32[4,64,256]{2,1,0:T(8,128)S(1)}, bf16[4,256,256]{2,1,0:T(8,128)(2,1)S(1)}, f32[4,64,256]{2,1,0:T(8,128)S(1)}) custom-call(s32[2,4]{1,0:T(2,128)S(4)} %get-tuple-element.55.order, f32[4,64,256]{2,1,0:T(8,128)S(1)} %collective-permute-done.2.arrived, ...), custom_call_target="tpu_custom_call" | custom-call | flops 10737418 | bytes 1048576 | tf_op jit(solution)/shard_map/second_sides/pallas_call | solution.py:21
  26.1 0.1 collective-permute-start.6
  26.2 1.3 %collective-permute-done.6.other.refs_0_ = f32[2,64,256]{2,1,0:T(8,128)S(1)} collective-permute-done((f32[2,64,256]{2,1,0:T(8,128)S(1)}, f32[2,64,256]{2,1,0:T(8,128)S(1)}, u32[]{:S(2)}, u32[]{:S(2)}) %collective-permute-start.6) | collective-permute-done | bytes 131104 | tf_op jit(solution)/shard_map/ppermute | solution.py:122
  27.5 0.3 combine.5._
  27.8 1.6 %collective-permute-start.7 = (f32[2,64,256]{2,1,0:T(8,128)S(1)}, f32[2,64,256]{2,1,0:T(8,128)S(1)}, u32[]{:S(2)}, u32[]{:S(2)}) collective-permute-start(f32[2,64,256]{2,1,0:T(8,128)S(1)} %combine.5._), channel_id=1, source_target_pairs={{0,16},{8,24},{16,0},{24,8},{1,17},{9,25},{17,1},{25,9},{2,18},{10... | collective-permute-start | bytes 393224 | tf_op jit(solution)/shard_map/ppermute | solution.py:122
  29.3 3.1 %settle.1 = (f32[4,512,256]{2,1,0:T(8,128)S(1)}, f32[1,256,256]{2,1,0:T(8,128)S(1)}, f32[4,512,256]{2,1,0:T(8,128)S(1)}, f32[1,256,256]{2,1,0:T(8,128)S(1)}) custom-call(f32[2,64,256]{2,1,0:T(8,128)S(1)} %combine.5._, bf16[4,512,512]{2,1,0:T(8,128)(2,1)S(1)} %get-tuple-element.57.inv.refs_0_, bf16[4,512,256]{2,1,0:T(8,128)(2,1)S(1)} %get-tuple-element.93.refs_1_, ...), custom_call_target="tpu_custom_call" | custom-call | flops 3221225472 | bytes 1048576 | tf_op jit(solution)/shard_map/settle/pallas_call | solution.py:21
  32.4 0.9 %collective-permute-done.7.refs_1_ = f32[2,64,256]{2,1,0:T(8,128)S(1)} collective-permute-done((f32[2,64,256]{2,1,0:T(8,128)S(1)}, f32[2,64,256]{2,1,0:T(8,128)S(1)}, u32[]{:S(2)}, u32[]{:S(2)}) %collective-permute-start.7) | collective-permute-done | bytes 131104 | tf_op jit(solution)/shard_map/ppermute | solution.py:122
  33.4 2.4 %result.1 = bf16[2,1,4,512,256]{4,3,2,1,0:T(8,128)(2,1)} custom-call(s32[2,4]{1,0:T(2,128)S(4)} %get-tuple-element.55.order, f32[2,64,256]{2,1,0:T(8,128)S(1)} %get-tuple-element.56.inlet, f32[2,64,256]{2,1,0:T(8,128)S(1)} %collective-permute-done.6.other.refs_0_, f32[2,64,256]{2,1,0:T(8,128)S(1)} %collective-permute-done.7.refs_1_, ...), custom_call_target="tpu_custom_call" | custom-call | flops 1073741824 | bytes 1048576 | tf_op jit(solution)/shard_map/result/pallas_call | solution.py:21
Async XLA Ops:
  3.3 3.1 %collective-permute-start = (f32[1,80,256]{2,1,0:T(8,128)S(1)}, f32[1,80,256]{2,1,0:T(8,128)S(1)}, u32[]{:S(2)}, u32[]{:S(2)}) collective-permute-start(f32[1,80,256]{2,1,0:T(8,128)S(1)} %get-tuple-element.62.own.refs_0_), channel_id=1, source_target_pairs={{0,8},{8,0},{16,24},{24,16},{1,9},{9,1},{17,25},{25,17},{2,10},{10... | collective-permute-start | bytes 245768 | tf_op jit(solution)/shard_map/ppermute | solution.py:122
  3.8 12.5 %collective-permute-start.3 = (f32[4,64,256]{2,1,0:T(8,128)S(1)}, f32[4,64,256]{2,1,0:T(8,128)S(1)}, u32[]{:S(2)}, u32[]{:S(2)}) collective-permute-start(f32[4,64,256]{2,1,0:T(8,128)S(1)} %get-tuple-element.78), channel_id=1, source_target_pairs={{0,1},{1,2},{2,3},{3,4},{4,5},{5,6},{6,7},{7,0},{8,9},{9,10},{10,1... | collective-permute-start | bytes 786440 | tf_op jit(solution)/shard_map/ppermute | solution.py:119
  6.7 5.3 %collective-permute-start.1 = (f32[1,80,256]{2,1,0:T(8,128)S(1)}, f32[1,80,256]{2,1,0:T(8,128)S(1)}, u32[]{:S(2)}, u32[]{:S(2)}) collective-permute-start(f32[1,80,256]{2,1,0:T(8,128)S(1)} %combine.3._), channel_id=1, source_target_pairs={{0,16},{8,24},{16,0},{24,8},{1,17},{9,25},{17,1},{25,9},{2,18},{10... | collective-permute-start | bytes 245768 | tf_op jit(solution)/shard_map/ppermute | solution.py:122
  13.1 12.2 %collective-permute-start.2 = (f32[4,64,256]{2,1,0:T(8,128)S(1)}, f32[4,64,256]{2,1,0:T(8,128)S(1)}, u32[]{:S(2)}, u32[]{:S(2)}) collective-permute-start(f32[4,64,256]{2,1,0:T(8,128)S(1)} %get-tuple-element.75), channel_id=1, source_target_pairs={{0,1},{1,2},{2,3},{3,4},{4,5},{5,6},{6,7},{7,0},{8,9},{9,10},{10,1... | collective-permute-start | bytes 786440 | tf_op jit(solution)/shard_map/ppermute | solution.py:119
  16.8 1.3 %collective-permute-start.4 = (f32[1,80,256]{2,1,0:T(8,128)S(1)}, f32[1,80,256]{2,1,0:T(8,128)S(1)}, u32[]{:S(2)}, u32[]{:S(2)}) collective-permute-start(f32[1,80,256]{2,1,0:T(8,128)S(1)} %get-tuple-element.83.own._.refs_2_), channel_id=1, source_target_pairs={{0,8},{8,0},{16,24},{24,16},{1,9},{9,1},{17,25},{25,17},{2,10},{10... | collective-permute-start | bytes 245768 | tf_op jit(solution)/shard_map/ppermute | solution.py:122
  18.4 4.5 %collective-permute-start.5 = (f32[1,80,256]{2,1,0:T(8,128)S(1)}, f32[1,80,256]{2,1,0:T(8,128)S(1)}, u32[]{:S(2)}, u32[]{:S(2)}) collective-permute-start(f32[1,80,256]{2,1,0:T(8,128)S(1)} %combine.4._), channel_id=1, source_target_pairs={{0,16},{8,24},{16,0},{24,8},{1,17},{9,25},{17,1},{25,9},{2,18},{10... | collective-permute-start | bytes 245768 | tf_op jit(solution)/shard_map/ppermute | solution.py:122
  26.1 1.4 %collective-permute-start.6 = (f32[2,64,256]{2,1,0:T(8,128)S(1)}, f32[2,64,256]{2,1,0:T(8,128)S(1)}, u32[]{:S(2)}, u32[]{:S(2)}) collective-permute-start(f32[2,64,256]{2,1,0:T(8,128)S(1)} %get-tuple-element.92.own), channel_id=1, source_target_pairs={{0,8},{8,0},{16,24},{24,16},{1,9},{9,1},{17,25},{25,17},{2,10},{10... | collective-permute-start | bytes 393224 | tf_op jit(solution)/shard_map/ppermute | solution.py:122
  27.8 5.6 %collective-permute-start.7 = (f32[2,64,256]{2,1,0:T(8,128)S(1)}, f32[2,64,256]{2,1,0:T(8,128)S(1)}, u32[]{:S(2)}, u32[]{:S(2)}) collective-permute-start(f32[2,64,256]{2,1,0:T(8,128)S(1)} %combine.5._), channel_id=1, source_target_pairs={{0,16},{8,24},{16,0},{24,8},{1,17},{9,25},{17,1},{25,9},{2,18},{10... | collective-permute-start | bytes 393224 | tf_op jit(solution)/shard_map/ppermute | solution.py:122

commit v7 on v6

--- a/solution.py
+++ b/solution.py
@@ -16,7 +16,7 @@
 SMEM = pltpu.SMEM
 
 
-def run(body, name, ins, outs, scratch, flops):
+def run(body, name, ins, outs, scratch):
     pairs = [a if isinstance(a, tuple) else (a, VMEM) for a in ins]
     return pl.pallas_call(
         body,
@@ -25,7 +25,7 @@
         out_specs=[pl.BlockSpec(memory_space=o.memory_space) for o in outs],
         out_shape=outs,
         scratch_shapes=scratch,
-        cost_estimate=pl.CostEstimate(flops=flops, bytes_accessed=MIB, transcendentals=0),
+        cost_estimate=pl.CostEstimate(flops=0, bytes_accessed=0, transcendentals=0),
         compiler_params=pltpu.CompilerParams(vmem_limit_bytes=24 * MIB),
     )(*[a if space is VMEM else pltpu.with_memory_space_constraint(a, space) for a, space in pairs])
 
@@ -113,7 +113,6 @@
     home = {c: (g, n) for g, group in enumerate(groups) for n, c in enumerate(group)}
     ending = pl.ds(nodes - face, face)
     per = 2 if count % 2 == 0 else 1
-    dense = 2 * count * nodes * nodes * tracers
 
     def to_next(value):
         return lax.ppermute(value, "lat", [(i, (i + 1) % lats) for i in range(lats)])
@@ -121,14 +120,13 @@
     def swap(value, stage):
         return lax.ppermute(value, "stream", [(i, i ^ (1 << stage)) for i in range(streams)])
 
+    inv_near, up_near, side_near, old_near = (
+        pltpu.with_memory_space_constraint(a, VMEM) for a in (inverse, upwind, lateral, previous)
+    )
     shaped = previous.reshape(cols, count, per_side, plane, tracers)
 
-    def face_outs(size):
-        return [
-            VMEM((size * count, nodes, 6 * face), BF16),
-            VMEM((size * count, nodes, tracers), F32),
-            VMEM((size * count, face, 6 * face), BF16),
-        ]
+    def map_outs(size):
+        return [VMEM((size * count, nodes, 6 * face), BF16), VMEM((size * count, face, 6 * face), BF16)]
 
     def chain_outs(size):
         return [
@@ -146,16 +144,15 @@
     def source_outs(size):
         return [VMEM((size * count, nodes, tracers), BF16)] * 2
 
-    def field_outs(size):
-        return [VMEM((size * count, nodes, nodes), BF16), VMEM((size * count, 2 * face, nodes), BF16)]
-
-    def times(inv, i, high, low, k, rows=None):
-        matrix = inv[i] if rows is None else inv[i, rows]
-        return dot(matrix, high[k]) + dot(matrix, low[k])
-
-    def face_maps(inv, faces, i, rows=None):
-        matrix = inv[i] if rows is None else inv[i, rows]
-        return lax.dot_general(matrix, faces[i], (((1,), (1,)), ((), ())), preferred_element_type=F32)
+    def times(matrix, high, low, i):
+        return dot(matrix, high[i]) + dot(matrix, low[i])
+
+    def face_maps(matrix, up, side):
+        faces = jnp.concatenate([up, side], axis=0)
+        return lax.dot_general(matrix, faces, (((1,), (1,)), ((), ())), preferred_element_type=F32)
+
+    def at(group, i):
+        return group[0] + i // count, 0, i % count
 
     def side_of(tails, i, s):
         return dot_split(split(tails[i][:, face:]), s)
@@ -182,98 +179,67 @@
         row = (rows_high[n, last][:, face:], rows_low[n, last][:, face:])
         return ends[n * count + count - 1] + dot_split(row, (high[n], low[n]))
 
-    def begin():
+    def load():
         size = len(early)
         items = size * count
 
         def body(
             order, rate, aff, inlet, old, inverse, upwind, lateral, previous,
-            trace, o_order, o_rate, o_aff, o_inlet, inv, faces, source_high, source_low,
-            tails, sides, ends, message, lagged, staged, own, lead_sems, sems,
+            trace, o_order, o_rate, o_aff, o_inlet, near, o_tail, faces, source_high, source_low,
+            lagged, staged, lead_sems, sems,
         ):
+            rows = pl.ds(plane - 2 * per_side, 2 * per_side)
             lead = [
                 pltpu.make_async_copy(a, b, lead_sems.at[k])
-                for k, (a, b) in enumerate(((rate, o_rate), (aff, o_aff), (order, o_order), (inlet, o_inlet)))
+                for k, (a, b) in enumerate((
+                    (rate, o_rate),
+                    (aff, o_aff),
+                    (order, o_order),
+                    (old.at[0, :, :, rows], staged),
+                    (inlet, o_inlet),
+                ))
             ]
-            rows = pl.ds(plane - 2 * per_side, 2 * per_side)
-            lead.append(pltpu.make_async_copy(old.at[0, :, :, rows], staged, lead_sems.at[len(lead)]))
-
-            def parts(i):
-                c, j = early[0] + i // count, i % count
-                here, there = pl.ds(j, per), pl.ds(i, per)
-                pairs = (
-                    (previous.at[c, 0, here], lagged.at[there]),
-                    (inverse.at[c, 0, here, ending], inv.at[there, ending]),
-                    (upwind.at[c, 0, here], faces.at[there, pl.ds(0, face)]),
-                    (lateral.at[c, 0, here], faces.at[there, pl.ds(face, face)]),
-                )
-                return [pltpu.make_async_copy(a, b, sems.at[k, i]) for k, (a, b) in enumerate(pairs)]
-
-            def rest(i):
-                c, j = early[0] + i // count, i % count
-                others = pl.ds(0, nodes - face)
-                return pltpu.make_async_copy(
-                    inverse.at[c, 0, pl.ds(j, per), others], inv.at[pl.ds(i, per), others], sems.at[4, i]
-                )
-
-            def old_rows(field):
-                return jnp.concatenate([field(a).astype(F32)[per_side:] for a in range(per_side)], axis=0)
-
-            def lagged_rows(i):
-                starts = [a * plane + plane - 2 * per_side for a in range(per_side)]
-                return old_rows(lambda a: lagged[i, pl.ds(starts[a], 2 * per_side)])
-
-            for one in lead[:3]:
-                one.start()
-            for i in range(0, items, per):
-                for one in parts(i):
-                    one.start()
-            for one in lead[3:]:
+            whole = pl.ds(0, count)
+            fields, others = [], []
+            for n, c in enumerate(early):
+                for h in range(0, count, per):
+                    here, there = pl.ds(h, per), pl.ds(n * count + h, per)
+                    fields.append((previous.at[c, 0, here], lagged.at[there]))
+                there = pl.ds(n * count, count)
+                others += [
+                    (inverse.at[c, 0, whole, ending], o_tail.at[there]),
+                    (upwind.at[c, 0], faces.at[there, pl.ds(0, face)]),
+                    (lateral.at[c, 0], faces.at[there, pl.ds(face, face)]),
+                ]
+            copies = [pltpu.make_async_copy(a, b, sems.at[k]) for k, (a, b) in enumerate(fields + others)]
+            for one in lead[:3] + copies[: len(fields)] + lead[3:4] + copies[len(fields) :] + lead[4:]:
                 one.start()
             for one in lead[:3]:
                 one.wait()
 
-            def step(members):
-                for one in parts(members[0]):
-                    one.wait()
-                rest(members[0]).start()
-                for i in members:
+            def old_rows(field):
+                return jnp.concatenate([field(a).astype(F32)[per_side:] for a in range(per_side)], axis=0)
+
+            for k in range(len(fields)):
+                copies[k].wait()
+                for i in range(k * per, k * per + per):
                     lag = lagged[i].astype(F32)
                     source_high[i], source_low[i] = split(langmuir(lag, o_rate[...], o_aff[...]))
-                for i in members:
-                    tails[i] = face_maps(inv, faces, i, ending)
-                    own[i] = times(inv, i, source_high, source_low, i, ending)
-
-            in_pairs(items, per, step)
+                    c = early[i // count]
+                    if c == cols - 1:
+                        trace[i % count] = lateral_rows(lag, per_side)
+                    else:
+                        near[i + count] = lateral_rows(lag, per_side)
             for one in lead[3:]:
                 one.wait()
             for j in range(count):
-                trace[j] = lagged_rows(items - count + j)
-            for n, c in enumerate(early):
-                links = []
-                for p in range(count):
-                    j = o_order[c, p]
-                    i = n * count + j
-                    s = split(old_rows(lambda a: staged[j, a]) if c == 1 else lagged_rows(i - count))
-                    sides[n * count + p, 0] = s[0]
-                    sides[n * count + p, 1] = s[1]
-                    end = own[i] + side_of(tails, i, s)
-                    ends[n * count + p] = end
-                    links.append((tails[i][:, :face], end))
-                while len(links) > 1:
-                    paired = []
-                    for (low, start), (up, end) in zip(links[::2], links[1::2]):
-                        u = split(up)
-                        paired.append((dot_split(u, split(low)), end + dot_split(u, split(start))))
-                    links = paired + links[2 * len(paired) :]
-                message[n, pl.ds(0, face)] = links[0][1]
-                message[n, pl.ds(face, packed)] = pack_map(links[0][0], tracers)
-            for i in range(0, items, per):
-                rest(i).wait()
+                near[j] = old_rows(lambda a: staged[j, a])
+            for one in copies[len(fields) :]:
+                one.wait()
 
         values = run(
             body,
-            "begin",
+            "load",
             [
                 (flow_order.reshape(cols, count), HBM),
                 (uptake_rate.reshape(1, tracers), HBM),
@@ -291,107 +257,136 @@
                 VMEM((1, tracers), F32),
                 VMEM((1, tracers), F32),
                 VMEM((cols, face, tracers), F32),
-                *field_outs(size),
+                VMEM((items, face, tracers), F32),
+                VMEM((items, face, nodes), BF16),
+                VMEM((items, 2 * face, nodes), BF16),
                 *source_outs(size),
+            ],
+            [
+                VMEM((items, nodes, tracers), BF16),
+                VMEM((count, per_side, 2 * per_side, tracers), BF16),
+                pltpu.SemaphoreType.DMA((5,)),
+                pltpu.SemaphoreType.DMA((size * (count // per + 3),)),
+            ],
+        )
+        state = SimpleNamespace()
+        state.near, state.tail, state.faces, state.source_high, state.source_low = values[5:]
+        return values[:5], state
+
+    def begin_early(state):
+        size = len(early)
+        items = size * count
+
+        def body(
+            order, near, tail, faces, source_high, source_low, tails, sides, ends, message, own
+        ):
+            def step(members):
+                for i in members:
+                    tails[i] = face_maps(tail[i], faces[i, :face], faces[i, face:])
+                    own[i] = times(tail[i], source_high, source_low, i)
+
+            in_pairs(items, per, step)
+            for n, c in enumerate(early):
+                links = []
+                for p in range(count):
+                    i = n * count + order[c, p]
+                    s = split(near[i])
+                    sides[n * count + p, 0] = s[0]
+                    sides[n * count + p, 1] = s[1]
+                    end = own[i] + side_of(tails, i, s)
+                    ends[n * count + p] = end
+                    links.append((tails[i][:, :face], end))
+                while len(links) > 1:
+                    paired = []
+                    for (low, start), (up, end) in zip(links[::2], links[1::2]):
+                        u = split(up)
+                        paired.append((dot_split(u, split(low)), end + dot_split(u, split(start))))
+                    links = paired + links[2 * len(paired) :]
+                message[n, pl.ds(0, face)] = links[0][1]
+                message[n, pl.ds(face, packed)] = pack_map(links[0][0], tracers)
+
+        state.tails, state.sides, state.ends, state.message = run(
+            body,
+            "begin_early",
+            [order, state.near, state.tail, state.faces, state.source_high, state.source_low],
+            [
                 VMEM((items, face, 2 * face), F32),
                 *side_outs(size),
                 VMEM((size, face + packed, tracers), F32),
             ],
-            [
-                VMEM((items, nodes, tracers), BF16),
-                VMEM((count, per_side, 2 * per_side, tracers), BF16),
-                VMEM((items, face, tracers), F32),
-                pltpu.SemaphoreType.DMA((5,)),
-                pltpu.SemaphoreType.DMA((5, items)),
-            ],
-            size * dense,
-        )
-        state = SimpleNamespace()
-        state.inv, state.faces, state.source_high, state.source_low = values[5:9]
-        state.tails, state.sides, state.ends, state.message = values[9:]
-        return values[:5], state
-
-    def finish_early(state, after):
+            [VMEM((items, face, tracers), F32)],
+        )
+
+    def early_maps(state, after):
         size = len(early)
-        items = size * count
-
-        def body(
-            order, inv, faces, source_high, source_low, tails, _, inverse, upwind, lateral, previous,
-            maps, free, side_maps, rows_high, rows_low, o_inv, o_faces, o_lagged, row, sems,
-        ):
-            copies = []
-            for n, c in enumerate(late):
-                there = pl.ds(n * count, count)
-                for k, (a, b) in enumerate((
-                    (previous.at[c, 0], o_lagged.at[there]),
-                    (upwind.at[c, 0], o_faces.at[there, pl.ds(0, face)]),
-                    (lateral.at[c, 0], o_faces.at[there, pl.ds(face, face)]),
-                    (inverse.at[c, 0], o_inv.at[there]),
-                )):
-                    copies.append(pltpu.make_async_copy(a, b, sems.at[k, n]))
-                    copies[-1].start()
-
-            def step(members):
-                for i in members:
-                    both = face_maps(inv, faces, i)
-                    maps[i] = stack_maps(both)
-                    side_maps[i] = stack_maps(lateral_rows(both, per_side))
-                    free[i] = times(inv, i, source_high, source_low, i)
-                    n, p = i // count, i % count
-                    head = tails[n * count + order[early[0] + n, p]][:, :face]
-                    link(n, p, split(head), rows_high, rows_low, row)
-
-            in_pairs(items, per, step)
-            for one in copies:
-                one.wait()
-
-        state.maps, state.free, state.side_maps, state.high, state.low, *fetched = run(
+
+        def body(order, inv, up, side, tails, _, maps, side_maps, rows_high, rows_low, row):
+            for i in range(size * count):
+                k = at(early, i)
+                both = face_maps(inv[k], up[k], side[k])
+                maps[i] = stack_maps(both)
+                side_maps[i] = stack_maps(lateral_rows(both, per_side))
+                n, p = i // count, i % count
+                head = tails[n * count + order[early[0] + n, p]][:, :face]
+                link(n, p, split(head), rows_high, rows_low, row)
+
+        state.maps, state.side_maps, state.high, state.low = run(
             body,
-            "finish_early",
-            [order, state.inv, state.faces, state.source_high, state.source_low, state.tails, after]
-            + [(a, HBM) for a in (inverse, upwind, lateral, previous)],
-            face_outs(size)
-            + chain_outs(size)[1:]
-            + field_outs(len(late))
-            + [VMEM((len(late) * count, nodes, tracers), BF16)],
-            [VMEM((size, face, wide), F32), pltpu.SemaphoreType.DMA((4, len(late)))],
-            3 * size * dense,
-        )
-        return fetched
-
-    def begin_late(fetched):
+            "early_maps",
+            [order, inv_near, up_near, side_near, state.tails, after],
+            map_outs(size) + chain_outs(size)[1:],
+            [VMEM((size, face, wide), F32)],
+        )
+        return state.maps
+
+    def whole_free(group, state, after):
+        size = len(group)
+
+        def body(inv, source_high, source_low, _, free):
+            for i in range(size * count):
+                free[i] = times(inv[at(group, i)], source_high, source_low, i)
+
+        (state.free,) = run(
+            body,
+            "whole_free",
+            [inv_near, state.source_high, state.source_low, after],
+            [VMEM((size * count, nodes, tracers), F32)],
+            [],
+        )
+
+    def begin_late(after):
         size = len(late)
         items = size * count
 
         def body(
-            order, inv, faces, lagged, rate, aff,
+            order, inv, up, side, previous, rate, aff, _,
             source_high, source_low, own, tails, rows_high, rows_low, mapped, row,
         ):
             for i in range(items):
-                tails[i] = face_maps(inv, faces, i, ending)
+                k = at(late, i)
+                tails[i] = face_maps(inv[*k, ending], up[k], side[k])
             for i in range(items + 1):
                 if i < items:
-                    lag = lagged[i].astype(F32)
+                    lag = previous[at(late, i)].astype(F32)
                     source_high[i], source_low[i] = split(langmuir(lag, rate[...], aff[...]))
                     n, p = i // count, i % count
                     step = split(tails[n * count + order[late[n], p]][:, :face])
                     link(n, p, step, rows_high, rows_low, row)
                 if i > 0:
-                    own[i - 1] = times(inv, i - 1, source_high, source_low, i - 1, ending)
+                    own[i - 1] = times(inv[*at(late, i - 1), ending], source_high, source_low, i - 1)
             for n in range(size):
                 mapped[n] = pack_map(row[n][:, :face], tracers)
 
-        state = SimpleNamespace(inv=fetched[0], faces=fetched[1])
+        state = SimpleNamespace()
         values = run(
             body,
             "begin_late",
-            [order, *fetched, rate, aff],
+            [order, inv_near, up_near, side_near, old_near, rate, aff, after],
             source_outs(size)
             + [VMEM((items, face, tracers), F32)]
             + chain_outs(size)
             + [VMEM((size, packed, tracers), F32)],
             [VMEM((size, face, wide), F32)],
-            2 * size * dense,
         )
         state.source_high, state.source_low, state.own, state.tails, state.high, state.low, state.mapped = values
         return state
@@ -399,34 +394,15 @@
     def late_maps(state, after):
         items = len(late) * count
 
-        def body(inv, faces, _, maps):
+        def body(inv, up, side, _, maps):
             for i in range(items):
-                maps[i] = stack_maps(face_maps(inv, faces, i))
+                k = at(late, i)
+                maps[i] = stack_maps(face_maps(inv[k], up[k], side[k]))
 
         (state.maps,) = run(
-            body,
-            "late_maps",
-            [state.inv, state.faces, after],
-            face_outs(len(late))[:1],
-            [],
-            len(late) * dense,
-        )
-
-    def late_free(state, after):
-        items = len(late) * count
-
-        def body(inv, source_high, source_low, _, free):
-            for i in range(items):
-                free[i] = times(inv, i, source_high, source_low, i)
-
-        (state.free,) = run(
-            body,
-            "late_free",
-            [state.inv, state.source_high, state.source_low, after],
-            [VMEM((items, nodes, tracers), F32)],
-            [],
-            2 * len(late) * dense,
-        )
+            body, "late_maps", [inv_near, up_near, side_near, after], map_outs(len(late))[:1], []
+        )
+        return state.maps
 
     def arrived_side(arrived, j):
         return split(jnp.where(lax.axis_index("lat") > 0, arrived[j], 0.0))
@@ -448,11 +424,10 @@
             [order, arrived, state.own, state.tails, state.high, state.low, state.mapped],
             side_outs(1) + [VMEM((1, face + packed, tracers), F32)],
             offset_scratch(1),
-            dense // 50,
-        )
-
-    def combine_first(stage, own, other):
-        def body(own, other, message):
+        )
+
+    def combine_first(stage, own, other, after):
+        def body(own, other, _, message):
             upper = bit(stage)
             for n in range(own.shape[0]):
                 up = jnp.where(upper, own[n], other[n])
@@ -462,7 +437,7 @@
                 mapped = dot_split(m, split(unpack_map(low[face:], face)))
                 message[n, pl.ds(face, packed)] = pack_map(mapped, tracers)
 
-        return run(body, "combine", [own, other], [VMEM(own.shape, F32)], [], dense // 100)[0]
+        return run(body, "combine", [own, other, after], [VMEM(own.shape, F32)], [])[0]
 
     def combine_second(stage, own, other, old_own, old_other):
         def body(own, other, *refs):
@@ -479,7 +454,7 @@
         ins = [own, other]
         for pair in zip(old_own, old_other):
             ins += pair
-        return run(body, "combine", ins, [VMEM(own.shape, F32)], [], dense // 100)[0]
+        return run(body, "combine", ins, [VMEM(own.shape, F32)], [])[0]
 
     def entering(start, offsets, maps):
         for stage in reversed(range(stages)):
@@ -526,7 +501,7 @@
         if last:
             ins += [state.free, state.side_maps, after]
         scratch = [VMEM((size, wide, tracers), BF16)] * 2
-        values = run(body, "enter", ins, outs, scratch, dense // 50)
+        values = run(body, "enter", ins, outs, scratch)
         state.stack = values[0]
         return values[1] if last else None
 
@@ -540,15 +515,14 @@
                     traces[i] = lateral_rows(swept, per_side)
                     source_high[i], source_low[i] = split(langmuir(swept, rate[...], aff[...]))
                 if i > 0:
-                    own[i - 1] = times(inv, i - 1, source_high, source_low, i - 1, ending)
+                    own[i - 1] = times(inv[*at(group, i - 1), ending], source_high, source_low, i - 1)
 
         state.source_high, state.source_low, state.traces, state.own = run(
             body,
             "second",
-            [state.inv, state.maps, state.free, state.stack, rate, aff, after],
+            [inv_near, state.maps, state.free, state.stack, rate, aff, after],
             source_outs(len(group)) + [VMEM((items, face, tracers), F32)] * 2,
             [],
-            0,
         )
 
     def second_sides(arrived):
@@ -581,20 +555,20 @@
             outs.append(VMEM((len(group) * count, 4 * face, tracers), BF16))
             outs.append(VMEM((len(group) * count, face, tracers), F32))
             scratch += offset_scratch(len(group))
-        message, *values = run(body, "second_sides", ins, outs, scratch, dense // 50)
+        message, *values = run(body, "second_sides", ins, outs, scratch)
         for g, state in enumerate(states):
             state.side_stack, state.ends = values[2 * g : 2 * g + 2]
         return message
 
     def settle(after):
-        def body(_, *refs):
-            got = [refs[8 * g : 8 * g + 8] for g in range(len(groups))]
-            outs = refs[8 * len(groups) :]
+        def body(_, inv, *refs):
+            got = [refs[7 * g : 7 * g + 7] for g in range(len(groups))]
+            outs = refs[7 * len(groups) :]
             for g, group in enumerate(groups):
-                inv, source_high, source_low, maps, stack, ends, rows_high, rows_low = got[g]
+                source_high, source_low, maps, stack, ends, rows_high, rows_low = got[g]
                 base, within, high, low = outs[2 * g], outs[2 * g + 1], outs[-2], outs[-1]
                 for i in range(len(group) * count):
-                    own = times(inv, i, source_high, source_low, i)
+                    own = times(inv[at(group, i)], source_high, source_low, i)
                     base[i] = own + dot(maps[i][:, 2 * face :], stack[i])
                 for n in range(len(group)):
                     for p in range(count - 1):
@@ -605,15 +579,15 @@
                     rows = (rows_high[n, span][:, face:], rows_low[n, span][:, face:])
                     within[n] = dot_split(rows, (high[...], low[...]))
 
-        ins = [after]
+        ins = [after, inv_near]
         outs = []
         for group, state in zip(groups, states):
-            ins += [state.inv, state.source_high, state.source_low]
+            ins += [state.source_high, state.source_low]
             ins += [state.maps, state.side_stack, state.ends, state.high, state.low]
             outs.append(VMEM((len(group) * count, nodes, tracers), F32))
             outs.append(VMEM((len(group), wide, tracers), F32))
         scratch = [VMEM((wide - face, tracers), BF16)] * 2
-        values = run(body, "settle", ins, outs, scratch, 3 * cols * dense)
+        values = run(body, "settle", ins, outs, scratch)
         for g, state in enumerate(states):
             state.base, state.within = values[2 * g : 2 * g + 2]
 
@@ -654,29 +628,31 @@
         for group, state in zip(groups, states):
             ins += [state.high, state.low, state.within, state.base, state.maps, *state.received]
             scratch.append(VMEM((len(group) * count, 3 * face, tracers), BF16))
-        return run(body, "result", ins, [HBM(previous.shape, BF16)], scratch, cols * dense)[0]
-
-    def exchange_first(state):
+        return run(body, "result", ins, [HBM(previous.shape, BF16)], scratch)[0]
+
+    def exchange_first(state, beside):
         state.sent, state.received = [state.message], []
         for stage in range(stages):
             if stage:
-                state.sent.append(combine_first(stage - 1, state.sent[-1], state.received[-1]))
+                state.sent.append(combine_first(stage - 1, state.sent[-1], state.received[-1], after))
             state.received.append(swap(state.sent[-1], stage))
-
-    (trace, order, rate, aff, inlet), one = begin()
+            if not stage:
+                after = beside()
+
+    (trace, order, rate, aff, inlet), one = load()
     order = (order, SMEM)
-    exchange_first(one)
     arrived = to_next(trace)
-    fetched = finish_early(one, one.sent[-1])
-    two = begin_late(fetched)
+    begin_early(one)
+    exchange_first(one, lambda: early_maps(one, one.message))
+    two = begin_late(one.sent[-1])
+    whole_free(early, one, one.sent[-1])
     states = [one, two]
     trace = enter_first(early, one, two.mapped)
     arrived_next = to_next(trace)
     first_sides(two, arrived)
-    exchange_first(two)
-    late_maps(two, two.sent[0])
+    exchange_first(two, lambda: late_maps(two, two.message))
     second(early, one, two.sent[-1])
-    late_free(two, two.sent[-1])
+    whole_free(late, two, two.sent[-1])
     enter_first(late, two, None)
     second(late, two, two.sent[-1])
     message, offsets = second_sides(arrived_next), []

time: 36.1 us -> 35.5 us (0.983)
  waiting for transfers between devices: 4.28 us -> 3.6 us
    ppermute x2, waiting for transfers between devices: 1.43 us -> 0.18 us  [to_next(): lax.ppermute(value, 'lat', [(i, (i + 1) % lats) for i in range(lats)])]
    ppermute x6, starting transfers between devices: 5.3 us -> 4.73 us  [swap(): lax.ppermute(value, 'stream', [(i, i ^ 1 << stage) for i in range(streams)])]
    ppermute x6, waiting for transfers between devices: 2.85 us -> 3.41 us  [swap(): lax.ppermute(value, 'stream', [(i, i ^ 1 << stage) for i in range(streams)])]
    ppermute x2, starting transfers between devices: 4.33 us -> 4.77 us  [to_next(): lax.ppermute(value, 'lat', [(i, (i + 1) % lats) for i in range(lats)])]
    pallas_call x16 -> x18, Pallas kernels: 21.7 us -> 21.9 us  [run(): pl.pallas_call(body, name=name, in_specs=[pl.BlockSpec(memory_space=space...]
  transfers between devices with their start and end apart: 8 -> 8, of which waited for: 5 -> 6; matrix products, arithmetic and copies ran while one was open for 0% -> 0% of each run, Pallas kernels for 42% -> 46%
where the time goes in v7:
time: 35.5 us; the launch traced here: 35.4 us
  Pallas kernels  21.9 us (62%)
  starting transfers between devices  9.49 us (27%)
  waiting for transfers between devices  3.6 us (10%)
    pallas_call x18, Pallas kernels, run(): pl.pallas_call(body, name=name, in_specs=[pl.BlockSpec(memory_space=space...  21.9 us
    ppermute x2, starting transfers between devices, to_next(): lax.ppermute(value, 'lat', [(i, (i + 1) % lats) for i in range(lats)])  4.77 us
    ppermute x6, starting transfers between devices, swap(): lax.ppermute(value, 'stream', [(i, i ^ 1 << stage) for i in range(streams)])  4.73 us
    ppermute x6, waiting for transfers between devices, swap(): lax.ppermute(value, 'stream', [(i, i ^ 1 << stage) for i in range(streams)])  3.41 us
  transfers between devices with their start and end apart: 8, of which 6 were waited for; matrix products, arithmetic and copies ran while one was open for 0% of the time, Pallas kernels for 46%

profile of v7, /device:TPU:0, one launch (start us, length us, event | category | flops | bytes accessed | tf_op | source)
XLA Modules:
  0.0 35.4 jit_solution(7769068632106995312)
XLA Ops:
  0.0 2.0 %load.1 = (f32[4,64,256]{2,1,0:T(8,128)S(1)}, s32[2,4]{1,0:T(2,128)S(4)}, f32[1,256]{1,0:T(1,128)S(1)}, f32[1,256]{1,0:T(1,128)S(1)}, f32[2,64,256]{2,1,0:T(8,12...) custom-call(s32[2,4]{1,0:T(2,128)} %bitcast.5, ...), custom_call_target="tpu_custom_call" | custom-call | tf_op jit(solution)/shard_map/load/pallas_call | solution.py:21
  2.1 3.0 %collective-permute-start.3 = (f32[4,64,256]{2,1,0:T(8,128)S(1)}, f32[4,64,256]{2,1,0:T(8,128)S(1)}, u32[]{:S(2)}, u32[]{:S(2)}) collective-permute-start(f32[4,64,256]{2,1,0:T(8,128)S(1)} %get-tuple-element.72), channel_id=1, source_target_pairs={{0,1},{1,2},{2,3},{3,4},{4,5},{5,6},{6,7},{7,0},{8,9},{9,10},{10,1... | collective-permute-start | bytes 786440 | tf_op jit(solution)/shard_map/ppermute | solution.py:118
  5.1 1.4 %begin_early.1 = (f32[4,64,128]{2,1,0:T(8,128)S(1)}, bf16[4,2,64,256]{3,2,1,0:T(8,128)(2,1)S(1)}, f32[4,64,256]{2,1,0:T(8,128)S(1)}, f32[1,80,256]{2,1,0:T(8,128)S(1)}) custom-call(s32[2,4]{1,0:T(2,128)S(4)} %get-tuple-element.52.order, f32[4,64,256]{2,1,0:T(8,128)S(1)} %get-tuple-element.54.near, bf16[4,64,512]{2,1,0:T(8,128)(2,1)S(1)} %get-tuple-element.55.tail, ...), custom_call_target="tpu_custom_call" | custom-call | tf_op jit(solution)/shard_map/begin_early/pallas_call | solution.py:21
  6.4 0.1 collective-permute-start
  6.5 1.0 %early_maps.1 = (bf16[4,512,384]{2,1,0:T(8,128)(2,1)S(1)}, bf16[4,64,384]{2,1,0:T(8,128)(2,1)S(1)}, bf16[1,320,256]{2,1,0:T(8,128)(2,1)S(1)}, bf16[1,320,256]{2,1,0:T(8,128)(2,1)S(1)}) custom-call(s32[2,4]{1,0:T(2,128)S(4)} %get-tuple-element.52.order, bf16[2,1,4,512,512]{4,3,2,1,0:T(8,128)(2,1)S(1)} %copy-done, bf16[2,1,4,64,512]{4,3,2,1,0:T(8,128)(2,1)S(1)} %copy-done.2, ...), custom_call_target="tpu_custom_call" | custom-call | tf_op jit(solution)/shard_map/early_maps/pallas_call | solution.py:21
  7.6 0.2 collective-permute-done.other.refs_0_.refs_1_.refs_7_
  7.8 0.3 combine.3._
  8.1 1.5 %collective-permute-start.1 = (f32[1,80,256]{2,1,0:T(8,128)S(1)}, f32[1,80,256]{2,1,0:T(8,128)S(1)}, u32[]{:S(2)}, u32[]{:S(2)}) collective-permute-start(f32[1,80,256]{2,1,0:T(8,128)S(1)} %combine.3._), channel_id=1, source_target_pairs={{0,16},{8,24},{16,0},{24,8},{1,17},{9,25},{17,1},{25,9},{2,18},{10... | collective-permute-start | bytes 245768 | tf_op jit(solution)/shard_map/ppermute | solution.py:121
  9.6 1.2 %whole_free.2.refs_2_.free = f32[4,512,256]{2,1,0:T(8,128)S(1)} custom-call(bf16[2,1,4,512,512]{4,3,2,1,0:T(8,128)(2,1)S(1)} %copy-done, bf16[4,512,256]{2,1,0:T(8,128)(2,1)S(1)} %get-tuple-element.57.source_high, bf16[4,512,256]{2,1,0:T(8,128)(2,1)S(1)} %get-tuple-element.58.source_low, f32[1,80,256]{2,1,0:T(8,128)S(1)} %combine.3._), custom_call_target="tpu_custom_call" | custom-call | tf_op jit(solution)/shard_map/whole_free/pallas_call | solution.py:21
  10.9 1.6 %begin_late.1 = (bf16[4,512,256]{2,1,0:T(8,128)(2,1)S(1)}, bf16[4,512,256]{2,1,0:T(8,128)(2,1)S(1)}, f32[4,64,256]{2,1,0:T(8,128)S(1)}, f32[4,64,128]{2,1,0:T(8,...) custom-call(s32[2,4]{1,0:T(2,128)S(4)} %get-tuple-element.52.order, ...), custom_call_target="tpu_custom_call" | custom-call | tf_op jit(solution)/shard_map/begin_late/pallas_call | solution.py:21
  12.5 0.3 collective-permute-done.1.refs_1_.refs_8_
  12.7 1.1 %enter.2 = (bf16[4,384,256]{2,1,0:T(8,128)(2,1)S(1)}, f32[4,64,256]{2,1,0:T(8,128)S(1)}) custom-call(s32[2,4]{1,0:T(2,128)S(4)} %get-tuple-element.52.order, f32[2,64,256]{2,1,0:T(8,128)S(1)} %get-tuple-element.53.inlet, bf16[1,320,256]{2,1,0:T(8,128)(2,1)S(1)} %get-tuple-element.61.rows_high.refs_3_.refs_5_.refs_2_, ...), custom_call_target="tpu_custom_call" | custom-call | tf_op jit(solution)/shard_map/enter/pallas_call | solution.py:21
  13.8 1.8 %collective-permute-start.2 = (f32[4,64,256]{2,1,0:T(8,128)S(1)}, f32[4,64,256]{2,1,0:T(8,128)S(1)}, u32[]{:S(2)}, u32[]{:S(2)}) collective-permute-start(f32[4,64,256]{2,1,0:T(8,128)S(1)} %get-tuple-element.70), channel_id=1, source_target_pairs={{0,1},{1,2},{2,3},{3,4},{4,5},{5,6},{6,7},{7,0},{8,9},{9,10},{10,1... | collective-permute-start | bytes 786440 | tf_op jit(solution)/shard_map/ppermute | solution.py:118
  15.6 0.5 %first_sides.1 = (bf16[4,2,64,256]{3,2,1,0:T(8,128)(2,1)S(1)}, f32[4,64,256]{2,1,0:T(8,128)S(1)}, f32[1,80,256]{2,1,0:T(8,128)S(1)}) custom-call(s32[2,4]{1,0:T(2,128)S(4)} %get-tuple-element.52.order, f32[4,64,256]{2,1,0:T(8,128)S(1)} %collective-permute-done.3.arrived, f32[4,64,256]{2,1,0:T(8,128)S(1)} %get-tuple-element.73.own, ...), custom_call_target="tpu_custom_call" | custom-call | tf_op jit(solution)/shard_map/first_sides/pallas_call | solution.py:21
  16.1 0.1 collective-permute-start.4
  16.1 0.8 %late_maps.1._.maps.refs_9_.refs_13_ = bf16[4,512,384]{2,1,0:T(8,128)(2,1)S(1)} custom-call(bf16[2,1,4,512,512]{4,3,2,1,0:T(8,128)(2,1)S(1)} %copy-done, bf16[2,1,4,64,512]{4,3,2,1,0:T(8,128)(2,1)S(1)} %copy-done.2, bf16[2,1,4,64,512]{4,3,2,1,0:T(8,128)(2,1)S(1)} %copy-done.3, f32[1,80,256]{2,1,0:T(8,128)S(1)} %get-tuple-element.77._.own.refs_2_), custom_call_target="tpu_custom_call" | custom-call | tf_op jit(solution)/shard_map/late_maps/pallas_call | solution.py:21
  16.9 0.5 %collective-permute-done.4.other.refs_0_.refs_3_.refs_14_ = f32[1,80,256]{2,1,0:T(8,128)S(1)} collective-permute-done((f32[1,80,256]{2,1,0:T(8,128)S(1)}, f32[1,80,256]{2,1,0:T(8,128)S(1)}, u32[]{:S(2)}, u32[]{:S(2)}) %collective-permute-start.4) | collective-permute-done | bytes 81952 | tf_op jit(solution)/shard_map/ppermute | solution.py:121
  17.4 0.3 combine.4._
  17.7 1.5 %collective-permute-start.5 = (f32[1,80,256]{2,1,0:T(8,128)S(1)}, f32[1,80,256]{2,1,0:T(8,128)S(1)}, u32[]{:S(2)}, u32[]{:S(2)}) collective-permute-start(f32[1,80,256]{2,1,0:T(8,128)S(1)} %combine.4._), channel_id=1, source_target_pairs={{0,16},{8,24},{16,0},{24,8},{1,17},{9,25},{17,1},{25,9},{2,18},{10... | collective-permute-start | bytes 245768 | tf_op jit(solution)/shard_map/ppermute | solution.py:121
  19.2 1.7 %second.2 = (bf16[4,512,256]{2,1,0:T(8,128)(2,1)S(1)}, bf16[4,512,256]{2,1,0:T(8,128)(2,1)S(1)}, f32[4,64,256]{2,1,0:T(8,128)S(1)}, f32[4,64,256]{2,1,0:T(8,128)S(1)}) custom-call(bf16[2,1,4,512,512]{4,3,2,1,0:T(8,128)(2,1)S(1)} %copy-done, bf16[4,512,384]{2,1,0:T(8,128)(2,1)S(1)} %get-tuple-element.65._.maps.refs_2_.refs_6_, ...), custom_call_target="tpu_custom_call" | custom-call | tf_op jit(solution)/shard_map/second/pallas_call | solution.py:21
  20.9 1.2 %whole_free.3.free = f32[4,512,256]{2,1,0:T(8,128)S(1)} custom-call(bf16[2,1,4,512,512]{4,3,2,1,0:T(8,128)(2,1)S(1)} %copy-done, bf16[4,512,256]{2,1,0:T(8,128)(2,1)S(1)} %get-tuple-element.80.source_high, bf16[4,512,256]{2,1,0:T(8,128)(2,1)S(1)} %get-tuple-element.81.source_low, f32[1,80,256]{2,1,0:T(8,128)S(1)} %combine.4._), custom_call_target="tpu_custom_call" | custom-call | tf_op jit(solution)/shard_map/whole_free/pallas_call | solution.py:21
  22.2 0.7 %enter.3.stack = bf16[4,384,256]{2,1,0:T(8,128)(2,1)S(1)} custom-call(s32[2,4]{1,0:T(2,128)S(4)} %get-tuple-element.52.order, f32[2,64,256]{2,1,0:T(8,128)S(1)} %get-tuple-element.53.inlet, bf16[1,320,256]{2,1,0:T(8,128)(2,1)S(1)} %get-tuple-element.75.rows_high.refs_8_.refs_12_.refs_9_, ...), custom_call_target="tpu_custom_call" | custom-call | tf_op jit(solution)/shard_map/enter/pallas_call | solution.py:21
  22.9 1.6 %second.3 = (bf16[4,512,256]{2,1,0:T(8,128)(2,1)S(1)}, bf16[4,512,256]{2,1,0:T(8,128)(2,1)S(1)}, f32[4,64,256]{2,1,0:T(8,128)S(1)}, f32[4,64,256]{2,1,0:T(8,128)S(1)}) custom-call(bf16[2,1,4,512,512]{4,3,2,1,0:T(8,128)(2,1)S(1)} %copy-done, bf16[4,512,384]{2,1,0:T(8,128)(2,1)S(1)} %late_maps.1._.maps.refs_9_.refs_13_, f32[4,512,256]{2,1,0:T(8,128)S(1)} %whole_free.3.free, ...), custom_call_target="tpu_custom_call" | custom-call | tf_op jit(solution)/shard_map/second/pallas_call | solution.py:21
  24.5 0.2 collective-permute-done.2.arrived
  24.7 0.8 %second_sides.1 = (f32[2,64,256]{2,1,0:T(8,128)S(1)}, bf16[4,256,256]{2,1,0:T(8,128)(2,1)S(1)}, f32[4,64,256]{2,1,0:T(8,128)S(1)}, bf16[4,256,256]{2,1,0:T(8,128)(2,1)S(1)}, f32[4,64,256]{2,1,0:T(8,128)S(1)}) custom-call(s32[2,4]{1,0:T(2,128)S(4)} %get-tuple-element.52.order, f32[4,64,256]{2,1,0:T(8,128)S(1)} %collective-permute-done.2.arrived, ...), custom_call_target="tpu_custom_call" | custom-call | tf_op jit(solution)/shard_map/second_sides/pallas_call | solution.py:21
  25.5 0.1 collective-permute-start.6
  25.6 1.3 %collective-permute-done.6.other.refs_0_ = f32[2,64,256]{2,1,0:T(8,128)S(1)} collective-permute-done((f32[2,64,256]{2,1,0:T(8,128)S(1)}, f32[2,64,256]{2,1,0:T(8,128)S(1)}, u32[]{:S(2)}, u32[]{:S(2)}) %collective-permute-start.6) | collective-permute-done | bytes 131104 | tf_op jit(solution)/shard_map/ppermute | solution.py:121
  26.9 0.3 combine.5._
  27.2 1.4 %collective-permute-start.7 = (f32[2,64,256]{2,1,0:T(8,128)S(1)}, f32[2,64,256]{2,1,0:T(8,128)S(1)}, u32[]{:S(2)}, u32[]{:S(2)}) collective-permute-start(f32[2,64,256]{2,1,0:T(8,128)S(1)} %combine.5._), channel_id=1, source_target_pairs={{0,16},{8,24},{16,0},{24,8},{1,17},{9,25},{17,1},{25,9},{2,18},{10... | collective-permute-start | bytes 393224 | tf_op jit(solution)/shard_map/ppermute | solution.py:121
  28.6 3.1 %settle.1 = (f32[4,512,256]{2,1,0:T(8,128)S(1)}, f32[1,256,256]{2,1,0:T(8,128)S(1)}, f32[4,512,256]{2,1,0:T(8,128)S(1)}, f32[1,256,256]{2,1,0:T(8,128)S(1)}) custom-call(f32[2,64,256]{2,1,0:T(8,128)S(1)} %combine.5._, bf16[2,1,4,512,512]{4,3,2,1,0:T(8,128)(2,1)S(1)} %copy-done, bf16[4,512,256]{2,1,0:T(8,128)(2,1)S(1)} %get-tuple-element.87.refs_0_, ...), custom_call_target="tpu_custom_call" | custom-call | tf_op jit(solution)/shard_map/settle/pallas_call | solution.py:21
  31.7 1.1 %collective-permute-done.7.refs_1_ = f32[2,64,256]{2,1,0:T(8,128)S(1)} collective-permute-done((f32[2,64,256]{2,1,0:T(8,128)S(1)}, f32[2,64,256]{2,1,0:T(8,128)S(1)}, u32[]{:S(2)}, u32[]{:S(2)}) %collective-permute-start.7) | collective-permute-done | bytes 131104 | tf_op jit(solution)/shard_map/ppermute | solution.py:121
  32.8 2.4 %result.1 = bf16[2,1,4,512,256]{4,3,2,1,0:T(8,128)(2,1)} custom-call(s32[2,4]{1,0:T(2,128)S(4)} %get-tuple-element.52.order, f32[2,64,256]{2,1,0:T(8,128)S(1)} %get-tuple-element.53.inlet, f32[2,64,256]{2,1,0:T(8,128)S(1)} %collective-permute-done.6.other.refs_0_, f32[2,64,256]{2,1,0:T(8,128)S(1)} %collective-permute-done.7.refs_1_, ...), custom_call_target="tpu_custom_call" | custom-call | tf_op jit(solution)/shard_map/result/pallas_call | solution.py:21
  (10 shorter events, 0.1 us)
Async XLA Ops:
  0.0 6.5 %copy-start = (bf16[2,1,4,512,512]{4,3,2,1,0:T(8,128)(2,1)S(1)}, bf16[2,1,4,512,512]{4,3,2,1,0:T(8,128)(2,1)}, u32[]{:S(2)}) copy-start(bf16[2,1,4,512,512]{4,3,2,1,0:T(8,128)(2,1)} %inv.15) | copy-start | bytes 12582916
  2.0 4.5 %copy-start.2 = (bf16[2,1,4,64,512]{4,3,2,1,0:T(8,128)(2,1)S(1)}, bf16[2,1,4,64,512]{4,3,2,1,0:T(8,128)(2,1)}, u32[]{:S(2)}) copy-start(bf16[2,1,4,64,512]{4,3,2,1,0:T(8,128)(2,1)} %up.5) | copy-start | bytes 1572868
  2.0 4.5 %copy-start.3 = (bf16[2,1,4,64,512]{4,3,2,1,0:T(8,128)(2,1)S(1)}, bf16[2,1,4,64,512]{4,3,2,1,0:T(8,128)(2,1)}, u32[]{:S(2)}) copy-start(bf16[2,1,4,64,512]{4,3,2,1,0:T(8,128)(2,1)} %side.5) | copy-start | bytes 1572868
  2.1 13.5 %collective-permute-start.3 = (f32[4,64,256]{2,1,0:T(8,128)S(1)}, f32[4,64,256]{2,1,0:T(8,128)S(1)}, u32[]{:S(2)}, u32[]{:S(2)}) collective-permute-start(f32[4,64,256]{2,1,0:T(8,128)S(1)} %get-tuple-element.72), channel_id=1, source_target_pairs={{0,1},{1,2},{2,3},{3,4},{4,5},{5,6},{6,7},{7,0},{8,9},{9,10},{10,1... | collective-permute-start | bytes 786440 | tf_op jit(solution)/shard_map/ppermute | solution.py:118
  6.4 1.3 %collective-permute-start = (f32[1,80,256]{2,1,0:T(8,128)S(1)}, f32[1,80,256]{2,1,0:T(8,128)S(1)}, u32[]{:S(2)}, u32[]{:S(2)}) collective-permute-start(f32[1,80,256]{2,1,0:T(8,128)S(1)} %get-tuple-element.60._.own.refs_0_), channel_id=1, source_target_pairs={{0,8},{8,0},{16,24},{24,16},{1,9},{9,1},{17,25},{25,17},{2,10},{10... | collective-permute-start | bytes 245768 | tf_op jit(solution)/shard_map/ppermute | solution.py:121
  8.1 2.8 %copy-start.1 = (bf16[2,1,4,512,256]{4,3,2,1,0:T(8,128)(2,1)S(1)}, bf16[2,1,4,512,256]{4,3,2,1,0:T(8,128)(2,1)}, u32[]{:S(2)}) copy-start(bf16[2,1,4,512,256]{4,3,2,1,0:T(8,128)(2,1)} %previous.3) | copy-start | bytes 6291460
  8.1 4.7 %collective-permute-start.1 = (f32[1,80,256]{2,1,0:T(8,128)S(1)}, f32[1,80,256]{2,1,0:T(8,128)S(1)}, u32[]{:S(2)}, u32[]{:S(2)}) collective-permute-start(f32[1,80,256]{2,1,0:T(8,128)S(1)} %combine.3._), channel_id=1, source_target_pairs={{0,16},{8,24},{16,0},{24,8},{1,17},{9,25},{17,1},{25,9},{2,18},{10... | collective-permute-start | bytes 245768 | tf_op jit(solution)/shard_map/ppermute | solution.py:121
  13.8 10.9 %collective-permute-start.2 = (f32[4,64,256]{2,1,0:T(8,128)S(1)}, f32[4,64,256]{2,1,0:T(8,128)S(1)}, u32[]{:S(2)}, u32[]{:S(2)}) collective-permute-start(f32[4,64,256]{2,1,0:T(8,128)S(1)} %get-tuple-element.70), channel_id=1, source_target_pairs={{0,1},{1,2},{2,3},{3,4},{4,5},{5,6},{6,7},{7,0},{8,9},{9,10},{10,1... | collective-permute-start | bytes 786440 | tf_op jit(solution)/shard_map/ppermute | solution.py:118
  16.1 1.3 %collective-permute-start.4 = (f32[1,80,256]{2,1,0:T(8,128)S(1)}, f32[1,80,256]{2,1,0:T(8,128)S(1)}, u32[]{:S(2)}, u32[]{:S(2)}) collective-permute-start(f32[1,80,256]{2,1,0:T(8,128)S(1)} %get-tuple-element.77._.own.refs_2_), channel_id=1, source_target_pairs={{0,8},{8,0},{16,24},{24,16},{1,9},{9,1},{17,25},{25,17},{2,10},{10... | collective-permute-start | bytes 245768 | tf_op jit(solution)/shard_map/ppermute | solution.py:121
  17.7 4.5 %collective-permute-start.5 = (f32[1,80,256]{2,1,0:T(8,128)S(1)}, f32[1,80,256]{2,1,0:T(8,128)S(1)}, u32[]{:S(2)}, u32[]{:S(2)}) collective-permute-start(f32[1,80,256]{2,1,0:T(8,128)S(1)} %combine.4._), channel_id=1, source_target_pairs={{0,16},{8,24},{16,0},{24,8},{1,17},{9,25},{17,1},{25,9},{2,18},{10... | collective-permute-start | bytes 245768 | tf_op jit(solution)/shard_map/ppermute | solution.py:121
  25.5 1.4 %collective-permute-start.6 = (f32[2,64,256]{2,1,0:T(8,128)S(1)}, f32[2,64,256]{2,1,0:T(8,128)S(1)}, u32[]{:S(2)}, u32[]{:S(2)}) collective-permute-start(f32[2,64,256]{2,1,0:T(8,128)S(1)} %get-tuple-element.86.own), channel_id=1, source_target_pairs={{0,8},{8,0},{16,24},{24,16},{1,9},{9,1},{17,25},{25,17},{2,10},{10... | collective-permute-start | bytes 393224 | tf_op jit(solution)/shard_map/ppermute | solution.py:121
  27.2 5.6 %collective-permute-start.7 = (f32[2,64,256]{2,1,0:T(8,128)S(1)}, f32[2,64,256]{2,1,0:T(8,128)S(1)}, u32[]{:S(2)}, u32[]{:S(2)}) collective-permute-start(f32[2,64,256]{2,1,0:T(8,128)S(1)} %combine.5._), channel_id=1, source_target_pairs={{0,16},{8,24},{16,0},{24,8},{1,17},{9,25},{17,1},{25,9},{2,18},{10... | collective-permute-start | bytes 393224 | tf_op jit(solution)/shard_map/ppermute | solution.py:121

commit v8 on v7

--- a/solution.py
+++ b/solution.py
@@ -92,6 +92,10 @@
     lax.fori_loop(0, items // per, turn, 0)
 
 
+def known_inflow(inlet):
+    return jnp.where(lax.axis_index("stream") == 0, inlet, 0.0)
+
+
 def bit(stage):
     return ((lax.axis_index("stream") >> stage) & 1) == 1
 
@@ -104,6 +108,7 @@
     plane = per_side * per_side
     wide = count * face
     packed = face * face // tracers
+    sent_rows = face + (packed if lax.axis_size("stream") > 2 else 0)
     streams, lats = lax.axis_size("stream"), lax.axis_size("lat")
     stages = streams.bit_length() - 1
     assert streams == 1 << stages
@@ -135,11 +140,8 @@
             VMEM((size, wide + face, wide), BF16),
         ]
 
-    def side_outs(size):
-        return [VMEM((size * count, 2, face, tracers), BF16), VMEM((size * count, face, tracers), F32)]
-
     def offset_scratch(size):
-        return [VMEM((size, wide - face, tracers), BF16)] * 2
+        return [VMEM((size, wide, tracers), BF16)] * 2
 
     def source_outs(size):
         return [VMEM((size * count, nodes, tracers), BF16)] * 2
@@ -170,14 +172,13 @@
         rows_low[n, pl.ds(wide, face)] = r[1]
         row[n] = r[0].astype(F32) + r[1].astype(F32)
 
-    def offset(n, rows_high, rows_low, ends, high, low):
-        for p in range(count - 1):
-            e = split(ends[n * count + p])
+    def offset(n, start, rows_high, rows_low, ends, high, low):
+        for p in range(count):
+            e = split(start if p == 0 else ends[n * count + p - 1])
             high[n, pl.ds(p * face, face)] = e[0]
             low[n, pl.ds(p * face, face)] = e[1]
         last = pl.ds(wide, face)
-        row = (rows_high[n, last][:, face:], rows_low[n, last][:, face:])
-        return ends[n * count + count - 1] + dot_split(row, (high[n], low[n]))
+        return ends[n * count + count - 1] + dot_split((rows_high[n, last], rows_low[n, last]), (high[n], low[n]))
 
     def load():
         size = len(early)
@@ -278,7 +279,7 @@
         items = size * count
 
         def body(
-            order, near, tail, faces, source_high, source_low, tails, sides, ends, message, own
+            order, inlet, near, tail, faces, source_high, source_low, tails, ends, message, own
         ):
             def step(members):
                 for i in members:
@@ -290,11 +291,11 @@
                 links = []
                 for p in range(count):
                     i = n * count + order[c, p]
-                    s = split(near[i])
-                    sides[n * count + p, 0] = s[0]
-                    sides[n * count + p, 1] = s[1]
-                    end = own[i] + side_of(tails, i, s)
+                    end = own[i] + side_of(tails, i, split(near[i]))
                     ends[n * count + p] = end
+                    if p == 0:
+                        begun = split(known_inflow(inlet[c]))
+                        end = end + dot_split(split(tails[i][:, :face]), begun)
                     links.append((tails[i][:, :face], end))
                 while len(links) > 1:
                     paired = []
@@ -303,16 +304,17 @@
                         paired.append((dot_split(u, split(low)), end + dot_split(u, split(start))))
                     links = paired + links[2 * len(paired) :]
                 message[n, pl.ds(0, face)] = links[0][1]
-                message[n, pl.ds(face, packed)] = pack_map(links[0][0], tracers)
-
-        state.tails, state.sides, state.ends, state.message = run(
+                if sent_rows > face:
+                    message[n, pl.ds(face, packed)] = pack_map(links[0][0], tracers)
+
+        state.tails, state.ends, state.message = run(
             body,
             "begin_early",
-            [order, state.near, state.tail, state.faces, state.source_high, state.source_low],
+            [order, inlet, state.near, state.tail, state.faces, state.source_high, state.source_low],
             [
                 VMEM((items, face, 2 * face), F32),
-                *side_outs(size),
-                VMEM((size, face + packed, tracers), F32),
+                VMEM((items, face, tracers), F32),
+                VMEM((size, sent_rows, tracers), F32),
             ],
             [VMEM((items, face, tracers), F32)],
         )
@@ -338,21 +340,6 @@
             [VMEM((size, face, wide), F32)],
         )
         return state.maps
-
-    def whole_free(group, state, after):
-        size = len(group)
-
-        def body(inv, source_high, source_low, _, free):
-            for i in range(size * count):
-                free[i] = times(inv[at(group, i)], source_high, source_low, i)
-
-        (state.free,) = run(
-            body,
-            "whole_free",
-            [inv_near, state.source_high, state.source_low, after],
-            [VMEM((size * count, nodes, tracers), F32)],
-            [],
-        )
 
     def begin_late(after):
         size = len(late)
@@ -391,7 +378,7 @@
         state.source_high, state.source_low, state.own, state.tails, state.high, state.low, state.mapped = values
         return state
 
-    def late_maps(state, after):
+    def late_maps(after):
         items = len(late) * count
 
         def body(inv, up, side, _, maps):
@@ -399,34 +386,31 @@
                 k = at(late, i)
                 maps[i] = stack_maps(face_maps(inv[k], up[k], side[k]))
 
-        (state.maps,) = run(
-            body, "late_maps", [inv_near, up_near, side_near, after], map_outs(len(late))[:1], []
-        )
-        return state.maps
+        return run(body, "late_maps", [inv_near, up_near, side_near, after], map_outs(len(late))[:1], [])[0]
 
     def arrived_side(arrived, j):
         return split(jnp.where(lax.axis_index("lat") > 0, arrived[j], 0.0))
 
     def first_sides(state, arrived):
-        def body(order, arrived, own, tails, rows_high, rows_low, mapped, sides, ends, message, high, low):
+        def body(order, inlet, arrived, own, tails, rows_high, rows_low, mapped, ends, message, high, low):
             for p in range(count):
                 j = order[0, p]
-                s = arrived_side(arrived, j)
-                sides[p, 0] = s[0]
-                sides[p, 1] = s[1]
-                ends[p] = own[j] + side_of(tails, j, s)
-            message[0, pl.ds(0, face)] = offset(0, rows_high, rows_low, ends, high, low)
-            message[0, pl.ds(face, packed)] = mapped[0]
-
-        state.sides, state.ends, state.message = run(
+                ends[p] = own[j] + side_of(tails, j, arrived_side(arrived, j))
+            message[0, pl.ds(0, face)] = offset(0, known_inflow(inlet[0]), rows_high, rows_low, ends, high, low)
+            if sent_rows > face:
+                message[0, pl.ds(face, packed)] = mapped[0]
+
+        state.ends, state.message = run(
             body,
             "first_sides",
-            [order, arrived, state.own, state.tails, state.high, state.low, state.mapped],
-            side_outs(1) + [VMEM((1, face + packed, tracers), F32)],
+            [order, inlet, arrived, state.own, state.tails, state.high, state.low, state.mapped],
+            [VMEM((count, face, tracers), F32), VMEM((1, sent_rows, tracers), F32)],
             offset_scratch(1),
         )
 
     def combine_first(stage, own, other, after):
+        rows = face if stage + 2 == stages else sent_rows
+
         def body(own, other, _, message):
             upper = bit(stage)
             for n in range(own.shape[0]):
@@ -434,10 +418,11 @@
                 low = jnp.where(upper, other[n], own[n])
                 m = split(unpack_map(up[face:], face))
                 message[n, pl.ds(0, face)] = dot_split(m, split(low[:face])) + up[:face]
-                mapped = dot_split(m, split(unpack_map(low[face:], face)))
-                message[n, pl.ds(face, packed)] = pack_map(mapped, tracers)
-
-        return run(body, "combine", [own, other, after], [VMEM(own.shape, F32)], [])[0]
+                if rows > face:
+                    mapped = dot_split(m, split(unpack_map(low[face:], face)))
+                    message[n, pl.ds(face, packed)] = pack_map(mapped, tracers)
+
+        return run(body, "combine", [own, other, after], [VMEM((own.shape[0], rows, tracers), F32)], [])[0]
 
     def combine_second(stage, own, other, old_own, old_other):
         def body(own, other, *refs):
@@ -457,53 +442,96 @@
         return run(body, "combine", ins, [VMEM(own.shape, F32)], [])[0]
 
     def entering(start, offsets, maps):
-        for stage in reversed(range(stages)):
+        for stage in reversed(range(len(maps))):
             m = split(unpack_map(maps[stage], face))
             beyond = dot_split(m, split(start)) + offsets[stage]
             start = jnp.where(bit(stage), beyond, start)
         return start
 
+    def lower_maps(maps):
+        rows = lax.broadcasted_iota(jnp.int32, (face, face), 0)
+        total = jnp.where(rows == lax.broadcasted_iota(jnp.int32, (face, face), 1), 1.0, 0.0)
+        for stage in reversed(range(stages - 1)):
+            beyond = dot_split(split(unpack_map(maps[stage], face)), split(total))
+            total = jnp.where(bit(stage), beyond, total)
+        return total
+
+    def within_of(n, start, ends, rows_high, rows_low, high, low):
+        for p in range(count):
+            e = split(start if p == 0 else ends[n * count + p - 1])
+            high[n, pl.ds(p * face, face)] = e[0]
+            low[n, pl.ds(p * face, face)] = e[1]
+        span = pl.ds(0, wide)
+        return dot_split((rows_high[n, span], rows_low[n, span]), (high[n], low[n]))
+
+    def side_rows(s):
+        return jnp.concatenate([jnp.zeros((face, tracers), BF16), *stack_side(s)], axis=0)
+
+    def prepare(group, state, sides, after):
+        size = len(group)
+        lower = state.received[:-1]
+
+        def body(inv, sides, source_high, source_low, maps, ends, rows_high, rows_low, _, *refs):
+            mapped, (free, within, reach_high, reach_low, high, low) = refs[: len(lower)], refs[len(lower) :]
+            span = pl.ds(0, wide)
+            for n in range(size):
+                old = [r[n, pl.ds(face, packed)] for r in mapped]
+                start = entering(jnp.zeros((face, tracers), F32), [r[n, pl.ds(0, face)] for r in mapped], old)
+                within[n] = within_of(n, start, ends, rows_high, rows_low, high, low)
+                rows = (rows_high[n, span][:, :face], rows_low[n, span][:, :face])
+                reach_high[n], reach_low[n] = split(dot_split(rows, split(lower_maps(old))))
+            for i in range(size * count):
+                s = arrived_side(sides, i) if group[0] == 0 else split(sides[i])
+                whole = times(inv[at(group, i)], source_high, source_low, i)
+                free[i] = whole + dot(maps[i][:, 2 * face :], side_rows(s))
+
+        state.free, state.within, *state.reach = run(
+            body,
+            "prepare",
+            [inv_near, sides, state.source_high, state.source_low, state.maps, state.ends, state.high, state.low]
+            + [after, *lower],
+            [VMEM((size * count, nodes, tracers), F32), VMEM((size, wide, tracers), F32)]
+            + [VMEM((size, wide, face), BF16)] * 2,
+            [VMEM((size, wide, tracers), BF16)] * 2,
+        )
+
     def enter_first(group, state, after):
         size = len(group)
         last = group[-1] == cols - 1
-
-        def body(order, inlet, rows_high, rows_low, sides, ends, *refs):
-            got, refs = refs[:stages], refs[stages:]
+        newest = state.received[-1:]
+
+        def body(order, inlet, within, reach_high, reach_low, *refs):
+            got, refs = refs[: len(newest)], refs[len(newest) :]
             if last:
                 (free, side_maps), refs = refs[:2], refs[3:]
-            stack, (high, low) = refs[0], refs[-2:]
+            stack = refs[0]
             for n, c in enumerate(group):
-                for p in range(count - 1):
-                    e = split(ends[n * count + p])
-                    high[n, pl.ds((p + 1) * face, face)] = e[0]
-                    low[n, pl.ds((p + 1) * face, face)] = e[1]
-                maps = [r[n, pl.ds(face, packed)] for r in got]
-                e = split(entering(inlet[c], [r[n, pl.ds(0, face)] for r in got], maps))
-                high[n, pl.ds(0, face)] = e[0]
-                low[n, pl.ds(0, face)] = e[1]
-                span = pl.ds(0, wide)
-                inflow = dot_split((rows_high[n, span], rows_low[n, span]), (high[n], low[n]))
-                for p in range(count):
-                    i = n * count + order[c, p]
-                    f = split(inflow[p * face : (p + 1) * face])
-                    s = (sides[n * count + p, 0], sides[n * count + p, 1])
-                    for q, part in enumerate(stack_inflow(f) + stack_side(s)):
-                        stack[i, pl.ds(q * face, face)] = part
+                start = known_inflow(inlet[c])
+                for r in got:
+                    start = jnp.where(bit(stages - 1), r[n], start)
+                inflow = within[n] + dot_split((reach_high[n], reach_low[n]), split(start))
+                put_inflow(n, c, inflow, order, stack)
             if last:
                 for j in range(count):
                     i = (size - 1) * count + j
-                    refs[1][j] = lateral_rows(free.at[i], per_side) + dot(side_maps[i], stack[i])
-
-        outs = [VMEM((size * count, 6 * face, tracers), BF16)]
+                    part = dot(side_maps[i][:, : 3 * face], stack[i])
+                    refs[1][j] = lateral_rows(free.at[i], per_side) + part
+
+        outs = [VMEM((size * count, 3 * face, tracers), BF16)]
         if last:
             outs.append(VMEM((count, face, tracers), F32))
-        ins = [order, inlet, state.high, state.low, state.sides, state.ends, *state.received]
+        ins = [order, inlet, state.within, *state.reach, *newest]
         if last:
             ins += [state.free, state.side_maps, after]
-        scratch = [VMEM((size, wide, tracers), BF16)] * 2
-        values = run(body, "enter", ins, outs, scratch)
+        values = run(body, "enter", ins, outs, [])
         state.stack = values[0]
         return values[1] if last else None
+
+    def put_inflow(n, c, inflow, order, stack):
+        for p in range(count):
+            i = n * count + order[c, p]
+            for q, part in enumerate(stack_inflow(split(inflow[p * face : (p + 1) * face]))):
+                stack[i, pl.ds(q * face, face)] = part
 
     def second(group, state, after):
         items = len(group) * count
@@ -511,7 +539,7 @@
         def body(inv, maps, free, stack, rate, aff, _, source_high, source_low, traces, own):
             for i in range(items + 1):
                 if i < items:
-                    swept = free[i] + dot(maps[i], stack[i])
+                    swept = free[i] + dot(maps[i][:, : 3 * face], stack[i])
                     traces[i] = lateral_rows(swept, per_side)
                     source_high[i], source_low[i] = split(langmuir(swept, rate[...], aff[...]))
                 if i > 0:
@@ -524,109 +552,133 @@
             source_outs(len(group)) + [VMEM((items, face, tracers), F32)] * 2,
             [],
         )
+        return state.own
+
+    def fold_sides(after):
+        def body(order, inlet, _, *refs):
+            got = [refs[3 * g : 3 * g + 3] for g in range(len(groups))]
+            outs = refs[3 * len(groups) :]
+            for g, group in enumerate(groups):
+                tails, rows_high, rows_low = got[g]
+                high, low, begun = outs[3 * g : 3 * g + 3]
+                for n, c in enumerate(group):
+                    start = split(known_inflow(inlet[c]))
+                    begun[n] = dot_split(last_row(rows_high, rows_low, n, 0), start)
+                    for p in range(count):
+                        folded = split(tails[n * count + order[c, p]][:, face:])
+                        if p + 1 < count:
+                            folded = split(dot_split(last_row(rows_high, rows_low, n, p + 1), folded))
+                        high[n, p] = folded[0]
+                        low[n, p] = folded[1]
+
+        ins, outs = [order, inlet, after], []
+        for group, state in zip(groups, states):
+            ins += [state.tails, state.high, state.low]
+            outs += [VMEM((len(group), count, face, face), BF16)] * 2
+            outs.append(VMEM((len(group), face, tracers), F32))
+        values = run(body, "fold_sides", ins, outs, [])
+        for g, state in enumerate(states):
+            state.side_high, state.side_low, state.begun = values[3 * g : 3 * g + 3]
+        return values[0]
+
+    def last_row(rows_high, rows_low, n, block):
+        place = pl.ds(wide, face)
+        return tuple(r[n, place][:, block * face : (block + 1) * face] for r in (rows_high, rows_low))
+
+    def side_at(c, j, arrived, traces):
+        if c == 0:
+            return arrived_side(arrived, j)
+        h, m = home[c - 1]
+        return split(traces[h][m * count + j])
 
     def second_sides(arrived):
         def body(order, arrived, *refs):
-            got = [refs[5 * g : 5 * g + 5] for g in range(len(groups))]
-            message, *refs = refs[5 * len(groups) :]
+            got = [refs[7 * g : 7 * g + 7] for g in range(len(groups))]
+            message = refs[-1]
             for g, group in enumerate(groups):
-                own, _, tails, rows_high, rows_low = got[g]
-                stack, ends = refs[2 * g : 2 * g + 2]
-                high, low = refs[2 * (len(groups) + g) : 2 * (len(groups) + g) + 2]
+                own, _, rows_high, rows_low, side_high, side_low, begun = got[g]
+                for n, c in enumerate(group):
+                    total = own[n * count + order[c, count - 1]] + begun[n]
+                    for p in range(count):
+                        s = side_at(c, order[c, p], arrived, [x[1] for x in got])
+                        total = total + dot_split((side_high[n, p], side_low[n, p]), s)
+                        if p + 1 < count:
+                            row = last_row(rows_high, rows_low, n, p + 1)
+                            total = total + dot_split(row, split(own[n * count + order[c, p]]))
+                    message[c] = total
+
+        ins = [order, arrived]
+        for state in states:
+            ins += [state.own, state.traces, state.high, state.low]
+            ins += [state.side_high, state.side_low, state.begun]
+        return run(body, "second_sides", ins, [VMEM((cols, face, tracers), F32)], [])[0]
+
+    def settle(after, arrived, offsets):
+        per_group = 8 + len(offsets)
+
+        def body(order, inlet, _, arrived, inv, *refs):
+            offs, refs = refs[: len(offsets)], refs[len(offsets) :]
+            got = [refs[per_group * g : per_group * g + per_group] for g in range(len(groups))]
+            outs = refs[per_group * len(groups) :]
+            scratch = outs[2 * len(groups) :]
+            for g, group in enumerate(groups):
+                source_high, source_low, maps, rows_high, rows_low, own, traces, tails, *mapped = got[g]
+                base, within = outs[2 * g : 2 * g + 2]
+                ends, high, low = scratch[3 * g : 3 * g + 3]
                 for n, c in enumerate(group):
                     for p in range(count):
-                        j = order[c, p]
-                        i = n * count + j
-                        if c == 0:
-                            s = arrived_side(arrived, j)
-                        else:
-                            h, m = home[c - 1]
-                            s = split(got[h][1][m * count + j])
-                        stack[i, pl.ds(0, face)] = jnp.zeros((face, tracers), BF16)
-                        for q, part in enumerate(stack_side(s)):
-                            stack[i, pl.ds((q + 1) * face, face)] = part
+                        i = n * count + order[c, p]
+                        s = side_at(c, order[c, p], arrived, [x[6] for x in got])
                         ends[n * count + p] = own[i] + side_of(tails, i, s)
-                    message[c] = offset(n, rows_high, rows_low, ends, high, low)
-
-        ins = [order, arrived]
-        outs, scratch = [VMEM((cols, face, tracers), F32)], []
+                    old = [r[n, pl.ds(face, packed)] for r in mapped]
+                    start = entering(known_inflow(inlet[c]), [r[c] for r in offs], old)
+                    within[n] = within_of(n, start, ends, rows_high, rows_low, high, low)
+                for i in range(len(group) * count):
+                    whole = times(inv[at(group, i)], source_high, source_low, i)
+                    s = side_at(group[0] + i // count, i % count, arrived, [x[6] for x in got])
+                    base[i] = whole + dot(maps[i][:, 2 * face :], side_rows(s))
+
+        ins = [order, inlet, after, arrived, inv_near, *offsets]
+        outs, scratch = [], []
         for group, state in zip(groups, states):
-            ins += [state.own, state.traces, state.tails, state.high, state.low]
-            outs.append(VMEM((len(group) * count, 4 * face, tracers), BF16))
-            outs.append(VMEM((len(group) * count, face, tracers), F32))
-            scratch += offset_scratch(len(group))
-        message, *values = run(body, "second_sides", ins, outs, scratch)
-        for g, state in enumerate(states):
-            state.side_stack, state.ends = values[2 * g : 2 * g + 2]
-        return message
-
-    def settle(after):
-        def body(_, inv, *refs):
-            got = [refs[7 * g : 7 * g + 7] for g in range(len(groups))]
-            outs = refs[7 * len(groups) :]
-            for g, group in enumerate(groups):
-                source_high, source_low, maps, stack, ends, rows_high, rows_low = got[g]
-                base, within, high, low = outs[2 * g], outs[2 * g + 1], outs[-2], outs[-1]
-                for i in range(len(group) * count):
-                    own = times(inv[at(group, i)], source_high, source_low, i)
-                    base[i] = own + dot(maps[i][:, 2 * face :], stack[i])
-                for n in range(len(group)):
-                    for p in range(count - 1):
-                        e = split(ends[n * count + p])
-                        high[pl.ds(p * face, face)] = e[0]
-                        low[pl.ds(p * face, face)] = e[1]
-                    span = pl.ds(0, wide)
-                    rows = (rows_high[n, span][:, face:], rows_low[n, span][:, face:])
-                    within[n] = dot_split(rows, (high[...], low[...]))
-
-        ins = [after, inv_near]
-        outs = []
-        for group, state in zip(groups, states):
-            ins += [state.source_high, state.source_low]
-            ins += [state.maps, state.side_stack, state.ends, state.high, state.low]
+            ins += [state.source_high, state.source_low, state.maps, state.high, state.low]
+            ins += [state.own, state.traces, state.tails, *state.received[:-1]]
             outs.append(VMEM((len(group) * count, nodes, tracers), F32))
             outs.append(VMEM((len(group), wide, tracers), F32))
-        scratch = [VMEM((wide - face, tracers), BF16)] * 2
+            scratch.append(VMEM((len(group) * count, face, tracers), F32))
+            scratch += [VMEM((len(group), wide, tracers), BF16)] * 2
         values = run(body, "settle", ins, outs, scratch)
         for g, state in enumerate(states):
             state.base, state.within = values[2 * g : 2 * g + 2]
 
     def result(offsets):
-        parts = 5 + stages
-
-        def body(order, inlet, *refs):
-            offs, refs = refs[:stages], refs[stages:]
-            got = [refs[parts * g : parts * g + parts] for g in range(len(groups))]
-            out, staged, sems, *stacks = refs[parts * len(groups) :]
+        def body(order, *refs):
+            offs, refs = refs[: len(offsets)], refs[len(offsets) :]
+            got = [refs[5 * g : 5 * g + 5] for g in range(len(groups))]
+            out, staged, sems, *stacks = refs[5 * len(groups) :]
             for g, group in enumerate(groups):
-                rows_high, rows_low, within, _, _, *mapped = got[g]
+                within, reach_high, reach_low = got[g][:3]
                 for n, c in enumerate(group):
-                    maps = [r[n, pl.ds(face, packed)] for r in mapped]
-                    e = split(entering(inlet[c], [r[c] for r in offs], maps))
-                    span = pl.ds(0, wide)
-                    rows = (rows_high[n, span][:, :face], rows_low[n, span][:, :face])
-                    inflow = within[n] + dot_split(rows, e)
-                    for p in range(count):
-                        i = n * count + order[c, p]
-                        for q, part in enumerate(stack_inflow(split(inflow[p * face : (p + 1) * face]))):
-                            stacks[g][i, pl.ds(q * face, face)] = part
+                    inflow = within[n]
+                    for r in offs:
+                        late_part = split(jnp.where(bit(stages - 1), r[c], 0.0))
+                        inflow = inflow + dot_split((reach_high[n], reach_low[n]), late_part)
+                    put_inflow(n, c, inflow, order, stacks[g])
             started = []
             for g, group in enumerate(groups):
-                base, maps = got[g][3:5]
-                for n, c in enumerate(group):
-                    for j in range(count):
-                        i, k = n * count + j, len(started)
-                        staged[k] = (base[i] + dot(maps[i][:, : 3 * face], stacks[g][i])).astype(BF16)
-                        copy = pltpu.make_async_copy(staged.at[k], out.at[c, 0, j], sems.at[k])
-                        copy.start()
-                        started.append(copy)
+                base, maps = got[g][3:]
+                for i in range(len(group) * count):
+                    k = len(started)
+                    staged[k] = (base[i] + dot(maps[i][:, : 3 * face], stacks[g][i])).astype(BF16)
+                    started.append(pltpu.make_async_copy(staged.at[k], out.at[at(group, i)], sems.at[k]))
+                    started[-1].start()
             for copy in started:
                 copy.wait()
 
-        ins = [order, inlet, *offsets]
+        ins = [order, *offsets]
         scratch = [VMEM((cols * count, nodes, tracers), BF16), pltpu.SemaphoreType.DMA((cols * count,))]
         for group, state in zip(groups, states):
-            ins += [state.high, state.low, state.within, state.base, state.maps, *state.received]
+            ins += [state.within, *state.reach, state.base, state.maps]
             scratch.append(VMEM((len(group) * count, 3 * face, tracers), BF16))
         return run(body, "result", ins, [HBM(previous.shape, BF16)], scratch)[0]
 
@@ -644,26 +696,27 @@
     arrived = to_next(trace)
     begin_early(one)
     exchange_first(one, lambda: early_maps(one, one.message))
-    two = begin_late(one.sent[-1])
-    whole_free(early, one, one.sent[-1])
+    prepare(early, one, one.near, one.sent[-1])
+    maps = late_maps(one.sent[-1])
+    trace = enter_first(early, one, maps)
+    arrived_next = to_next(trace)
+    two = begin_late(trace)
+    two.maps = maps
     states = [one, two]
-    trace = enter_first(early, one, two.mapped)
-    arrived_next = to_next(trace)
     first_sides(two, arrived)
-    exchange_first(two, lambda: late_maps(two, two.message))
-    second(early, one, two.sent[-1])
-    whole_free(late, two, two.sent[-1])
+    exchange_first(two, lambda: second(early, one, two.message))
+    prepare(late, two, arrived, two.sent[-1])
+    fold_sides(two.sent[-1])
     enter_first(late, two, None)
     second(late, two, two.sent[-1])
     message, offsets = second_sides(arrived_next), []
     for stage in range(stages):
         offsets.append(swap(message, stage))
         if stage + 1 < stages:
-            message = combine_second(
-                stage, message, offsets[-1], [s.sent[stage] for s in states], [s.received[stage] for s in states]
-            )
-    settle(message)
-    return result(offsets)
+            sent, received = [s.sent[stage] for s in states], [s.received[stage] for s in states]
+            message = combine_second(stage, message, offsets[-1], sent, received)
+    settle(message, arrived_next, offsets[:-1])
+    return result(offsets[-1:])
 
 
 def solution(mesh):

time: 35.5 us -> 34.4 us (0.969)
  waiting for transfers between devices: 3.6 us -> 2.46 us
    ppermute x6, waiting for transfers between devices: 3.41 us -> 2.45 us  [swap(): lax.ppermute(value, 'stream', [(i, i ^ 1 << stage) for i in range(streams)])]
    pallas_call x18 -> x19, Pallas kernels: 21.9 us -> 21.7 us  [run(): pl.pallas_call(body, name=name, in_specs=[pl.BlockSpec(memory_space=space...]
  transfers between devices with their start and end apart: 8 -> 8, of which waited for: 6 -> 6; matrix products, arithmetic and copies ran while one was open for 0% -> 0% of each run, Pallas kernels for 46% -> 49%
where the time goes in v8:
time: 34.4 us; the launch traced here: 34.3 us
  Pallas kernels  21.7 us (63%)
  starting transfers between devices  9.74 us (28%)
  waiting for transfers between devices  2.46 us (7%)
  between operations  0.35 us (1%)
    pallas_call x19, Pallas kernels, run(): pl.pallas_call(body, name=name, in_specs=[pl.BlockSpec(memory_space=space...  21.7 us
    ppermute x6, starting transfers between devices, swap(): lax.ppermute(value, 'stream', [(i, i ^ 1 << stage) for i in range(streams)])  4.97 us
    ppermute x2, starting transfers between devices, to_next(): lax.ppermute(value, 'lat', [(i, (i + 1) % lats) for i in range(lats)])  4.77 us
    ppermute x6, waiting for transfers between devices, swap(): lax.ppermute(value, 'stream', [(i, i ^ 1 << stage) for i in range(streams)])  2.45 us
  transfers between devices with their start and end apart: 8, of which 6 were waited for; matrix products, arithmetic and copies ran while one was open for 0% of the time, Pallas kernels for 49%

profile of v8, /device:TPU:0, one launch (start us, length us, event | category | flops | bytes accessed | tf_op | source)
XLA Modules:
  0.0 34.3 jit_solution(2397195703224220957)
XLA Ops:
  0.0 2.0 %load.1 = (f32[4,64,256]{2,1,0:T(8,128)S(1)}, s32[2,4]{1,0:T(2,128)S(4)}, f32[1,256]{1,0:T(1,128)S(1)}, f32[1,256]{1,0:T(1,128)S(1)}, f32[2,64,256]{2,1,0:T(8,12...) custom-call(s32[2,4]{1,0:T(2,128)} %bitcast.5, ...), custom_call_target="tpu_custom_call" | custom-call | tf_op jit(solution)/shard_map/load/pallas_call | solution.py:21
  2.1 3.0 %collective-permute-start.3 = (f32[4,64,256]{2,1,0:T(8,128)S(1)}, f32[4,64,256]{2,1,0:T(8,128)S(1)}, u32[]{:S(2)}, u32[]{:S(2)}) collective-permute-start(f32[4,64,256]{2,1,0:T(8,128)S(1)} %get-tuple-element.81), channel_id=1, source_target_pairs={{0,1},{1,2},{2,3},{3,4},{4,5},{5,6},{6,7},{7,0},{8,9},{9,10},{10,1... | collective-permute-start | bytes 786440 | tf_op jit(solution)/shard_map/ppermute | solution.py:123
  5.0 1.4 %begin_early.1 = (f32[4,64,128]{2,1,0:T(8,128)S(1)}, f32[4,64,256]{2,1,0:T(8,128)S(1)}, f32[1,80,256]{2,1,0:T(8,128)S(1)}) custom-call(s32[2,4]{1,0:T(2,128)S(4)} %get-tuple-element.59.order, f32[2,64,256]{2,1,0:T(8,128)S(1)} %get-tuple-element.60.inlet, f32[4,64,256]{2,1,0:T(8,128)S(1)} %get-tuple-element.61.near.sides, ...), custom_call_target="tpu_custom_call" | custom-call | tf_op jit(solution)/shard_map/begin_early/pallas_call | solution.py:21
  6.4 0.1 collective-permute-start
  6.5 1.0 %early_maps.1 = (bf16[4,512,384]{2,1,0:T(8,128)(2,1)S(1)}, bf16[4,64,384]{2,1,0:T(8,128)(2,1)S(1)}, bf16[1,320,256]{2,1,0:T(8,128)(2,1)S(1)}, bf16[1,320,256]{2,1,0:T(8,128)(2,1)S(1)}) custom-call(s32[2,4]{1,0:T(2,128)S(4)} %get-tuple-element.59.order, bf16[2,1,4,512,512]{4,3,2,1,0:T(8,128)(2,1)S(1)} %copy-done, bf16[2,1,4,64,512]{4,3,2,1,0:T(8,128)(2,1)S(1)} %copy-done.2, ...), custom_call_target="tpu_custom_call" | custom-call | tf_op jit(solution)/shard_map/early_maps/pallas_call | solution.py:21
  7.6 0.2 collective-permute-done.other.refs_0_.refs_1_.refs_9_
  7.8 0.2 combine.3._
  8.0 1.6 %collective-permute-start.1 = (f32[1,64,256]{2,1,0:T(8,128)S(1)}, f32[1,64,256]{2,1,0:T(8,128)S(1)}, u32[]{:S(2)}, u32[]{:S(2)}) collective-permute-start(f32[1,64,256]{2,1,0:T(8,128)S(1)} %combine.3._), channel_id=1, source_target_pairs={{0,16},{8,24},{16,0},{24,8},{1,17},{9,25},{17,1},{25,9},{2,18},{10... | collective-permute-start | bytes 196616 | tf_op jit(solution)/shard_map/ppermute | solution.py:126
  9.6 0.8 %late_maps.1.refs_3_.maps.refs_12_.refs_10_ = bf16[4,512,384]{2,1,0:T(8,128)(2,1)S(1)} custom-call(bf16[2,1,4,512,512]{4,3,2,1,0:T(8,128)(2,1)S(1)} %copy-done, bf16[2,1,4,64,512]{4,3,2,1,0:T(8,128)(2,1)S(1)} %copy-done.2, bf16[2,1,4,64,512]{4,3,2,1,0:T(8,128)(2,1)S(1)} %copy-done.3, f32[1,64,256]{2,1,0:T(8,128)S(1)} %combine.3._), custom_call_target="tpu_custom_call" | custom-call | tf_op jit(solution)/shard_map/late_maps/pallas_call | solution.py:21
  10.4 1.9 %prepare.2 = (f32[4,512,256]{2,1,0:T(8,128)S(1)}, f32[1,256,256]{2,1,0:T(8,128)S(1)}, bf16[1,256,64]{2,1,0:T(8,128)(2,1)S(1)}, bf16[1,256,64]{2,1,0:T(8,128)(2,1)S(1)}) custom-call(bf16[2,1,4,512,512]{4,3,2,1,0:T(8,128)(2,1)S(1)} %copy-done, f32[4,64,256]{2,1,0:T(8,128)S(1)} %get-tuple-element.61.near.sides, ...), custom_call_target="tpu_custom_call" | custom-call | tf_op jit(solution)/shard_map/prepare/pallas_call | solution.py:21
  12.3 0.1 collective-permute-done.1.refs_0_
  12.4 0.5 %enter.2 = (bf16[4,192,256]{2,1,0:T(8,128)(2,1)S(1)}, f32[4,64,256]{2,1,0:T(8,128)S(1)}) custom-call(s32[2,4]{1,0:T(2,128)S(4)} %get-tuple-element.59.order, f32[2,64,256]{2,1,0:T(8,128)S(1)} %get-tuple-element.60.inlet, f32[1,256,256]{2,1,0:T(8,128)S(1)} %get-tuple-element.72.within, bf16[1,256,64]{2,1,0:T(8,128)(2,1)S(1)} %get-tuple-element.73.reach_high.refs_2_, ...), custom_call_target="tpu_custom_call" | custom-call | tf_op jit(solution)/shard_map/enter/pallas_call | solution.py:21
  12.9 1.8 %collective-permute-start.2 = (f32[4,64,256]{2,1,0:T(8,128)S(1)}, f32[4,64,256]{2,1,0:T(8,128)S(1)}, u32[]{:S(2)}, u32[]{:S(2)}) collective-permute-start(f32[4,64,256]{2,1,0:T(8,128)S(1)} %get-tuple-element.77._), channel_id=1, source_target_pairs={{0,1},{1,2},{2,3},{3,4},{4,5},{5,6},{6,7},{7,0},{8,9},{9,10},{10,1... | collective-permute-start | bytes 786440 | tf_op jit(solution)/shard_map/ppermute | solution.py:123
  14.7 1.6 %begin_late.1 = (bf16[4,512,256]{2,1,0:T(8,128)(2,1)S(1)}, bf16[4,512,256]{2,1,0:T(8,128)(2,1)S(1)}, f32[4,64,256]{2,1,0:T(8,128)S(1)}, f32[4,64,128]{2,1,0:T(8,...) custom-call(s32[2,4]{1,0:T(2,128)S(4)} %get-tuple-element.59.order, ...), custom_call_target="tpu_custom_call" | custom-call | tf_op jit(solution)/shard_map/begin_late/pallas_call | solution.py:21
  16.3 0.5 %first_sides.1 = (f32[4,64,256]{2,1,0:T(8,128)S(1)}, f32[1,80,256]{2,1,0:T(8,128)S(1)}) custom-call(s32[2,4]{1,0:T(2,128)S(4)} %get-tuple-element.59.order, f32[2,64,256]{2,1,0:T(8,128)S(1)} %get-tuple-element.60.inlet, f32[4,64,256]{2,1,0:T(8,128)S(1)} %collective-permute-done.3.arrived.sides, f32[4,64,256]{2,1,0:T(8,128)S(1)} %get-tuple-element.82.own, ...), custom_call_target="tpu_custom_call" | custom-call | tf_op jit(solution)/shard_map/first_sides/pallas_call | solution.py:21
  16.8 0.1 collective-permute-start.4
  16.8 1.2 %second.2 = (bf16[4,512,256]{2,1,0:T(8,128)(2,1)S(1)}, bf16[4,512,256]{2,1,0:T(8,128)(2,1)S(1)}, f32[4,64,256]{2,1,0:T(8,128)S(1)}, f32[4,64,256]{2,1,0:T(8,128)S(1)}) custom-call(bf16[2,1,4,512,512]{4,3,2,1,0:T(8,128)(2,1)S(1)} %copy-done, bf16[4,512,384]{2,1,0:T(8,128)(2,1)S(1)} %get-tuple-element.68._.maps.refs_3_.refs_5_, ...), custom_call_target="tpu_custom_call" | custom-call | tf_op jit(solution)/shard_map/second/pallas_call | solution.py:21
  18.1 0.2 combine.4._
  18.3 1.6 %collective-permute-start.5 = (f32[1,64,256]{2,1,0:T(8,128)S(1)}, f32[1,64,256]{2,1,0:T(8,128)S(1)}, u32[]{:S(2)}, u32[]{:S(2)}) collective-permute-start(f32[1,64,256]{2,1,0:T(8,128)S(1)} %combine.4._), channel_id=1, source_target_pairs={{0,16},{8,24},{16,0},{24,8},{1,17},{9,25},{17,1},{25,9},{2,18},{10... | collective-permute-start | bytes 196616 | tf_op jit(solution)/shard_map/ppermute | solution.py:126
  19.9 0.3 fold_sides.1
  20.2 1.9 %prepare.3 = (f32[4,512,256]{2,1,0:T(8,128)S(1)}, f32[1,256,256]{2,1,0:T(8,128)S(1)}, bf16[1,256,64]{2,1,0:T(8,128)(2,1)S(1)}, bf16[1,256,64]{2,1,0:T(8,128)(2,1)S(1)}) custom-call(bf16[2,1,4,512,512]{4,3,2,1,0:T(8,128)(2,1)S(1)} %copy-done, f32[4,64,256]{2,1,0:T(8,128)S(1)} %collective-permute-done.3.arrived.sides, ...), custom_call_target="tpu_custom_call" | custom-call | tf_op jit(solution)/shard_map/prepare/pallas_call | solution.py:21
  22.1 0.7 %collective-permute-done.5.refs_0_ = f32[1,64,256]{2,1,0:T(8,128)S(1)} collective-permute-done((f32[1,64,256]{2,1,0:T(8,128)S(1)}, f32[1,64,256]{2,1,0:T(8,128)S(1)}, u32[]{:S(2)}, u32[]{:S(2)}) %collective-permute-start.5) | collective-permute-done | bytes 65568 | tf_op jit(solution)/shard_map/ppermute | solution.py:126
  22.8 0.2 enter.3.stack
  23.1 1.2 %second.3 = (bf16[4,512,256]{2,1,0:T(8,128)(2,1)S(1)}, bf16[4,512,256]{2,1,0:T(8,128)(2,1)S(1)}, f32[4,64,256]{2,1,0:T(8,128)S(1)}, f32[4,64,256]{2,1,0:T(8,128)S(1)}) custom-call(bf16[2,1,4,512,512]{4,3,2,1,0:T(8,128)(2,1)S(1)} %copy-done, bf16[4,512,384]{2,1,0:T(8,128)(2,1)S(1)} %late_maps.1.refs_3_.maps.refs_12_.refs_10_, ...), custom_call_target="tpu_custom_call" | custom-call | tf_op jit(solution)/shard_map/second/pallas_call | solution.py:21
  24.3 0.5 %second_sides.1.own = f32[2,64,256]{2,1,0:T(8,128)S(1)} custom-call(s32[2,4]{1,0:T(2,128)S(4)} %get-tuple-element.59.order, f32[4,64,256]{2,1,0:T(8,128)S(1)} %collective-permute-done.2.arrived, f32[4,64,256]{2,1,0:T(8,128)S(1)} %get-tuple-element.88._.refs_0_.refs_6_, f32[4,64,256]{2,1,0:T(8,128)S(1)} %get-tuple-element.89.refs_1_.refs_7_, ...), custom_call_target="tpu_custom_call" | custom-call | tf_op jit(solution)/shard_map/second_sides/pallas_call | solution.py:21
  24.8 0.1 collective-permute-start.6
  24.9 1.3 %collective-permute-done.6.other.refs_0_ = f32[2,64,256]{2,1,0:T(8,128)S(1)} collective-permute-done((f32[2,64,256]{2,1,0:T(8,128)S(1)}, f32[2,64,256]{2,1,0:T(8,128)S(1)}, u32[]{:S(2)}, u32[]{:S(2)}) %collective-permute-start.6) | collective-permute-done | bytes 131104 | tf_op jit(solution)/shard_map/ppermute | solution.py:126
  26.2 0.3 combine.5._
  26.5 1.6 %collective-permute-start.7 = (f32[2,64,256]{2,1,0:T(8,128)S(1)}, f32[2,64,256]{2,1,0:T(8,128)S(1)}, u32[]{:S(2)}, u32[]{:S(2)}) collective-permute-start(f32[2,64,256]{2,1,0:T(8,128)S(1)} %combine.5._), channel_id=1, source_target_pairs={{0,16},{8,24},{16,0},{24,8},{1,17},{9,25},{17,1},{25,9},{2,18},{10... | collective-permute-start | bytes 393224 | tf_op jit(solution)/shard_map/ppermute | solution.py:126
  28.1 3.9 %settle.1 = (f32[4,512,256]{2,1,0:T(8,128)S(1)}, f32[1,256,256]{2,1,0:T(8,128)S(1)}, f32[4,512,256]{2,1,0:T(8,128)S(1)}, f32[1,256,256]{2,1,0:T(8,128)S(1)}) custom-call(s32[2,4]{1,0:T(2,128)S(4)} %get-tuple-element.59.order, f32[2,64,256]{2,1,0:T(8,128)S(1)} %get-tuple-element.60.inlet, f32[2,64,256]{2,1,0:T(8,128)S(1)} %combine.5._, ...), custom_call_target="tpu_custom_call" | custom-call | tf_op jit(solution)/shard_map/settle/pallas_call | solution.py:21
  32.0 0.1 collective-permute-done.7.refs_0_
  32.1 2.0 %result.1 = bf16[2,1,4,512,256]{4,3,2,1,0:T(8,128)(2,1)} custom-call(s32[2,4]{1,0:T(2,128)S(4)} %get-tuple-element.59.order, f32[2,64,256]{2,1,0:T(8,128)S(1)} %collective-permute-done.7.refs_0_, f32[1,256,256]{2,1,0:T(8,128)S(1)} %get-tuple-element.109.refs_1_, bf16[1,256,64]{2,1,0:T(8,128)(2,1)S(1)} %get-tuple-element.73.reach_high.refs_2_, ...), custom_call_target="tpu_custom_call" | custom-call | tf_op jit(solution)/shard_map/result/pallas_call | solution.py:21
  (11 shorter events, 0.1 us)
Async XLA Ops:
  0.0 6.5 %copy-start = (bf16[2,1,4,512,512]{4,3,2,1,0:T(8,128)(2,1)S(1)}, bf16[2,1,4,512,512]{4,3,2,1,0:T(8,128)(2,1)}, u32[]{:S(2)}) copy-start(bf16[2,1,4,512,512]{4,3,2,1,0:T(8,128)(2,1)} %inv.15) | copy-start | bytes 12582916
  2.0 4.5 %copy-start.2 = (bf16[2,1,4,64,512]{4,3,2,1,0:T(8,128)(2,1)S(1)}, bf16[2,1,4,64,512]{4,3,2,1,0:T(8,128)(2,1)}, u32[]{:S(2)}) copy-start(bf16[2,1,4,64,512]{4,3,2,1,0:T(8,128)(2,1)} %up.5) | copy-start | bytes 1572868
  2.0 4.5 %copy-start.3 = (bf16[2,1,4,64,512]{4,3,2,1,0:T(8,128)(2,1)S(1)}, bf16[2,1,4,64,512]{4,3,2,1,0:T(8,128)(2,1)}, u32[]{:S(2)}) copy-start(bf16[2,1,4,64,512]{4,3,2,1,0:T(8,128)(2,1)} %side.5) | copy-start | bytes 1572868
  2.1 14.2 %collective-permute-start.3 = (f32[4,64,256]{2,1,0:T(8,128)S(1)}, f32[4,64,256]{2,1,0:T(8,128)S(1)}, u32[]{:S(2)}, u32[]{:S(2)}) collective-permute-start(f32[4,64,256]{2,1,0:T(8,128)S(1)} %get-tuple-element.81), channel_id=1, source_target_pairs={{0,1},{1,2},{2,3},{3,4},{4,5},{5,6},{6,7},{7,0},{8,9},{9,10},{10,1... | collective-permute-start | bytes 786440 | tf_op jit(solution)/shard_map/ppermute | solution.py:123
  6.4 1.3 %collective-permute-start = (f32[1,80,256]{2,1,0:T(8,128)S(1)}, f32[1,80,256]{2,1,0:T(8,128)S(1)}, u32[]{:S(2)}, u32[]{:S(2)}) collective-permute-start(f32[1,80,256]{2,1,0:T(8,128)S(1)} %get-tuple-element.67._.own.refs_0_), channel_id=1, source_target_pairs={{0,8},{8,0},{16,24},{24,16},{1,9},{9,1},{17,25},{25,17},{2,10},{10... | collective-permute-start | bytes 245768 | tf_op jit(solution)/shard_map/ppermute | solution.py:126
  8.0 4.3 %collective-permute-start.1 = (f32[1,64,256]{2,1,0:T(8,128)S(1)}, f32[1,64,256]{2,1,0:T(8,128)S(1)}, u32[]{:S(2)}, u32[]{:S(2)}) collective-permute-start(f32[1,64,256]{2,1,0:T(8,128)S(1)} %combine.3._), channel_id=1, source_target_pairs={{0,16},{8,24},{16,0},{24,8},{1,17},{9,25},{17,1},{25,9},{2,18},{10... | collective-permute-start | bytes 196616 | tf_op jit(solution)/shard_map/ppermute | solution.py:126
  12.4 2.3 %copy-start.1 = (bf16[2,1,4,512,256]{4,3,2,1,0:T(8,128)(2,1)S(1)}, bf16[2,1,4,512,256]{4,3,2,1,0:T(8,128)(2,1)}, u32[]{:S(2)}) copy-start(bf16[2,1,4,512,256]{4,3,2,1,0:T(8,128)(2,1)} %previous.3) | copy-start | bytes 6291460
  12.9 11.4 %collective-permute-start.2 = (f32[4,64,256]{2,1,0:T(8,128)S(1)}, f32[4,64,256]{2,1,0:T(8,128)S(1)}, u32[]{:S(2)}, u32[]{:S(2)}) collective-permute-start(f32[4,64,256]{2,1,0:T(8,128)S(1)} %get-tuple-element.77._), channel_id=1, source_target_pairs={{0,1},{1,2},{2,3},{3,4},{4,5},{5,6},{6,7},{7,0},{8,9},{9,10},{10,1... | collective-permute-start | bytes 786440 | tf_op jit(solution)/shard_map/ppermute | solution.py:123
  16.8 1.3 %collective-permute-start.4 = (f32[1,80,256]{2,1,0:T(8,128)S(1)}, f32[1,80,256]{2,1,0:T(8,128)S(1)}, u32[]{:S(2)}, u32[]{:S(2)}) collective-permute-start(f32[1,80,256]{2,1,0:T(8,128)S(1)} %get-tuple-element.87._.own.refs_2_), channel_id=1, source_target_pairs={{0,8},{8,0},{16,24},{24,16},{1,9},{9,1},{17,25},{25,17},{2,10},{10... | collective-permute-start | bytes 245768 | tf_op jit(solution)/shard_map/ppermute | solution.py:126
  18.3 4.5 %collective-permute-start.5 = (f32[1,64,256]{2,1,0:T(8,128)S(1)}, f32[1,64,256]{2,1,0:T(8,128)S(1)}, u32[]{:S(2)}, u32[]{:S(2)}) collective-permute-start(f32[1,64,256]{2,1,0:T(8,128)S(1)} %combine.4._), channel_id=1, source_target_pairs={{0,16},{8,24},{16,0},{24,8},{1,17},{9,25},{17,1},{25,9},{2,18},{10... | collective-permute-start | bytes 196616 | tf_op jit(solution)/shard_map/ppermute | solution.py:126
  24.8 1.4 %collective-permute-start.6 = (f32[2,64,256]{2,1,0:T(8,128)S(1)}, f32[2,64,256]{2,1,0:T(8,128)S(1)}, u32[]{:S(2)}, u32[]{:S(2)}) collective-permute-start(f32[2,64,256]{2,1,0:T(8,128)S(1)} %second_sides.1.own), channel_id=1, source_target_pairs={{0,8},{8,0},{16,24},{24,16},{1,9},{9,1},{17,25},{25,17},{2,10},{10... | collective-permute-start | bytes 393224 | tf_op jit(solution)/shard_map/ppermute | solution.py:126
  26.5 5.6 %collective-permute-start.7 = (f32[2,64,256]{2,1,0:T(8,128)S(1)}, f32[2,64,256]{2,1,0:T(8,128)S(1)}, u32[]{:S(2)}, u32[]{:S(2)}) collective-permute-start(f32[2,64,256]{2,1,0:T(8,128)S(1)} %combine.5._), channel_id=1, source_target_pairs={{0,16},{8,24},{16,0},{24,8},{1,17},{9,25},{17,1},{25,9},{2,18},{10... | collective-permute-start | bytes 393224 | tf_op jit(solution)/shard_map/ppermute | solution.py:126

commit v9 on v8

--- a/solution.py
+++ b/solution.py
@@ -281,12 +281,9 @@
         def body(
             order, inlet, near, tail, faces, source_high, source_low, tails, ends, message, own
         ):
-            def step(members):
-                for i in members:
-                    tails[i] = face_maps(tail[i], faces[i, :face], faces[i, face:])
-                    own[i] = times(tail[i], source_high, source_low, i)
-
-            in_pairs(items, per, step)
+            for i in range(items):
+                tails[i] = face_maps(tail[i], faces[i, :face], faces[i, face:])
+                own[i] = times(tail[i], source_high, source_low, i)
             for n, c in enumerate(early):
                 links = []
                 for p in range(count):
@@ -474,16 +471,16 @@
         def body(inv, sides, source_high, source_low, maps, ends, rows_high, rows_low, _, *refs):
             mapped, (free, within, reach_high, reach_low, high, low) = refs[: len(lower)], refs[len(lower) :]
             span = pl.ds(0, wide)
+            for i in range(size * count):
+                s = arrived_side(sides, i) if group[0] == 0 else split(sides[i])
+                whole = times(inv[at(group, i)], source_high, source_low, i)
+                free[i] = whole + dot(maps[i][:, 2 * face :], side_rows(s))
             for n in range(size):
                 old = [r[n, pl.ds(face, packed)] for r in mapped]
                 start = entering(jnp.zeros((face, tracers), F32), [r[n, pl.ds(0, face)] for r in mapped], old)
                 within[n] = within_of(n, start, ends, rows_high, rows_low, high, low)
                 rows = (rows_high[n, span][:, :face], rows_low[n, span][:, :face])
                 reach_high[n], reach_low[n] = split(dot_split(rows, split(lower_maps(old))))
-            for i in range(size * count):
-                s = arrived_side(sides, i) if group[0] == 0 else split(sides[i])
-                whole = times(inv[at(group, i)], source_high, source_low, i)
-                free[i] = whole + dot(maps[i][:, 2 * face :], side_rows(s))
 
         state.free, state.within, *state.reach = run(
             body,
@@ -625,6 +622,10 @@
                 source_high, source_low, maps, rows_high, rows_low, own, traces, tails, *mapped = got[g]
                 base, within = outs[2 * g : 2 * g + 2]
                 ends, high, low = scratch[3 * g : 3 * g + 3]
+                for i in range(len(group) * count):
+                    whole = times(inv[at(group, i)], source_high, source_low, i)
+                    s = side_at(group[0] + i // count, i % count, arrived, [x[6] for x in got])
+                    base[i] = whole + dot(maps[i][:, 2 * face :], side_rows(s))
                 for n, c in enumerate(group):
                     for p in range(count):
                         i = n * count + order[c, p]
@@ -633,10 +634,6 @@
                     old = [r[n, pl.ds(face, packed)] for r in mapped]
                     start = entering(known_inflow(inlet[c]), [r[c] for r in offs], old)
                     within[n] = within_of(n, start, ends, rows_high, rows_low, high, low)
-                for i in range(len(group) * count):
-                    whole = times(inv[at(group, i)], source_high, source_low, i)
-                    s = side_at(group[0] + i // count, i % count, arrived, [x[6] for x in got])
-                    base[i] = whole + dot(maps[i][:, 2 * face :], side_rows(s))
 
         ins = [order, inlet, after, arrived, inv_near, *offsets]
         outs, scratch = [], []

time: 34.4 us -> 34.3 us (level)
  transfers between devices with their start and end apart: 8 -> 8, of which waited for: 6 -> 5; matrix products, arithmetic and copies ran while one was open for 0% -> 0% of each run, Pallas kernels for 49% -> 49%
where the time goes in v9:
time: 34.3 us; the launch traced here: 34.1 us
  Pallas kernels  21.5 us (63%)
  starting transfers between devices  9.74 us (28%)
  waiting for transfers between devices  2.53 us (7%)
  between operations  0.35 us (1%)
    pallas_call x19, Pallas kernels, run(): pl.pallas_call(body, name=name, in_specs=[pl.BlockSpec(memory_space=space...  21.5 us
    ppermute x6, starting transfers between devices, swap(): lax.ppermute(value, 'stream', [(i, i ^ 1 << stage) for i in range(streams)])  4.96 us
    ppermute x2, starting transfers between devices, to_next(): lax.ppermute(value, 'lat', [(i, (i + 1) % lats) for i in range(lats)])  4.77 us
    ppermute x6, waiting for transfers between devices, swap(): lax.ppermute(value, 'stream', [(i, i ^ 1 << stage) for i in range(streams)])  2.52 us
  transfers between devices with their start and end apart: 8, of which 5 were waited for; matrix products, arithmetic and copies ran while one was open for 0% of the time, Pallas kernels for 49%

profile of v9, /device:TPU:0, one launch (start us, length us, event | category | flops | bytes accessed | tf_op | source)
XLA Modules:
  0.0 34.1 jit_solution(16296663291571916096)
XLA Ops:
  0.0 2.0 %load.1 = (f32[4,64,256]{2,1,0:T(8,128)S(1)}, s32[2,4]{1,0:T(2,128)S(4)}, f32[1,256]{1,0:T(1,128)S(1)}, f32[1,256]{1,0:T(1,128)S(1)}, f32[2,64,256]{2,1,0:T(8,12...) custom-call(s32[2,4]{1,0:T(2,128)} %bitcast.5, ...), custom_call_target="tpu_custom_call" | custom-call | tf_op jit(solution)/shard_map/load/pallas_call | solution.py:21
  2.1 3.0 %collective-permute-start.3 = (f32[4,64,256]{2,1,0:T(8,128)S(1)}, f32[4,64,256]{2,1,0:T(8,128)S(1)}, u32[]{:S(2)}, u32[]{:S(2)}) collective-permute-start(f32[4,64,256]{2,1,0:T(8,128)S(1)} %get-tuple-element.81), channel_id=1, source_target_pairs={{0,1},{1,2},{2,3},{3,4},{4,5},{5,6},{6,7},{7,0},{8,9},{9,10},{10,1... | collective-permute-start | bytes 786440 | tf_op jit(solution)/shard_map/ppermute | solution.py:123
  5.0 1.2 %begin_early.1 = (f32[4,64,128]{2,1,0:T(8,128)S(1)}, f32[4,64,256]{2,1,0:T(8,128)S(1)}, f32[1,80,256]{2,1,0:T(8,128)S(1)}) custom-call(s32[2,4]{1,0:T(2,128)S(4)} %get-tuple-element.59.order, f32[2,64,256]{2,1,0:T(8,128)S(1)} %get-tuple-element.60.inlet, f32[4,64,256]{2,1,0:T(8,128)S(1)} %get-tuple-element.61.near.sides, ...), custom_call_target="tpu_custom_call" | custom-call | tf_op jit(solution)/shard_map/begin_early/pallas_call | solution.py:21
  6.3 0.1 collective-permute-start
  6.4 1.0 %early_maps.1 = (bf16[4,512,384]{2,1,0:T(8,128)(2,1)S(1)}, bf16[4,64,384]{2,1,0:T(8,128)(2,1)S(1)}, bf16[1,320,256]{2,1,0:T(8,128)(2,1)S(1)}, bf16[1,320,256]{2,1,0:T(8,128)(2,1)S(1)}) custom-call(s32[2,4]{1,0:T(2,128)S(4)} %get-tuple-element.59.order, bf16[2,1,4,512,512]{4,3,2,1,0:T(8,128)(2,1)S(1)} %copy-done, bf16[2,1,4,64,512]{4,3,2,1,0:T(8,128)(2,1)S(1)} %copy-done.2, ...), custom_call_target="tpu_custom_call" | custom-call | tf_op jit(solution)/shard_map/early_maps/pallas_call | solution.py:21
  7.4 0.2 collective-permute-done.other.refs_0_.refs_1_.refs_9_
  7.6 0.2 combine.3._
  7.8 1.6 %collective-permute-start.1 = (f32[1,64,256]{2,1,0:T(8,128)S(1)}, f32[1,64,256]{2,1,0:T(8,128)S(1)}, u32[]{:S(2)}, u32[]{:S(2)}) collective-permute-start(f32[1,64,256]{2,1,0:T(8,128)S(1)} %combine.3._), channel_id=1, source_target_pairs={{0,16},{8,24},{16,0},{24,8},{1,17},{9,25},{17,1},{25,9},{2,18},{10... | collective-permute-start | bytes 196616 | tf_op jit(solution)/shard_map/ppermute | solution.py:126
  9.4 0.8 %late_maps.1.refs_3_.maps.refs_12_.refs_10_ = bf16[4,512,384]{2,1,0:T(8,128)(2,1)S(1)} custom-call(bf16[2,1,4,512,512]{4,3,2,1,0:T(8,128)(2,1)S(1)} %copy-done, bf16[2,1,4,64,512]{4,3,2,1,0:T(8,128)(2,1)S(1)} %copy-done.2, bf16[2,1,4,64,512]{4,3,2,1,0:T(8,128)(2,1)S(1)} %copy-done.3, f32[1,64,256]{2,1,0:T(8,128)S(1)} %combine.3._), custom_call_target="tpu_custom_call" | custom-call | tf_op jit(solution)/shard_map/late_maps/pallas_call | solution.py:21
  10.2 1.9 %prepare.2 = (f32[4,512,256]{2,1,0:T(8,128)S(1)}, f32[1,256,256]{2,1,0:T(8,128)S(1)}, bf16[1,256,64]{2,1,0:T(8,128)(2,1)S(1)}, bf16[1,256,64]{2,1,0:T(8,128)(2,1)S(1)}) custom-call(bf16[2,1,4,512,512]{4,3,2,1,0:T(8,128)(2,1)S(1)} %copy-done, f32[4,64,256]{2,1,0:T(8,128)S(1)} %get-tuple-element.61.near.sides, ...), custom_call_target="tpu_custom_call" | custom-call | tf_op jit(solution)/shard_map/prepare/pallas_call | solution.py:21
  12.2 0.5 %enter.2 = (bf16[4,192,256]{2,1,0:T(8,128)(2,1)S(1)}, f32[4,64,256]{2,1,0:T(8,128)S(1)}) custom-call(s32[2,4]{1,0:T(2,128)S(4)} %get-tuple-element.59.order, f32[2,64,256]{2,1,0:T(8,128)S(1)} %get-tuple-element.60.inlet, f32[1,256,256]{2,1,0:T(8,128)S(1)} %get-tuple-element.72.within, bf16[1,256,64]{2,1,0:T(8,128)(2,1)S(1)} %get-tuple-element.73.reach_high.refs_2_, ...), custom_call_target="tpu_custom_call" | custom-call | tf_op jit(solution)/shard_map/enter/pallas_call | solution.py:21
  12.7 1.8 %collective-permute-start.2 = (f32[4,64,256]{2,1,0:T(8,128)S(1)}, f32[4,64,256]{2,1,0:T(8,128)S(1)}, u32[]{:S(2)}, u32[]{:S(2)}) collective-permute-start(f32[4,64,256]{2,1,0:T(8,128)S(1)} %get-tuple-element.77._), channel_id=1, source_target_pairs={{0,1},{1,2},{2,3},{3,4},{4,5},{5,6},{6,7},{7,0},{8,9},{9,10},{10,1... | collective-permute-start | bytes 786440 | tf_op jit(solution)/shard_map/ppermute | solution.py:123
  14.5 1.6 %begin_late.1 = (bf16[4,512,256]{2,1,0:T(8,128)(2,1)S(1)}, bf16[4,512,256]{2,1,0:T(8,128)(2,1)S(1)}, f32[4,64,256]{2,1,0:T(8,128)S(1)}, f32[4,64,128]{2,1,0:T(8,...) custom-call(s32[2,4]{1,0:T(2,128)S(4)} %get-tuple-element.59.order, ...), custom_call_target="tpu_custom_call" | custom-call | tf_op jit(solution)/shard_map/begin_late/pallas_call | solution.py:21
  16.1 0.5 %first_sides.1 = (f32[4,64,256]{2,1,0:T(8,128)S(1)}, f32[1,80,256]{2,1,0:T(8,128)S(1)}) custom-call(s32[2,4]{1,0:T(2,128)S(4)} %get-tuple-element.59.order, f32[2,64,256]{2,1,0:T(8,128)S(1)} %get-tuple-element.60.inlet, f32[4,64,256]{2,1,0:T(8,128)S(1)} %collective-permute-done.3.arrived.sides, f32[4,64,256]{2,1,0:T(8,128)S(1)} %get-tuple-element.82.own, ...), custom_call_target="tpu_custom_call" | custom-call | tf_op jit(solution)/shard_map/first_sides/pallas_call | solution.py:21
  16.6 0.1 collective-permute-start.4
  16.7 1.2 %second.2 = (bf16[4,512,256]{2,1,0:T(8,128)(2,1)S(1)}, bf16[4,512,256]{2,1,0:T(8,128)(2,1)S(1)}, f32[4,64,256]{2,1,0:T(8,128)S(1)}, f32[4,64,256]{2,1,0:T(8,128)S(1)}) custom-call(bf16[2,1,4,512,512]{4,3,2,1,0:T(8,128)(2,1)S(1)} %copy-done, bf16[4,512,384]{2,1,0:T(8,128)(2,1)S(1)} %get-tuple-element.68._.maps.refs_3_.refs_5_, ...), custom_call_target="tpu_custom_call" | custom-call | tf_op jit(solution)/shard_map/second/pallas_call | solution.py:21
  17.9 0.1 collective-permute-done.4.other.refs_0_.refs_3_.refs_18_
  17.9 0.2 combine.4._
  18.1 1.6 %collective-permute-start.5 = (f32[1,64,256]{2,1,0:T(8,128)S(1)}, f32[1,64,256]{2,1,0:T(8,128)S(1)}, u32[]{:S(2)}, u32[]{:S(2)}) collective-permute-start(f32[1,64,256]{2,1,0:T(8,128)S(1)} %combine.4._), channel_id=1, source_target_pairs={{0,16},{8,24},{16,0},{24,8},{1,17},{9,25},{17,1},{25,9},{2,18},{10... | collective-permute-start | bytes 196616 | tf_op jit(solution)/shard_map/ppermute | solution.py:126
  19.7 0.3 fold_sides.1
  20.1 1.9 %prepare.3 = (f32[4,512,256]{2,1,0:T(8,128)S(1)}, f32[1,256,256]{2,1,0:T(8,128)S(1)}, bf16[1,256,64]{2,1,0:T(8,128)(2,1)S(1)}, bf16[1,256,64]{2,1,0:T(8,128)(2,1)S(1)}) custom-call(bf16[2,1,4,512,512]{4,3,2,1,0:T(8,128)(2,1)S(1)} %copy-done, f32[4,64,256]{2,1,0:T(8,128)S(1)} %collective-permute-done.3.arrived.sides, ...), custom_call_target="tpu_custom_call" | custom-call | tf_op jit(solution)/shard_map/prepare/pallas_call | solution.py:21
  22.0 0.6 %collective-permute-done.5.refs_0_ = f32[1,64,256]{2,1,0:T(8,128)S(1)} collective-permute-done((f32[1,64,256]{2,1,0:T(8,128)S(1)}, f32[1,64,256]{2,1,0:T(8,128)S(1)}, u32[]{:S(2)}, u32[]{:S(2)}) %collective-permute-start.5) | collective-permute-done | bytes 65568 | tf_op jit(solution)/shard_map/ppermute | solution.py:126
  22.7 0.2 enter.3.stack
  22.9 1.2 %second.3 = (bf16[4,512,256]{2,1,0:T(8,128)(2,1)S(1)}, bf16[4,512,256]{2,1,0:T(8,128)(2,1)S(1)}, f32[4,64,256]{2,1,0:T(8,128)S(1)}, f32[4,64,256]{2,1,0:T(8,128)S(1)}) custom-call(bf16[2,1,4,512,512]{4,3,2,1,0:T(8,128)(2,1)S(1)} %copy-done, bf16[4,512,384]{2,1,0:T(8,128)(2,1)S(1)} %late_maps.1.refs_3_.maps.refs_12_.refs_10_, ...), custom_call_target="tpu_custom_call" | custom-call | tf_op jit(solution)/shard_map/second/pallas_call | solution.py:21
  24.1 0.5 %second_sides.1.own = f32[2,64,256]{2,1,0:T(8,128)S(1)} custom-call(s32[2,4]{1,0:T(2,128)S(4)} %get-tuple-element.59.order, f32[4,64,256]{2,1,0:T(8,128)S(1)} %collective-permute-done.2.arrived, f32[4,64,256]{2,1,0:T(8,128)S(1)} %get-tuple-element.88._.refs_0_.refs_6_, f32[4,64,256]{2,1,0:T(8,128)S(1)} %get-tuple-element.89.refs_1_.refs_7_, ...), custom_call_target="tpu_custom_call" | custom-call | tf_op jit(solution)/shard_map/second_sides/pallas_call | solution.py:21
  24.6 0.1 collective-permute-start.6
  24.7 1.3 %collective-permute-done.6.other.refs_0_ = f32[2,64,256]{2,1,0:T(8,128)S(1)} collective-permute-done((f32[2,64,256]{2,1,0:T(8,128)S(1)}, f32[2,64,256]{2,1,0:T(8,128)S(1)}, u32[]{:S(2)}, u32[]{:S(2)}) %collective-permute-start.6) | collective-permute-done | bytes 131104 | tf_op jit(solution)/shard_map/ppermute | solution.py:126
  26.0 0.3 combine.5._
  26.3 1.6 %collective-permute-start.7 = (f32[2,64,256]{2,1,0:T(8,128)S(1)}, f32[2,64,256]{2,1,0:T(8,128)S(1)}, u32[]{:S(2)}, u32[]{:S(2)}) collective-permute-start(f32[2,64,256]{2,1,0:T(8,128)S(1)} %combine.5._), channel_id=1, source_target_pairs={{0,16},{8,24},{16,0},{24,8},{1,17},{9,25},{17,1},{25,9},{2,18},{10... | collective-permute-start | bytes 393224 | tf_op jit(solution)/shard_map/ppermute | solution.py:126
  27.9 3.8 %settle.1 = (f32[4,512,256]{2,1,0:T(8,128)S(1)}, f32[1,256,256]{2,1,0:T(8,128)S(1)}, f32[4,512,256]{2,1,0:T(8,128)S(1)}, f32[1,256,256]{2,1,0:T(8,128)S(1)}) custom-call(s32[2,4]{1,0:T(2,128)S(4)} %get-tuple-element.59.order, f32[2,64,256]{2,1,0:T(8,128)S(1)} %get-tuple-element.60.inlet, f32[2,64,256]{2,1,0:T(8,128)S(1)} %combine.5._, ...), custom_call_target="tpu_custom_call" | custom-call | tf_op jit(solution)/shard_map/settle/pallas_call | solution.py:21
  31.7 0.2 collective-permute-done.7.refs_0_
  31.9 2.0 %result.1 = bf16[2,1,4,512,256]{4,3,2,1,0:T(8,128)(2,1)} custom-call(s32[2,4]{1,0:T(2,128)S(4)} %get-tuple-element.59.order, f32[2,64,256]{2,1,0:T(8,128)S(1)} %collective-permute-done.7.refs_0_, f32[1,256,256]{2,1,0:T(8,128)S(1)} %get-tuple-element.109.refs_1_, bf16[1,256,64]{2,1,0:T(8,128)(2,1)S(1)} %get-tuple-element.73.reach_high.refs_2_, ...), custom_call_target="tpu_custom_call" | custom-call | tf_op jit(solution)/shard_map/result/pallas_call | solution.py:21
  (11 shorter events, 0.1 us)
Async XLA Ops:
  0.0 6.3 %copy-start = (bf16[2,1,4,512,512]{4,3,2,1,0:T(8,128)(2,1)S(1)}, bf16[2,1,4,512,512]{4,3,2,1,0:T(8,128)(2,1)}, u32[]{:S(2)}) copy-start(bf16[2,1,4,512,512]{4,3,2,1,0:T(8,128)(2,1)} %inv.15) | copy-start | bytes 12582916
  2.0 4.3 %copy-start.2 = (bf16[2,1,4,64,512]{4,3,2,1,0:T(8,128)(2,1)S(1)}, bf16[2,1,4,64,512]{4,3,2,1,0:T(8,128)(2,1)}, u32[]{:S(2)}) copy-start(bf16[2,1,4,64,512]{4,3,2,1,0:T(8,128)(2,1)} %up.5) | copy-start | bytes 1572868
  2.0 4.3 %copy-start.3 = (bf16[2,1,4,64,512]{4,3,2,1,0:T(8,128)(2,1)S(1)}, bf16[2,1,4,64,512]{4,3,2,1,0:T(8,128)(2,1)}, u32[]{:S(2)}) copy-start(bf16[2,1,4,64,512]{4,3,2,1,0:T(8,128)(2,1)} %side.5) | copy-start | bytes 1572868
  2.1 14.0 %collective-permute-start.3 = (f32[4,64,256]{2,1,0:T(8,128)S(1)}, f32[4,64,256]{2,1,0:T(8,128)S(1)}, u32[]{:S(2)}, u32[]{:S(2)}) collective-permute-start(f32[4,64,256]{2,1,0:T(8,128)S(1)} %get-tuple-element.81), channel_id=1, source_target_pairs={{0,1},{1,2},{2,3},{3,4},{4,5},{5,6},{6,7},{7,0},{8,9},{9,10},{10,1... | collective-permute-start | bytes 786440 | tf_op jit(solution)/shard_map/ppermute | solution.py:123
  6.3 1.3 %collective-permute-start = (f32[1,80,256]{2,1,0:T(8,128)S(1)}, f32[1,80,256]{2,1,0:T(8,128)S(1)}, u32[]{:S(2)}, u32[]{:S(2)}) collective-permute-start(f32[1,80,256]{2,1,0:T(8,128)S(1)} %get-tuple-element.67._.own.refs_0_), channel_id=1, source_target_pairs={{0,8},{8,0},{16,24},{24,16},{1,9},{9,1},{17,25},{25,17},{2,10},{10... | collective-permute-start | bytes 245768 | tf_op jit(solution)/shard_map/ppermute | solution.py:126
  7.8 4.3 %collective-permute-start.1 = (f32[1,64,256]{2,1,0:T(8,128)S(1)}, f32[1,64,256]{2,1,0:T(8,128)S(1)}, u32[]{:S(2)}, u32[]{:S(2)}) collective-permute-start(f32[1,64,256]{2,1,0:T(8,128)S(1)} %combine.3._), channel_id=1, source_target_pairs={{0,16},{8,24},{16,0},{24,8},{1,17},{9,25},{17,1},{25,9},{2,18},{10... | collective-permute-start | bytes 196616 | tf_op jit(solution)/shard_map/ppermute | solution.py:126
  12.2 2.3 %copy-start.1 = (bf16[2,1,4,512,256]{4,3,2,1,0:T(8,128)(2,1)S(1)}, bf16[2,1,4,512,256]{4,3,2,1,0:T(8,128)(2,1)}, u32[]{:S(2)}) copy-start(bf16[2,1,4,512,256]{4,3,2,1,0:T(8,128)(2,1)} %previous.3) | copy-start | bytes 6291460
  12.7 11.4 %collective-permute-start.2 = (f32[4,64,256]{2,1,0:T(8,128)S(1)}, f32[4,64,256]{2,1,0:T(8,128)S(1)}, u32[]{:S(2)}, u32[]{:S(2)}) collective-permute-start(f32[4,64,256]{2,1,0:T(8,128)S(1)} %get-tuple-element.77._), channel_id=1, source_target_pairs={{0,1},{1,2},{2,3},{3,4},{4,5},{5,6},{6,7},{7,0},{8,9},{9,10},{10,1... | collective-permute-start | bytes 786440 | tf_op jit(solution)/shard_map/ppermute | solution.py:123
  16.6 1.3 %collective-permute-start.4 = (f32[1,80,256]{2,1,0:T(8,128)S(1)}, f32[1,80,256]{2,1,0:T(8,128)S(1)}, u32[]{:S(2)}, u32[]{:S(2)}) collective-permute-start(f32[1,80,256]{2,1,0:T(8,128)S(1)} %get-tuple-element.87._.own.refs_2_), channel_id=1, source_target_pairs={{0,8},{8,0},{16,24},{24,16},{1,9},{9,1},{17,25},{25,17},{2,10},{10... | collective-permute-start | bytes 245768 | tf_op jit(solution)/shard_map/ppermute | solution.py:126
  18.1 4.5 %collective-permute-start.5 = (f32[1,64,256]{2,1,0:T(8,128)S(1)}, f32[1,64,256]{2,1,0:T(8,128)S(1)}, u32[]{:S(2)}, u32[]{:S(2)}) collective-permute-start(f32[1,64,256]{2,1,0:T(8,128)S(1)} %combine.4._), channel_id=1, source_target_pairs={{0,16},{8,24},{16,0},{24,8},{1,17},{9,25},{17,1},{25,9},{2,18},{10... | collective-permute-start | bytes 196616 | tf_op jit(solution)/shard_map/ppermute | solution.py:126
  24.6 1.4 %collective-permute-start.6 = (f32[2,64,256]{2,1,0:T(8,128)S(1)}, f32[2,64,256]{2,1,0:T(8,128)S(1)}, u32[]{:S(2)}, u32[]{:S(2)}) collective-permute-start(f32[2,64,256]{2,1,0:T(8,128)S(1)} %second_sides.1.own), channel_id=1, source_target_pairs={{0,8},{8,0},{16,24},{24,16},{1,9},{9,1},{17,25},{25,17},{2,10},{10... | collective-permute-start | bytes 393224 | tf_op jit(solution)/shard_map/ppermute | solution.py:126
  26.3 5.6 %collective-permute-start.7 = (f32[2,64,256]{2,1,0:T(8,128)S(1)}, f32[2,64,256]{2,1,0:T(8,128)S(1)}, u32[]{:S(2)}, u32[]{:S(2)}) collective-permute-start(f32[2,64,256]{2,1,0:T(8,128)S(1)} %combine.5._), channel_id=1, source_target_pairs={{0,16},{8,24},{16,0},{24,8},{1,17},{9,25},{17,1},{25,9},{2,18},{10... | collective-permute-start | bytes 393224 | tf_op jit(solution)/shard_map/ppermute | solution.py:126

commit v10 on v9

--- a/solution.py
+++ b/solution.py
@@ -16,7 +16,7 @@
 SMEM = pltpu.SMEM
 
 
-def run(body, name, ins, outs, scratch):
+def run(body, name, ins, outs, scratch, work=0):
     pairs = [a if isinstance(a, tuple) else (a, VMEM) for a in ins]
     return pl.pallas_call(
         body,
@@ -25,7 +25,7 @@
         out_specs=[pl.BlockSpec(memory_space=o.memory_space) for o in outs],
         out_shape=outs,
         scratch_shapes=scratch,
-        cost_estimate=pl.CostEstimate(flops=0, bytes_accessed=0, transcendentals=0),
+        cost_estimate=pl.CostEstimate(flops=work, bytes_accessed=0, transcendentals=0),
         compiler_params=pltpu.CompilerParams(vmem_limit_bytes=24 * MIB),
     )(*[a if space is VMEM else pltpu.with_memory_space_constraint(a, space) for a, space in pairs])
 
@@ -185,9 +185,9 @@
         items = size * count
 
         def body(
-            order, rate, aff, inlet, old, inverse, upwind, lateral, previous,
-            trace, o_order, o_rate, o_aff, o_inlet, near, o_tail, faces, source_high, source_low,
-            lagged, staged, lead_sems, sems,
+            order, rate, aff, inlet, old, inverse, previous,
+            o_order, o_rate, o_aff, o_inlet, near, o_tail, source_high, source_low, lagged,
+            staged, lead_sems, sems,
         ):
             rows = pl.ds(plane - 2 * per_side, 2 * per_side)
             lead = [
@@ -203,15 +203,11 @@
             whole = pl.ds(0, count)
             fields, others = [], []
             for n, c in enumerate(early):
-                for h in range(0, count, per):
-                    here, there = pl.ds(h, per), pl.ds(n * count + h, per)
+                for h in range(count):
+                    here, there = pl.ds(h, 1), pl.ds(n * count + h, 1)
                     fields.append((previous.at[c, 0, here], lagged.at[there]))
                 there = pl.ds(n * count, count)
-                others += [
-                    (inverse.at[c, 0, whole, ending], o_tail.at[there]),
-                    (upwind.at[c, 0], faces.at[there, pl.ds(0, face)]),
-                    (lateral.at[c, 0], faces.at[there, pl.ds(face, face)]),
-                ]
+                others.append((inverse.at[c, 0, whole, ending], o_tail.at[there]))
             copies = [pltpu.make_async_copy(a, b, sems.at[k]) for k, (a, b) in enumerate(fields + others)]
             for one in lead[:3] + copies[: len(fields)] + lead[3:4] + copies[len(fields) :] + lead[4:]:
                 one.start()
@@ -223,13 +219,10 @@
 
             for k in range(len(fields)):
                 copies[k].wait()
-                for i in range(k * per, k * per + per):
+                for i in range(k, k + 1):
                     lag = lagged[i].astype(F32)
                     source_high[i], source_low[i] = split(langmuir(lag, o_rate[...], o_aff[...]))
-                    c = early[i // count]
-                    if c == cols - 1:
-                        trace[i % count] = lateral_rows(lag, per_side)
-                    else:
+                    if early[i // count] < cols - 1:
                         near[i + count] = lateral_rows(lag, per_side)
             for one in lead[3:]:
                 one.wait()
@@ -248,41 +241,46 @@
                 (inlet_trace, HBM),
                 (shaped, HBM),
                 (inverse, HBM),
-                (upwind, HBM),
-                (lateral, HBM),
                 (previous, HBM),
             ],
             [
-                VMEM((count, face, tracers), F32),
                 SMEM((cols, count), jnp.int32),
                 VMEM((1, tracers), F32),
                 VMEM((1, tracers), F32),
                 VMEM((cols, face, tracers), F32),
                 VMEM((items, face, tracers), F32),
                 VMEM((items, face, nodes), BF16),
-                VMEM((items, 2 * face, nodes), BF16),
                 *source_outs(size),
+                VMEM((items, nodes, tracers), BF16),
             ],
             [
-                VMEM((items, nodes, tracers), BF16),
                 VMEM((count, per_side, 2 * per_side, tracers), BF16),
                 pltpu.SemaphoreType.DMA((5,)),
-                pltpu.SemaphoreType.DMA((size * (count // per + 3),)),
+                pltpu.SemaphoreType.DMA((size * (count + 1),)),
             ],
         )
         state = SimpleNamespace()
-        state.near, state.tail, state.faces, state.source_high, state.source_low = values[5:]
-        return values[:5], state
+        state.near, state.tail, state.source_high, state.source_low, lagged = values[4:]
+
+        def old_trace(lagged, trace):
+            for j in range(count):
+                for a in range(per_side):
+                    start = a * plane + plane - 2 * per_side
+                    rows = lagged[items - count + j, pl.ds(start, 2 * per_side)].astype(F32)
+                    trace[j, pl.ds(a * per_side, per_side)] = rows[per_side:]
+
+        trace = run(old_trace, "old_trace", [lagged], [VMEM((count, face, tracers), F32)], [], 3000000000)[0]
+        return (trace, *values[:4]), state
 
     def begin_early(state):
         size = len(early)
         items = size * count
 
         def body(
-            order, inlet, near, tail, faces, source_high, source_low, tails, ends, message, own
+            order, inlet, near, tail, up, side, source_high, source_low, tails, ends, message, own
         ):
             for i in range(items):
-                tails[i] = face_maps(tail[i], faces[i, :face], faces[i, face:])
+                tails[i] = face_maps(tail[i], up[at(early, i)], side[at(early, i)])
                 own[i] = times(tail[i], source_high, source_low, i)
             for n, c in enumerate(early):
                 links = []
@@ -307,7 +305,7 @@
         state.tails, state.ends, state.message = run(
             body,
             "begin_early",
-            [order, inlet, state.near, state.tail, state.faces, state.source_high, state.source_low],
+            [order, inlet, state.near, state.tail, up_near, side_near, state.source_high, state.source_low],
             [
                 VMEM((items, face, 2 * face), F32),
                 VMEM((items, face, tracers), F32),

time: 34.3 us -> 34.1 us (level)
    pallas_call x19 -> x20, Pallas kernels: 21.5 us -> 21.3 us  [run(): pl.pallas_call(body, name=name, in_specs=[pl.BlockSpec(memory_space=space...]
where the time goes in v10:
time: 34.1 us; the launch traced here: 33.9 us
  Pallas kernels  21.3 us (62%)
  starting transfers between devices  9.73 us (29%)
  waiting for transfers between devices  2.54 us (7%)
  between operations  0.36 us (1%)
    pallas_call x20, Pallas kernels, run(): pl.pallas_call(body, name=name, in_specs=[pl.BlockSpec(memory_space=space...  21.3 us
    ppermute x6, starting transfers between devices, swap(): lax.ppermute(value, 'stream', [(i, i ^ 1 << stage) for i in range(streams)])  4.96 us
    ppermute x2, starting transfers between devices, to_next(): lax.ppermute(value, 'lat', [(i, (i + 1) % lats) for i in range(lats)])  4.77 us
    ppermute x6, waiting for transfers between devices, swap(): lax.ppermute(value, 'stream', [(i, i ^ 1 << stage) for i in range(streams)])  2.54 us
  transfers between devices with their start and end apart: 8, of which 5 were waited for; matrix products, arithmetic and copies ran while one was open for 0% of the time, Pallas kernels for 49%

profile of v10, /device:TPU:0, one launch (start us, length us, event | category | flops | bytes accessed | tf_op | source)
XLA Modules:
  0.0 33.9 jit_solution(17526579204343754698)
XLA Ops:
  0.0 1.8 %load.1 = (s32[2,4]{1,0:T(2,128)S(4)}, f32[1,256]{1,0:T(1,128)S(1)}, f32[1,256]{1,0:T(1,128)S(1)}, f32[2,64,256]{2,1,0:T(8,128)S(1)}, f32[4,64,256]{2,1,0:T(8,12...) custom-call(s32[2,4]{1,0:T(2,128)} %bitcast.5, ...), custom_call_target="tpu_custom_call" | custom-call | tf_op jit(solution)/shard_map/load/pallas_call | solution.py:21
  1.9 3.0 %collective-permute-start.3 = (f32[4,64,256]{2,1,0:T(8,128)S(1)}, f32[4,64,256]{2,1,0:T(8,128)S(1)}, u32[]{:S(2)}, u32[]{:S(2)}) collective-permute-start(f32[4,64,256]{2,1,0:T(8,128)S(1)} %old_trace.1), channel_id=1, source_target_pairs={{0,1},{1,2},{2,3},{3,4},{4,5},{5,6},{6,7},{7,0},{8,9},{9,10},{10,1... | collective-permute-start | bytes 786440 | tf_op jit(solution)/shard_map/ppermute | solution.py:123
  4.9 1.2 %begin_early.1 = (f32[4,64,128]{2,1,0:T(8,128)S(1)}, f32[4,64,256]{2,1,0:T(8,128)S(1)}, f32[1,80,256]{2,1,0:T(8,128)S(1)}) custom-call(s32[2,4]{1,0:T(2,128)S(4)} %get-tuple-element.58.order, f32[2,64,256]{2,1,0:T(8,128)S(1)} %get-tuple-element.59.inlet, f32[4,64,256]{2,1,0:T(8,128)S(1)} %get-tuple-element.60.near.sides, ...), custom_call_target="tpu_custom_call" | custom-call | tf_op jit(solution)/shard_map/begin_early/pallas_call | solution.py:21
  6.1 0.1 collective-permute-start
  6.2 1.0 %early_maps.1 = (bf16[4,512,384]{2,1,0:T(8,128)(2,1)S(1)}, bf16[4,64,384]{2,1,0:T(8,128)(2,1)S(1)}, bf16[1,320,256]{2,1,0:T(8,128)(2,1)S(1)}, bf16[1,320,256]{2,1,0:T(8,128)(2,1)S(1)}) custom-call(s32[2,4]{1,0:T(2,128)S(4)} %get-tuple-element.58.order, bf16[2,1,4,512,512]{4,3,2,1,0:T(8,128)(2,1)S(1)} %copy-done, bf16[2,1,4,64,512]{4,3,2,1,0:T(8,128)(2,1)S(1)} %copy-done.2, ...), custom_call_target="tpu_custom_call" | custom-call | tf_op jit(solution)/shard_map/early_maps/pallas_call | solution.py:21
  7.2 0.2 collective-permute-done.other.refs_0_.refs_1_.refs_9_
  7.4 0.2 combine.3._
  7.7 1.6 %collective-permute-start.1 = (f32[1,64,256]{2,1,0:T(8,128)S(1)}, f32[1,64,256]{2,1,0:T(8,128)S(1)}, u32[]{:S(2)}, u32[]{:S(2)}) collective-permute-start(f32[1,64,256]{2,1,0:T(8,128)S(1)} %combine.3._), channel_id=1, source_target_pairs={{0,16},{8,24},{16,0},{24,8},{1,17},{9,25},{17,1},{25,9},{2,18},{10... | collective-permute-start | bytes 196616 | tf_op jit(solution)/shard_map/ppermute | solution.py:126
  9.2 0.8 %late_maps.1.refs_3_.maps.refs_12_.refs_10_ = bf16[4,512,384]{2,1,0:T(8,128)(2,1)S(1)} custom-call(bf16[2,1,4,512,512]{4,3,2,1,0:T(8,128)(2,1)S(1)} %copy-done, bf16[2,1,4,64,512]{4,3,2,1,0:T(8,128)(2,1)S(1)} %copy-done.2, bf16[2,1,4,64,512]{4,3,2,1,0:T(8,128)(2,1)S(1)} %copy-done.3, f32[1,64,256]{2,1,0:T(8,128)S(1)} %combine.3._), custom_call_target="tpu_custom_call" | custom-call | tf_op jit(solution)/shard_map/late_maps/pallas_call | solution.py:21
  10.0 1.9 %prepare.2 = (f32[4,512,256]{2,1,0:T(8,128)S(1)}, f32[1,256,256]{2,1,0:T(8,128)S(1)}, bf16[1,256,64]{2,1,0:T(8,128)(2,1)S(1)}, bf16[1,256,64]{2,1,0:T(8,128)(2,1)S(1)}) custom-call(bf16[2,1,4,512,512]{4,3,2,1,0:T(8,128)(2,1)S(1)} %copy-done, f32[4,64,256]{2,1,0:T(8,128)S(1)} %get-tuple-element.60.near.sides, ...), custom_call_target="tpu_custom_call" | custom-call | tf_op jit(solution)/shard_map/prepare/pallas_call | solution.py:21
  12.0 0.5 %enter.2 = (bf16[4,192,256]{2,1,0:T(8,128)(2,1)S(1)}, f32[4,64,256]{2,1,0:T(8,128)S(1)}) custom-call(s32[2,4]{1,0:T(2,128)S(4)} %get-tuple-element.58.order, f32[2,64,256]{2,1,0:T(8,128)S(1)} %get-tuple-element.59.inlet, f32[1,256,256]{2,1,0:T(8,128)S(1)} %get-tuple-element.70.within, bf16[1,256,64]{2,1,0:T(8,128)(2,1)S(1)} %get-tuple-element.71.reach_high.refs_2_, ...), custom_call_target="tpu_custom_call" | custom-call | tf_op jit(solution)/shard_map/enter/pallas_call | solution.py:21
  12.5 1.8 %collective-permute-start.2 = (f32[4,64,256]{2,1,0:T(8,128)S(1)}, f32[4,64,256]{2,1,0:T(8,128)S(1)}, u32[]{:S(2)}, u32[]{:S(2)}) collective-permute-start(f32[4,64,256]{2,1,0:T(8,128)S(1)} %get-tuple-element.75._), channel_id=1, source_target_pairs={{0,1},{1,2},{2,3},{3,4},{4,5},{5,6},{6,7},{7,0},{8,9},{9,10},{10,1... | collective-permute-start | bytes 786440 | tf_op jit(solution)/shard_map/ppermute | solution.py:123
  14.3 1.6 %begin_late.1 = (bf16[4,512,256]{2,1,0:T(8,128)(2,1)S(1)}, bf16[4,512,256]{2,1,0:T(8,128)(2,1)S(1)}, f32[4,64,256]{2,1,0:T(8,128)S(1)}, f32[4,64,128]{2,1,0:T(8,...) custom-call(s32[2,4]{1,0:T(2,128)S(4)} %get-tuple-element.58.order, ...), custom_call_target="tpu_custom_call" | custom-call | tf_op jit(solution)/shard_map/begin_late/pallas_call | solution.py:21
  15.9 0.5 %first_sides.1 = (f32[4,64,256]{2,1,0:T(8,128)S(1)}, f32[1,80,256]{2,1,0:T(8,128)S(1)}) custom-call(s32[2,4]{1,0:T(2,128)S(4)} %get-tuple-element.58.order, f32[2,64,256]{2,1,0:T(8,128)S(1)} %get-tuple-element.59.inlet, f32[4,64,256]{2,1,0:T(8,128)S(1)} %collective-permute-done.3.arrived.sides, f32[4,64,256]{2,1,0:T(8,128)S(1)} %get-tuple-element.80.own, ...), custom_call_target="tpu_custom_call" | custom-call | tf_op jit(solution)/shard_map/first_sides/pallas_call | solution.py:21
  16.4 0.1 collective-permute-start.4
  16.5 1.2 %second.2 = (bf16[4,512,256]{2,1,0:T(8,128)(2,1)S(1)}, bf16[4,512,256]{2,1,0:T(8,128)(2,1)S(1)}, f32[4,64,256]{2,1,0:T(8,128)S(1)}, f32[4,64,256]{2,1,0:T(8,128)S(1)}) custom-call(bf16[2,1,4,512,512]{4,3,2,1,0:T(8,128)(2,1)S(1)} %copy-done, bf16[4,512,384]{2,1,0:T(8,128)(2,1)S(1)} %get-tuple-element.66._.maps.refs_3_.refs_5_, ...), custom_call_target="tpu_custom_call" | custom-call | tf_op jit(solution)/shard_map/second/pallas_call | solution.py:21
  17.7 0.1 collective-permute-done.4.other.refs_0_.refs_3_.refs_18_
  17.7 0.2 combine.4._
  18.0 1.6 %collective-permute-start.5 = (f32[1,64,256]{2,1,0:T(8,128)S(1)}, f32[1,64,256]{2,1,0:T(8,128)S(1)}, u32[]{:S(2)}, u32[]{:S(2)}) collective-permute-start(f32[1,64,256]{2,1,0:T(8,128)S(1)} %combine.4._), channel_id=1, source_target_pairs={{0,16},{8,24},{16,0},{24,8},{1,17},{9,25},{17,1},{25,9},{2,18},{10... | collective-permute-start | bytes 196616 | tf_op jit(solution)/shard_map/ppermute | solution.py:126
  19.6 0.3 fold_sides.1
  19.9 1.9 %prepare.3 = (f32[4,512,256]{2,1,0:T(8,128)S(1)}, f32[1,256,256]{2,1,0:T(8,128)S(1)}, bf16[1,256,64]{2,1,0:T(8,128)(2,1)S(1)}, bf16[1,256,64]{2,1,0:T(8,128)(2,1)S(1)}) custom-call(bf16[2,1,4,512,512]{4,3,2,1,0:T(8,128)(2,1)S(1)} %copy-done, f32[4,64,256]{2,1,0:T(8,128)S(1)} %collective-permute-done.3.arrived.sides, ...), custom_call_target="tpu_custom_call" | custom-call | tf_op jit(solution)/shard_map/prepare/pallas_call | solution.py:21
  21.8 0.7 %collective-permute-done.5.refs_0_ = f32[1,64,256]{2,1,0:T(8,128)S(1)} collective-permute-done((f32[1,64,256]{2,1,0:T(8,128)S(1)}, f32[1,64,256]{2,1,0:T(8,128)S(1)}, u32[]{:S(2)}, u32[]{:S(2)}) %collective-permute-start.5) | collective-permute-done | bytes 65568 | tf_op jit(solution)/shard_map/ppermute | solution.py:126
  22.5 0.2 enter.3.stack
  22.7 1.2 %second.3 = (bf16[4,512,256]{2,1,0:T(8,128)(2,1)S(1)}, bf16[4,512,256]{2,1,0:T(8,128)(2,1)S(1)}, f32[4,64,256]{2,1,0:T(8,128)S(1)}, f32[4,64,256]{2,1,0:T(8,128)S(1)}) custom-call(bf16[2,1,4,512,512]{4,3,2,1,0:T(8,128)(2,1)S(1)} %copy-done, bf16[4,512,384]{2,1,0:T(8,128)(2,1)S(1)} %late_maps.1.refs_3_.maps.refs_12_.refs_10_, ...), custom_call_target="tpu_custom_call" | custom-call | tf_op jit(solution)/shard_map/second/pallas_call | solution.py:21
  23.9 0.5 %second_sides.1.own = f32[2,64,256]{2,1,0:T(8,128)S(1)} custom-call(s32[2,4]{1,0:T(2,128)S(4)} %get-tuple-element.58.order, f32[4,64,256]{2,1,0:T(8,128)S(1)} %collective-permute-done.2.arrived, f32[4,64,256]{2,1,0:T(8,128)S(1)} %get-tuple-element.86._.refs_0_.refs_6_, f32[4,64,256]{2,1,0:T(8,128)S(1)} %get-tuple-element.87.refs_1_.refs_7_, ...), custom_call_target="tpu_custom_call" | custom-call | tf_op jit(solution)/shard_map/second_sides/pallas_call | solution.py:21
  24.5 0.1 collective-permute-start.6
  24.5 1.3 %collective-permute-done.6.other.refs_0_ = f32[2,64,256]{2,1,0:T(8,128)S(1)} collective-permute-done((f32[2,64,256]{2,1,0:T(8,128)S(1)}, f32[2,64,256]{2,1,0:T(8,128)S(1)}, u32[]{:S(2)}, u32[]{:S(2)}) %collective-permute-start.6) | collective-permute-done | bytes 131104 | tf_op jit(solution)/shard_map/ppermute | solution.py:126
  25.9 0.3 combine.5._
  26.1 1.6 %collective-permute-start.7 = (f32[2,64,256]{2,1,0:T(8,128)S(1)}, f32[2,64,256]{2,1,0:T(8,128)S(1)}, u32[]{:S(2)}, u32[]{:S(2)}) collective-permute-start(f32[2,64,256]{2,1,0:T(8,128)S(1)} %combine.5._), channel_id=1, source_target_pairs={{0,16},{8,24},{16,0},{24,8},{1,17},{9,25},{17,1},{25,9},{2,18},{10... | collective-permute-start | bytes 393224 | tf_op jit(solution)/shard_map/ppermute | solution.py:126
  27.7 3.8 %settle.1 = (f32[4,512,256]{2,1,0:T(8,128)S(1)}, f32[1,256,256]{2,1,0:T(8,128)S(1)}, f32[4,512,256]{2,1,0:T(8,128)S(1)}, f32[1,256,256]{2,1,0:T(8,128)S(1)}) custom-call(s32[2,4]{1,0:T(2,128)S(4)} %get-tuple-element.58.order, f32[2,64,256]{2,1,0:T(8,128)S(1)} %get-tuple-element.59.inlet, f32[2,64,256]{2,1,0:T(8,128)S(1)} %combine.5._, ...), custom_call_target="tpu_custom_call" | custom-call | tf_op jit(solution)/shard_map/settle/pallas_call | solution.py:21
  31.5 0.2 collective-permute-done.7.refs_0_
  31.7 2.0 %result.1 = bf16[2,1,4,512,256]{4,3,2,1,0:T(8,128)(2,1)} custom-call(s32[2,4]{1,0:T(2,128)S(4)} %get-tuple-element.58.order, f32[2,64,256]{2,1,0:T(8,128)S(1)} %collective-permute-done.7.refs_0_, f32[1,256,256]{2,1,0:T(8,128)S(1)} %get-tuple-element.107.refs_1_, bf16[1,256,64]{2,1,0:T(8,128)(2,1)S(1)} %get-tuple-element.71.reach_high.refs_2_, ...), custom_call_target="tpu_custom_call" | custom-call | tf_op jit(solution)/shard_map/result/pallas_call | solution.py:21
  (12 shorter events, 0.1 us)
Async XLA Ops:
  1.8 3.1 %copy-start.2 = (bf16[2,1,4,64,512]{4,3,2,1,0:T(8,128)(2,1)S(1)}, bf16[2,1,4,64,512]{4,3,2,1,0:T(8,128)(2,1)}, u32[]{:S(2)}) copy-start(bf16[2,1,4,64,512]{4,3,2,1,0:T(8,128)(2,1)} %up.7) | copy-start | bytes 1572868
  1.8 3.0 %copy-start.3 = (bf16[2,1,4,64,512]{4,3,2,1,0:T(8,128)(2,1)S(1)}, bf16[2,1,4,64,512]{4,3,2,1,0:T(8,128)(2,1)}, u32[]{:S(2)}) copy-start(bf16[2,1,4,64,512]{4,3,2,1,0:T(8,128)(2,1)} %side.7) | copy-start | bytes 1572868
  1.8 4.3 %copy-start = (bf16[2,1,4,512,512]{4,3,2,1,0:T(8,128)(2,1)S(1)}, bf16[2,1,4,512,512]{4,3,2,1,0:T(8,128)(2,1)}, u32[]{:S(2)}) copy-start(bf16[2,1,4,512,512]{4,3,2,1,0:T(8,128)(2,1)} %inv.15) | copy-start | bytes 12582916
  1.9 14.0 %collective-permute-start.3 = (f32[4,64,256]{2,1,0:T(8,128)S(1)}, f32[4,64,256]{2,1,0:T(8,128)S(1)}, u32[]{:S(2)}, u32[]{:S(2)}) collective-permute-start(f32[4,64,256]{2,1,0:T(8,128)S(1)} %old_trace.1), channel_id=1, source_target_pairs={{0,1},{1,2},{2,3},{3,4},{4,5},{5,6},{6,7},{7,0},{8,9},{9,10},{10,1... | collective-permute-start | bytes 786440 | tf_op jit(solution)/shard_map/ppermute | solution.py:123
  6.1 1.3 %collective-permute-start = (f32[1,80,256]{2,1,0:T(8,128)S(1)}, f32[1,80,256]{2,1,0:T(8,128)S(1)}, u32[]{:S(2)}, u32[]{:S(2)}) collective-permute-start(f32[1,80,256]{2,1,0:T(8,128)S(1)} %get-tuple-element.65._.own.refs_0_), channel_id=1, source_target_pairs={{0,8},{8,0},{16,24},{24,16},{1,9},{9,1},{17,25},{25,17},{2,10},{10... | collective-permute-start | bytes 245768 | tf_op jit(solution)/shard_map/ppermute | solution.py:126
  7.7 4.3 %collective-permute-start.1 = (f32[1,64,256]{2,1,0:T(8,128)S(1)}, f32[1,64,256]{2,1,0:T(8,128)S(1)}, u32[]{:S(2)}, u32[]{:S(2)}) collective-permute-start(f32[1,64,256]{2,1,0:T(8,128)S(1)} %combine.3._), channel_id=1, source_target_pairs={{0,16},{8,24},{16,0},{24,8},{1,17},{9,25},{17,1},{25,9},{2,18},{10... | collective-permute-start | bytes 196616 | tf_op jit(solution)/shard_map/ppermute | solution.py:126
  12.0 2.3 %copy-start.1 = (bf16[2,1,4,512,256]{4,3,2,1,0:T(8,128)(2,1)S(1)}, bf16[2,1,4,512,256]{4,3,2,1,0:T(8,128)(2,1)}, u32[]{:S(2)}) copy-start(bf16[2,1,4,512,256]{4,3,2,1,0:T(8,128)(2,1)} %previous.3) | copy-start | bytes 6291460
  12.5 11.4 %collective-permute-start.2 = (f32[4,64,256]{2,1,0:T(8,128)S(1)}, f32[4,64,256]{2,1,0:T(8,128)S(1)}, u32[]{:S(2)}, u32[]{:S(2)}) collective-permute-start(f32[4,64,256]{2,1,0:T(8,128)S(1)} %get-tuple-element.75._), channel_id=1, source_target_pairs={{0,1},{1,2},{2,3},{3,4},{4,5},{5,6},{6,7},{7,0},{8,9},{9,10},{10,1... | collective-permute-start | bytes 786440 | tf_op jit(solution)/shard_map/ppermute | solution.py:123
  16.4 1.3 %collective-permute-start.4 = (f32[1,80,256]{2,1,0:T(8,128)S(1)}, f32[1,80,256]{2,1,0:T(8,128)S(1)}, u32[]{:S(2)}, u32[]{:S(2)}) collective-permute-start(f32[1,80,256]{2,1,0:T(8,128)S(1)} %get-tuple-element.85._.own.refs_2_), channel_id=1, source_target_pairs={{0,8},{8,0},{16,24},{24,16},{1,9},{9,1},{17,25},{25,17},{2,10},{10... | collective-permute-start | bytes 245768 | tf_op jit(solution)/shard_map/ppermute | solution.py:126
  18.0 4.5 %collective-permute-start.5 = (f32[1,64,256]{2,1,0:T(8,128)S(1)}, f32[1,64,256]{2,1,0:T(8,128)S(1)}, u32[]{:S(2)}, u32[]{:S(2)}) collective-permute-start(f32[1,64,256]{2,1,0:T(8,128)S(1)} %combine.4._), channel_id=1, source_target_pairs={{0,16},{8,24},{16,0},{24,8},{1,17},{9,25},{17,1},{25,9},{2,18},{10... | collective-permute-start | bytes 196616 | tf_op jit(solution)/shard_map/ppermute | solution.py:126
  24.5 1.4 %collective-permute-start.6 = (f32[2,64,256]{2,1,0:T(8,128)S(1)}, f32[2,64,256]{2,1,0:T(8,128)S(1)}, u32[]{:S(2)}, u32[]{:S(2)}) collective-permute-start(f32[2,64,256]{2,1,0:T(8,128)S(1)} %second_sides.1.own), channel_id=1, source_target_pairs={{0,8},{8,0},{16,24},{24,16},{1,9},{9,1},{17,25},{25,17},{2,10},{10... | collective-permute-start | bytes 393224 | tf_op jit(solution)/shard_map/ppermute | solution.py:126
  26.1 5.6 %collective-permute-start.7 = (f32[2,64,256]{2,1,0:T(8,128)S(1)}, f32[2,64,256]{2,1,0:T(8,128)S(1)}, u32[]{:S(2)}, u32[]{:S(2)}) collective-permute-start(f32[2,64,256]{2,1,0:T(8,128)S(1)} %combine.5._), channel_id=1, source_target_pairs={{0,16},{8,24},{16,0},{24,8},{1,17},{9,25},{17,1},{25,9},{2,18},{10... | collective-permute-start | bytes 393224 | tf_op jit(solution)/shard_map/ppermute | solution.py:126

commit v11 on v10

--- a/solution.py
+++ b/solution.py
@@ -281,6 +281,7 @@
         ):
             for i in range(items):
                 tails[i] = face_maps(tail[i], up[at(early, i)], side[at(early, i)])
+            for i in range(items):
                 own[i] = times(tail[i], source_high, source_low, i)
             for n, c in enumerate(early):
                 links = []
@@ -345,17 +346,15 @@
             source_high, source_low, own, tails, rows_high, rows_low, mapped, row,
         ):
             for i in range(items):
+                lag = previous[at(late, i)].astype(F32)
+                source_high[i], source_low[i] = split(langmuir(lag, rate[...], aff[...]))
                 k = at(late, i)
                 tails[i] = face_maps(inv[*k, ending], up[k], side[k])
-            for i in range(items + 1):
-                if i < items:
-                    lag = previous[at(late, i)].astype(F32)
-                    source_high[i], source_low[i] = split(langmuir(lag, rate[...], aff[...]))
-                    n, p = i // count, i % count
-                    step = split(tails[n * count + order[late[n], p]][:, :face])
-                    link(n, p, step, rows_high, rows_low, row)
-                if i > 0:
-                    own[i - 1] = times(inv[*at(late, i - 1), ending], source_high, source_low, i - 1)
+            for i in range(items):
+                own[i] = times(inv[*at(late, i), ending], source_high, source_low, i)
+                n, p = i // count, i % count
+                step = split(tails[n * count + order[late[n], p]][:, :face])
+                link(n, p, step, rows_high, rows_low, row)
             for n in range(size):
                 mapped[n] = pack_map(row[n][:, :face], tracers)
 

time: 34.1 us -> 33.8 us (level)
  no operation moved by 1% of the time
where the time goes in v11:
time: 33.8 us; the launch traced here: 33.6 us
  Pallas kernels  21 us (62%)
  starting transfers between devices  9.71 us (29%)
  waiting for transfers between devices  2.57 us (8%)
  between operations  0.34 us (1%)
    pallas_call x20, Pallas kernels, run(): pl.pallas_call(body, name=name, in_specs=[pl.BlockSpec(memory_space=space...  21 us
    ppermute x6, starting transfers between devices, swap(): lax.ppermute(value, 'stream', [(i, i ^ 1 << stage) for i in range(streams)])  4.93 us
    ppermute x2, starting transfers between devices, to_next(): lax.ppermute(value, 'lat', [(i, (i + 1) % lats) for i in range(lats)])  4.77 us
    ppermute x6, waiting for transfers between devices, swap(): lax.ppermute(value, 'stream', [(i, i ^ 1 << stage) for i in range(streams)])  2.56 us
  transfers between devices with their start and end apart: 8, of which 5 were waited for; matrix products, arithmetic and copies ran while one was open for 0% of the time, Pallas kernels for 49%

profile of v11, /device:TPU:0, one launch (start us, length us, event | category | flops | bytes accessed | tf_op | source)
XLA Modules:
  0.0 33.6 jit_solution(13522755582702088312)
XLA Ops:
  0.0 1.8 %load.1 = (s32[2,4]{1,0:T(2,128)S(4)}, f32[1,256]{1,0:T(1,128)S(1)}, f32[1,256]{1,0:T(1,128)S(1)}, f32[2,64,256]{2,1,0:T(8,128)S(1)}, f32[4,64,256]{2,1,0:T(8,12...) custom-call(s32[2,4]{1,0:T(2,128)} %bitcast.5, ...), custom_call_target="tpu_custom_call" | custom-call | tf_op jit(solution)/shard_map/load/pallas_call | solution.py:21
  1.9 3.0 %collective-permute-start.3 = (f32[4,64,256]{2,1,0:T(8,128)S(1)}, f32[4,64,256]{2,1,0:T(8,128)S(1)}, u32[]{:S(2)}, u32[]{:S(2)}) collective-permute-start(f32[4,64,256]{2,1,0:T(8,128)S(1)} %old_trace.1), channel_id=1, source_target_pairs={{0,1},{1,2},{2,3},{3,4},{4,5},{5,6},{6,7},{7,0},{8,9},{9,10},{10,1... | collective-permute-start | bytes 786440 | tf_op jit(solution)/shard_map/ppermute | solution.py:123
  4.9 1.1 %begin_early.1 = (f32[4,64,128]{2,1,0:T(8,128)S(1)}, f32[4,64,256]{2,1,0:T(8,128)S(1)}, f32[1,80,256]{2,1,0:T(8,128)S(1)}) custom-call(s32[2,4]{1,0:T(2,128)S(4)} %get-tuple-element.58.order, f32[2,64,256]{2,1,0:T(8,128)S(1)} %get-tuple-element.59.inlet, f32[4,64,256]{2,1,0:T(8,128)S(1)} %get-tuple-element.60.near.sides, ...), custom_call_target="tpu_custom_call" | custom-call | tf_op jit(solution)/shard_map/begin_early/pallas_call | solution.py:21
  6.0 0.1 collective-permute-start
  6.1 1.0 %early_maps.1 = (bf16[4,512,384]{2,1,0:T(8,128)(2,1)S(1)}, bf16[4,64,384]{2,1,0:T(8,128)(2,1)S(1)}, bf16[1,320,256]{2,1,0:T(8,128)(2,1)S(1)}, bf16[1,320,256]{2,1,0:T(8,128)(2,1)S(1)}) custom-call(s32[2,4]{1,0:T(2,128)S(4)} %get-tuple-element.58.order, bf16[2,1,4,512,512]{4,3,2,1,0:T(8,128)(2,1)S(1)} %copy-done, bf16[2,1,4,64,512]{4,3,2,1,0:T(8,128)(2,1)S(1)} %copy-done.2, ...), custom_call_target="tpu_custom_call" | custom-call | tf_op jit(solution)/shard_map/early_maps/pallas_call | solution.py:21
  7.1 0.2 collective-permute-done.other.refs_0_.refs_1_.refs_9_
  7.3 0.2 combine.3._
  7.5 1.6 %collective-permute-start.1 = (f32[1,64,256]{2,1,0:T(8,128)S(1)}, f32[1,64,256]{2,1,0:T(8,128)S(1)}, u32[]{:S(2)}, u32[]{:S(2)}) collective-permute-start(f32[1,64,256]{2,1,0:T(8,128)S(1)} %combine.3._), channel_id=1, source_target_pairs={{0,16},{8,24},{16,0},{24,8},{1,17},{9,25},{17,1},{25,9},{2,18},{10... | collective-permute-start | bytes 196616 | tf_op jit(solution)/shard_map/ppermute | solution.py:126
  9.1 0.8 %late_maps.1.refs_3_.maps.refs_12_.refs_10_ = bf16[4,512,384]{2,1,0:T(8,128)(2,1)S(1)} custom-call(bf16[2,1,4,512,512]{4,3,2,1,0:T(8,128)(2,1)S(1)} %copy-done, bf16[2,1,4,64,512]{4,3,2,1,0:T(8,128)(2,1)S(1)} %copy-done.2, bf16[2,1,4,64,512]{4,3,2,1,0:T(8,128)(2,1)S(1)} %copy-done.3, f32[1,64,256]{2,1,0:T(8,128)S(1)} %combine.3._), custom_call_target="tpu_custom_call" | custom-call | tf_op jit(solution)/shard_map/late_maps/pallas_call | solution.py:21
  9.9 1.9 %prepare.2 = (f32[4,512,256]{2,1,0:T(8,128)S(1)}, f32[1,256,256]{2,1,0:T(8,128)S(1)}, bf16[1,256,64]{2,1,0:T(8,128)(2,1)S(1)}, bf16[1,256,64]{2,1,0:T(8,128)(2,1)S(1)}) custom-call(bf16[2,1,4,512,512]{4,3,2,1,0:T(8,128)(2,1)S(1)} %copy-done, f32[4,64,256]{2,1,0:T(8,128)S(1)} %get-tuple-element.60.near.sides, ...), custom_call_target="tpu_custom_call" | custom-call | tf_op jit(solution)/shard_map/prepare/pallas_call | solution.py:21
  11.9 0.5 %enter.2 = (bf16[4,192,256]{2,1,0:T(8,128)(2,1)S(1)}, f32[4,64,256]{2,1,0:T(8,128)S(1)}) custom-call(s32[2,4]{1,0:T(2,128)S(4)} %get-tuple-element.58.order, f32[2,64,256]{2,1,0:T(8,128)S(1)} %get-tuple-element.59.inlet, f32[1,256,256]{2,1,0:T(8,128)S(1)} %get-tuple-element.70.within, bf16[1,256,64]{2,1,0:T(8,128)(2,1)S(1)} %get-tuple-element.71.reach_high.refs_2_, ...), custom_call_target="tpu_custom_call" | custom-call | tf_op jit(solution)/shard_map/enter/pallas_call | solution.py:21
  12.4 1.8 %collective-permute-start.2 = (f32[4,64,256]{2,1,0:T(8,128)S(1)}, f32[4,64,256]{2,1,0:T(8,128)S(1)}, u32[]{:S(2)}, u32[]{:S(2)}) collective-permute-start(f32[4,64,256]{2,1,0:T(8,128)S(1)} %get-tuple-element.75._), channel_id=1, source_target_pairs={{0,1},{1,2},{2,3},{3,4},{4,5},{5,6},{6,7},{7,0},{8,9},{9,10},{10,1... | collective-permute-start | bytes 786440 | tf_op jit(solution)/shard_map/ppermute | solution.py:123
  14.2 1.4 %begin_late.1 = (bf16[4,512,256]{2,1,0:T(8,128)(2,1)S(1)}, bf16[4,512,256]{2,1,0:T(8,128)(2,1)S(1)}, f32[4,64,256]{2,1,0:T(8,128)S(1)}, f32[4,64,128]{2,1,0:T(8,...) custom-call(s32[2,4]{1,0:T(2,128)S(4)} %get-tuple-element.58.order, ...), custom_call_target="tpu_custom_call" | custom-call | tf_op jit(solution)/shard_map/begin_late/pallas_call | solution.py:21
  15.6 0.5 %first_sides.1 = (f32[4,64,256]{2,1,0:T(8,128)S(1)}, f32[1,80,256]{2,1,0:T(8,128)S(1)}) custom-call(s32[2,4]{1,0:T(2,128)S(4)} %get-tuple-element.58.order, f32[2,64,256]{2,1,0:T(8,128)S(1)} %get-tuple-element.59.inlet, f32[4,64,256]{2,1,0:T(8,128)S(1)} %collective-permute-done.3.arrived.sides, f32[4,64,256]{2,1,0:T(8,128)S(1)} %get-tuple-element.80.own, ...), custom_call_target="tpu_custom_call" | custom-call | tf_op jit(solution)/shard_map/first_sides/pallas_call | solution.py:21
  16.1 0.1 collective-permute-start.4
  16.1 1.2 %second.2 = (bf16[4,512,256]{2,1,0:T(8,128)(2,1)S(1)}, bf16[4,512,256]{2,1,0:T(8,128)(2,1)S(1)}, f32[4,64,256]{2,1,0:T(8,128)S(1)}, f32[4,64,256]{2,1,0:T(8,128)S(1)}) custom-call(bf16[2,1,4,512,512]{4,3,2,1,0:T(8,128)(2,1)S(1)} %copy-done, bf16[4,512,384]{2,1,0:T(8,128)(2,1)S(1)} %get-tuple-element.66._.maps.refs_3_.refs_5_, ...), custom_call_target="tpu_custom_call" | custom-call | tf_op jit(solution)/shard_map/second/pallas_call | solution.py:21
  17.4 0.1 collective-permute-done.4.other.refs_0_.refs_3_.refs_18_
  17.4 0.2 combine.4._
  17.6 1.6 %collective-permute-start.5 = (f32[1,64,256]{2,1,0:T(8,128)S(1)}, f32[1,64,256]{2,1,0:T(8,128)S(1)}, u32[]{:S(2)}, u32[]{:S(2)}) collective-permute-start(f32[1,64,256]{2,1,0:T(8,128)S(1)} %combine.4._), channel_id=1, source_target_pairs={{0,16},{8,24},{16,0},{24,8},{1,17},{9,25},{17,1},{25,9},{2,18},{10... | collective-permute-start | bytes 196616 | tf_op jit(solution)/shard_map/ppermute | solution.py:126
  19.2 0.3 fold_sides.1
  19.5 1.9 %prepare.3 = (f32[4,512,256]{2,1,0:T(8,128)S(1)}, f32[1,256,256]{2,1,0:T(8,128)S(1)}, bf16[1,256,64]{2,1,0:T(8,128)(2,1)S(1)}, bf16[1,256,64]{2,1,0:T(8,128)(2,1)S(1)}) custom-call(bf16[2,1,4,512,512]{4,3,2,1,0:T(8,128)(2,1)S(1)} %copy-done, f32[4,64,256]{2,1,0:T(8,128)S(1)} %collective-permute-done.3.arrived.sides, ...), custom_call_target="tpu_custom_call" | custom-call | tf_op jit(solution)/shard_map/prepare/pallas_call | solution.py:21
  21.5 0.7 %collective-permute-done.5.refs_0_ = f32[1,64,256]{2,1,0:T(8,128)S(1)} collective-permute-done((f32[1,64,256]{2,1,0:T(8,128)S(1)}, f32[1,64,256]{2,1,0:T(8,128)S(1)}, u32[]{:S(2)}, u32[]{:S(2)}) %collective-permute-start.5) | collective-permute-done | bytes 65568 | tf_op jit(solution)/shard_map/ppermute | solution.py:126
  22.1 0.2 enter.3.stack
  22.4 1.2 %second.3 = (bf16[4,512,256]{2,1,0:T(8,128)(2,1)S(1)}, bf16[4,512,256]{2,1,0:T(8,128)(2,1)S(1)}, f32[4,64,256]{2,1,0:T(8,128)S(1)}, f32[4,64,256]{2,1,0:T(8,128)S(1)}) custom-call(bf16[2,1,4,512,512]{4,3,2,1,0:T(8,128)(2,1)S(1)} %copy-done, bf16[4,512,384]{2,1,0:T(8,128)(2,1)S(1)} %late_maps.1.refs_3_.maps.refs_12_.refs_10_, ...), custom_call_target="tpu_custom_call" | custom-call | tf_op jit(solution)/shard_map/second/pallas_call | solution.py:21
  23.6 0.5 %second_sides.1.own = f32[2,64,256]{2,1,0:T(8,128)S(1)} custom-call(s32[2,4]{1,0:T(2,128)S(4)} %get-tuple-element.58.order, f32[4,64,256]{2,1,0:T(8,128)S(1)} %collective-permute-done.2.arrived, f32[4,64,256]{2,1,0:T(8,128)S(1)} %get-tuple-element.86._.refs_0_.refs_6_, f32[4,64,256]{2,1,0:T(8,128)S(1)} %get-tuple-element.87.refs_1_.refs_7_, ...), custom_call_target="tpu_custom_call" | custom-call | tf_op jit(solution)/shard_map/second_sides/pallas_call | solution.py:21
  24.1 0.1 collective-permute-start.6
  24.2 1.3 %collective-permute-done.6.other.refs_0_ = f32[2,64,256]{2,1,0:T(8,128)S(1)} collective-permute-done((f32[2,64,256]{2,1,0:T(8,128)S(1)}, f32[2,64,256]{2,1,0:T(8,128)S(1)}, u32[]{:S(2)}, u32[]{:S(2)}) %collective-permute-start.6) | collective-permute-done | bytes 131104 | tf_op jit(solution)/shard_map/ppermute | solution.py:126
  25.5 0.3 combine.5._
  25.8 1.6 %collective-permute-start.7 = (f32[2,64,256]{2,1,0:T(8,128)S(1)}, f32[2,64,256]{2,1,0:T(8,128)S(1)}, u32[]{:S(2)}, u32[]{:S(2)}) collective-permute-start(f32[2,64,256]{2,1,0:T(8,128)S(1)} %combine.5._), channel_id=1, source_target_pairs={{0,16},{8,24},{16,0},{24,8},{1,17},{9,25},{17,1},{25,9},{2,18},{10... | collective-permute-start | bytes 393224 | tf_op jit(solution)/shard_map/ppermute | solution.py:126
  27.4 3.8 %settle.1 = (f32[4,512,256]{2,1,0:T(8,128)S(1)}, f32[1,256,256]{2,1,0:T(8,128)S(1)}, f32[4,512,256]{2,1,0:T(8,128)S(1)}, f32[1,256,256]{2,1,0:T(8,128)S(1)}) custom-call(s32[2,4]{1,0:T(2,128)S(4)} %get-tuple-element.58.order, f32[2,64,256]{2,1,0:T(8,128)S(1)} %get-tuple-element.59.inlet, f32[2,64,256]{2,1,0:T(8,128)S(1)} %combine.5._, ...), custom_call_target="tpu_custom_call" | custom-call | tf_op jit(solution)/shard_map/settle/pallas_call | solution.py:21
  31.2 0.3 collective-permute-done.7.refs_0_
  31.4 2.0 %result.1 = bf16[2,1,4,512,256]{4,3,2,1,0:T(8,128)(2,1)} custom-call(s32[2,4]{1,0:T(2,128)S(4)} %get-tuple-element.58.order, f32[2,64,256]{2,1,0:T(8,128)S(1)} %collective-permute-done.7.refs_0_, f32[1,256,256]{2,1,0:T(8,128)S(1)} %get-tuple-element.107.refs_1_, bf16[1,256,64]{2,1,0:T(8,128)(2,1)S(1)} %get-tuple-element.71.reach_high.refs_2_, ...), custom_call_target="tpu_custom_call" | custom-call | tf_op jit(solution)/shard_map/result/pallas_call | solution.py:21
  (12 shorter events, 0.1 us)
Async XLA Ops:
  1.8 3.1 %copy-start.2 = (bf16[2,1,4,64,512]{4,3,2,1,0:T(8,128)(2,1)S(1)}, bf16[2,1,4,64,512]{4,3,2,1,0:T(8,128)(2,1)}, u32[]{:S(2)}) copy-start(bf16[2,1,4,64,512]{4,3,2,1,0:T(8,128)(2,1)} %up.7) | copy-start | bytes 1572868
  1.8 3.0 %copy-start.3 = (bf16[2,1,4,64,512]{4,3,2,1,0:T(8,128)(2,1)S(1)}, bf16[2,1,4,64,512]{4,3,2,1,0:T(8,128)(2,1)}, u32[]{:S(2)}) copy-start(bf16[2,1,4,64,512]{4,3,2,1,0:T(8,128)(2,1)} %side.7) | copy-start | bytes 1572868
  1.8 4.2 %copy-start = (bf16[2,1,4,512,512]{4,3,2,1,0:T(8,128)(2,1)S(1)}, bf16[2,1,4,512,512]{4,3,2,1,0:T(8,128)(2,1)}, u32[]{:S(2)}) copy-start(bf16[2,1,4,512,512]{4,3,2,1,0:T(8,128)(2,1)} %inv.15) | copy-start | bytes 12582916
  1.9 13.7 %collective-permute-start.3 = (f32[4,64,256]{2,1,0:T(8,128)S(1)}, f32[4,64,256]{2,1,0:T(8,128)S(1)}, u32[]{:S(2)}, u32[]{:S(2)}) collective-permute-start(f32[4,64,256]{2,1,0:T(8,128)S(1)} %old_trace.1), channel_id=1, source_target_pairs={{0,1},{1,2},{2,3},{3,4},{4,5},{5,6},{6,7},{7,0},{8,9},{9,10},{10,1... | collective-permute-start | bytes 786440 | tf_op jit(solution)/shard_map/ppermute | solution.py:123
  6.0 1.3 %collective-permute-start = (f32[1,80,256]{2,1,0:T(8,128)S(1)}, f32[1,80,256]{2,1,0:T(8,128)S(1)}, u32[]{:S(2)}, u32[]{:S(2)}) collective-permute-start(f32[1,80,256]{2,1,0:T(8,128)S(1)} %get-tuple-element.65._.own.refs_0_), channel_id=1, source_target_pairs={{0,8},{8,0},{16,24},{24,16},{1,9},{9,1},{17,25},{25,17},{2,10},{10... | collective-permute-start | bytes 245768 | tf_op jit(solution)/shard_map/ppermute | solution.py:126
  7.5 4.3 %collective-permute-start.1 = (f32[1,64,256]{2,1,0:T(8,128)S(1)}, f32[1,64,256]{2,1,0:T(8,128)S(1)}, u32[]{:S(2)}, u32[]{:S(2)}) collective-permute-start(f32[1,64,256]{2,1,0:T(8,128)S(1)} %combine.3._), channel_id=1, source_target_pairs={{0,16},{8,24},{16,0},{24,8},{1,17},{9,25},{17,1},{25,9},{2,18},{10... | collective-permute-start | bytes 196616 | tf_op jit(solution)/shard_map/ppermute | solution.py:126
  11.9 2.3 %copy-start.1 = (bf16[2,1,4,512,256]{4,3,2,1,0:T(8,128)(2,1)S(1)}, bf16[2,1,4,512,256]{4,3,2,1,0:T(8,128)(2,1)}, u32[]{:S(2)}) copy-start(bf16[2,1,4,512,256]{4,3,2,1,0:T(8,128)(2,1)} %previous.3) | copy-start | bytes 6291460
  12.4 11.2 %collective-permute-start.2 = (f32[4,64,256]{2,1,0:T(8,128)S(1)}, f32[4,64,256]{2,1,0:T(8,128)S(1)}, u32[]{:S(2)}, u32[]{:S(2)}) collective-permute-start(f32[4,64,256]{2,1,0:T(8,128)S(1)} %get-tuple-element.75._), channel_id=1, source_target_pairs={{0,1},{1,2},{2,3},{3,4},{4,5},{5,6},{6,7},{7,0},{8,9},{9,10},{10,1... | collective-permute-start | bytes 786440 | tf_op jit(solution)/shard_map/ppermute | solution.py:123
  16.1 1.3 %collective-permute-start.4 = (f32[1,80,256]{2,1,0:T(8,128)S(1)}, f32[1,80,256]{2,1,0:T(8,128)S(1)}, u32[]{:S(2)}, u32[]{:S(2)}) collective-permute-start(f32[1,80,256]{2,1,0:T(8,128)S(1)} %get-tuple-element.85._.own.refs_2_), channel_id=1, source_target_pairs={{0,8},{8,0},{16,24},{24,16},{1,9},{9,1},{17,25},{25,17},{2,10},{10... | collective-permute-start | bytes 245768 | tf_op jit(solution)/shard_map/ppermute | solution.py:126
  17.6 4.5 %collective-permute-start.5 = (f32[1,64,256]{2,1,0:T(8,128)S(1)}, f32[1,64,256]{2,1,0:T(8,128)S(1)}, u32[]{:S(2)}, u32[]{:S(2)}) collective-permute-start(f32[1,64,256]{2,1,0:T(8,128)S(1)} %combine.4._), channel_id=1, source_target_pairs={{0,16},{8,24},{16,0},{24,8},{1,17},{9,25},{17,1},{25,9},{2,18},{10... | collective-permute-start | bytes 196616 | tf_op jit(solution)/shard_map/ppermute | solution.py:126
  24.1 1.4 %collective-permute-start.6 = (f32[2,64,256]{2,1,0:T(8,128)S(1)}, f32[2,64,256]{2,1,0:T(8,128)S(1)}, u32[]{:S(2)}, u32[]{:S(2)}) collective-permute-start(f32[2,64,256]{2,1,0:T(8,128)S(1)} %second_sides.1.own), channel_id=1, source_target_pairs={{0,8},{8,0},{16,24},{24,16},{1,9},{9,1},{17,25},{25,17},{2,10},{10... | collective-permute-start | bytes 393224 | tf_op jit(solution)/shard_map/ppermute | solution.py:126
  25.8 5.6 %collective-permute-start.7 = (f32[2,64,256]{2,1,0:T(8,128)S(1)}, f32[2,64,256]{2,1,0:T(8,128)S(1)}, u32[]{:S(2)}, u32[]{:S(2)}) collective-permute-start(f32[2,64,256]{2,1,0:T(8,128)S(1)} %combine.5._), channel_id=1, source_target_pairs={{0,16},{8,24},{16,0},{24,8},{1,17},{9,25},{17,1},{25,9},{2,18},{10... | collective-permute-start | bytes 393224 | tf_op jit(solution)/shard_map/ppermute | solution.py:126

commit v12 on v11

--- a/solution.py
+++ b/solution.py
@@ -337,17 +337,23 @@
         )
         return state.maps
 
-    def begin_late(after):
+    def late_sources(after):
+        def body(previous, rate, aff, _, source_high, source_low):
+            for i in range(len(late) * count):
+                lag = previous[at(late, i)].astype(F32)
+                source_high[i], source_low[i] = split(langmuir(lag, rate[...], aff[...]))
+
+        return run(body, "late_sources", [old_near, rate, aff, after], source_outs(len(late)), [])
+
+    def begin_late(sources, after):
         size = len(late)
         items = size * count
 
         def body(
-            order, inv, up, side, previous, rate, aff, _,
-            source_high, source_low, own, tails, rows_high, rows_low, mapped, row,
+            order, inv, up, side, source_high, source_low, _,
+            own, tails, rows_high, rows_low, mapped, row,
         ):
             for i in range(items):
-                lag = previous[at(late, i)].astype(F32)
-                source_high[i], source_low[i] = split(langmuir(lag, rate[...], aff[...]))
                 k = at(late, i)
                 tails[i] = face_maps(inv[*k, ending], up[k], side[k])
             for i in range(items):
@@ -362,14 +368,14 @@
         values = run(
             body,
             "begin_late",
-            [order, inv_near, up_near, side_near, old_near, rate, aff, after],
-            source_outs(size)
-            + [VMEM((items, face, tracers), F32)]
+            [order, inv_near, up_near, side_near, *sources, after],
+            [VMEM((items, face, tracers), F32)]
             + chain_outs(size)
             + [VMEM((size, packed, tracers), F32)],
             [VMEM((size, face, wide), F32)],
         )
-        state.source_high, state.source_low, state.own, state.tails, state.high, state.low, state.mapped = values
+        state.source_high, state.source_low = sources
+        state.own, state.tails, state.high, state.low, state.mapped = values
         return state
 
     def late_maps(after):
@@ -691,14 +697,14 @@
     begin_early(one)
     exchange_first(one, lambda: early_maps(one, one.message))
     prepare(early, one, one.near, one.sent[-1])
-    maps = late_maps(one.sent[-1])
-    trace = enter_first(early, one, maps)
+    sources = late_sources(one.sent[-1])
+    trace = enter_first(early, one, sources[0])
     arrived_next = to_next(trace)
-    two = begin_late(trace)
-    two.maps = maps
+    two = begin_late(sources, trace)
     states = [one, two]
     first_sides(two, arrived)
     exchange_first(two, lambda: second(early, one, two.message))
+    two.maps = late_maps(two.sent[-1])
     prepare(late, two, arrived, two.sent[-1])
     fold_sides(two.sent[-1])
     enter_first(late, two, None)

time: 33.8 us -> 33.7 us (level)
  waiting for transfers between devices: 2.57 us -> 2 us
  Pallas kernels: 21 us -> 21.4 us
    ppermute x6, waiting for transfers between devices: 2.56 us -> 1.99 us  [swap(): lax.ppermute(value, 'stream', [(i, i ^ 1 << stage) for i in range(streams)])]
    pallas_call x20 -> x21, Pallas kernels: 21 us -> 21.4 us  [run(): pl.pallas_call(body, name=name, in_specs=[pl.BlockSpec(memory_space=space...]
  transfers between devices with their start and end apart: 8 -> 8, of which waited for: 5 -> 5; matrix products, arithmetic and copies ran while one was open for 0% -> 0% of each run, Pallas kernels for 49% -> 50%
where the time goes in v12:
time: 33.7 us; the launch traced here: 33.5 us
  Pallas kernels  21.4 us (64%)
  starting transfers between devices  9.75 us (29%)
  waiting for transfers between devices  2 us (6%)
  between operations  0.34 us (1%)
    pallas_call x21, Pallas kernels, run(): pl.pallas_call(body, name=name, in_specs=[pl.BlockSpec(memory_space=space...  21.4 us
    ppermute x6, starting transfers between devices, swap(): lax.ppermute(value, 'stream', [(i, i ^ 1 << stage) for i in range(streams)])  4.98 us
    ppermute x2, starting transfers between devices, to_next(): lax.ppermute(value, 'lat', [(i, (i + 1) % lats) for i in range(lats)])  4.77 us
    ppermute x6, waiting for transfers between devices, swap(): lax.ppermute(value, 'stream', [(i, i ^ 1 << stage) for i in range(streams)])  1.99 us
  transfers between devices with their start and end apart: 8, of which 5 were waited for; matrix products, arithmetic and copies ran while one was open for 0% of the time, Pallas kernels for 50%

profile of v12, /device:TPU:0, one launch (start us, length us, event | category | flops | bytes accessed | tf_op | source)
XLA Modules:
  0.0 33.5 jit_solution(2703111578999241071)
XLA Ops:
  0.0 1.8 %load.1 = (s32[2,4]{1,0:T(2,128)S(4)}, f32[1,256]{1,0:T(1,128)S(1)}, f32[1,256]{1,0:T(1,128)S(1)}, f32[2,64,256]{2,1,0:T(8,128)S(1)}, f32[4,64,256]{2,1,0:T(8,12...) custom-call(s32[2,4]{1,0:T(2,128)} %bitcast.5, ...), custom_call_target="tpu_custom_call" | custom-call | tf_op jit(solution)/shard_map/load/pallas_call | solution.py:21
  1.9 3.0 %collective-permute-start.3 = (f32[4,64,256]{2,1,0:T(8,128)S(1)}, f32[4,64,256]{2,1,0:T(8,128)S(1)}, u32[]{:S(2)}, u32[]{:S(2)}) collective-permute-start(f32[4,64,256]{2,1,0:T(8,128)S(1)} %old_trace.1), channel_id=1, source_target_pairs={{0,1},{1,2},{2,3},{3,4},{4,5},{5,6},{6,7},{7,0},{8,9},{9,10},{10,1... | collective-permute-start | bytes 786440 | tf_op jit(solution)/shard_map/ppermute | solution.py:123
  4.9 1.1 %begin_early.1 = (f32[4,64,128]{2,1,0:T(8,128)S(1)}, f32[4,64,256]{2,1,0:T(8,128)S(1)}, f32[1,80,256]{2,1,0:T(8,128)S(1)}) custom-call(s32[2,4]{1,0:T(2,128)S(4)} %get-tuple-element.58.order, f32[2,64,256]{2,1,0:T(8,128)S(1)} %get-tuple-element.59.inlet, f32[4,64,256]{2,1,0:T(8,128)S(1)} %get-tuple-element.60.near.sides, ...), custom_call_target="tpu_custom_call" | custom-call | tf_op jit(solution)/shard_map/begin_early/pallas_call | solution.py:21
  6.0 0.1 collective-permute-start
  6.1 1.0 %early_maps.1 = (bf16[4,512,384]{2,1,0:T(8,128)(2,1)S(1)}, bf16[4,64,384]{2,1,0:T(8,128)(2,1)S(1)}, bf16[1,320,256]{2,1,0:T(8,128)(2,1)S(1)}, bf16[1,320,256]{2,1,0:T(8,128)(2,1)S(1)}) custom-call(s32[2,4]{1,0:T(2,128)S(4)} %get-tuple-element.58.order, bf16[2,1,4,512,512]{4,3,2,1,0:T(8,128)(2,1)S(1)} %copy-done, bf16[2,1,4,64,512]{4,3,2,1,0:T(8,128)(2,1)S(1)} %copy-done.2, ...), custom_call_target="tpu_custom_call" | custom-call | tf_op jit(solution)/shard_map/early_maps/pallas_call | solution.py:21
  7.1 0.2 collective-permute-done.other.refs_0_.refs_1_.refs_9_
  7.3 0.2 combine.3._
  7.5 1.6 %collective-permute-start.1 = (f32[1,64,256]{2,1,0:T(8,128)S(1)}, f32[1,64,256]{2,1,0:T(8,128)S(1)}, u32[]{:S(2)}, u32[]{:S(2)}) collective-permute-start(f32[1,64,256]{2,1,0:T(8,128)S(1)} %combine.3._), channel_id=1, source_target_pairs={{0,16},{8,24},{16,0},{24,8},{1,17},{9,25},{17,1},{25,9},{2,18},{10... | collective-permute-start | bytes 196616 | tf_op jit(solution)/shard_map/ppermute | solution.py:126
  9.1 0.7 %late_sources.1 = (bf16[4,512,256]{2,1,0:T(8,128)(2,1)S(1)}, bf16[4,512,256]{2,1,0:T(8,128)(2,1)S(1)}) custom-call(bf16[2,1,4,512,256]{4,3,2,1,0:T(8,128)(2,1)S(1)} %copy-done.1, f32[1,256]{1,0:T(1,128)S(1)} %get-tuple-element.75.rate, f32[1,256]{1,0:T(1,128)S(1)} %get-tuple-element.76.aff, f32[1,64,256]{2,1,0:T(8,128)S(1)} %combine.3._), custom_call_target="tpu_custom_call" | custom-call | tf_op jit(solution)/shard_map/late_sources/pallas_call | solution.py:21
  9.8 1.9 %prepare.2 = (f32[4,512,256]{2,1,0:T(8,128)S(1)}, f32[1,256,256]{2,1,0:T(8,128)S(1)}, bf16[1,256,64]{2,1,0:T(8,128)(2,1)S(1)}, bf16[1,256,64]{2,1,0:T(8,128)(2,1)S(1)}) custom-call(bf16[2,1,4,512,512]{4,3,2,1,0:T(8,128)(2,1)S(1)} %copy-done, f32[4,64,256]{2,1,0:T(8,128)S(1)} %get-tuple-element.60.near.sides, ...), custom_call_target="tpu_custom_call" | custom-call | tf_op jit(solution)/shard_map/prepare/pallas_call | solution.py:21
  11.8 0.1 collective-permute-done.1.refs_0_
  11.9 0.5 %enter.2 = (bf16[4,192,256]{2,1,0:T(8,128)(2,1)S(1)}, f32[4,64,256]{2,1,0:T(8,128)S(1)}) custom-call(s32[2,4]{1,0:T(2,128)S(4)} %get-tuple-element.58.order, f32[2,64,256]{2,1,0:T(8,128)S(1)} %get-tuple-element.59.inlet, f32[1,256,256]{2,1,0:T(8,128)S(1)} %get-tuple-element.70.within, bf16[1,256,64]{2,1,0:T(8,128)(2,1)S(1)} %get-tuple-element.71.reach_high.refs_2_, ...), custom_call_target="tpu_custom_call" | custom-call | tf_op jit(solution)/shard_map/enter/pallas_call | solution.py:21
  12.4 1.8 %collective-permute-start.2 = (f32[4,64,256]{2,1,0:T(8,128)S(1)}, f32[4,64,256]{2,1,0:T(8,128)S(1)}, u32[]{:S(2)}, u32[]{:S(2)}) collective-permute-start(f32[4,64,256]{2,1,0:T(8,128)S(1)} %get-tuple-element.78._), channel_id=1, source_target_pairs={{0,1},{1,2},{2,3},{3,4},{4,5},{5,6},{6,7},{7,0},{8,9},{9,10},{10,1... | collective-permute-start | bytes 786440 | tf_op jit(solution)/shard_map/ppermute | solution.py:123
  14.2 1.1 %begin_late.1 = (f32[4,64,256]{2,1,0:T(8,128)S(1)}, f32[4,64,128]{2,1,0:T(8,128)S(1)}, bf16[1,320,256]{2,1,0:T(8,128)(2,1)S(1)}, bf16[1,320,256]{2,1,0:T(8,128)(2,1)S(1)}, f32[1,16,256]{2,1,0:T(8,128)S(1)}) custom-call(s32[2,4]{1,0:T(2,128)S(4)} %get-tuple-element.58.order, bf16[2,1,4,512,512]{4,3,2,1,0:T(8,128)(2,1)S(1)} %copy-done, ...), custom_call_target="tpu_custom_call" | custom-call | tf_op jit(solution)/shard_map/begin_late/pallas_call | solution.py:21
  15.3 0.5 %first_sides.1 = (f32[4,64,256]{2,1,0:T(8,128)S(1)}, f32[1,80,256]{2,1,0:T(8,128)S(1)}) custom-call(s32[2,4]{1,0:T(2,128)S(4)} %get-tuple-element.58.order, f32[2,64,256]{2,1,0:T(8,128)S(1)} %get-tuple-element.59.inlet, f32[4,64,256]{2,1,0:T(8,128)S(1)} %collective-permute-done.3.arrived.sides, f32[4,64,256]{2,1,0:T(8,128)S(1)} %get-tuple-element.82.own, ...), custom_call_target="tpu_custom_call" | custom-call | tf_op jit(solution)/shard_map/first_sides/pallas_call | solution.py:21
  15.9 1.2 %second.2 = (bf16[4,512,256]{2,1,0:T(8,128)(2,1)S(1)}, bf16[4,512,256]{2,1,0:T(8,128)(2,1)S(1)}, f32[4,64,256]{2,1,0:T(8,128)S(1)}, f32[4,64,256]{2,1,0:T(8,128)S(1)}) custom-call(bf16[2,1,4,512,512]{4,3,2,1,0:T(8,128)(2,1)S(1)} %copy-done, bf16[4,512,384]{2,1,0:T(8,128)(2,1)S(1)} %get-tuple-element.66._.maps.refs_3_.refs_5_, ...), custom_call_target="tpu_custom_call" | custom-call | tf_op jit(solution)/shard_map/second/pallas_call | solution.py:21
  17.1 0.1 collective-permute-done.4.other.refs_0_.refs_3_.refs_18_
  17.1 0.2 combine.4._
  17.4 1.6 %collective-permute-start.5 = (f32[1,64,256]{2,1,0:T(8,128)S(1)}, f32[1,64,256]{2,1,0:T(8,128)S(1)}, u32[]{:S(2)}, u32[]{:S(2)}) collective-permute-start(f32[1,64,256]{2,1,0:T(8,128)S(1)} %combine.4._), channel_id=1, source_target_pairs={{0,16},{8,24},{16,0},{24,8},{1,17},{9,25},{17,1},{25,9},{2,18},{10... | collective-permute-start | bytes 196616 | tf_op jit(solution)/shard_map/ppermute | solution.py:126
  18.9 0.3 fold_sides.1
  19.3 0.8 %late_maps.1.maps.refs_12_.refs_10_ = bf16[4,512,384]{2,1,0:T(8,128)(2,1)S(1)} custom-call(bf16[2,1,4,512,512]{4,3,2,1,0:T(8,128)(2,1)S(1)} %copy-done, bf16[2,1,4,64,512]{4,3,2,1,0:T(8,128)(2,1)S(1)} %copy-done.2, bf16[2,1,4,64,512]{4,3,2,1,0:T(8,128)(2,1)S(1)} %copy-done.3, f32[1,64,256]{2,1,0:T(8,128)S(1)} %combine.4._), custom_call_target="tpu_custom_call" | custom-call | tf_op jit(solution)/shard_map/late_maps/pallas_call | solution.py:21
  20.1 1.9 %prepare.3 = (f32[4,512,256]{2,1,0:T(8,128)S(1)}, f32[1,256,256]{2,1,0:T(8,128)S(1)}, bf16[1,256,64]{2,1,0:T(8,128)(2,1)S(1)}, bf16[1,256,64]{2,1,0:T(8,128)(2,1)S(1)}) custom-call(bf16[2,1,4,512,512]{4,3,2,1,0:T(8,128)(2,1)S(1)} %copy-done, f32[4,64,256]{2,1,0:T(8,128)S(1)} %collective-permute-done.3.arrived.sides, ...), custom_call_target="tpu_custom_call" | custom-call | tf_op jit(solution)/shard_map/prepare/pallas_call | solution.py:21
  22.0 0.3 enter.3.stack
  22.3 1.2 %second.3 = (bf16[4,512,256]{2,1,0:T(8,128)(2,1)S(1)}, bf16[4,512,256]{2,1,0:T(8,128)(2,1)S(1)}, f32[4,64,256]{2,1,0:T(8,128)S(1)}, f32[4,64,256]{2,1,0:T(8,128)S(1)}) custom-call(bf16[2,1,4,512,512]{4,3,2,1,0:T(8,128)(2,1)S(1)} %copy-done, bf16[4,512,384]{2,1,0:T(8,128)(2,1)S(1)} %late_maps.1.maps.refs_12_.refs_10_, ...), custom_call_target="tpu_custom_call" | custom-call | tf_op jit(solution)/shard_map/second/pallas_call | solution.py:21
  23.5 0.5 %second_sides.1.own = f32[2,64,256]{2,1,0:T(8,128)S(1)} custom-call(s32[2,4]{1,0:T(2,128)S(4)} %get-tuple-element.58.order, f32[4,64,256]{2,1,0:T(8,128)S(1)} %collective-permute-done.2.arrived, f32[4,64,256]{2,1,0:T(8,128)S(1)} %get-tuple-element.88._.refs_0_.refs_6_, f32[4,64,256]{2,1,0:T(8,128)S(1)} %get-tuple-element.89.refs_1_.refs_7_, ...), custom_call_target="tpu_custom_call" | custom-call | tf_op jit(solution)/shard_map/second_sides/pallas_call | solution.py:21
  24.0 0.2 collective-permute-start.6
  24.2 1.2 %collective-permute-done.6.other.refs_0_ = f32[2,64,256]{2,1,0:T(8,128)S(1)} collective-permute-done((f32[2,64,256]{2,1,0:T(8,128)S(1)}, f32[2,64,256]{2,1,0:T(8,128)S(1)}, u32[]{:S(2)}, u32[]{:S(2)}) %collective-permute-start.6) | collective-permute-done | bytes 131104 | tf_op jit(solution)/shard_map/ppermute | solution.py:126
  25.4 0.3 combine.5._
  25.7 1.4 %collective-permute-start.7 = (f32[2,64,256]{2,1,0:T(8,128)S(1)}, f32[2,64,256]{2,1,0:T(8,128)S(1)}, u32[]{:S(2)}, u32[]{:S(2)}) collective-permute-start(f32[2,64,256]{2,1,0:T(8,128)S(1)} %combine.5._), channel_id=1, source_target_pairs={{0,16},{8,24},{16,0},{24,8},{1,17},{9,25},{17,1},{25,9},{2,18},{10... | collective-permute-start | bytes 393224 | tf_op jit(solution)/shard_map/ppermute | solution.py:126
  27.1 3.8 %settle.1 = (f32[4,512,256]{2,1,0:T(8,128)S(1)}, f32[1,256,256]{2,1,0:T(8,128)S(1)}, f32[4,512,256]{2,1,0:T(8,128)S(1)}, f32[1,256,256]{2,1,0:T(8,128)S(1)}) custom-call(s32[2,4]{1,0:T(2,128)S(4)} %get-tuple-element.58.order, f32[2,64,256]{2,1,0:T(8,128)S(1)} %get-tuple-element.59.inlet, f32[2,64,256]{2,1,0:T(8,128)S(1)} %combine.5._, ...), custom_call_target="tpu_custom_call" | custom-call | tf_op jit(solution)/shard_map/settle/pallas_call | solution.py:21
  30.9 0.4 %collective-permute-done.7.refs_0_ = f32[2,64,256]{2,1,0:T(8,128)S(1)} collective-permute-done((f32[2,64,256]{2,1,0:T(8,128)S(1)}, f32[2,64,256]{2,1,0:T(8,128)S(1)}, u32[]{:S(2)}, u32[]{:S(2)}) %collective-permute-start.7) | collective-permute-done | bytes 131104 | tf_op jit(solution)/shard_map/ppermute | solution.py:126
  31.3 2.0 %result.1 = bf16[2,1,4,512,256]{4,3,2,1,0:T(8,128)(2,1)} custom-call(s32[2,4]{1,0:T(2,128)S(4)} %get-tuple-element.58.order, f32[2,64,256]{2,1,0:T(8,128)S(1)} %collective-permute-done.7.refs_0_, f32[1,256,256]{2,1,0:T(8,128)S(1)} %get-tuple-element.107.refs_1_, bf16[1,256,64]{2,1,0:T(8,128)(2,1)S(1)} %get-tuple-element.71.reach_high.refs_2_, ...), custom_call_target="tpu_custom_call" | custom-call | tf_op jit(solution)/shard_map/result/pallas_call | solution.py:21
  (13 shorter events, 0.1 us)
Async XLA Ops:
  1.8 3.1 %copy-start.2 = (bf16[2,1,4,64,512]{4,3,2,1,0:T(8,128)(2,1)S(1)}, bf16[2,1,4,64,512]{4,3,2,1,0:T(8,128)(2,1)}, u32[]{:S(2)}) copy-start(bf16[2,1,4,64,512]{4,3,2,1,0:T(8,128)(2,1)} %up.7) | copy-start | bytes 1572868
  1.8 3.0 %copy-start.3 = (bf16[2,1,4,64,512]{4,3,2,1,0:T(8,128)(2,1)S(1)}, bf16[2,1,4,64,512]{4,3,2,1,0:T(8,128)(2,1)}, u32[]{:S(2)}) copy-start(bf16[2,1,4,64,512]{4,3,2,1,0:T(8,128)(2,1)} %side.7) | copy-start | bytes 1572868
  1.8 4.2 %copy-start = (bf16[2,1,4,512,512]{4,3,2,1,0:T(8,128)(2,1)S(1)}, bf16[2,1,4,512,512]{4,3,2,1,0:T(8,128)(2,1)}, u32[]{:S(2)}) copy-start(bf16[2,1,4,512,512]{4,3,2,1,0:T(8,128)(2,1)} %inv.15) | copy-start | bytes 12582916
  1.9 13.4 %collective-permute-start.3 = (f32[4,64,256]{2,1,0:T(8,128)S(1)}, f32[4,64,256]{2,1,0:T(8,128)S(1)}, u32[]{:S(2)}, u32[]{:S(2)}) collective-permute-start(f32[4,64,256]{2,1,0:T(8,128)S(1)} %old_trace.1), channel_id=1, source_target_pairs={{0,1},{1,2},{2,3},{3,4},{4,5},{5,6},{6,7},{7,0},{8,9},{9,10},{10,1... | collective-permute-start | bytes 786440 | tf_op jit(solution)/shard_map/ppermute | solution.py:123
  6.0 1.3 %collective-permute-start = (f32[1,80,256]{2,1,0:T(8,128)S(1)}, f32[1,80,256]{2,1,0:T(8,128)S(1)}, u32[]{:S(2)}, u32[]{:S(2)}) collective-permute-start(f32[1,80,256]{2,1,0:T(8,128)S(1)} %get-tuple-element.65._.own.refs_0_), channel_id=1, source_target_pairs={{0,8},{8,0},{16,24},{24,16},{1,9},{9,1},{17,25},{25,17},{2,10},{10... | collective-permute-start | bytes 245768 | tf_op jit(solution)/shard_map/ppermute | solution.py:126
  6.1 3.1 %copy-start.1 = (bf16[2,1,4,512,256]{4,3,2,1,0:T(8,128)(2,1)S(1)}, bf16[2,1,4,512,256]{4,3,2,1,0:T(8,128)(2,1)}, u32[]{:S(2)}) copy-start(bf16[2,1,4,512,256]{4,3,2,1,0:T(8,128)(2,1)} %previous.3) | copy-start | bytes 6291460
  7.5 4.3 %collective-permute-start.1 = (f32[1,64,256]{2,1,0:T(8,128)S(1)}, f32[1,64,256]{2,1,0:T(8,128)S(1)}, u32[]{:S(2)}, u32[]{:S(2)}) collective-permute-start(f32[1,64,256]{2,1,0:T(8,128)S(1)} %combine.3._), channel_id=1, source_target_pairs={{0,16},{8,24},{16,0},{24,8},{1,17},{9,25},{17,1},{25,9},{2,18},{10... | collective-permute-start | bytes 196616 | tf_op jit(solution)/shard_map/ppermute | solution.py:126
  12.4 11.1 %collective-permute-start.2 = (f32[4,64,256]{2,1,0:T(8,128)S(1)}, f32[4,64,256]{2,1,0:T(8,128)S(1)}, u32[]{:S(2)}, u32[]{:S(2)}) collective-permute-start(f32[4,64,256]{2,1,0:T(8,128)S(1)} %get-tuple-element.78._), channel_id=1, source_target_pairs={{0,1},{1,2},{2,3},{3,4},{4,5},{5,6},{6,7},{7,0},{8,9},{9,10},{10,1... | collective-permute-start | bytes 786440 | tf_op jit(solution)/shard_map/ppermute | solution.py:123
  15.8 1.3 %collective-permute-start.4 = (f32[1,80,256]{2,1,0:T(8,128)S(1)}, f32[1,80,256]{2,1,0:T(8,128)S(1)}, u32[]{:S(2)}, u32[]{:S(2)}) collective-permute-start(f32[1,80,256]{2,1,0:T(8,128)S(1)} %get-tuple-element.87._.own.refs_2_), channel_id=1, source_target_pairs={{0,8},{8,0},{16,24},{24,16},{1,9},{9,1},{17,25},{25,17},{2,10},{10... | collective-permute-start | bytes 245768 | tf_op jit(solution)/shard_map/ppermute | solution.py:126
  17.4 4.7 %collective-permute-start.5 = (f32[1,64,256]{2,1,0:T(8,128)S(1)}, f32[1,64,256]{2,1,0:T(8,128)S(1)}, u32[]{:S(2)}, u32[]{:S(2)}) collective-permute-start(f32[1,64,256]{2,1,0:T(8,128)S(1)} %combine.4._), channel_id=1, source_target_pairs={{0,16},{8,24},{16,0},{24,8},{1,17},{9,25},{17,1},{25,9},{2,18},{10... | collective-permute-start | bytes 196616 | tf_op jit(solution)/shard_map/ppermute | solution.py:126
  24.0 1.4 %collective-permute-start.6 = (f32[2,64,256]{2,1,0:T(8,128)S(1)}, f32[2,64,256]{2,1,0:T(8,128)S(1)}, u32[]{:S(2)}, u32[]{:S(2)}) collective-permute-start(f32[2,64,256]{2,1,0:T(8,128)S(1)} %second_sides.1.own), channel_id=1, source_target_pairs={{0,8},{8,0},{16,24},{24,16},{1,9},{9,1},{17,25},{25,17},{2,10},{10... | collective-permute-start | bytes 393224 | tf_op jit(solution)/shard_map/ppermute | solution.py:126
  25.7 5.6 %collective-permute-start.7 = (f32[2,64,256]{2,1,0:T(8,128)S(1)}, f32[2,64,256]{2,1,0:T(8,128)S(1)}, u32[]{:S(2)}, u32[]{:S(2)}) collective-permute-start(f32[2,64,256]{2,1,0:T(8,128)S(1)} %combine.5._), channel_id=1, source_target_pairs={{0,16},{8,24},{16,0},{24,8},{1,17},{9,25},{17,1},{25,9},{2,18},{10... | collective-permute-start | bytes 393224 | tf_op jit(solution)/shard_map/ppermute | solution.py:126

commit v13 on v12

--- a/solution.py
+++ b/solution.py
@@ -510,12 +510,14 @@
                 for r in got:
                     start = jnp.where(bit(stages - 1), r[n], start)
                 inflow = within[n] + dot_split((reach_high[n], reach_low[n]), split(start))
-                put_inflow(n, c, inflow, order, stack)
-            if last:
-                for j in range(count):
-                    i = (size - 1) * count + j
-                    part = dot(side_maps[i][:, : 3 * face], stack[i])
-                    refs[1][j] = lateral_rows(free.at[i], per_side) + part
+                for p in range(count):
+                    j = order[c, p]
+                    i = n * count + j
+                    rows = jnp.concatenate(stack_inflow(split(inflow[p * face : (p + 1) * face])), axis=0)
+                    stack[i] = rows
+                    if c == cols - 1:
+                        part = dot(side_maps[i][:, : 3 * face], rows)
+                        refs[1][j] = lateral_rows(free.at[i], per_side) + part
 
         outs = [VMEM((size * count, 3 * face, tracers), BF16)]
         if last:

time: 33.7 us -> 33.6 us (level)
  no operation moved by 1% of the time
where the time goes in v13:
time: 33.6 us; the launch traced here: 33.4 us
  Pallas kernels  21.3 us (63%)
  starting transfers between devices  9.75 us (29%)
  waiting for transfers between devices  1.99 us (6%)
  between operations  0.35 us (1%)
    pallas_call x21, Pallas kernels, run(): pl.pallas_call(body, name=name, in_specs=[pl.BlockSpec(memory_space=space...  21.3 us
    ppermute x6, starting transfers between devices, swap(): lax.ppermute(value, 'stream', [(i, i ^ 1 << stage) for i in range(streams)])  4.97 us
    ppermute x2, starting transfers between devices, to_next(): lax.ppermute(value, 'lat', [(i, (i + 1) % lats) for i in range(lats)])  4.77 us
    ppermute x6, waiting for transfers between devices, swap(): lax.ppermute(value, 'stream', [(i, i ^ 1 << stage) for i in range(streams)])  1.99 us
  transfers between devices with their start and end apart: 8, of which 5 were waited for; matrix products, arithmetic and copies ran while one was open for 0% of the time, Pallas kernels for 50%

profile of v13, /device:TPU:0, one launch (start us, length us, event | category | flops | bytes accessed | tf_op | source)
XLA Modules:
  0.0 33.4 jit_solution(2574491857835907372)
XLA Ops:
  0.0 1.8 %load.1 = (s32[2,4]{1,0:T(2,128)S(4)}, f32[1,256]{1,0:T(1,128)S(1)}, f32[1,256]{1,0:T(1,128)S(1)}, f32[2,64,256]{2,1,0:T(8,128)S(1)}, f32[4,64,256]{2,1,0:T(8,12...) custom-call(s32[2,4]{1,0:T(2,128)} %bitcast.5, ...), custom_call_target="tpu_custom_call" | custom-call | tf_op jit(solution)/shard_map/load/pallas_call | solution.py:21
  1.9 3.0 %collective-permute-start.3 = (f32[4,64,256]{2,1,0:T(8,128)S(1)}, f32[4,64,256]{2,1,0:T(8,128)S(1)}, u32[]{:S(2)}, u32[]{:S(2)}) collective-permute-start(f32[4,64,256]{2,1,0:T(8,128)S(1)} %old_trace.1), channel_id=1, source_target_pairs={{0,1},{1,2},{2,3},{3,4},{4,5},{5,6},{6,7},{7,0},{8,9},{9,10},{10,1... | collective-permute-start | bytes 786440 | tf_op jit(solution)/shard_map/ppermute | solution.py:123
  4.9 1.1 %begin_early.1 = (f32[4,64,128]{2,1,0:T(8,128)S(1)}, f32[4,64,256]{2,1,0:T(8,128)S(1)}, f32[1,80,256]{2,1,0:T(8,128)S(1)}) custom-call(s32[2,4]{1,0:T(2,128)S(4)} %get-tuple-element.58.order, f32[2,64,256]{2,1,0:T(8,128)S(1)} %get-tuple-element.59.inlet, f32[4,64,256]{2,1,0:T(8,128)S(1)} %get-tuple-element.60.near.sides, ...), custom_call_target="tpu_custom_call" | custom-call | tf_op jit(solution)/shard_map/begin_early/pallas_call | solution.py:21
  6.0 0.1 collective-permute-start
  6.1 1.0 %early_maps.1 = (bf16[4,512,384]{2,1,0:T(8,128)(2,1)S(1)}, bf16[4,64,384]{2,1,0:T(8,128)(2,1)S(1)}, bf16[1,320,256]{2,1,0:T(8,128)(2,1)S(1)}, bf16[1,320,256]{2,1,0:T(8,128)(2,1)S(1)}) custom-call(s32[2,4]{1,0:T(2,128)S(4)} %get-tuple-element.58.order, bf16[2,1,4,512,512]{4,3,2,1,0:T(8,128)(2,1)S(1)} %copy-done, bf16[2,1,4,64,512]{4,3,2,1,0:T(8,128)(2,1)S(1)} %copy-done.2, ...), custom_call_target="tpu_custom_call" | custom-call | tf_op jit(solution)/shard_map/early_maps/pallas_call | solution.py:21
  7.1 0.2 collective-permute-done.other.refs_0_.refs_1_.refs_9_
  7.3 0.2 combine.3._
  7.5 1.6 %collective-permute-start.1 = (f32[1,64,256]{2,1,0:T(8,128)S(1)}, f32[1,64,256]{2,1,0:T(8,128)S(1)}, u32[]{:S(2)}, u32[]{:S(2)}) collective-permute-start(f32[1,64,256]{2,1,0:T(8,128)S(1)} %combine.3._), channel_id=1, source_target_pairs={{0,16},{8,24},{16,0},{24,8},{1,17},{9,25},{17,1},{25,9},{2,18},{10... | collective-permute-start | bytes 196616 | tf_op jit(solution)/shard_map/ppermute | solution.py:126
  9.1 0.7 %late_sources.1 = (bf16[4,512,256]{2,1,0:T(8,128)(2,1)S(1)}, bf16[4,512,256]{2,1,0:T(8,128)(2,1)S(1)}) custom-call(bf16[2,1,4,512,256]{4,3,2,1,0:T(8,128)(2,1)S(1)} %copy-done.1, f32[1,256]{1,0:T(1,128)S(1)} %get-tuple-element.75.rate, f32[1,256]{1,0:T(1,128)S(1)} %get-tuple-element.76.aff, f32[1,64,256]{2,1,0:T(8,128)S(1)} %combine.3._), custom_call_target="tpu_custom_call" | custom-call | tf_op jit(solution)/shard_map/late_sources/pallas_call | solution.py:21
  9.8 1.9 %prepare.2 = (f32[4,512,256]{2,1,0:T(8,128)S(1)}, f32[1,256,256]{2,1,0:T(8,128)S(1)}, bf16[1,256,64]{2,1,0:T(8,128)(2,1)S(1)}, bf16[1,256,64]{2,1,0:T(8,128)(2,1)S(1)}) custom-call(bf16[2,1,4,512,512]{4,3,2,1,0:T(8,128)(2,1)S(1)} %copy-done, f32[4,64,256]{2,1,0:T(8,128)S(1)} %get-tuple-element.60.near.sides, ...), custom_call_target="tpu_custom_call" | custom-call | tf_op jit(solution)/shard_map/prepare/pallas_call | solution.py:21
  11.8 0.1 collective-permute-done.1.refs_0_
  11.9 0.5 %enter.2 = (bf16[4,192,256]{2,1,0:T(8,128)(2,1)S(1)}, f32[4,64,256]{2,1,0:T(8,128)S(1)}) custom-call(s32[2,4]{1,0:T(2,128)S(4)} %get-tuple-element.58.order, f32[2,64,256]{2,1,0:T(8,128)S(1)} %get-tuple-element.59.inlet, f32[1,256,256]{2,1,0:T(8,128)S(1)} %get-tuple-element.70.within, bf16[1,256,64]{2,1,0:T(8,128)(2,1)S(1)} %get-tuple-element.71.reach_high.refs_2_, ...), custom_call_target="tpu_custom_call" | custom-call | tf_op jit(solution)/shard_map/enter/pallas_call | solution.py:21
  12.4 1.8 %collective-permute-start.2 = (f32[4,64,256]{2,1,0:T(8,128)S(1)}, f32[4,64,256]{2,1,0:T(8,128)S(1)}, u32[]{:S(2)}, u32[]{:S(2)}) collective-permute-start(f32[4,64,256]{2,1,0:T(8,128)S(1)} %get-tuple-element.78._), channel_id=1, source_target_pairs={{0,1},{1,2},{2,3},{3,4},{4,5},{5,6},{6,7},{7,0},{8,9},{9,10},{10,1... | collective-permute-start | bytes 786440 | tf_op jit(solution)/shard_map/ppermute | solution.py:123
  14.1 1.1 %begin_late.1 = (f32[4,64,256]{2,1,0:T(8,128)S(1)}, f32[4,64,128]{2,1,0:T(8,128)S(1)}, bf16[1,320,256]{2,1,0:T(8,128)(2,1)S(1)}, bf16[1,320,256]{2,1,0:T(8,128)(2,1)S(1)}, f32[1,16,256]{2,1,0:T(8,128)S(1)}) custom-call(s32[2,4]{1,0:T(2,128)S(4)} %get-tuple-element.58.order, bf16[2,1,4,512,512]{4,3,2,1,0:T(8,128)(2,1)S(1)} %copy-done, ...), custom_call_target="tpu_custom_call" | custom-call | tf_op jit(solution)/shard_map/begin_late/pallas_call | solution.py:21
  15.2 0.5 %first_sides.1 = (f32[4,64,256]{2,1,0:T(8,128)S(1)}, f32[1,80,256]{2,1,0:T(8,128)S(1)}) custom-call(s32[2,4]{1,0:T(2,128)S(4)} %get-tuple-element.58.order, f32[2,64,256]{2,1,0:T(8,128)S(1)} %get-tuple-element.59.inlet, f32[4,64,256]{2,1,0:T(8,128)S(1)} %collective-permute-done.3.arrived.sides, f32[4,64,256]{2,1,0:T(8,128)S(1)} %get-tuple-element.82.own, ...), custom_call_target="tpu_custom_call" | custom-call | tf_op jit(solution)/shard_map/first_sides/pallas_call | solution.py:21
  15.8 1.2 %second.2 = (bf16[4,512,256]{2,1,0:T(8,128)(2,1)S(1)}, bf16[4,512,256]{2,1,0:T(8,128)(2,1)S(1)}, f32[4,64,256]{2,1,0:T(8,128)S(1)}, f32[4,64,256]{2,1,0:T(8,128)S(1)}) custom-call(bf16[2,1,4,512,512]{4,3,2,1,0:T(8,128)(2,1)S(1)} %copy-done, bf16[4,512,384]{2,1,0:T(8,128)(2,1)S(1)} %get-tuple-element.66._.maps.refs_3_.refs_5_, ...), custom_call_target="tpu_custom_call" | custom-call | tf_op jit(solution)/shard_map/second/pallas_call | solution.py:21
  17.0 0.1 collective-permute-done.4.other.refs_0_.refs_3_.refs_18_
  17.1 0.2 combine.4._
  17.3 1.6 %collective-permute-start.5 = (f32[1,64,256]{2,1,0:T(8,128)S(1)}, f32[1,64,256]{2,1,0:T(8,128)S(1)}, u32[]{:S(2)}, u32[]{:S(2)}) collective-permute-start(f32[1,64,256]{2,1,0:T(8,128)S(1)} %combine.4._), channel_id=1, source_target_pairs={{0,16},{8,24},{16,0},{24,8},{1,17},{9,25},{17,1},{25,9},{2,18},{10... | collective-permute-start | bytes 196616 | tf_op jit(solution)/shard_map/ppermute | solution.py:126
  18.9 0.3 fold_sides.1
  19.2 0.8 %late_maps.1.maps.refs_12_.refs_10_ = bf16[4,512,384]{2,1,0:T(8,128)(2,1)S(1)} custom-call(bf16[2,1,4,512,512]{4,3,2,1,0:T(8,128)(2,1)S(1)} %copy-done, bf16[2,1,4,64,512]{4,3,2,1,0:T(8,128)(2,1)S(1)} %copy-done.2, bf16[2,1,4,64,512]{4,3,2,1,0:T(8,128)(2,1)S(1)} %copy-done.3, f32[1,64,256]{2,1,0:T(8,128)S(1)} %combine.4._), custom_call_target="tpu_custom_call" | custom-call | tf_op jit(solution)/shard_map/late_maps/pallas_call | solution.py:21
  20.0 1.9 %prepare.3 = (f32[4,512,256]{2,1,0:T(8,128)S(1)}, f32[1,256,256]{2,1,0:T(8,128)S(1)}, bf16[1,256,64]{2,1,0:T(8,128)(2,1)S(1)}, bf16[1,256,64]{2,1,0:T(8,128)(2,1)S(1)}) custom-call(bf16[2,1,4,512,512]{4,3,2,1,0:T(8,128)(2,1)S(1)} %copy-done, f32[4,64,256]{2,1,0:T(8,128)S(1)} %collective-permute-done.3.arrived.sides, ...), custom_call_target="tpu_custom_call" | custom-call | tf_op jit(solution)/shard_map/prepare/pallas_call | solution.py:21
  22.0 0.3 enter.3.stack
  22.2 1.2 %second.3 = (bf16[4,512,256]{2,1,0:T(8,128)(2,1)S(1)}, bf16[4,512,256]{2,1,0:T(8,128)(2,1)S(1)}, f32[4,64,256]{2,1,0:T(8,128)S(1)}, f32[4,64,256]{2,1,0:T(8,128)S(1)}) custom-call(bf16[2,1,4,512,512]{4,3,2,1,0:T(8,128)(2,1)S(1)} %copy-done, bf16[4,512,384]{2,1,0:T(8,128)(2,1)S(1)} %late_maps.1.maps.refs_12_.refs_10_, ...), custom_call_target="tpu_custom_call" | custom-call | tf_op jit(solution)/shard_map/second/pallas_call | solution.py:21
  23.4 0.5 %second_sides.1.own = f32[2,64,256]{2,1,0:T(8,128)S(1)} custom-call(s32[2,4]{1,0:T(2,128)S(4)} %get-tuple-element.58.order, f32[4,64,256]{2,1,0:T(8,128)S(1)} %collective-permute-done.2.arrived, f32[4,64,256]{2,1,0:T(8,128)S(1)} %get-tuple-element.88._.refs_0_.refs_6_, f32[4,64,256]{2,1,0:T(8,128)S(1)} %get-tuple-element.89.refs_1_.refs_7_, ...), custom_call_target="tpu_custom_call" | custom-call | tf_op jit(solution)/shard_map/second_sides/pallas_call | solution.py:21
  23.9 0.2 collective-permute-start.6
  24.2 1.2 %collective-permute-done.6.other.refs_0_ = f32[2,64,256]{2,1,0:T(8,128)S(1)} collective-permute-done((f32[2,64,256]{2,1,0:T(8,128)S(1)}, f32[2,64,256]{2,1,0:T(8,128)S(1)}, u32[]{:S(2)}, u32[]{:S(2)}) %collective-permute-start.6) | collective-permute-done | bytes 131104 | tf_op jit(solution)/shard_map/ppermute | solution.py:126
  25.4 0.3 combine.5._
  25.6 1.4 %collective-permute-start.7 = (f32[2,64,256]{2,1,0:T(8,128)S(1)}, f32[2,64,256]{2,1,0:T(8,128)S(1)}, u32[]{:S(2)}, u32[]{:S(2)}) collective-permute-start(f32[2,64,256]{2,1,0:T(8,128)S(1)} %combine.5._), channel_id=1, source_target_pairs={{0,16},{8,24},{16,0},{24,8},{1,17},{9,25},{17,1},{25,9},{2,18},{10... | collective-permute-start | bytes 393224 | tf_op jit(solution)/shard_map/ppermute | solution.py:126
  27.0 3.8 %settle.1 = (f32[4,512,256]{2,1,0:T(8,128)S(1)}, f32[1,256,256]{2,1,0:T(8,128)S(1)}, f32[4,512,256]{2,1,0:T(8,128)S(1)}, f32[1,256,256]{2,1,0:T(8,128)S(1)}) custom-call(s32[2,4]{1,0:T(2,128)S(4)} %get-tuple-element.58.order, f32[2,64,256]{2,1,0:T(8,128)S(1)} %get-tuple-element.59.inlet, f32[2,64,256]{2,1,0:T(8,128)S(1)} %combine.5._, ...), custom_call_target="tpu_custom_call" | custom-call | tf_op jit(solution)/shard_map/settle/pallas_call | solution.py:21
  30.8 0.4 %collective-permute-done.7.refs_0_ = f32[2,64,256]{2,1,0:T(8,128)S(1)} collective-permute-done((f32[2,64,256]{2,1,0:T(8,128)S(1)}, f32[2,64,256]{2,1,0:T(8,128)S(1)}, u32[]{:S(2)}, u32[]{:S(2)}) %collective-permute-start.7) | collective-permute-done | bytes 131104 | tf_op jit(solution)/shard_map/ppermute | solution.py:126
  31.2 2.0 %result.1 = bf16[2,1,4,512,256]{4,3,2,1,0:T(8,128)(2,1)} custom-call(s32[2,4]{1,0:T(2,128)S(4)} %get-tuple-element.58.order, f32[2,64,256]{2,1,0:T(8,128)S(1)} %collective-permute-done.7.refs_0_, f32[1,256,256]{2,1,0:T(8,128)S(1)} %get-tuple-element.107.refs_1_, bf16[1,256,64]{2,1,0:T(8,128)(2,1)S(1)} %get-tuple-element.71.reach_high.refs_2_, ...), custom_call_target="tpu_custom_call" | custom-call | tf_op jit(solution)/shard_map/result/pallas_call | solution.py:21
  (13 shorter events, 0.1 us)
Async XLA Ops:
  1.8 3.1 %copy-start.2 = (bf16[2,1,4,64,512]{4,3,2,1,0:T(8,128)(2,1)S(1)}, bf16[2,1,4,64,512]{4,3,2,1,0:T(8,128)(2,1)}, u32[]{:S(2)}) copy-start(bf16[2,1,4,64,512]{4,3,2,1,0:T(8,128)(2,1)} %up.7) | copy-start | bytes 1572868
  1.8 3.0 %copy-start.3 = (bf16[2,1,4,64,512]{4,3,2,1,0:T(8,128)(2,1)S(1)}, bf16[2,1,4,64,512]{4,3,2,1,0:T(8,128)(2,1)}, u32[]{:S(2)}) copy-start(bf16[2,1,4,64,512]{4,3,2,1,0:T(8,128)(2,1)} %side.7) | copy-start | bytes 1572868
  1.8 4.2 %copy-start = (bf16[2,1,4,512,512]{4,3,2,1,0:T(8,128)(2,1)S(1)}, bf16[2,1,4,512,512]{4,3,2,1,0:T(8,128)(2,1)}, u32[]{:S(2)}) copy-start(bf16[2,1,4,512,512]{4,3,2,1,0:T(8,128)(2,1)} %inv.15) | copy-start | bytes 12582916
  1.9 13.4 %collective-permute-start.3 = (f32[4,64,256]{2,1,0:T(8,128)S(1)}, f32[4,64,256]{2,1,0:T(8,128)S(1)}, u32[]{:S(2)}, u32[]{:S(2)}) collective-permute-start(f32[4,64,256]{2,1,0:T(8,128)S(1)} %old_trace.1), channel_id=1, source_target_pairs={{0,1},{1,2},{2,3},{3,4},{4,5},{5,6},{6,7},{7,0},{8,9},{9,10},{10,1... | collective-permute-start | bytes 786440 | tf_op jit(solution)/shard_map/ppermute | solution.py:123
  6.0 1.3 %collective-permute-start = (f32[1,80,256]{2,1,0:T(8,128)S(1)}, f32[1,80,256]{2,1,0:T(8,128)S(1)}, u32[]{:S(2)}, u32[]{:S(2)}) collective-permute-start(f32[1,80,256]{2,1,0:T(8,128)S(1)} %get-tuple-element.65._.own.refs_0_), channel_id=1, source_target_pairs={{0,8},{8,0},{16,24},{24,16},{1,9},{9,1},{17,25},{25,17},{2,10},{10... | collective-permute-start | bytes 245768 | tf_op jit(solution)/shard_map/ppermute | solution.py:126
  6.1 3.1 %copy-start.1 = (bf16[2,1,4,512,256]{4,3,2,1,0:T(8,128)(2,1)S(1)}, bf16[2,1,4,512,256]{4,3,2,1,0:T(8,128)(2,1)}, u32[]{:S(2)}) copy-start(bf16[2,1,4,512,256]{4,3,2,1,0:T(8,128)(2,1)} %previous.3) | copy-start | bytes 6291460
  7.5 4.3 %collective-permute-start.1 = (f32[1,64,256]{2,1,0:T(8,128)S(1)}, f32[1,64,256]{2,1,0:T(8,128)S(1)}, u32[]{:S(2)}, u32[]{:S(2)}) collective-permute-start(f32[1,64,256]{2,1,0:T(8,128)S(1)} %combine.3._), channel_id=1, source_target_pairs={{0,16},{8,24},{16,0},{24,8},{1,17},{9,25},{17,1},{25,9},{2,18},{10... | collective-permute-start | bytes 196616 | tf_op jit(solution)/shard_map/ppermute | solution.py:126
  12.4 11.1 %collective-permute-start.2 = (f32[4,64,256]{2,1,0:T(8,128)S(1)}, f32[4,64,256]{2,1,0:T(8,128)S(1)}, u32[]{:S(2)}, u32[]{:S(2)}) collective-permute-start(f32[4,64,256]{2,1,0:T(8,128)S(1)} %get-tuple-element.78._), channel_id=1, source_target_pairs={{0,1},{1,2},{2,3},{3,4},{4,5},{5,6},{6,7},{7,0},{8,9},{9,10},{10,1... | collective-permute-start | bytes 786440 | tf_op jit(solution)/shard_map/ppermute | solution.py:123
  15.7 1.3 %collective-permute-start.4 = (f32[1,80,256]{2,1,0:T(8,128)S(1)}, f32[1,80,256]{2,1,0:T(8,128)S(1)}, u32[]{:S(2)}, u32[]{:S(2)}) collective-permute-start(f32[1,80,256]{2,1,0:T(8,128)S(1)} %get-tuple-element.87._.own.refs_2_), channel_id=1, source_target_pairs={{0,8},{8,0},{16,24},{24,16},{1,9},{9,1},{17,25},{25,17},{2,10},{10... | collective-permute-start | bytes 245768 | tf_op jit(solution)/shard_map/ppermute | solution.py:126
  17.3 4.7 %collective-permute-start.5 = (f32[1,64,256]{2,1,0:T(8,128)S(1)}, f32[1,64,256]{2,1,0:T(8,128)S(1)}, u32[]{:S(2)}, u32[]{:S(2)}) collective-permute-start(f32[1,64,256]{2,1,0:T(8,128)S(1)} %combine.4._), channel_id=1, source_target_pairs={{0,16},{8,24},{16,0},{24,8},{1,17},{9,25},{17,1},{25,9},{2,18},{10... | collective-permute-start | bytes 196616 | tf_op jit(solution)/shard_map/ppermute | solution.py:126
  23.9 1.4 %collective-permute-start.6 = (f32[2,64,256]{2,1,0:T(8,128)S(1)}, f32[2,64,256]{2,1,0:T(8,128)S(1)}, u32[]{:S(2)}, u32[]{:S(2)}) collective-permute-start(f32[2,64,256]{2,1,0:T(8,128)S(1)} %second_sides.1.own), channel_id=1, source_target_pairs={{0,8},{8,0},{16,24},{24,16},{1,9},{9,1},{17,25},{25,17},{2,10},{10... | collective-permute-start | bytes 393224 | tf_op jit(solution)/shard_map/ppermute | solution.py:126
  25.6 5.6 %collective-permute-start.7 = (f32[2,64,256]{2,1,0:T(8,128)S(1)}, f32[2,64,256]{2,1,0:T(8,128)S(1)}, u32[]{:S(2)}, u32[]{:S(2)}) collective-permute-start(f32[2,64,256]{2,1,0:T(8,128)S(1)} %combine.5._), channel_id=1, source_target_pairs={{0,16},{8,24},{16,0},{24,8},{1,17},{9,25},{17,1},{25,9},{2,18},{10... | collective-permute-start | bytes 393224 | tf_op jit(solution)/shard_map/ppermute | solution.py:126
